TPU v7x, 128 devices: a whole 4x4x4 slice. The times are simulated.
128 devices in a mesh: seq: 32 (over z, y, core), exp: 4 (over x).
Axes of the slice: x: 4, y: 4, z: 4, core: 2. Of those that a mesh axis runs over, the one named last changes fastest.
Arguments:
- queries: bfloat16 [2, 8192, 4096], P(None, 'seq', 'exp'), may hold values from -6 to 6
- keys: bfloat16 [2, 8192, 4096], P(None, 'seq', 'exp'), may hold values from -6 to 6
- payload_vectors: bfloat16 [2, 8192, 4096], P(None, 'seq', 'exp'), may hold values from -6 to 6
- log_decay: float32 [2, 8192, 32], P(None, 'seq', 'exp'), may hold values from -1 to 0
- attn_gain: float32 [4096], P('exp'), may hold values from 0.5 to 1.5
- out_weight: bfloat16 [4096, 6144], P('exp', 'seq'), may hold values from -0.09375 to 0.09375
- residual: bfloat16 [2, 8192, 6144], P(None, ('seq', 'exp')), may hold values from -12 to 12
- norm_gain: float32 [6144], replicated, may hold values from 0.5 to 1.5
- router_weight: bfloat16 [6144, 32], replicated, may hold values from -0.078125 to 0.078125
- picks: int32 [2, 8192, 2], P(None, ('seq', 'exp')), may hold values from 0 to 31, as said below
- gate_weight: bfloat16 [4, 9216, 6144], P('exp', 'seq'), may hold values from -0.078125 to 0.078125
- up_weight: bfloat16 [4, 9216, 6144], P('exp', 'seq'), may hold values from -0.078125 to 0.078125
- down_weight: bfloat16 [4, 9216, 6144], P('exp', 'seq'), may hold values from -0.0625 to 0.0625
Outputs:
- layer_out: bfloat16 [2, 8192, 6144], P(None, ('seq', 'exp'))
Inputs may be any that keep to these rules, and one draw needn't show every extreme that they name: `picks`: each row names two different experts; among the 128 rows of one device (its positions of every sequence) each expert below 4 is named at most 12 times, and one of them exactly 12 times.
All inputs are finite; a program needn't handle non-finite values.
Results may differ from a plain program's by a relative error of at most 0.015.
Values may be sent and summed in bfloat16 or wider, within the bound.
No kernel may reach another device: no remote copies, remote signals or barrier semaphores. Data moves between devices by JAX's collectives and lax.ppermute only.
A program may use at most 192 MiB of HBM per device.

v0:
```python
import jax
import jax.numpy as jnp
from jax import lax
from jax.sharding import PartitionSpec as P

HEAD = 128


highest = lax.Precision.HIGHEST


def carried_in(shard, axis, combine, identity):
    length, position = (lax.axis_size(axis), lax.axis_index(axis))
    everything = jax.tree.map(lambda part: lax.all_gather(part, axis), shard)
    start = jax.tree.map(
        lambda part, zero: jnp.broadcast_to(jnp.asarray(zero, part.dtype), part.shape),
        shard,
        identity,
    )

    def hop(k, before):
        reached = k < position
        new = combine(before, jax.tree.map(lambda part: part[k], everything))
        return jax.tree.map(lambda a, b: jnp.where(reached, a, b), new, before)

    return lax.fori_loop(0, length, hop, start)


def block_parts(q_blk, k_blk, v_blk, d_blk):
    vf = v_blk.astype(jnp.float32)
    cum = jnp.cumsum(d_blk, axis=1)
    scores = jnp.einsum("sthd,sjhd->shtj", q_blk, k_blk, preferred_element_type=jnp.float32)
    turned = jnp.transpose(cum, (0, 2, 1))
    spread = turned[:, :, :, None] - turned[:, :, None, :]
    steps = cum.shape[1]
    later = lax.broadcasted_iota(jnp.int32, (steps, steps), 0) >= lax.broadcasted_iota(
        jnp.int32, (steps, steps), 1
    )
    weights = jnp.where(later, jnp.exp(jnp.minimum(spread, 0.0)), 0.0) * scores
    inner = jnp.einsum("shtj,sjhd->sthd", weights, vf, precision=highest)
    final = cum[:, -1, :]
    qscaled = q_blk.astype(jnp.float32) * jnp.exp(cum)[..., None]
    kscaled = k_blk.astype(jnp.float32) * jnp.exp(final[:, None, :] - cum)[..., None]
    update = jnp.einsum("sjhd,sjhe->shde", kscaled, vf, precision=highest)
    return (inner, qscaled, jnp.exp(final), update)


def link(earlier, later):
    return (earlier[0] * later[0], later[0][:, :, None, None] * earlier[1] + later[1])


def carried_output(parts, state_in):
    return parts[0] + jnp.einsum("sthd,shde->sthe", parts[1], state_in, precision=highest)


def gate_pair(inputs, routes, router_weight):
    logits = jnp.dot(inputs, router_weight, preferred_element_type=jnp.float32)
    labels = lax.broadcasted_iota(jnp.int32, (1, logits.shape[1]), 1)
    first = jnp.sum(jnp.where(routes[:, 0:1] == labels, logits, 0.0), -1)
    second = jnp.sum(jnp.where(routes[:, 1:2] == labels, logits, 0.0), -1)
    return (jax.nn.sigmoid(first - second), jax.nn.sigmoid(second - first))


def shards(
    queries,
    keys,
    payload_vectors,
    log_decay,
    attn_gain,
    out_weight,
    residual,
    norm_gain,
    router_weight,
    picks,
    gate_weight,
    up_weight,
    down_weight,
):
    seq_count, positions, width = queries.shape
    heads_here = width // HEAD

    def heads_view(array):
        return array.reshape(array.shape[0], positions, heads_here, HEAD)

    q_all = heads_view(queries)
    k_all = heads_view(keys)
    v_all = heads_view(payload_vectors)
    parts = block_parts(q_all, k_all, v_all, log_decay)
    initial = (jnp.ones_like(parts[2]), jnp.zeros_like(parts[3]))
    prefix = carried_in((parts[2], parts[3]), "seq", link, initial)
    head_out = carried_output(parts, prefix[1])
    gains = attn_gain.reshape(heads_here, HEAD)
    normed = (
        head_out * lax.rsqrt(jnp.mean(head_out * head_out, -1, keepdims=True) + 1e-06) * gains
    ).astype(jnp.bfloat16)
    slice_len = residual.shape[1]
    rows_here = seq_count * slice_len
    shares_all = positions // slice_len
    ordered = (
        normed.reshape(seq_count, shares_all, slice_len, width)
        .transpose(1, 0, 2, 3)
        .reshape(shares_all * rows_here, width)
    )
    projected = jnp.dot(
        ordered,
        lax.all_gather(out_weight, "seq", axis=1, tiled=True),
        preferred_element_type=jnp.float32,
    )
    mixed = lax.psum_scatter(
        projected.astype(jnp.bfloat16), "exp", scatter_dimension=0, tiled=True
    ).astype(jnp.float32)
    hidden_state = residual.reshape(rows_here, -1).astype(jnp.float32) + mixed
    moe_in = (
        hidden_state
        * lax.rsqrt(jnp.mean(hidden_state * hidden_state, -1, keepdims=True) + 1e-06)
        * norm_gain
    ).astype(jnp.bfloat16)
    routes = picks.reshape(rows_here, 2)
    flight = lax.axis_size("exp")
    experts = router_weight.shape[1]
    capacity = max(2, 3 * rows_here // 32, 2 * ((rows_here + experts - 2) // (experts - 1)))
    gathered_rows, gathered_routes = (
        lax.all_gather(moe_in, "exp", axis=0, tiled=True),
        lax.all_gather(routes.astype(jnp.bfloat16), "exp", axis=0, tiled=True),
    )
    all_routes = gathered_routes.astype(jnp.int32)
    first_gate, second_gate = gate_pair(gathered_rows, all_routes, router_weight)
    mine = lax.axis_index("exp")
    hit_first = all_routes[:, 0] == mine
    hit_second = all_routes[:, 1] == mine
    chosen = (hit_first | hit_second).astype(jnp.int32)
    weight = jnp.where(hit_first, first_gate, 0.0) + jnp.where(hit_second, second_gate, 0.0)
    rank = jnp.cumsum(chosen) - chosen
    slot_ids = lax.broadcasted_iota(jnp.int32, (1, flight * capacity), 1)
    place = (rank[:, None] == slot_ids) & (chosen[:, None] > 0)
    outgoing = jnp.einsum(
        "rc,rd->cd", place.astype(jnp.bfloat16), gathered_rows, preferred_element_type=jnp.float32
    ).astype(jnp.bfloat16)
    piece = lax.all_gather(outgoing, "seq", axis=0, tiled=True)
    gate = lax.dot_general(
        piece, gate_weight[0], (((1,), (1,)), ((), ())), preferred_element_type=jnp.float32
    )
    upper = lax.dot_general(
        piece, up_weight[0], (((1,), (1,)), ((), ())), preferred_element_type=jnp.float32
    )
    hidden_all = (jax.nn.silu(gate) * upper).astype(jnp.bfloat16)
    summed = lax.psum_scatter(
        jnp.dot(hidden_all, down_weight[0], preferred_element_type=jnp.float32).astype(
            jnp.bfloat16
        ),
        "seq",
        scatter_dimension=0,
        tiled=True,
    )
    served = summed.astype(jnp.float32)
    scatter_weights = place.astype(jnp.float32) * weight[:, None]

    def spread(start, count):
        return jnp.dot(scatter_weights, served, precision=highest)

    moe = lax.psum_scatter(
        spread(jnp.int32(0), rows_here * lax.axis_size("exp")),
        "exp",
        scatter_dimension=0,
        tiled=True,
    )
    return (hidden_state + moe).astype(jnp.bfloat16).reshape(seq_count, slice_len, -1)


def solution(mesh):
    placed = (
        P(None, "seq", "exp"),
        P(None, "seq", "exp"),
        P(None, "seq", "exp"),
        P(None, "seq", "exp"),
        P("exp"),
        P("exp", "seq"),
        P(None, ("seq", "exp"), None),
        P(),
        P(),
        P(None, ("seq", "exp"), None),
        P("exp", "seq", None),
        P("exp", "seq", None),
        P("exp", "seq", None),
    )
    return jax.shard_map(
        shards, mesh=mesh, in_specs=placed, out_specs=P(None, ("seq", "exp"), None), check_vma=False
    )
```

profile of v0, /device:TPU:0, one launch (start us, length us, event | category | flops | bytes accessed | tf_op | source)
XLA Modules:
  0.0 781.8 jit_solution(5310215688362074520)
XLA Ops:
  20.5 3.8 fusion.21
  26.8 28.7 %all-gather = f32[64,1,8]{2,1,0:T(1,128)} all-gather(f32[2,1,8]{2,1,0:T(1,128)} %bitcast.120), channel_id=2, replica_groups=mesh['seq'=32,'exp'=4] {'seq'}, dimensions={0}, use_global_device_ids=true | all-gather | bytes 2112 | tf_op jit(solution)/shard_map/all_gather | solution.py:14
  57.8 4.9 fusion.1
  62.7 78.2 %all-gather.13.cloned.1.call-done = f32[64,8,128,128]{3,2,1,0:T(8,128)} async-done(((f32[2,8,128,128]{3,2,1,0:T(8,128)}), f32[64,8,128,128]{3,2,1,0:T(8,128)}) %all-gather.13.cloned.1.call-update) | async-done | bytes 33554448 | tf_op jit(solution)/shard_map/all_gather | solution.py:14
  141.0 108.0 %while.14 = (s32[]{:T(128)}, f32[2,8,128,128]{3,2,1,0:T(8,128)}, s32[]{:T(128)}, f32[32,2,8]{2,1,0:T(2,128)}, f32[32,2,8,128,128]{4,3,2,1,0:T(8,128)}, /*index=5*/s32[]{:T(128)}, s32[]{:T(128)}) while((s32[]{:T(128)}, f32[2,8,128,128]{3,2,1,0:T(8,128)}, s32[]{:T(128)}, f32[32,2,8]{2,1,0:T(2,128)}, ...), condition=%wide.region_3.4_spmd.clone, body=%wide.region_2.3_spmd.clone.sunk | while | flops 1048580 | bytes 3146025 | solution.py:26
  148.0 2.7 fusion.74
  151.4 2.8 fusion.74
  154.8 2.7 fusion.74
  158.2 2.7 fusion.74
  161.6 2.7 fusion.74
  165.0 2.7 fusion.74
  175.1 2.7 fusion.74
  181.9 2.7 fusion.74
  185.2 2.8 fusion.74
  188.7 2.8 fusion.74
  192.2 2.7 fusion.74
  195.6 2.9 fusion.74
  199.2 2.7 fusion.74
  249.0 5.0 multiply_reduce_fusion.1
  262.4 11.7 %convolution_convert_fusion.1 = bf16[512,6144]{1,0:T(8,128)(2,1)} fusion(bf16[512,1024]{1,0:T(8,128)(2,1)} %bitcast.106, bf16[1024,6144]{0,1:T(8,128)(2,1)} %all-gather.7.cloned.1.call-done), kind=kOutput, calls=%fused_computation.4 | convolution fusion | flops 6445596672 | bytes 19922944 | tf_op jit(solution)/shard_map/dot_general | solution.py:104
  274.1 63.2 %reduce-scatter.4.cloned.1.call-done = bf16[128,6144]{1,0:T(8,128)(2,1)} async-done(((bf16[512,6144]{1,0:T(8,128)(2,1)}), bf16[128,6144]{1,0:T(8,128)(2,1)}) %reduce-scatter.4.cloned.1.call-update) | async-done | bytes 1572880 | tf_op jit(solution)/shard_map/reduce_scatter | solution.py:109
  342.8 8.0 %all_gather.26 = bf16[512,2]{0,1:T(2,128)(2,1)S(1)} all-gather(bf16[128,2]{0,1:T(2,128)(2,1)S(1)} %convert_element_type.68), channel_id=1, replica_groups=mesh['seq'=32,'exp'=4] {'exp'}, dimensions={0}, use_global_device_ids=true | all-gather | bytes 2560 | tf_op jit(solution)/shard_map/all_gather | solution.py:124
  354.0 54.3 %all-gather.9.cloned.1.call-done = bf16[512,6144]{1,0:T(8,128)(2,1)} async-done(((bf16[128,6144]{1,0:T(8,128)(2,1)}), bf16[512,6144]{1,0:T(8,128)(2,1)}) %all-gather.9.cloned.1.call-update) | async-done | bytes 6291472 | tf_op jit(solution)/shard_map/all_gather | solution.py:123
  408.2 4.9 convolution_convert_fusion.2
  413.3 78.3 %all-gather.11.cloned.1.call-done = bf16[1536,6144]{1,0:T(8,128)(2,1)} async-done(((bf16[48,6144]{1,0:T(8,128)(2,1)}), bf16[1536,6144]{1,0:T(8,128)(2,1)}) %all-gather.11.cloned.1.call-update) | async-done | bytes 18874384 | tf_op jit(solution)/shard_map/all_gather | solution.py:139
  491.6 11.7 %fusion.10 = f32[1536,288]{0,1:T(8,128)} fusion(bf16[1536,6144]{1,0:T(8,128)(2,1)} %all-gather.11.cloned.1.call-done, bf16[1,288,6144]{2,1,0:T(8,128)(2,1)} %param.25), kind=kOutput, calls=%fused_computation.15 | convolution fusion | flops 5435817984 | bytes 24182784 | tf_op jit(solution)/shard_map/dot_general | solution.py:140
  503.2 23.1 %convolution_convert_fusion = bf16[1536,6144]{1,0:T(8,128)(2,1)} fusion(bf16[1,288,6144]{2,1,0:T(8,128)(2,1)S(1)} %copy-done, bf16[1536,6144]{1,0:T(8,128)(2,1)} %all-gather.11.cloned.1.call-done, bf16[1,288,6144]{2,1,0:T(8,128)(2,1)} %param.26, f32[1536,288]{0,1:T(8,128)} %fusion.10), kind=kOutput, calls=%fused_computation.3 | convolution fusion | flops 10883727360 | bytes 46596096 | tf_op jit(solution)/shard_map/dot_general | solution.py:148
  527.3 4.8 select_reduce_fusion
  532.1 115.4 %reduce-scatter.6.cloned.1.call-done = bf16[48,6144]{1,0:T(8,128)(2,1)} async-done(((bf16[1536,6144]{1,0:T(8,128)(2,1)}), bf16[48,6144]{1,0:T(8,128)(2,1)}) %reduce-scatter.6.cloned.1.call-update) | async-done | bytes 589840 | tf_op jit(solution)/shard_map/reduce_scatter | solution.py:147
  647.6 9.2 %fusion.43 = f32[512,6144]{1,0:T(8,128)} fusion(bf16[48,6144]{1,0:T(8,128)(2,1)} %reduce-scatter.6.cloned.1.call-done, f32[512]{0:T(512)S(1)} %bitcast.112, s32[512]{0:T(512)S(1)} %bitcast.109, pred[512]{0:T(512)(128)(4,1)S(1)} %get-tuple-element.130), kind=kOutput, calls=%fused_computation.47 | convolution fusion | flops 1812013056 | bytes 13177344 | tf_op jit(solution)/shard_map/dot_general | solution.py:159
  656.8 113.6 %reduce-scatter.8.cloned.1.call-done = f32[128,6144]{1,0:T(8,128)} async-done(((f32[512,6144]{1,0:T(8,128)}), f32[128,6144]{1,0:T(8,128)}) %reduce-scatter.8.cloned.1.call-update) | async-done | bytes 3145744 | tf_op jit(solution)/shard_map/reduce_scatter | solution.py:161
  770.4 4.5 add_convert_fusion
  (120 shorter events, 109.0 us)
Async XLA Ops:
  6.5 496.7 %copy-start = (bf16[1,288,6144]{2,1,0:T(8,128)(2,1)S(1)}, bf16[1,288,6144]{2,1,0:T(8,128)(2,1)}, u32[]{:S(2)}) copy-start(bf16[1,288,6144]{2,1,0:T(8,128)(2,1)} %param.27) | copy-start | bytes 10616836
  6.5 134.4 %all-gather.13.cloned.1.call-start = ((), (), s32[]{:S(2)}) async-start(), calls=%async_computation.9 | async-start | bytes 34603008 | tf_op jit(solution)/shard_map/all_gather | solution.py:14
  24.3 238.1 %all-gather.7.cloned.1.call-start = ((), (), s32[]{:S(2)}) async-start(), calls=%async_computation.3 | async-start | bytes 12976128 | tf_op jit(solution)/shard_map/all_gather | solution.py:106
  25.0 312.3 %reduce-scatter.4.cloned.1.call-start = ((), (), s32[]{:S(2)}) async-start(), calls=%async_computation.4 | async-start | bytes 7864320 | tf_op jit(solution)/shard_map/reduce_scatter | solution.py:109
  55.5 2.3 copy-start.4
  55.5 2.3 copy-start.6
  249.0 5.0 copy-start.7
  274.1 134.2 %all-gather.9.cloned.1.call-start = ((), (), s32[]{:S(2)}) async-start(), calls=%async_computation.5 | async-start | bytes 7864320 | tf_op jit(solution)/shard_map/all_gather | solution.py:123
  337.3 2.6 copy-start.2
  337.3 2.8 copy-start.3
  340.2 2.6 copy-start.8
  342.7 148.9 %all-gather.11.cloned.1.call-start = ((), (), s32[]{:S(2)}) async-start(), calls=%async_computation.6 | async-start | bytes 19464192 | tf_op jit(solution)/shard_map/all_gather | solution.py:139
  413.2 234.4 %reduce-scatter.6.cloned.1.call-start = ((), (), s32[]{:S(2)}) async-start(), calls=%async_computation.7 | async-start | bytes 19464192 | tf_op jit(solution)/shard_map/reduce_scatter | solution.py:147
  526.3 1.0 copy-start.5
  526.3 244.1 %reduce-scatter.8.cloned.1.call-start = ((), (), s32[]{:S(2)}) async-start(), calls=%async_computation.8 | async-start | bytes 15728640 | tf_op jit(solution)/shard_map/reduce_scatter | solution.py:161
  656.8 118.2 %copy-start.1 = (bf16[1,288,6144]{2,1,0:T(8,128)(2,1)S(1)}, bf16[1,288,6144]{2,1,0:T(8,128)(2,1)}, u32[]{:S(2)}) copy-start(bf16[1,288,6144]{2,1,0:T(8,128)(2,1)} %param.27) | copy-start | bytes 10616836
Sparse Core Ops, SparseCore 0:
  24.4 116.5 all-gather.12
  143.2 62.1 all-gather.6
  274.2 63.1 reduce-scatter.3
  342.8 65.3 all-gather.8
  413.3 78.1 all-gather.10
  526.5 121.0 reduce-scatter.5
  656.9 113.4 reduce-scatter.7
where the time goes:
time: 785 us; the launch traced here: 782 us
  waiting for transfers between devices  504 us (64%)
  other arithmetic  106 us (14%)
  matrix products  81.3 us (10%)
  local copies, waits for them, and re-layouts  39.8 us (5%)
  blocking collectives  36.6 us (5%)
  between operations  13.7 us (2%)
    reduce_scatter x1, waiting for transfers between devices, shards(): lax.psum_scatter(jnp.dot(hidden_all, down_weight[0], preferred_element_ty...  115 us
    reduce_scatter x1, waiting for transfers between devices, shards(): lax.psum_scatter(spread(jnp.int32(0), rows_here * lax.axis_size('exp')),...  114 us
    select_n x32, other arithmetic, hop(): return jax.tree.map(lambda a, b: jnp.where(reached, a, b), new, before)  86.9 us
    all_gather x1, waiting for transfers between devices, shards(): piece = lax.all_gather(outgoing, 'seq', axis=0, tiled=True)  78.3 us
    all_gather x1, waiting for transfers between devices, carried_in(): everything = jax.tree.map(lambda part: lax.all_gather(part, axis), shard)  78.2 us
    reduce_scatter x1, waiting for transfers between devices, shards(): lax.psum_scatter(projected.astype(jnp.bfloat16), 'exp', scatter_dimension...  63.2 us
    all_gather x1, waiting for transfers between devices, shards(): lax.all_gather(moe_in, 'exp', axis=0, tiled=True)  54.3 us
    all_gather x1, blocking collectives, carried_in(): everything = jax.tree.map(lambda part: lax.all_gather(part, axis), shard)  28.7 us
  transfers between devices with their start and end apart: 7, of which 6 were waited for; matrix products, arithmetic and copies ran while one was open for 18% of the time, Pallas kernels for 0%

commit v1 on v0

v1 whole, which is shorter than its diff:
```python
import functools

import jax
import jax.numpy as jnp
from jax import lax
from jax.experimental import pallas as pl
from jax.experimental.pallas import tpu as pltpu
from jax.sharding import Mesh, PartitionSpec as P

HEAD = 128
BF = jnp.bfloat16
F32 = jnp.float32
HI = lax.Precision.HIGHEST
SEQ = ("z", "y", "core")
DEC = 16
OFFS = (1, 3, 2, 0)
JREL = {0: 0, 3: 1, 1: 2, 2: 3}


def ring(n, k):
    return [(i, (i + k) % n) for i in range(n)]


def mm(a, b):
    return jnp.dot(a, b, preferred_element_type=F32)


def mm0(a, b):
    return lax.dot_general(a, b, (((0,), (0,)), ((), ())), preferred_element_type=F32)


def split(a):
    hi = a.astype(BF)
    return hi, (a - hi.astype(F32)).astype(BF)


def local_kernel(q_ref, k_ref, v_ref, d_ref, inner_ref, state_ref, cum_ref):
    steps, heads = d_ref.shape[1], d_ref.shape[2]
    row = lax.broadcasted_iota(jnp.int32, (steps, steps), 0)
    col = lax.broadcasted_iota(jnp.int32, (steps, steps), 1)
    later = row >= col
    decay = d_ref[0]
    cum = jnp.dot(later.astype(F32), decay, precision=HI, preferred_element_type=F32)
    cum_ref[0] = cum
    turned = cum.T
    final = cum[steps - 1 : steps, :]
    tail = jnp.exp(final - cum)
    ends = jnp.exp(final)
    piece = lax.broadcasted_iota(jnp.int32, (DEC, HEAD), 0)
    half = HEAD // 2
    for h in range(heads):
        sl = slice(h * HEAD, (h + 1) * HEAD)
        q, k, v = q_ref[0, :, sl], k_ref[0, :, sl], v_ref[0, :, sl]
        scores = lax.dot_general(q, k, (((1,), (1,)), ((), ())), preferred_element_type=F32)
        spread = cum[:, h : h + 1] - turned[h : h + 1, :]
        weights = jnp.where(later, jnp.exp(jnp.minimum(spread, 0.0)), 0.0) * scores
        whi, wlo = split(weights)
        inner_ref[0, :, sl] = mm(whi, v) + mm(wlo, v)
        khi, klo = split(k.astype(F32) * tail[:, h : h + 1])
        update = (mm0(khi, v) + mm0(klo, v)).astype(BF)
        end = jnp.broadcast_to(ends[:, h : h + 1], (DEC, HEAD))
        e1 = end.astype(BF).astype(F32)
        e2 = (end - e1).astype(BF).astype(F32)
        e3 = end - e1 - e2
        rows = jnp.where(piece == 0, e1, jnp.where(piece == 1, e2, jnp.where(piece == 2, e3, 0.0)))
        for r in range(2):
            state_ref[2 * h + r, :half, :] = update[r * half : (r + 1) * half]
            state_ref[2 * h + r, half:, :] = rows.astype(BF)


def local_part(q, k, v, d):
    seqs, steps, width = q.shape
    heads = width // HEAD
    half = HEAD // 2
    block = pl.BlockSpec((1, steps, width), lambda s: (s, 0, 0))
    thin = pl.BlockSpec((1, steps, heads), lambda s: (s, 0, 0))
    return pl.pallas_call(
        local_kernel,
        grid=(seqs,),
        in_specs=[block, block, block, thin],
        out_specs=[block, pl.BlockSpec((2 * heads, half + DEC, HEAD), lambda s: (s, 0, 0)), thin],
        out_shape=[
            jax.ShapeDtypeStruct((seqs, steps, width), F32),
            jax.ShapeDtypeStruct((seqs * heads * 2, half + DEC, HEAD), BF),
            jax.ShapeDtypeStruct((seqs, steps, heads), F32),
        ],
        compiler_params=pltpu.CompilerParams(vmem_limit_bytes=48 * 2**20),
        name="local_attention",
    )(q, k, v, d)


def scan_kernel(in_ref, out_ref):
    blocks = in_ref.shape[0]
    half = out_ref.shape[1]
    carry = jnp.zeros(out_ref.shape[1:], F32)
    for n in range(blocks):
        out_ref[n] = carry.astype(BF)
        dec = in_ref[n, half:, :].astype(F32)
        carry = carry * (dec[0:1] + dec[1:2] + dec[2:3]) + in_ref[n, :half, :].astype(F32)


def scan_states(arrived):
    blocks, rows, width = arrived.shape
    return pl.pallas_call(
        scan_kernel,
        out_shape=jax.ShapeDtypeStruct((blocks, rows - DEC, width), BF),
        compiler_params=pltpu.CompilerParams(vmem_limit_bytes=48 * 2**20),
        name="state_prefix",
    )(arrived)


def carry_kernel(me_ref, q_ref, inner_ref, cum_ref, state_ref, gain_ref, out_ref):
    shares, slice_len = out_ref.shape[0], out_ref.shape[2]
    heads = cum_ref.shape[2]
    grow = jnp.exp(cum_ref[0])
    me = me_ref[0]
    for h in range(heads):
        sl = slice(h * HEAD, (h + 1) * HEAD)
        head = inner_ref[0, :, sl] + mm(q_ref[0, :, sl], state_ref[h]) * grow[:, h : h + 1]
        scale = lax.rsqrt(jnp.mean(head * head, -1, keepdims=True) + 1e-06)
        normed = (head * scale * gain_ref[:, sl]).astype(BF)
        for a in range(shares):
            out_ref[lax.rem(a - me + shares, shares), 0, :, sl] = normed[
                a * slice_len : (a + 1) * slice_len
            ]


def carried(me, q, inner, cum, state, gain, shares):
    seqs, steps, width = q.shape
    heads = width // HEAD
    block = pl.BlockSpec((1, steps, width), lambda s: (s, 0, 0))
    return pl.pallas_call(
        carry_kernel,
        grid=(seqs,),
        in_specs=[
            pl.BlockSpec(memory_space=pltpu.SMEM),
            block,
            block,
            pl.BlockSpec((1, steps, heads), lambda s: (s, 0, 0)),
            pl.BlockSpec((heads, HEAD, HEAD), lambda s: (s, 0, 0)),
            pl.BlockSpec((1, width), lambda s: (0, 0)),
        ],
        out_specs=pl.BlockSpec((shares, 1, steps // shares, width), lambda s: (0, s, 0, 0)),
        out_shape=jax.ShapeDtypeStruct((shares, seqs, steps // shares, width), BF),
        compiler_params=pltpu.CompilerParams(vmem_limit_bytes=48 * 2**20),
        name="carried_norm",
    )(me, q, inner, cum, state, gain)


def route_kernel(cap, me_ref, routes_ref, place_ref):
    flight, rows = routes_ref.shape[1] // 128, 128
    total = routes_ref.shape[1]
    me = me_ref[0]
    a = lax.broadcasted_iota(jnp.int32, (total, total), 0)
    b = lax.broadcasted_iota(jnp.int32, (total, total), 1)
    before = ((a < b) & (a // rows == b // rows)).astype(BF)
    first, second = routes_ref[0:1, :], routes_ref[1:2, :]
    home = lax.broadcasted_iota(jnp.int32, (1, total), 1) // rows
    slots = lax.broadcasted_iota(jnp.int32, (flight * cap, total), 0)
    for r, off in enumerate(OFFS):
        expert = lax.rem(me + off, flight)
        chosen = ((first == expert) | (second == expert)).astype(F32)
        rank = mm(jnp.broadcast_to(chosen, (8, total)).astype(BF), before)[0:1].astype(jnp.int32)
        start = jnp.zeros((1, total), jnp.int32)
        for delta in range(flight):
            start = jnp.where(home == delta, cap * JREL[(delta - off) % 4], start)
        target = jnp.where(chosen > 0.0, start + rank, -1)
        hits = (slots == target).astype(F32).astype(BF)
        place_ref[r * flight * cap : (r + 1) * flight * cap, :] = hits


def call(kernel, name, outs, *args, **kw):
    limit = kw.pop("vmem", 40)
    return pl.pallas_call(
        kernel,
        out_shape=[jax.ShapeDtypeStruct(s, d) for s, d in outs],
        compiler_params=pltpu.CompilerParams(vmem_limit_bytes=limit * 2**20),
        name=name,
        **kw,
    )(*args)


VM = pl.BlockSpec(memory_space=pltpu.VMEM)
SM = pl.BlockSpec(memory_space=pltpu.SMEM)
ANY = pl.BlockSpec(memory_space=pl.ANY)


def route(me, routes, cap):
    total = routes.shape[1]
    flight = total // 128
    return call(
        functools.partial(route_kernel, cap),
        "route",
        [((flight * flight * cap, total), BF)],
        me,
        routes,
        in_specs=[SM, VM],
        out_specs=[VM],
    )[0]


def nt(a, b):
    return lax.dot_general(a, b, (((1,), (1,)), ((), ())), preferred_element_type=F32)


def selected_kernel(place_ref, normed_ref, weight_ref, res_ref, o0, o1, o2, o3, picked):
    rows = res_ref.shape[0]

    @pl.when(pl.program_id(0) == 0)
    def _():
        picked[...] = mm(place_ref[...], normed_ref[...]).astype(BF)

    full = nt(picked[...], weight_ref[...]) + mm(place_ref[:, :rows], res_ref[...])
    full = full.astype(BF)
    size = o0.shape[0]
    for i, o in enumerate((o0, o1, o2, o3)):
        o[...] = full[i * size : (i + 1) * size]


def selected(place, normed, weight, res, tile=1024):
    picks, (model, width) = place.shape[0], weight.shape
    rows = res.shape[0]
    size = picks // 4
    whole = lambda a: pl.BlockSpec(a.shape, lambda n: (0, 0))
    return call(
        selected_kernel,
        "selected_projection",
        [((size, model), BF)] * 4,
        place,
        normed,
        weight,
        res,
        grid=(model // tile,),
        in_specs=[
            whole(place),
            whole(normed),
            pl.BlockSpec((tile, width), lambda n: (n, 0)),
            pl.BlockSpec((rows, tile), lambda n: (0, n)),
        ],
        out_specs=[pl.BlockSpec((size, tile), lambda n: (0, n))] * 4,
        scratch_shapes=[pltpu.VMEM((picks, width), BF)],
    )


def whole_kernel(normed_ref, weight_ref, o0, o1, o2, o3):
    full = nt(normed_ref[...], weight_ref[...]).astype(BF)
    size = o0.shape[0]
    for i, o in enumerate((o0, o1, o2, o3)):
        o[...] = full[i * size : (i + 1) * size]


def whole_projection(normed, weight, tile=1024):
    total, (model, width) = normed.shape[0], weight.shape
    size = total // 4
    return call(
        whole_kernel,
        "whole_projection",
        [((size, model), BF)] * 4,
        normed,
        weight,
        grid=(model // tile,),
        in_specs=[
            pl.BlockSpec(normed.shape, lambda n: (0, 0)),
            pl.BlockSpec((tile, width), lambda n: (n, 0)),
        ],
        out_specs=[pl.BlockSpec((size, tile), lambda n: (0, n))] * 4,
        cost_estimate=pl.CostEstimate(
            flops=2 * total * model * width, bytes_accessed=4 * model * width, transcendentals=0
        ),
    )


def norm_kernel(a, b, c, d, gain, o0, o1):
    x = a[...].astype(F32) + b[...].astype(F32) + c[...].astype(F32) + d[...].astype(F32)
    x = x * lax.rsqrt(jnp.mean(x * x, -1, keepdims=True) + 1e-06) * gain[...]
    half = o0.shape[1]
    o0[...] = x[:, :half].astype(BF)
    o1[...] = x[:, half:].astype(BF)


def stack_kernel(a0, a1, a2, a3, b0, b1, b2, b3, p0, p1, p2, o0, o1, q0, q1, q2):
    for i, (a, b) in enumerate(((a0, b0), (a1, b1), (a2, b2), (a3, b3))):
        o0[i] = a[...]
        o1[i] = b[...]


def expert_kernel(half_steps, *refs):
    xa, xb = refs[0:5], refs[5:10]
    gate0, gate1, up0, up1, down0, down1 = refs[10:16]
    oa, ob = refs[16:21], refs[21:26]
    x, gates, uppers, hidden = refs[26:]
    step = pl.program_id(0)
    rows, units = xa[0].shape[1], gate0.shape[0]
    steps = 2 * half_steps

    def piece(refs, u, v):
        if u < 3:
            return refs[u].at[v]
        return refs[3].at[v] if v < 2 else refs[4].at[v - 2]

    def span(z, y):
        return pl.ds((z * 4 + y) * rows, rows)

    @pl.when(step < half_steps)
    def _():
        for z in range(4):
            for y in range(4):
                x[span(z, y), :] = piece(xa, z, y)[...]

    @pl.when((step >= half_steps) & (step < steps))
    def _():
        for z in range(4):
            for y in range(4):
                x[span(z, y), :] = piece(xb, y, z)[...]

    @pl.when(step < steps)
    def _():
        for i, (g, u) in enumerate(((gate0, up0), (gate1, up1))):
            sl = slice(i * units, (i + 1) * units)
            new_g, new_u = nt(g[...], x[...]), nt(u[...], x[...])

            @pl.when(step == 0)
            def _():
                gates[sl, :] = new_g
                uppers[sl, :] = new_u

            @pl.when(step > 0)
            def _():
                gates[sl, :] += new_g
                uppers[sl, :] += new_u

    @pl.when(step == steps - 1)
    def _():
        g = gates[...]
        hidden[...] = (g / (1.0 + jnp.exp(-g)) * uppers[...]).T.astype(BF)

    def out(write):
        full = mm(hidden[:, :units], down0[...]) + mm(hidden[:, units:], down1[...])
        for z in range(4):
            for y in range(4):
                at = (z * 4 + y) * rows
                write(z, y, full[at : at + rows].astype(BF))

    @pl.when((step >= steps) & (step < steps + half_steps))
    def _():
        def write(z, y, v):
            piece(oa, z, y)[...] = v

        out(write)

    @pl.when(step >= steps + half_steps)
    def _():
        def write(z, y, v):
            piece(ob, y, z)[...] = v

        out(write)


def expert(xa, xb, gates, ups, downs, tile=1024):
    rows, half = xa[0].shape[1], xa[0].shape[2]
    units = gates[0].shape[0]
    n = half // tile

    def clip(low):
        return lambda s: jnp.clip(s - low, 0, n - 1)

    def cols(low):
        at = clip(low)
        return [pl.BlockSpec((k, rows, tile), lambda s: (0, 0, at(s))) for k in (4, 4, 4, 2, 2)]

    first = pl.BlockSpec((units, tile), lambda s: (0, jnp.clip(s, 0, 2 * n - 1)))
    last = pl.BlockSpec((units, tile), lambda s: (0, jnp.clip(s - 2 * n, 0, 2 * n - 1)))
    total = 16 * rows
    outs = call(
        functools.partial(expert_kernel, n),
        "expert",
        [((k, rows, half), BF) for k in (4, 4, 4, 2, 2)] * 2,
        *xa,
        *xb,
        *gates,
        *ups,
        *downs,
        grid=(4 * n,),
        in_specs=cols(0) + cols(n) + [first] * 4 + [last] * 2,
        out_specs=cols(2 * n) + cols(3 * n),
        scratch_shapes=[
            pltpu.VMEM((total, tile), BF),
            pltpu.VMEM((2 * units, total), F32),
            pltpu.VMEM((2 * units, total), F32),
            pltpu.VMEM((total, 2 * units), BF),
        ],
        vmem=56,
    )
    return outs[:5], outs[5:]


def fold_kernel(bl0, ab0, up0, dn0, bl1, ab1, up1, dn1, ob0, oa0, ob1, oa1):
    for below, above, up, down, o_below, o_above in (
        (bl0, ab0, up0, dn0, ob0, oa0),
        (bl1, ab1, up1, dn1, ob1, oa1),
    ):
        o_above[0:2] = (above[0:2].astype(F32) + up[...].astype(F32)).astype(BF)
        o_above[2:4] = above[2:4]
        o_below[0:2] = below[0:2]
        o_below[2:4] = (below[2:4].astype(F32) + down[...].astype(F32)).astype(BF)


def phase_kernel(m0, u0, d0, m1, u1, d1, *outs):
    for k, (m, u, d) in enumerate(((m0, u0, d0), (m1, u1, d1))):
        total = m[...].astype(F32) + u[...].astype(F32) + d[...].astype(F32)
        for i in range(4):
            outs[4 * k + i][...] = total[i].astype(BF)


def served_kernel(cap, a0, a1, a2, a3, b0, b1, b2, b3, o0, o1, o2, o3):
    half = a0.shape[1]
    rows = a0.shape[0]
    padded = o0.shape[0]
    r = lax.broadcasted_iota(jnp.int32, (padded, rows), 0)
    c = lax.broadcasted_iota(jnp.int32, (padded, rows), 1)
    for k, parts in enumerate(((a0, a1, a2, a3), (b0, b1, b2, b3))):
        total = sum(p[...].astype(F32) for p in parts).astype(BF)
        for i, o in enumerate((o0, o1, o2, o3)):
            pick = ((c == r + i * cap) & (r < cap)).astype(F32).astype(BF)
            o[:, k * half : (k + 1) * half] = mm(pick, total).astype(BF)


def home_kernel(me_ref, routes_ref, res, own, r1, r2, r3, gain, router, late, hidden_ref, hi_ref, lo_ref):
    x = res[...].astype(F32)
    for p in (own, r1, r2, r3):
        x = x + p[...].astype(F32)
    hidden_ref[...] = x
    normed = (x * lax.rsqrt(jnp.mean(x * x, -1, keepdims=True) + 1e-06) * gain[...]).astype(BF)
    logits = mm(normed, router[...])
    rows, experts = logits.shape
    labels = lax.broadcasted_iota(jnp.int32, (rows, experts), 1)
    one, two = routes_ref[:, 0:1], routes_ref[:, 1:2]
    first = jnp.sum(jnp.where(one == labels, logits, 0.0), -1, keepdims=True)
    second = jnp.sum(jnp.where(two == labels, logits, 0.0), -1, keepdims=True)
    gate0 = 1.0 / (1.0 + jnp.exp(second - first))
    gate1 = 1.0 / (1.0 + jnp.exp(first - second))
    cols = hi_ref.shape[1]
    place = lax.broadcasted_iota(jnp.int32, (rows, cols), 1)
    a = lax.broadcasted_iota(jnp.int32, (rows, rows), 0)
    b = lax.broadcasted_iota(jnp.int32, (rows, rows), 1)
    before = (b < a).astype(F32).astype(BF)
    total = jnp.zeros((rows, cols), F32)
    for j, off in enumerate((0, 1, 3, 2)):
        expert_id = lax.rem(me_ref[0] + off, 4)
        hit0, hit1 = (one == expert_id).astype(F32), (two == expert_id).astype(F32)
        chosen = hit0 + hit1
        rank = mm(before, jnp.broadcast_to(chosen, (rows, 128)).astype(BF))[:, 0:1].astype(jnp.int32)
        total = total + jnp.where(place == rank + 16 * j, hit0 * gate0 + hit1 * gate1, 0.0)
    hi, lo = split(total)
    hi_ref[...] = hi
    lo_ref[...] = lo


def final_kernel(hidden, hi, lo, b0, b1, b2, b3, out, back):
    for i, b in enumerate((b0, b1, b2, b3)):
        back[16 * i : 16 * i + 16, :] = b[...]
    moe = mm(hi[...], back[...]) + mm(lo[...], back[...])
    out[...] = (hidden[...] + moe).astype(BF)


def up_one(x, axis):
    return lax.ppermute(x, axis, ring(4, 1))


def down_one(x, axis):
    return lax.ppermute(x, axis, ring(4, -1))


def across(x, axis):
    return lax.ppermute(x, axis, ring(4, 2))


def far_sides(below, above, axis):
    return up_one(below[:2], axis), down_one(above[2:], axis)


def shards(
    queries,
    keys,
    payload_vectors,
    log_decay,
    attn_gain,
    out_weight,
    residual,
    norm_gain,
    router_weight,
    picks,
    gate_weight,
    up_weight,
    down_weight,
):
    seqs, positions, width = queries.shape
    slice_len, model = residual.shape[1], residual.shape[2]
    shares = positions // slice_len
    rows = seqs * slice_len
    cap = 3 * rows // 32
    half = model // 2
    me = lax.axis_index("x").astype(jnp.int32).reshape(1)

    weight_out = lax.all_gather(out_weight.T, SEQ, axis=0, tiled=True)
    swap = ring(2, 1)
    gates, ups, downs = [
        (w[0], lax.ppermute(w[0], "core", swap)) for w in (gate_weight, up_weight, down_weight)
    ]
    routes = picks.reshape(rows, 2)
    turned = routes.T
    all_routes = jnp.concatenate(
        [turned] + [lax.ppermute(turned, "x", ring(4, -delta)) for delta in (1, 2, 3)], axis=1
    )

    inner, states, cum = local_part(queries, keys, payload_vectors, log_decay)
    arrived = lax.all_to_all(states, SEQ, 0, 0, tiled=True)
    prefix = lax.all_to_all(scan_states(arrived), SEQ, 0, 0, tiled=True)
    prefix = prefix.reshape(seqs * width // HEAD, HEAD, HEAD)
    normed = carried(
        me, queries, inner, cum, prefix, attn_gain.reshape(1, width), shares
    ).reshape(shares * rows, width)

    place = route(me, all_routes, cap)
    flat = residual.reshape(rows, model)
    gain = norm_gain.reshape(1, model)
    to_up, to_down, to_far, here = selected(place, normed, weight_out, flat)
    own, d1, d2, d3 = whole_projection(normed, weight_out)

    size = here.shape[0]
    a0, b0 = call(
        norm_kernel,
        "selected_norm",
        [((size, half), BF)] * 2,
        here,
        up_one(to_up, "x"),
        down_one(to_down, "x"),
        across(to_far, "x"),
        gain,
        in_specs=[VM] * 5,
        out_specs=[VM] * 2,
    )

    a4, b4, d1, d2, d3 = call(
        stack_kernel,
        "stack",
        [((4, size, half), BF)] * 2 + [((rows, model), BF)] * 3,
        a0,
        up_one(a0, "y"),
        down_one(a0, "y"),
        across(a0, "y"),
        b0,
        up_one(b0, "z"),
        down_one(b0, "z"),
        across(b0, "z"),
        d1,
        d2,
        d3,
        in_specs=[VM] * 8 + [ANY] * 3,
        out_specs=[VM] * 2 + [ANY] * 3,
        input_output_aliases={8: 2, 9: 3, 10: 4},
    )
    a_below, a_above = up_one(a4, "z"), down_one(a4, "z")
    b_below, b_above = up_one(b4, "y"), down_one(b4, "y")
    a_far, b_far = far_sides(a_below, a_above, "z"), far_sides(b_below, b_above, "y")

    oa, ob = expert(
        (a4, a_below, a_above, *a_far), (b4, b_below, b_above, *b_far), gates, ups, downs
    )
    a_below, a_above, b_below, b_above = call(
        fold_kernel,
        "fold",
        [((4, size, half), BF)] * 4,
        oa[1],
        oa[2],
        up_one(oa[3], "z"),
        down_one(oa[4], "z"),
        ob[1],
        ob[2],
        up_one(ob[3], "y"),
        down_one(ob[4], "y"),
        in_specs=[VM] * 8,
        out_specs=[VM] * 4,
    )
    parts = call(
        phase_kernel,
        "phase",
        [((size, half), BF)] * 8,
        oa[0],
        up_one(a_above, "z"),
        down_one(a_below, "z"),
        ob[0],
        up_one(b_above, "y"),
        down_one(b_below, "y"),
        in_specs=[VM] * 6,
        out_specs=[VM] * 8,
    )
    s0, s1, s2, s3 = call(
        functools.partial(served_kernel, cap),
        "served",
        [((16, model), BF)] * 4,
        parts[0],
        up_one(parts[2], "y"),
        down_one(parts[1], "y"),
        across(parts[3], "y"),
        parts[4],
        up_one(parts[6], "z"),
        down_one(parts[5], "z"),
        across(parts[7], "z"),
        in_specs=[VM] * 8,
        out_specs=[VM] * 4,
    )

    hidden, hi, lo = call(
        home_kernel,
        "home",
        [((rows, model), F32), ((rows, 64), BF), ((rows, 64), BF)],
        me,
        routes,
        flat,
        own,
        up_one(d1, "x"),
        across(d2, "x"),
        down_one(d3, "x"),
        gain,
        router_weight,
        parts[0],
        in_specs=[SM] + [VM] * 8 + [ANY],
        out_specs=[VM] * 3,
        vmem=56,
    )
    out = call(
        final_kernel,
        "combine",
        [((rows, model), BF)],
        hidden,
        hi,
        lo,
        s0,
        down_one(s1, "x"),
        up_one(s2, "x"),
        across(s3, "x"),
        in_specs=[VM] * 7,
        out_specs=[VM],
        scratch_shapes=[pltpu.VMEM((64, model), BF)],
    )[0]
    return out.reshape(seqs, slice_len, model)


def solution(mesh):
    shape = dict(mesh.shape)
    grid = Mesh(mesh.devices.reshape(4, shape["seq"] // 8, 2, shape["exp"]), SEQ + ("x",))
    everyone = SEQ + ("x",)
    placed = (
        P(None, SEQ, "x"),
        P(None, SEQ, "x"),
        P(None, SEQ, "x"),
        P(None, SEQ, "x"),
        P("x"),
        P("x", SEQ),
        P(None, everyone, None),
        P(),
        P(),
        P(None, everyone, None),
        P("x", SEQ, None),
        P("x", SEQ, None),
        P("x", SEQ, None),
    )
    return jax.shard_map(
        shards, mesh=grid, in_specs=placed, out_specs=P(None, everyone, None), check_vma=False
    )
```

time: 785 us -> 401 us (0.51)
  waiting for transfers between devices: 504 us -> 203 us
  other arithmetic: 106 us -> 0.01 us
  matrix products: 81.3 us -> 0 us
  Pallas kernels: 0 us -> 78.7 us
  starting transfers between devices: 0.51 us -> 55.7 us
  local copies, waits for them, and re-layouts: 39.8 us -> 24.4 us
  blocking collectives: 36.6 us -> 25 us
    reduce_scatter x3 -> x0, waiting for transfers between devices: 292 us -> none  [the longest x1 115 us: shards(): lax.psum_scatter(jnp.dot(hidden_all, down_weight[0], preferred_element_ty...]
    all_gather x4 -> x1, waiting for transfers between devices: 211 us -> 16.4 us  [shards(): weight_out = lax.all_gather(out_weight.T, SEQ, axis=0, tiled=True)]
    ppermute x0 -> x43, waiting for transfers between devices: none -> 180 us  [the longest x15 92.5 us: up_one(): return lax.ppermute(x, axis, ring(4, 1))]
    select_n x32 -> x0, other arithmetic: 86.9 us -> none  [hop(): return jax.tree.map(lambda a, b: jnp.where(reached, a, b), new, before)]
    dot_general x10 -> x0, matrix products: 81.3 us -> none  [the longest x1 23.1 us: shards(): jnp.dot(hidden_all, down_weight[0], preferred_element_type=jnp.float32)]
    pallas_call x0 -> x14, Pallas kernels: none -> 78.7 us  [the longest x11 69.6 us: call(): pl.pallas_call(kernel, out_shape=[jax.ShapeDtypeStruct(s, d) for s, d in...]
    ppermute x0 -> x43, starting transfers between devices: none -> 51.8 us  [the longest x15 29.4 us: down_one(): return lax.ppermute(x, axis, ring(4, -1))]
    all_gather x2 -> x0, blocking collectives: 36.6 us -> none  [the longest x1 28.7 us: carried_in(): everything = jax.tree.map(lambda part: lax.all_gather(part, axis), shard)]
  transfers between devices with their start and end apart: 7 -> 45, of which waited for: 6 -> 28; matrix products, arithmetic and copies ran while one was open for 18% -> 1% of each run, Pallas kernels for 0% -> 7%
where the time goes in v1:
time: 401 us; the launch traced here: 400 us
  waiting for transfers between devices  203 us (51%)
  Pallas kernels  78.7 us (20%)
  starting transfers between devices  55.7 us (14%)
  blocking collectives  25 us (6%)
  local copies, waits for them, and re-layouts  24.4 us (6%)
  between operations  13.7 us (3%)
    ppermute x15, waiting for transfers between devices, up_one(): return lax.ppermute(x, axis, ring(4, 1))  92.5 us
    pallas_call x11, Pallas kernels, call(): pl.pallas_call(kernel, out_shape=[jax.ShapeDtypeStruct(s, d) for s, d in...  69.6 us
    ppermute x15, waiting for transfers between devices, down_one(): return lax.ppermute(x, axis, ring(4, -1))  62.7 us
    ppermute x15, starting transfers between devices, down_one(): return lax.ppermute(x, axis, ring(4, -1))  29.4 us
    all_to_all x1, blocking collectives, shards(): arrived = lax.all_to_all(states, SEQ, 0, 0, tiled=True)  25 us
    unnamed x87, local copies, waits for them, and re-layouts  24.1 us
    ppermute x7, waiting for transfers between devices, across(): return lax.ppermute(x, axis, ring(4, 2))  20.4 us
    all_gather x1, waiting for transfers between devices, shards(): weight_out = lax.all_gather(out_weight.T, SEQ, axis=0, tiled=True)  16.4 us
  transfers between devices with their start and end apart: 45, of which 28 were waited for; matrix products, arithmetic and copies ran while one was open for 1% of the time, Pallas kernels for 7%

profile of v1, /device:TPU:0, one launch (start us, length us, event | category | flops | bytes accessed | tf_op | source)
XLA Modules:
  0.0 400.1 jit_solution(800226424893746832)
XLA Ops:
  11.8 6.0 %local_attention.1 = (f32[2,256,1024]{2,1,0:T(8,128)}, bf16[32,80,128]{2,1,0:T(8,128)(2,1)S(1)}, f32[2,256,8]{2,1,0:T(8,128)S(1)}) custom-call(bf16[2,256,1024]{2,1,0:T(8,128)(2,1)S(1)} %copy-done.1, bf16[2,256,1024]{2,1,0:T(8,128)(2,1)S(1)} %copy-done.18, bf16[2,256,1024]{2,1,0:T(8,128)(2,1)S(1)} %copy-done.19, f32[2,256,8]{2,1,0:T(8,128)S(1)} %copy.22.d_ref), custom_call_target="tpu_custom_call" | custom-call | tf_op jit(solution)/shard_map/local_attention/pallas_call | solution.py:77
  17.8 25.0 %all_to_all.10.in_ref = bf16[32,80,128]{2,1,0:T(8,128)(2,1)S(1)} all-to-all(bf16[32,80,128]{2,1,0:T(8,128)(2,1)S(1)} %get-tuple-element.54), channel_id=1, replica_groups=mesh['z'=4,'y'=4,'core'=2,'x'=4] {'z','y','core'}, dimensions={0} | all-to-all | bytes 1310720 | tf_op jit(solution)/shard_map/all_to_all | solution.py:517
  43.8 3.9 all-to-all-start.1
  47.8 2.7 collective-permute-start
  53.8 2.8 collective-permute-done.1
  57.7 5.0 %all-to-all-done.1 = bf16[32,64,128]{2,1,0:T(8,128)(2,1)S(1)} async-done(((bf16[32,64,128]{2,1,0:T(8,128)(2,1)}), bf16[32,64,128]{2,1,0:T(8,128)(2,1)S(1)}, u32[]{:S(2)}, u32[]{:S(2)}) %all-to-all-start.1) | async-done | bytes 524320 | tf_op jit(solution)/shard_map/all_to_all | solution.py:518
  68.5 16.4 %all-gather.2.cloned.1.call-done.weight_ref = bf16[6144,1024]{1,0:T(8,128)(2,1)} async-done(((bf16[192,1024]{1,0:T(8,128)(2,1)}), bf16[6144,1024]{1,0:T(8,128)(2,1)}) %all-gather.2.cloned.1.call-update) | async-done | bytes 12582928 | tf_op jit(solution)/shard_map/all_gather | solution.py:505
  86.2 10.6 %selected_projection.1 = (bf16[48,6144]{1,0:T(8,128)(2,1)S(1)}, bf16[48,6144]{1,0:T(8,128)(2,1)S(1)}, bf16[48,6144]{1,0:T(8,128)(2,1)S(1)}, bf16[48,6144]{1,0:T(8,128)(2,1)S(1)}) custom-call(bf16[192,512]{1,0:T(8,128)(2,1)S(1)} %route.1.place_ref, bf16[512,1024]{1,0:T(8,128)(2,1)S(1)} %bitcast.16, ...), custom_call_target="tpu_custom_call" | custom-call | tf_op jit(solution)/shard_map/selected_projection/pallas_call | solution.py:174
  101.8 11.7 %collective-permute-done.3.b = bf16[48,6144]{1,0:T(8,128)(2,1)S(1)} collective-permute-done((bf16[48,6144]{1,0:T(8,128)(2,1)S(1)}, bf16[48,6144]{1,0:T(8,128)(2,1)S(1)}, u32[]{:S(2)}, u32[]{:S(2)}) %collective-permute-start.3) | collective-permute-done | bytes 589856 | tf_op jit(solution)/shard_map/ppermute | solution.py:467
  113.5 11.9 %collective-permute-done.4.c = bf16[48,6144]{1,0:T(8,128)(2,1)S(1)} collective-permute-done((bf16[48,6144]{1,0:T(8,128)(2,1)S(1)}, bf16[48,6144]{1,0:T(8,128)(2,1)S(1)}, u32[]{:S(2)}, u32[]{:S(2)}) %collective-permute-start.4) | collective-permute-done | bytes 589856 | tf_op jit(solution)/shard_map/ppermute | solution.py:471
  132.1 10.1 %collective-permute-done.10.b2 = bf16[48,3072]{1,0:T(8,128)(2,1)S(1)} collective-permute-done((bf16[48,3072]{1,0:T(8,128)(2,1)S(1)}, bf16[48,3072]{1,0:T(8,128)(2,1)S(1)}, u32[]{:S(2)}, u32[]{:S(2)}) %collective-permute-start.10) | collective-permute-done | bytes 294944 | tf_op jit(solution)/shard_map/ppermute | solution.py:471
  142.4 9.5 %collective-permute-done.7.a2 = bf16[48,3072]{1,0:T(8,128)(2,1)S(1)} collective-permute-done((bf16[48,3072]{1,0:T(8,128)(2,1)S(1)}, bf16[48,3072]{1,0:T(8,128)(2,1)S(1)}, u32[]{:S(2)}, u32[]{:S(2)}) %collective-permute-start.7) | collective-permute-done | bytes 294944 | tf_op jit(solution)/shard_map/ppermute | solution.py:471
  151.9 10.3 %whole_projection.1 = (bf16[128,6144]{1,0:T(8,128)(2,1)S(1)}, bf16[128,6144]{1,0:T(8,128)(2,1)S(1)}, bf16[128,6144]{1,0:T(8,128)(2,1)S(1)}, bf16[128,6144]{1,0:T(8,128)(2,1)S(1)}) custom-call(bf16[512,1024]{1,0:T(8,128)(2,1)S(1)} %bitcast.17, bf16[6144,1024]{1,0:T(8,128)(2,1)} %all-gather.2.cloned.1.call-done.weight_ref), custom_call_target="tpu_custom_call" | custom-call | flops 6442450944 | bytes 25165824 | tf_op jit(solution)/shard_map/whole_projection/pallas_call | solution.py:174
  163.4 3.7 collective-permute-start.16
  167.0 19.4 %collective-permute-done.15.refs_1_ = bf16[4,48,3072]{2,1,0:T(8,128)(2,1)S(1)} collective-permute-done((bf16[4,48,3072]{2,1,0:T(8,128)(2,1)S(1)}, bf16[4,48,3072]{2,1,0:T(8,128)(2,1)S(1)}, u32[]{:S(2)}, u32[]{:S(2)}) %collective-permute-start.15) | collective-permute-done | bytes 1179680 | tf_op jit(solution)/shard_map/ppermute | solution.py:467
  189.8 19.6 %collective-permute-done.19.refs_6_ = bf16[4,48,3072]{2,1,0:T(8,128)(2,1)S(1)} collective-permute-done((bf16[4,48,3072]{2,1,0:T(8,128)(2,1)S(1)}, bf16[4,48,3072]{2,1,0:T(8,128)(2,1)S(1)}, u32[]{:S(2)}, u32[]{:S(2)}) %collective-permute-start.19) | collective-permute-done | bytes 1179680 | tf_op jit(solution)/shard_map/ppermute | solution.py:467
  209.4 3.7 collective-permute-done.20.refs_7_
  213.4 2.8 collective-permute-start.21
  217.6 2.8 collective-permute-done.17.refs_3_
  220.4 5.3 %collective-permute-done.18.refs_4_ = bf16[2,48,3072]{2,1,0:T(8,128)(2,1)S(1)} collective-permute-done((bf16[2,48,3072]{2,1,0:T(8,128)(2,1)S(1)}, bf16[2,48,3072]{2,1,0:T(8,128)(2,1)S(1)}, u32[]{:S(2)}, u32[]{:S(2)}) %collective-permute-start.18) | collective-permute-done | bytes 589856 | tf_op jit(solution)/shard_map/ppermute | solution.py:471
  230.2 34.7 %expert.1 = (bf16[4,48,3072]{2,1,0:T(8,128)(2,1)}, bf16[4,48,3072]{2,1,0:T(8,128)(2,1)}, bf16[4,48,3072]{2,1,0:T(8,128)(2,1)}, bf16[2,48,3072]{2,1,0:T(8,128)(2,...) custom-call(bf16[4,48,3072]{2,1,0:T(8,128)(2,1)} %copy-done.16, ...), custom_call_target="tpu_custom_call" | custom-call | tf_op jit(solution)/shard_map/expert/pallas_call | solution.py:174
  265.2 3.0 collective-permute-start.27
  271.5 6.8 %collective-permute-done.26.up0 = bf16[2,48,3072]{2,1,0:T(8,128)(2,1)S(1)} collective-permute-done((bf16[2,48,3072]{2,1,0:T(8,128)(2,1)}, bf16[2,48,3072]{2,1,0:T(8,128)(2,1)S(1)}, u32[]{:S(2)}, u32[]{:S(2)}) %collective-permute-start.26) | collective-permute-done | bytes 589856 | tf_op jit(solution)/shard_map/ppermute | solution.py:467
  286.7 3.2 collective-permute-start.31
  294.0 16.9 %collective-permute-done.30.u0 = bf16[4,48,3072]{2,1,0:T(8,128)(2,1)S(1)} collective-permute-done((bf16[4,48,3072]{2,1,0:T(8,128)(2,1)S(1)}, bf16[4,48,3072]{2,1,0:T(8,128)(2,1)S(1)}, u32[]{:S(2)}, u32[]{:S(2)}) %collective-permute-start.30) | collective-permute-done | bytes 1179680 | tf_op jit(solution)/shard_map/ppermute | solution.py:467
  318.6 7.3 %collective-permute-done.34.a1 = bf16[48,3072]{1,0:T(8,128)(2,1)S(1)} collective-permute-done((bf16[48,3072]{1,0:T(8,128)(2,1)S(1)}, bf16[48,3072]{1,0:T(8,128)(2,1)S(1)}, u32[]{:S(2)}, u32[]{:S(2)}) %collective-permute-start.34) | collective-permute-done | bytes 294944 | tf_op jit(solution)/shard_map/ppermute | solution.py:467
  327.8 6.2 %collective-permute-done.36.a3 = bf16[48,3072]{1,0:T(8,128)(2,1)S(1)} collective-permute-done((bf16[48,3072]{1,0:T(8,128)(2,1)S(1)}, bf16[48,3072]{1,0:T(8,128)(2,1)S(1)}, u32[]{:S(2)}, u32[]{:S(2)}) %collective-permute-start.36) | collective-permute-done | bytes 294944 | tf_op jit(solution)/shard_map/ppermute | solution.py:475
  340.8 5.5 %collective-permute-done.39.b3 = bf16[48,3072]{1,0:T(8,128)(2,1)S(1)} collective-permute-done((bf16[48,3072]{1,0:T(8,128)(2,1)S(1)}, bf16[48,3072]{1,0:T(8,128)(2,1)S(1)}, u32[]{:S(2)}, u32[]{:S(2)}) %collective-permute-start.39) | collective-permute-done | bytes 294944 | tf_op jit(solution)/shard_map/ppermute | solution.py:475
  355.4 7.0 %collective-permute-done.13.r2 = bf16[128,6144]{1,0:T(8,128)(2,1)} collective-permute-done((bf16[128,6144]{1,0:T(8,128)(2,1)S(1)}, bf16[128,6144]{1,0:T(8,128)(2,1)}, u32[]{:S(2)}, u32[]{:S(2)}) %collective-permute-start.13) | collective-permute-done | bytes 1572896 | tf_op jit(solution)/shard_map/ppermute | solution.py:475
  362.4 17.2 %collective-permute-done.14.r3 = bf16[128,6144]{1,0:T(8,128)(2,1)} collective-permute-done((bf16[128,6144]{1,0:T(8,128)(2,1)S(1)}, bf16[128,6144]{1,0:T(8,128)(2,1)}, u32[]{:S(2)}, u32[]{:S(2)}) %collective-permute-start.14) | collective-permute-done | bytes 1572896 | tf_op jit(solution)/shard_map/ppermute | solution.py:471
  379.7 7.0 %home.1 = (f32[128,6144]{1,0:T(8,128)}, bf16[128,64]{1,0:T(8,128)(2,1)}, bf16[128,64]{1,0:T(8,128)(2,1)}) custom-call(s32[1]{0:T(128)} %bitcast.me_ref, s32[128,2]{1,0:T(8,128)} %bitcast.32, bf16[128,6144]{1,0:T(8,128)(2,1)} %bitcast.14, bf16[128,6144]{1,0:T(8,128)(2,1)} %copy-done.8, bf16[128,6144]{1,0:T(8,128)(2,1)} %copy-done.35, ...), custom_call_target="tpu_custom_call" | custom-call | tf_op jit(solution)/shard_map/home/pallas_call | solution.py:174
  390.1 3.2 combine.1
  (170 shorter events, 85.2 us)
Async XLA Ops:
  6.5 78.4 %all-gather.2.cloned.1.call-start = ((), (), s32[]{:S(2)}) async-start(), calls=%async_computation.2 | async-start | bytes 12976128 | tf_op jit(solution)/shard_map/all_gather | solution.py:505
  43.8 19.0 %all-to-all-start.1 = ((bf16[32,64,128]{2,1,0:T(8,128)(2,1)}), bf16[32,64,128]{2,1,0:T(8,128)(2,1)S(1)}, u32[]{:S(2)}, u32[]{:S(2)}) async-start(bf16[32,64,128]{2,1,0:T(8,128)(2,1)} %state_prefix.1), calls=%async_computation.1 | async-start | bytes 1048576 | tf_op jit(solution)/shard_map/all_to_all | solution.py:518
  96.7 16.8 %collective-permute-start.3 = (bf16[48,6144]{1,0:T(8,128)(2,1)S(1)}, bf16[48,6144]{1,0:T(8,128)(2,1)S(1)}, u32[]{:S(2)}, u32[]{:S(2)}) collective-permute-start(bf16[48,6144]{1,0:T(8,128)(2,1)S(1)} %get-tuple-element.57), channel_id=1, source_target_pairs={{0,1},{1,2},{2,3},{3,0},{4,5},{5,6},{6,7},{7,4},{8,9},{9,10},{10,1... | collective-permute-start | bytes 1769480 | tf_op jit(solution)/shard_map/ppermute | solution.py:467
  98.3 27.2 %collective-permute-start.4 = (bf16[48,6144]{1,0:T(8,128)(2,1)S(1)}, bf16[48,6144]{1,0:T(8,128)(2,1)S(1)}, u32[]{:S(2)}, u32[]{:S(2)}) collective-permute-start(bf16[48,6144]{1,0:T(8,128)(2,1)S(1)} %get-tuple-element.58), channel_id=1, source_target_pairs={{0,3},{1,0},{2,1},{3,2},{4,7},{5,4},{6,5},{7,6},{8,11},{9,8},{10,9... | collective-permute-start | bytes 1769480 | tf_op jit(solution)/shard_map/ppermute | solution.py:471
  100.0 27.0 %collective-permute-start.5 = (bf16[48,6144]{1,0:T(8,128)(2,1)S(1)}, bf16[48,6144]{1,0:T(8,128)(2,1)S(1)}, u32[]{:S(2)}, u32[]{:S(2)}) collective-permute-start(bf16[48,6144]{1,0:T(8,128)(2,1)S(1)} %get-tuple-element.59), channel_id=1, source_target_pairs={{0,2},{1,3},{2,0},{3,1},{4,6},{5,7},{6,4},{7,5},{8,10},{9,11},{10,... | collective-permute-start | bytes 1769480 | tf_op jit(solution)/shard_map/ppermute | solution.py:475
  127.7 14.5 %collective-permute-start.10 = (bf16[48,3072]{1,0:T(8,128)(2,1)S(1)}, bf16[48,3072]{1,0:T(8,128)(2,1)S(1)}, u32[]{:S(2)}, u32[]{:S(2)}) collective-permute-start(bf16[48,3072]{1,0:T(8,128)(2,1)S(1)} %get-tuple-element.61.b0), channel_id=1, source_target_pairs={{0,96},{32,0},{64,32},{96,64},{1,97},{33,1},{65,33},{97,65},{2,98}... | collective-permute-start | bytes 884744 | tf_op jit(solution)/shard_map/ppermute | solution.py:471
  130.0 83.4 %collective-permute-start.23 = (bf16[288,6144]{1,0:T(8,128)(2,1)S(1)}, bf16[288,6144]{1,0:T(8,128)(2,1)}, u32[]{:S(2)}, u32[]{:S(2)}) collective-permute-start(bf16[288,6144]{1,0:T(8,128)(2,1)S(1)} %bitcast.23), channel_id=1, source_target_pairs={{0,4},{4,0},{1,5},{5,1},{2,6},{6,2},{3,7},{7,3},{8,12},{12,8},{9,1... | collective-permute-start | bytes 10616840 | tf_op jit(solution)/shard_map/ppermute | solution.py:508
  130.0 86.2 %collective-permute-start.24 = (bf16[288,6144]{1,0:T(8,128)(2,1)S(1)}, bf16[288,6144]{1,0:T(8,128)(2,1)}, u32[]{:S(2)}, u32[]{:S(2)}) collective-permute-start(bf16[288,6144]{1,0:T(8,128)(2,1)S(1)} %bitcast.25), channel_id=1, source_target_pairs={{0,4},{4,0},{1,5},{5,1},{2,6},{6,2},{3,7},{7,3},{8,12},{12,8},{9,1... | collective-permute-start | bytes 10616840 | tf_op jit(solution)/shard_map/ppermute | solution.py:508
  130.5 11.7 %collective-permute-start.11 = (bf16[48,3072]{1,0:T(8,128)(2,1)S(1)}, bf16[48,3072]{1,0:T(8,128)(2,1)S(1)}, u32[]{:S(2)}, u32[]{:S(2)}) collective-permute-start(bf16[48,3072]{1,0:T(8,128)(2,1)S(1)} %get-tuple-element.61.b0), channel_id=1, source_target_pairs={{0,64},{32,96},{64,0},{96,32},{1,65},{33,97},{65,1},{97,33},{2,66}... | collective-permute-start | bytes 884744 | tf_op jit(solution)/shard_map/ppermute | solution.py:475
  142.2 75.4 %collective-permute-start.25 = (bf16[288,6144]{1,0:T(8,128)(2,1)S(1)}, bf16[288,6144]{1,0:T(8,128)(2,1)}, u32[]{:S(2)}, u32[]{:S(2)}) collective-permute-start(bf16[288,6144]{1,0:T(8,128)(2,1)S(1)} %bitcast.27), channel_id=1, source_target_pairs={{0,4},{4,0},{1,5},{5,1},{2,6},{6,2},{3,7},{7,3},{8,12},{12,8},{9,1... | collective-permute-start | bytes 10616840 | tf_op jit(solution)/shard_map/ppermute | solution.py:508
  142.3 19.9 %collective-permute-start.8 = (bf16[48,3072]{1,0:T(8,128)(2,1)S(1)}, bf16[48,3072]{1,0:T(8,128)(2,1)S(1)}, u32[]{:S(2)}, u32[]{:S(2)}) collective-permute-start(bf16[48,3072]{1,0:T(8,128)(2,1)S(1)} %get-tuple-element.60.a0), channel_id=1, source_target_pairs={{0,16},{8,24},{16,0},{24,8},{1,17},{9,25},{17,1},{25,9},{2,18},{10... | collective-permute-start | bytes 884744 | tf_op jit(solution)/shard_map/ppermute | solution.py:475
  163.4 23.1 %collective-permute-start.15 = (bf16[4,48,3072]{2,1,0:T(8,128)(2,1)S(1)}, bf16[4,48,3072]{2,1,0:T(8,128)(2,1)S(1)}, u32[]{:S(2)}, u32[]{:S(2)}) collective-permute-start(bf16[4,48,3072]{2,1,0:T(8,128)(2,1)S(1)} %get-tuple-element.68.refs_0_), channel_id=1, source_target_pairs={{0,32},{32,64},{64,96},{96,0},{1,33},{33,65},{65,97},{97,1},{2,34}... | collective-permute-start | bytes 3538952 | tf_op jit(solution)/shard_map/ppermute | solution.py:467
  163.4 23.6 %collective-permute-start.16 = (bf16[4,48,3072]{2,1,0:T(8,128)(2,1)S(1)}, bf16[4,48,3072]{2,1,0:T(8,128)(2,1)S(1)}, u32[]{:S(2)}, u32[]{:S(2)}) collective-permute-start(bf16[4,48,3072]{2,1,0:T(8,128)(2,1)S(1)} %get-tuple-element.68.refs_0_), channel_id=1, source_target_pairs={{0,96},{32,0},{64,32},{96,64},{1,97},{33,1},{65,33},{97,65},{2,98}... | collective-permute-start | bytes 3538952 | tf_op jit(solution)/shard_map/ppermute | solution.py:471
  186.4 22.9 %collective-permute-start.19 = (bf16[4,48,3072]{2,1,0:T(8,128)(2,1)S(1)}, bf16[4,48,3072]{2,1,0:T(8,128)(2,1)S(1)}, u32[]{:S(2)}, u32[]{:S(2)}) collective-permute-start(bf16[4,48,3072]{2,1,0:T(8,128)(2,1)S(1)} %get-tuple-element.69.refs_5_), channel_id=1, source_target_pairs={{0,8},{8,16},{16,24},{24,0},{1,9},{9,17},{17,25},{25,1},{2,10},{10... | collective-permute-start | bytes 3538952 | tf_op jit(solution)/shard_map/ppermute | solution.py:467
  187.0 26.2 %collective-permute-start.20 = (bf16[4,48,3072]{2,1,0:T(8,128)(2,1)S(1)}, bf16[4,48,3072]{2,1,0:T(8,128)(2,1)S(1)}, u32[]{:S(2)}, u32[]{:S(2)}) collective-permute-start(bf16[4,48,3072]{2,1,0:T(8,128)(2,1)S(1)} %get-tuple-element.69.refs_5_), channel_id=1, source_target_pairs={{0,24},{8,0},{16,8},{24,16},{1,25},{9,1},{17,9},{25,17},{2,26},{10... | collective-permute-start | bytes 3538952 | tf_op jit(solution)/shard_map/ppermute | solution.py:471
  213.1 12.6 %collective-permute-start.18 = (bf16[2,48,3072]{2,1,0:T(8,128)(2,1)S(1)}, bf16[2,48,3072]{2,1,0:T(8,128)(2,1)S(1)}, u32[]{:S(2)}, u32[]{:S(2)}) collective-permute-start(bf16[2,48,3072]{2,1,0:T(8,128)(2,1)S(1)} %slice.17), channel_id=1, source_target_pairs={{0,96},{32,0},{64,32},{96,64},{1,97},{33,1},{65,33},{97,65},{2,98}... | collective-permute-start | bytes 1769480 | tf_op jit(solution)/shard_map/ppermute | solution.py:471
  213.4 13.9 %collective-permute-start.21 = (bf16[2,48,3072]{2,1,0:T(8,128)(2,1)S(1)}, bf16[2,48,3072]{2,1,0:T(8,128)(2,1)S(1)}, u32[]{:S(2)}, u32[]{:S(2)}) collective-permute-start(bf16[2,48,3072]{2,1,0:T(8,128)(2,1)S(1)} %slice.18), channel_id=1, source_target_pairs={{0,8},{8,16},{16,24},{24,0},{1,9},{9,17},{17,25},{25,1},{2,10},{10... | collective-permute-start | bytes 1769480 | tf_op jit(solution)/shard_map/ppermute | solution.py:467
  216.2 13.2 %collective-permute-start.22 = (bf16[2,48,3072]{2,1,0:T(8,128)(2,1)S(1)}, bf16[2,48,3072]{2,1,0:T(8,128)(2,1)S(1)}, u32[]{:S(2)}, u32[]{:S(2)}) collective-permute-start(bf16[2,48,3072]{2,1,0:T(8,128)(2,1)S(1)} %slice.19), channel_id=1, source_target_pairs={{0,24},{8,0},{16,8},{24,16},{1,25},{9,1},{17,9},{25,17},{2,26},{10... | collective-permute-start | bytes 1769480 | tf_op jit(solution)/shard_map/ppermute | solution.py:471
  264.9 13.3 %collective-permute-start.26 = (bf16[2,48,3072]{2,1,0:T(8,128)(2,1)}, bf16[2,48,3072]{2,1,0:T(8,128)(2,1)S(1)}, u32[]{:S(2)}, u32[]{:S(2)}) collective-permute-start(bf16[2,48,3072]{2,1,0:T(8,128)(2,1)} %get-tuple-element.73), channel_id=1, source_target_pairs={{0,32},{32,64},{64,96},{96,0},{1,33},{33,65},{65,97},{97,1},{2,34}... | collective-permute-start | bytes 1769480 | tf_op jit(solution)/shard_map/ppermute | solution.py:467
  265.2 13.0 %collective-permute-start.27 = (bf16[2,48,3072]{2,1,0:T(8,128)(2,1)}, bf16[2,48,3072]{2,1,0:T(8,128)(2,1)S(1)}, u32[]{:S(2)}, u32[]{:S(2)}) collective-permute-start(bf16[2,48,3072]{2,1,0:T(8,128)(2,1)} %get-tuple-element.74), channel_id=1, source_target_pairs={{0,96},{32,0},{64,32},{96,64},{1,97},{33,1},{65,33},{97,65},{2,98}... | collective-permute-start | bytes 1769480 | tf_op jit(solution)/shard_map/ppermute | solution.py:471
  268.2 12.7 %collective-permute-start.28 = (bf16[2,48,3072]{2,1,0:T(8,128)(2,1)}, bf16[2,48,3072]{2,1,0:T(8,128)(2,1)S(1)}, u32[]{:S(2)}, u32[]{:S(2)}) collective-permute-start(bf16[2,48,3072]{2,1,0:T(8,128)(2,1)} %get-tuple-element.77), channel_id=1, source_target_pairs={{0,8},{8,16},{16,24},{24,0},{1,9},{9,17},{17,25},{25,1},{2,10},{10... | collective-permute-start | bytes 1769480 | tf_op jit(solution)/shard_map/ppermute | solution.py:467
  286.6 24.2 %collective-permute-start.30 = (bf16[4,48,3072]{2,1,0:T(8,128)(2,1)S(1)}, bf16[4,48,3072]{2,1,0:T(8,128)(2,1)S(1)}, u32[]{:S(2)}, u32[]{:S(2)}) collective-permute-start(bf16[4,48,3072]{2,1,0:T(8,128)(2,1)S(1)} %get-tuple-element.79), channel_id=1, source_target_pairs={{0,32},{32,64},{64,96},{96,0},{1,33},{33,65},{65,97},{97,1},{2,34}... | collective-permute-start | bytes 3538952 | tf_op jit(solution)/shard_map/ppermute | solution.py:467
  286.7 25.0 %collective-permute-start.31 = (bf16[4,48,3072]{2,1,0:T(8,128)(2,1)S(1)}, bf16[4,48,3072]{2,1,0:T(8,128)(2,1)S(1)}, u32[]{:S(2)}, u32[]{:S(2)}) collective-permute-start(bf16[4,48,3072]{2,1,0:T(8,128)(2,1)S(1)} %get-tuple-element.80), channel_id=1, source_target_pairs={{0,96},{32,0},{64,32},{96,64},{1,97},{33,1},{65,33},{97,65},{2,98}... | collective-permute-start | bytes 3538952 | tf_op jit(solution)/shard_map/ppermute | solution.py:471
  289.9 24.5 %collective-permute-start.32 = (bf16[4,48,3072]{2,1,0:T(8,128)(2,1)S(1)}, bf16[4,48,3072]{2,1,0:T(8,128)(2,1)S(1)}, u32[]{:S(2)}, u32[]{:S(2)}) collective-permute-start(bf16[4,48,3072]{2,1,0:T(8,128)(2,1)S(1)} %get-tuple-element.82), channel_id=1, source_target_pairs={{0,8},{8,16},{16,24},{24,0},{1,9},{9,17},{17,25},{25,1},{2,10},{10... | collective-permute-start | bytes 3538952 | tf_op jit(solution)/shard_map/ppermute | solution.py:467
  291.3 23.1 %collective-permute-start.33 = (bf16[4,48,3072]{2,1,0:T(8,128)(2,1)S(1)}, bf16[4,48,3072]{2,1,0:T(8,128)(2,1)S(1)}, u32[]{:S(2)}, u32[]{:S(2)}) collective-permute-start(bf16[4,48,3072]{2,1,0:T(8,128)(2,1)S(1)} %get-tuple-element.83), channel_id=1, source_target_pairs={{0,24},{8,0},{16,8},{24,16},{1,25},{9,1},{17,9},{25,17},{2,26},{10... | collective-permute-start | bytes 3538952 | tf_op jit(solution)/shard_map/ppermute | solution.py:471
  293.1 58.7 %collective-permute-start.12 = (bf16[128,6144]{1,0:T(8,128)(2,1)S(1)}, bf16[128,6144]{1,0:T(8,128)(2,1)S(1)}, u32[]{:S(2)}, u32[]{:S(2)}) collective-permute-start(bf16[128,6144]{1,0:T(8,128)(2,1)S(1)} %get-tuple-element.65), channel_id=1, source_target_pairs={{0,1},{1,2},{2,3},{3,0},{4,5},{5,6},{6,7},{7,4},{8,9},{9,10},{10,1... | collective-permute-start | bytes 4718600 | tf_op jit(solution)/shard_map/ppermute | solution.py:467
  310.9 51.6 %collective-permute-start.13 = (bf16[128,6144]{1,0:T(8,128)(2,1)S(1)}, bf16[128,6144]{1,0:T(8,128)(2,1)}, u32[]{:S(2)}, u32[]{:S(2)}) collective-permute-start(bf16[128,6144]{1,0:T(8,128)(2,1)S(1)} %get-tuple-element.66), channel_id=1, source_target_pairs={{0,2},{1,3},{2,0},{3,1},{4,6},{5,7},{6,4},{7,5},{8,10},{9,11},{10,... | collective-permute-start | bytes 4718600 | tf_op jit(solution)/shard_map/ppermute | solution.py:475
  311.7 68.0 %collective-permute-start.14 = (bf16[128,6144]{1,0:T(8,128)(2,1)S(1)}, bf16[128,6144]{1,0:T(8,128)(2,1)}, u32[]{:S(2)}, u32[]{:S(2)}) collective-permute-start(bf16[128,6144]{1,0:T(8,128)(2,1)S(1)} %get-tuple-element.67), channel_id=1, source_target_pairs={{0,3},{1,0},{2,1},{3,2},{4,7},{5,4},{6,5},{7,6},{8,11},{9,8},{10,9... | collective-permute-start | bytes 4718600 | tf_op jit(solution)/shard_map/ppermute | solution.py:471
  316.4 11.4 %collective-permute-start.35 = (bf16[48,3072]{1,0:T(8,128)(2,1)S(1)}, bf16[48,3072]{1,0:T(8,128)(2,1)S(1)}, u32[]{:S(2)}, u32[]{:S(2)}) collective-permute-start(bf16[48,3072]{1,0:T(8,128)(2,1)S(1)} %get-tuple-element.89), channel_id=1, source_target_pairs={{0,24},{8,0},{16,8},{24,16},{1,25},{9,1},{17,9},{25,17},{2,26},{10... | collective-permute-start | bytes 884744 | tf_op jit(solution)/shard_map/ppermute | solution.py:471
  348.4 38.3 %collective-permute-start.40 = (bf16[16,6144]{1,0:T(8,128)(2,1)}, bf16[16,6144]{1,0:T(8,128)(2,1)}, u32[]{:S(2)}, u32[]{:S(2)}) collective-permute-start(bf16[16,6144]{1,0:T(8,128)(2,1)} %get-tuple-element.96), channel_id=1, source_target_pairs={{0,3},{1,0},{2,1},{3,2},{4,7},{5,4},{6,5},{7,6},{8,11},{9,8},{10,9... | collective-permute-start | bytes 589832 | tf_op jit(solution)/shard_map/ppermute | solution.py:471
  349.7 36.9 %collective-permute-start.41 = (bf16[16,6144]{1,0:T(8,128)(2,1)}, bf16[16,6144]{1,0:T(8,128)(2,1)}, u32[]{:S(2)}, u32[]{:S(2)}) collective-permute-start(bf16[16,6144]{1,0:T(8,128)(2,1)} %get-tuple-element.97), channel_id=1, source_target_pairs={{0,1},{1,2},{2,3},{3,0},{4,5},{5,6},{6,7},{7,4},{8,9},{9,10},{10,1... | collective-permute-start | bytes 589832 | tf_op jit(solution)/shard_map/ppermute | solution.py:467
  353.0 33.7 %collective-permute-start.42 = (bf16[16,6144]{1,0:T(8,128)(2,1)}, bf16[16,6144]{1,0:T(8,128)(2,1)}, u32[]{:S(2)}, u32[]{:S(2)}) collective-permute-start(bf16[16,6144]{1,0:T(8,128)(2,1)} %get-tuple-element.98), channel_id=1, source_target_pairs={{0,2},{1,3},{2,0},{3,1},{4,6},{5,7},{6,4},{7,5},{8,10},{9,11},{10,... | collective-permute-start | bytes 589832 | tf_op jit(solution)/shard_map/ppermute | solution.py:475
  (55 other events, 795.9 us)
Sparse Core Ops, SparseCore 0:
  9.6 75.2 all-gather.1

commit v2 on v1

--- a/solution.py
+++ b/solution.py
@@ -109,23 +109,22 @@
     )(arrived)
 
 
-def carry_kernel(me_ref, q_ref, inner_ref, cum_ref, state_ref, gain_ref, out_ref):
+def carry_kernel(q_ref, inner_ref, cum_ref, state_ref, gain_ref, out_ref):
     shares, slice_len = out_ref.shape[0], out_ref.shape[2]
     heads = cum_ref.shape[2]
     grow = jnp.exp(cum_ref[0])
-    me = me_ref[0]
     for h in range(heads):
         sl = slice(h * HEAD, (h + 1) * HEAD)
         head = inner_ref[0, :, sl] + mm(q_ref[0, :, sl], state_ref[h]) * grow[:, h : h + 1]
         scale = lax.rsqrt(jnp.mean(head * head, -1, keepdims=True) + 1e-06)
         normed = (head * scale * gain_ref[:, sl]).astype(BF)
         for a in range(shares):
-            out_ref[lax.rem(a - me + shares, shares), 0, :, sl] = normed[
+            out_ref[a, 0, :, sl] = normed[
                 a * slice_len : (a + 1) * slice_len
             ]
 
 
-def carried(me, q, inner, cum, state, gain, shares):
+def carried(q, inner, cum, state, gain, shares):
     seqs, steps, width = q.shape
     heads = width // HEAD
     block = pl.BlockSpec((1, steps, width), lambda s: (s, 0, 0))
@@ -133,7 +132,6 @@
         carry_kernel,
         grid=(seqs,),
         in_specs=[
-            pl.BlockSpec(memory_space=pltpu.SMEM),
             block,
             block,
             pl.BlockSpec((1, steps, heads), lambda s: (s, 0, 0)),
@@ -144,10 +142,10 @@
         out_shape=jax.ShapeDtypeStruct((shares, seqs, steps // shares, width), BF),
         compiler_params=pltpu.CompilerParams(vmem_limit_bytes=48 * 2**20),
         name="carried_norm",
-    )(me, q, inner, cum, state, gain)
-
-
-def route_kernel(cap, me_ref, routes_ref, place_ref):
+    )(q, inner, cum, state, gain)
+
+
+def route_kernel(cap, me_ref, routes_ref, place_ref, own_ref):
     flight, rows = routes_ref.shape[1] // 128, 128
     total = routes_ref.shape[1]
     me = me_ref[0]
@@ -166,7 +164,11 @@
             start = jnp.where(home == delta, cap * JREL[(delta - off) % 4], start)
         target = jnp.where(chosen > 0.0, start + rank, -1)
         hits = (slots == target).astype(F32).astype(BF)
-        place_ref[r * flight * cap : (r + 1) * flight * cap, :] = hits
+        span = slice(r * flight * cap, (r + 1) * flight * cap)
+        own_ref[span, :] = hits[:, :rows]
+        for delta in range(flight):
+            at = pl.multiple_of(lax.rem(me + delta, flight) * rows, rows)
+            place_ref[span, pl.ds(at, rows)] = hits[:, delta * rows : (delta + 1) * rows]
 
 
 def call(kernel, name, outs, *args, **kw):
@@ -191,33 +193,32 @@
     return call(
         functools.partial(route_kernel, cap),
         "route",
-        [((flight * flight * cap, total), BF)],
+        [((flight * flight * cap, n), BF) for n in (total, 128)],
         me,
         routes,
         in_specs=[SM, VM],
-        out_specs=[VM],
-    )[0]
+        out_specs=[VM, VM],
+    )
 
 
 def nt(a, b):
     return lax.dot_general(a, b, (((1,), (1,)), ((), ())), preferred_element_type=F32)
 
 
-def selected_kernel(place_ref, normed_ref, weight_ref, res_ref, o0, o1, o2, o3, picked):
-    rows = res_ref.shape[0]
+def selected_kernel(place_ref, own_ref, normed_ref, weight_ref, res_ref, o0, o1, o2, o3, picked):
 
     @pl.when(pl.program_id(0) == 0)
     def _():
         picked[...] = mm(place_ref[...], normed_ref[...]).astype(BF)
 
-    full = nt(picked[...], weight_ref[...]) + mm(place_ref[:, :rows], res_ref[...])
+    full = nt(picked[...], weight_ref[...]) + mm(own_ref[...], res_ref[...])
     full = full.astype(BF)
     size = o0.shape[0]
     for i, o in enumerate((o0, o1, o2, o3)):
         o[...] = full[i * size : (i + 1) * size]
 
 
-def selected(place, normed, weight, res, tile=1024):
+def selected(place, own, normed, weight, res, tile=1024):
     picks, (model, width) = place.shape[0], weight.shape
     rows = res.shape[0]
     size = picks // 4
@@ -227,12 +228,14 @@
         "selected_projection",
         [((size, model), BF)] * 4,
         place,
+        own,
         normed,
         weight,
         res,
         grid=(model // tile,),
         in_specs=[
             whole(place),
+            whole(own),
             whole(normed),
             pl.BlockSpec((tile, width), lambda n: (n, 0)),
             pl.BlockSpec((rows, tile), lambda n: (0, n)),
@@ -242,20 +245,16 @@
     )
 
 
-def whole_kernel(normed_ref, weight_ref, o0, o1, o2, o3):
-    full = nt(normed_ref[...], weight_ref[...]).astype(BF)
-    size = o0.shape[0]
-    for i, o in enumerate((o0, o1, o2, o3)):
-        o[...] = full[i * size : (i + 1) * size]
+def whole_kernel(normed_ref, weight_ref, out_ref):
+    out_ref[...] = nt(normed_ref[...], weight_ref[...]).astype(BF)
 
 
 def whole_projection(normed, weight, tile=1024):
     total, (model, width) = normed.shape[0], weight.shape
-    size = total // 4
     return call(
         whole_kernel,
         "whole_projection",
-        [((size, model), BF)] * 4,
+        [((total, model), BF)],
         normed,
         weight,
         grid=(model // tile,),
@@ -263,14 +262,14 @@
             pl.BlockSpec(normed.shape, lambda n: (0, 0)),
             pl.BlockSpec((tile, width), lambda n: (n, 0)),
         ],
-        out_specs=[pl.BlockSpec((size, tile), lambda n: (0, n))] * 4,
+        out_specs=[pl.BlockSpec((total, tile), lambda n: (0, n))],
         cost_estimate=pl.CostEstimate(
             flops=2 * total * model * width, bytes_accessed=4 * model * width, transcendentals=0
         ),
-    )
-
-
-def norm_kernel(a, b, c, d, gain, o0, o1):
+    )[0]
+
+
+def norm_kernel(a, b, c, d, gain, held, o0, o1, same):
     x = a[...].astype(F32) + b[...].astype(F32) + c[...].astype(F32) + d[...].astype(F32)
     x = x * lax.rsqrt(jnp.mean(x * x, -1, keepdims=True) + 1e-06) * gain[...]
     half = o0.shape[1]
@@ -278,118 +277,78 @@
     o1[...] = x[:, half:].astype(BF)
 
 
-def stack_kernel(a0, a1, a2, a3, b0, b1, b2, b3, p0, p1, p2, o0, o1, q0, q1, q2):
+def stack_kernel(a0, a1, a2, a3, b0, b1, b2, b3, w0, w1, w2, o0, o1, *same):
     for i, (a, b) in enumerate(((a0, b0), (a1, b1), (a2, b2), (a3, b3))):
         o0[i] = a[...]
         o1[i] = b[...]
 
 
-def expert_kernel(half_steps, *refs):
+def expert_kernel(tile, *refs):
     xa, xb = refs[0:5], refs[5:10]
-    gate0, gate1, up0, up1, down0, down1 = refs[10:16]
-    oa, ob = refs[16:21], refs[21:26]
-    x, gates, uppers, hidden = refs[26:]
-    step = pl.program_id(0)
-    rows, units = xa[0].shape[1], gate0.shape[0]
-    steps = 2 * half_steps
+    gate, up, down = refs[10:13]
+    oa, ob = refs[13:18], refs[18:23]
+    x, gates, uppers, hidden = refs[23:]
+    rows, half = xa[0].shape[1], xa[0].shape[2]
 
     def piece(refs, u, v):
         if u < 3:
-            return refs[u].at[v]
-        return refs[3].at[v] if v < 2 else refs[4].at[v - 2]
-
-    def span(z, y):
-        return pl.ds((z * 4 + y) * rows, rows)
-
-    @pl.when(step < half_steps)
-    def _():
+            return refs[u], v
+        return (refs[3], v) if v < 2 else (refs[4], v - 2)
+
+    def pieces(refs, flip):
         for z in range(4):
             for y in range(4):
-                x[span(z, y), :] = piece(xa, z, y)[...]
-
-    @pl.when((step >= half_steps) & (step < steps))
-    def _():
-        for z in range(4):
-            for y in range(4):
-                x[span(z, y), :] = piece(xb, y, z)[...]
-
-    @pl.when(step < steps)
-    def _():
-        for i, (g, u) in enumerate(((gate0, up0), (gate1, up1))):
-            sl = slice(i * units, (i + 1) * units)
-            new_g, new_u = nt(g[...], x[...]), nt(u[...], x[...])
-
-            @pl.when(step == 0)
-            def _():
-                gates[sl, :] = new_g
-                uppers[sl, :] = new_u
-
-            @pl.when(step > 0)
-            def _():
-                gates[sl, :] += new_g
-                uppers[sl, :] += new_u
-
-    @pl.when(step == steps - 1)
-    def _():
-        g = gates[...]
-        hidden[...] = (g / (1.0 + jnp.exp(-g)) * uppers[...]).T.astype(BF)
-
-    def out(write):
-        full = mm(hidden[:, :units], down0[...]) + mm(hidden[:, units:], down1[...])
-        for z in range(4):
-            for y in range(4):
-                at = (z * 4 + y) * rows
-                write(z, y, full[at : at + rows].astype(BF))
-
-    @pl.when((step >= steps) & (step < steps + half_steps))
-    def _():
-        def write(z, y, v):
-            piece(oa, z, y)[...] = v
-
-        out(write)
-
-    @pl.when(step >= steps + half_steps)
-    def _():
-        def write(z, y, v):
-            piece(ob, y, z)[...] = v
-
-        out(write)
-
-
-def expert(xa, xb, gates, ups, downs, tile=1024):
+                ref, i = piece(refs, y, z) if flip else piece(refs, z, y)
+                yield (z * 4 + y) * rows, ref, i
+
+    gates[...] = jnp.zeros_like(gates)
+    uppers[...] = jnp.zeros_like(uppers)
+    for k, (refs_x, flip) in enumerate(((xa, False), (xb, True))):
+
+        @pl.loop(0, half // tile)
+        def _(c):
+            at = pl.ds(pl.multiple_of(c * tile, tile), tile)
+            wide = pl.ds(pl.multiple_of(k * half + c * tile, tile), tile)
+            for row, ref, i in pieces(refs_x, flip):
+                x[row : row + rows, :] = ref[i, :, at]
+            gates[...] += nt(gate[:, wide], x[...])
+            uppers[...] += nt(up[:, wide], x[...])
+
+    g = gates[...]
+    hidden[...] = (g / (1.0 + jnp.exp(-g)) * uppers[...]).T.astype(BF)
+    for k, (refs_o, flip) in enumerate(((oa, False), (ob, True))):
+
+        @pl.loop(0, half // tile)
+        def _(c):
+            at = pl.ds(pl.multiple_of(c * tile, tile), tile)
+            wide = pl.ds(pl.multiple_of(k * half + c * tile, tile), tile)
+            full = mm(hidden[...], down[:, wide]).astype(BF)
+            for row, ref, i in pieces(refs_o, flip):
+                ref[i, :, at] = full[row : row + rows]
+
+
+def expert(xa, xb, gate, up, down, tile=1024):
     rows, half = xa[0].shape[1], xa[0].shape[2]
-    units = gates[0].shape[0]
-    n = half // tile
-
-    def clip(low):
-        return lambda s: jnp.clip(s - low, 0, n - 1)
-
-    def cols(low):
-        at = clip(low)
-        return [pl.BlockSpec((k, rows, tile), lambda s: (0, 0, at(s))) for k in (4, 4, 4, 2, 2)]
-
-    first = pl.BlockSpec((units, tile), lambda s: (0, jnp.clip(s, 0, 2 * n - 1)))
-    last = pl.BlockSpec((units, tile), lambda s: (0, jnp.clip(s - 2 * n, 0, 2 * n - 1)))
+    units = gate.shape[0]
     total = 16 * rows
     outs = call(
-        functools.partial(expert_kernel, n),
+        functools.partial(expert_kernel, tile),
         "expert",
         [((k, rows, half), BF) for k in (4, 4, 4, 2, 2)] * 2,
         *xa,
         *xb,
-        *gates,
-        *ups,
-        *downs,
-        grid=(4 * n,),
-        in_specs=cols(0) + cols(n) + [first] * 4 + [last] * 2,
-        out_specs=cols(2 * n) + cols(3 * n),
+        gate,
+        up,
+        down,
+        in_specs=[VM] * 13,
+        out_specs=[VM] * 10,
         scratch_shapes=[
             pltpu.VMEM((total, tile), BF),
-            pltpu.VMEM((2 * units, total), F32),
-            pltpu.VMEM((2 * units, total), F32),
-            pltpu.VMEM((total, 2 * units), BF),
+            pltpu.VMEM((units, total), F32),
+            pltpu.VMEM((units, total), F32),
+            pltpu.VMEM((total, units), BF),
         ],
-        vmem=56,
+        vmem=20,
     )
     return outs[:5], outs[5:]
 
@@ -425,10 +384,8 @@
             o[:, k * half : (k + 1) * half] = mm(pick, total).astype(BF)
 
 
-def home_kernel(me_ref, routes_ref, res, own, r1, r2, r3, gain, router, late, hidden_ref, hi_ref, lo_ref):
-    x = res[...].astype(F32)
-    for p in (own, r1, r2, r3):
-        x = x + p[...].astype(F32)
+def home_kernel(me_ref, routes_ref, res, mixed, gain, router, late, hidden_ref, hi_ref, lo_ref):
+    x = res[...].astype(F32) + mixed[...].astype(F32)
     hidden_ref[...] = x
     normed = (x * lax.rsqrt(jnp.mean(x * x, -1, keepdims=True) + 1e-06) * gain[...]).astype(BF)
     logits = mm(normed, router[...])
@@ -503,9 +460,9 @@
     me = lax.axis_index("x").astype(jnp.int32).reshape(1)
 
     weight_out = lax.all_gather(out_weight.T, SEQ, axis=0, tiled=True)
-    swap = ring(2, 1)
-    gates, ups, downs = [
-        (w[0], lax.ppermute(w[0], "core", swap)) for w in (gate_weight, up_weight, down_weight)
+    gate, up, down = [
+        lax.all_gather(w[0], "core", axis=0, tiled=True)
+        for w in (gate_weight, up_weight, down_weight)
     ]
     routes = picks.reshape(rows, 2)
     turned = routes.T
@@ -518,33 +475,36 @@
     prefix = lax.all_to_all(scan_states(arrived), SEQ, 0, 0, tiled=True)
     prefix = prefix.reshape(seqs * width // HEAD, HEAD, HEAD)
     normed = carried(
-        me, queries, inner, cum, prefix, attn_gain.reshape(1, width), shares
+        queries, inner, cum, prefix, attn_gain.reshape(1, width), shares
     ).reshape(shares * rows, width)
 
-    place = route(me, all_routes, cap)
+    place, own_place = route(me, all_routes, cap)
     flat = residual.reshape(rows, model)
     gain = norm_gain.reshape(1, model)
-    to_up, to_down, to_far, here = selected(place, normed, weight_out, flat)
-    own, d1, d2, d3 = whole_projection(normed, weight_out)
+    to_up, to_down, to_far, here = selected(place, own_place, normed, weight_out, flat)
+    whole = whole_projection(normed, weight_out)
 
     size = here.shape[0]
-    a0, b0 = call(
+    a0, b0, whole = call(
         norm_kernel,
         "selected_norm",
-        [((size, half), BF)] * 2,
+        [((size, half), BF)] * 2 + [(whole.shape, BF)],
         here,
         up_one(to_up, "x"),
         down_one(to_down, "x"),
         across(to_far, "x"),
         gain,
-        in_specs=[VM] * 5,
-        out_specs=[VM] * 2,
-    )
-
-    a4, b4, d1, d2, d3 = call(
+        whole,
+        in_specs=[VM] * 5 + [ANY],
+        out_specs=[VM] * 2 + [ANY],
+        input_output_aliases={5: 2},
+    )
+    mixed = lax.psum_scatter(whole, "x", scatter_dimension=0, tiled=True)
+
+    a4, b4, gate, up, down = call(
         stack_kernel,
         "stack",
-        [((4, size, half), BF)] * 2 + [((rows, model), BF)] * 3,
+        [((4, size, half), BF)] * 2 + [(w.shape, BF) for w in (gate, up, down)],
         a0,
         up_one(a0, "y"),
         down_one(a0, "y"),
@@ -553,9 +513,9 @@
         up_one(b0, "z"),
         down_one(b0, "z"),
         across(b0, "z"),
-        d1,
-        d2,
-        d3,
+        gate,
+        up,
+        down,
         in_specs=[VM] * 8 + [ANY] * 3,
         out_specs=[VM] * 2 + [ANY] * 3,
         input_output_aliases={8: 2, 9: 3, 10: 4},
@@ -565,7 +525,7 @@
     a_far, b_far = far_sides(a_below, a_above, "z"), far_sides(b_below, b_above, "y")
 
     oa, ob = expert(
-        (a4, a_below, a_above, *a_far), (b4, b_below, b_above, *b_far), gates, ups, downs
+        (a4, a_below, a_above, *a_far), (b4, b_below, b_above, *b_far), gate, up, down
     )
     a_below, a_above, b_below, b_above = call(
         fold_kernel,
@@ -618,14 +578,11 @@
         me,
         routes,
         flat,
-        own,
-        up_one(d1, "x"),
-        across(d2, "x"),
-        down_one(d3, "x"),
+        mixed,
         gain,
         router_weight,
         parts[0],
-        in_specs=[SM] + [VM] * 8 + [ANY],
+        in_specs=[SM] + [VM] * 5 + [ANY],
         out_specs=[VM] * 3,
         vmem=56,
     )

time: 401 us -> 332 us (0.83)
  waiting for transfers between devices: 203 us -> 140 us
  Pallas kernels: 78.7 us -> 63.2 us
  starting transfers between devices: 55.7 us -> 62 us
    ppermute x15 -> x14, waiting for transfers between devices: 92.5 us -> 43.8 us  [up_one(): return lax.ppermute(x, axis, ring(4, 1))]
    pallas_call x11, Pallas kernels: 69.6 us -> 54.2 us  [call(): pl.pallas_call(kernel, out_shape=[jax.ShapeDtypeStruct(s, d) for s, d in...]
    ppermute x15 -> x14, waiting for transfers between devices: 62.7 us -> 47.7 us  [down_one(): return lax.ppermute(x, axis, ring(4, -1))]
    all_gather x0 -> x3, waiting for transfers between devices: none -> 12.3 us  [shards(): lax.all_gather(w[0], 'core', axis=0, tiled=True)]
    ppermute x7 -> x6, waiting for transfers between devices: 20.4 us -> 8.85 us  [across(): return lax.ppermute(x, axis, ring(4, 2))]
    ppermute x15 -> x14, starting transfers between devices: 29.4 us -> 37.9 us  [down_one(): return lax.ppermute(x, axis, ring(4, -1))]
    ppermute x15 -> x14, starting transfers between devices: 11.9 us -> 4.59 us  [up_one(): return lax.ppermute(x, axis, ring(4, 1))]
    ppermute x7 -> x6, starting transfers between devices: 5.47 us -> 9.77 us  [across(): return lax.ppermute(x, axis, ring(4, 2))]
  transfers between devices with their start and end apart: 45 -> 43, of which waited for: 28 -> 24; matrix products, arithmetic and copies ran while one was open for 1% -> 1% of each run, Pallas kernels for 7% -> 18%
where the time goes in v2:
time: 332 us; the launch traced here: 331 us
  waiting for transfers between devices  140 us (42%)
  Pallas kernels  63.2 us (19%)
  starting transfers between devices  62 us (19%)
  local copies, waits for them, and re-layouts  26.8 us (8%)
  blocking collectives  25.2 us (8%)
  between operations  13.5 us (4%)
    pallas_call x11, Pallas kernels, call(): pl.pallas_call(kernel, out_shape=[jax.ShapeDtypeStruct(s, d) for s, d in...  54.2 us
    ppermute x14, waiting for transfers between devices, down_one(): return lax.ppermute(x, axis, ring(4, -1))  47.7 us
    ppermute x14, waiting for transfers between devices, up_one(): return lax.ppermute(x, axis, ring(4, 1))  43.8 us
    ppermute x14, starting transfers between devices, down_one(): return lax.ppermute(x, axis, ring(4, -1))  37.9 us
    unnamed x53, local copies, waits for them, and re-layouts  26.3 us
    all_to_all x1, blocking collectives, shards(): arrived = lax.all_to_all(states, SEQ, 0, 0, tiled=True)  25.2 us
    all_gather x1, waiting for transfers between devices, shards(): weight_out = lax.all_gather(out_weight.T, SEQ, axis=0, tiled=True)  16.7 us
    all_gather x3, waiting for transfers between devices, shards(): lax.all_gather(w[0], 'core', axis=0, tiled=True)  12.3 us
  transfers between devices with their start and end apart: 43, of which 24 were waited for; matrix products, arithmetic and copies ran while one was open for 1% of the time, Pallas kernels for 18%

profile of v2, /device:TPU:0, one launch (start us, length us, event | category | flops | bytes accessed | tf_op | source)
XLA Modules:
  0.0 330.7 jit_solution(6631688190315761645)
XLA Ops:
  10.6 6.0 %local_attention.1 = (f32[2,256,1024]{2,1,0:T(8,128)}, bf16[32,80,128]{2,1,0:T(8,128)(2,1)S(1)}, f32[2,256,8]{2,1,0:T(8,128)S(1)}) custom-call(bf16[2,256,1024]{2,1,0:T(8,128)(2,1)S(1)} %copy-done.6, bf16[2,256,1024]{2,1,0:T(8,128)(2,1)S(1)} %copy-done.11, bf16[2,256,1024]{2,1,0:T(8,128)(2,1)S(1)} %copy-done.12, f32[2,256,8]{2,1,0:T(8,128)S(1)} %copy.27.d_ref), custom_call_target="tpu_custom_call" | custom-call | tf_op jit(solution)/shard_map/local_attention/pallas_call | solution.py:77
  17.3 25.2 %all_to_all.10.in_ref = bf16[32,80,128]{2,1,0:T(8,128)(2,1)S(1)} all-to-all(bf16[32,80,128]{2,1,0:T(8,128)(2,1)S(1)} %get-tuple-element.55), channel_id=1, replica_groups=mesh['z'=4,'y'=4,'core'=2,'x'=4] {'z','y','core'}, dimensions={0} | all-to-all | bytes 1310720 | tf_op jit(solution)/shard_map/all_to_all | solution.py:474
  43.4 3.9 %all-to-all-start.1 = ((bf16[32,64,128]{2,1,0:T(8,128)(2,1)}), bf16[32,64,128]{2,1,0:T(8,128)(2,1)S(1)}, u32[]{:S(2)}, u32[]{:S(2)}) async-start(bf16[32,64,128]{2,1,0:T(8,128)(2,1)} %state_prefix.1), calls=%async_computation.1 | async-start | bytes 1048576 | tf_op jit(solution)/shard_map/all_to_all | solution.py:475
  57.1 5.6 %all-to-all-done.1 = bf16[32,64,128]{2,1,0:T(8,128)(2,1)S(1)} async-done(((bf16[32,64,128]{2,1,0:T(8,128)(2,1)}), bf16[32,64,128]{2,1,0:T(8,128)(2,1)S(1)}, u32[]{:S(2)}, u32[]{:S(2)}) %all-to-all-start.1) | async-done | bytes 524320 | tf_op jit(solution)/shard_map/all_to_all | solution.py:475
  67.8 16.7 %all-gather.8.cloned.1.call-done.weight_ref = bf16[6144,1024]{1,0:T(8,128)(2,1)} async-done(((bf16[192,1024]{1,0:T(8,128)(2,1)}), bf16[6144,1024]{1,0:T(8,128)(2,1)}) %all-gather.8.cloned.1.call-update) | async-done | bytes 12582928 | tf_op jit(solution)/shard_map/all_gather | solution.py:462
  85.4 9.3 %selected_projection.1 = (bf16[48,6144]{1,0:T(8,128)(2,1)S(1)}, bf16[48,6144]{1,0:T(8,128)(2,1)S(1)}, bf16[48,6144]{1,0:T(8,128)(2,1)S(1)}, bf16[48,6144]{1,0:T(8,128)(2,1)S(1)}) custom-call(bf16[192,512]{1,0:T(8,128)(2,1)S(1)} %copy-done.16, bf16[192,128]{1,0:T(8,128)(2,1)S(1)} %get-tuple-element.52.own_ref, bf16[512,1024]{1,0:T(8,128)(2,1)S(1)} %bitcast.18, ...), custom_call_target="tpu_custom_call" | custom-call | tf_op jit(solution)/shard_map/selected_projection/pallas_call | solution.py:176
  99.8 10.4 %whole_projection.1.held = bf16[512,6144]{1,0:T(8,128)(2,1)S(1)} custom-call(bf16[512,1024]{1,0:T(8,128)(2,1)S(1)} %bitcast.19, bf16[6144,1024]{1,0:T(8,128)(2,1)} %all-gather.8.cloned.1.call-done.weight_ref), custom_call_target="tpu_custom_call" | custom-call | flops 6442450944 | bytes 25165824 | tf_op jit(solution)/shard_map/whole_projection/pallas_call | solution.py:176
  111.5 11.9 %collective-permute-done.4.c = bf16[48,6144]{1,0:T(8,128)(2,1)S(1)} collective-permute-done((bf16[48,6144]{1,0:T(8,128)(2,1)S(1)}, bf16[48,6144]{1,0:T(8,128)(2,1)S(1)}, u32[]{:S(2)}, u32[]{:S(2)}) %collective-permute-start.4) | collective-permute-done | bytes 589856 | tf_op jit(solution)/shard_map/ppermute | solution.py:428
  128.4 3.0 collective-permute-start.8
  136.7 3.2 collective-permute-done.8.a3
  141.0 12.3 %all-gather.14.cloned.1.call-done = bf16[1,576,6144]{2,1,0:T(8,128)(2,1)} async-done(((bf16[1,288,6144]{2,1,0:T(8,128)(2,1)}), bf16[1,576,6144]{2,1,0:T(8,128)(2,1)}) %all-gather.14.cloned.1.call-update) | async-done | bytes 7077904 | tf_op jit(solution)/shard_map/all_gather | solution.py:464
  153.3 3.0 copy-done
  156.4 2.9 copy-done.1
  159.3 3.0 collective-permute-start.13
  162.3 2.7 collective-permute-start.17
  165.1 22.9 %collective-permute-done.13.refs_2_ = bf16[4,48,3072]{2,1,0:T(8,128)(2,1)S(1)} collective-permute-done((bf16[4,48,3072]{2,1,0:T(8,128)(2,1)S(1)}, bf16[4,48,3072]{2,1,0:T(8,128)(2,1)S(1)}, u32[]{:S(2)}, u32[]{:S(2)}) %collective-permute-start.13) | collective-permute-done | bytes 1179680 | tf_op jit(solution)/shard_map/ppermute | solution.py:428
  188.1 3.8 %collective-permute-start.15 = (bf16[2,48,3072]{2,1,0:T(8,128)(2,1)S(1)}, bf16[2,48,3072]{2,1,0:T(8,128)(2,1)S(1)}, u32[]{:S(2)}, u32[]{:S(2)}) collective-permute-start(bf16[2,48,3072]{2,1,0:T(8,128)(2,1)S(1)} %slice.17), channel_id=1, source_target_pairs={{0,96},{32,0},{64,32},{96,64},{1,97},{33,1},{65,33},{97,65},{2,98}... | collective-permute-start | bytes 1769480 | tf_op jit(solution)/shard_map/ppermute | solution.py:428
  192.0 2.8 collective-permute-start.19
  195.0 9.2 %collective-permute-done.15.refs_4_ = bf16[2,48,3072]{2,1,0:T(8,128)(2,1)S(1)} collective-permute-done((bf16[2,48,3072]{2,1,0:T(8,128)(2,1)S(1)}, bf16[2,48,3072]{2,1,0:T(8,128)(2,1)S(1)}, u32[]{:S(2)}, u32[]{:S(2)}) %collective-permute-start.15) | collective-permute-done | bytes 589856 | tf_op jit(solution)/shard_map/ppermute | solution.py:428
  204.2 3.5 %collective-permute-done.14.refs_3_ = bf16[2,48,3072]{2,1,0:T(8,128)(2,1)S(1)} collective-permute-done((bf16[2,48,3072]{2,1,0:T(8,128)(2,1)S(1)}, bf16[2,48,3072]{2,1,0:T(8,128)(2,1)S(1)}, u32[]{:S(2)}, u32[]{:S(2)}) %collective-permute-start.14) | collective-permute-done | bytes 589856 | tf_op jit(solution)/shard_map/ppermute | solution.py:424
  207.7 2.7 collective-permute-done.18.refs_8_
  210.4 3.1 copy-done.2
  213.6 3.0 copy-done.3
  216.6 24.5 %expert.1 = (bf16[4,48,3072]{2,1,0:T(8,128)(2,1)S(1)}, bf16[4,48,3072]{2,1,0:T(8,128)(2,1)S(1)}, bf16[4,48,3072]{2,1,0:T(8,128)(2,1)S(1)}, bf16[2,48,3072]{2,1,0...) custom-call(bf16[4,48,3072]{2,1,0:T(8,128)(2,1)S(1)} %get-tuple-elem, ...), custom_call_target="tpu_custom_call" | custom-call | tf_op jit(solution)/shard_map/expert/pallas_call | solution.py:176
  241.2 3.2 collective-permute-start.21
  244.4 3.2 collective-permute-start.23
  247.6 8.3 %collective-permute-done.20.up0 = bf16[2,48,3072]{2,1,0:T(8,128)(2,1)S(1)} collective-permute-done((bf16[2,48,3072]{2,1,0:T(8,128)(2,1)S(1)}, bf16[2,48,3072]{2,1,0:T(8,128)(2,1)S(1)}, u32[]{:S(2)}, u32[]{:S(2)}) %collective-permute-start.20) | collective-permute-done | bytes 589856 | tf_op jit(solution)/shard_map/ppermute | solution.py:424
  259.3 3.2 collective-permute-start.25
  262.5 3.2 collective-permute-start.27
  265.7 19.4 %collective-permute-done.24.u0 = bf16[4,48,3072]{2,1,0:T(8,128)(2,1)S(1)} collective-permute-done((bf16[4,48,3072]{2,1,0:T(8,128)(2,1)S(1)}, bf16[4,48,3072]{2,1,0:T(8,128)(2,1)S(1)}, u32[]{:S(2)}, u32[]{:S(2)}) %collective-permute-start.24) | collective-permute-done | bytes 1179680 | tf_op jit(solution)/shard_map/ppermute | solution.py:424
  293.4 3.2 collective-permute-start.32
  312.9 4.7 %home.1 = (f32[128,6144]{1,0:T(8,128)}, bf16[128,64]{1,0:T(8,128)(2,1)}, bf16[128,64]{1,0:T(8,128)(2,1)}) custom-call(s32[1]{0:T(128)} %bitcast.me_ref, s32[128,2]{1,0:T(8,128)} %bitcast.29, bf16[128,6144]{1,0:T(8,128)(2,1)} %bitcast.16, bf16[128,6144]{1,0:T(8,128)(2,1)} %reduce-scatter.2.cloned.1.call-done.mixed, f32[1,6144]{1,0:T(1,128)} %bitcast.21, ...), custom_call_target="tpu_custom_call" | custom-call | tf_op jit(solution)/shard_map/home/pallas_call | solution.py:176
  (136 shorter events, 74.0 us)
Async XLA Ops:
  6.5 78.0 %all-gather.8.cloned.1.call-start = ((), (), s32[]{:S(2)}) async-start(), calls=%async_computation.3 | async-start | bytes 12976128 | tf_op jit(solution)/shard_map/all_gather | solution.py:462
  7.3 133.7 %all-gather.10.cloned.1.call-start = ((), (), s32[]{:S(2)}) async-start(), calls=%async_computation.5 | async-start | bytes 10616832 | tf_op jit(solution)/shard_map/all_gather | solution.py:464
  8.0 133.0 %all-gather.12.cloned.1.call-start = ((), (), s32[]{:S(2)}) async-start(), calls=%async_computation.6 | async-start | bytes 10616832 | tf_op jit(solution)/shard_map/all_gather | solution.py:464
  8.8 144.5 %all-gather.14.cloned.1.call-start = ((), (), s32[]{:S(2)}) async-start(), calls=%async_computation.7 | async-start | bytes 10616832 | tf_op jit(solution)/shard_map/all_gather | solution.py:464
  43.4 19.2 %all-to-all-start.1 = ((bf16[32,64,128]{2,1,0:T(8,128)(2,1)}), bf16[32,64,128]{2,1,0:T(8,128)(2,1)S(1)}, u32[]{:S(2)}, u32[]{:S(2)}) async-start(bf16[32,64,128]{2,1,0:T(8,128)(2,1)} %state_prefix.1), calls=%async_computation.1 | async-start | bytes 1048576 | tf_op jit(solution)/shard_map/all_to_all | solution.py:475
  47.3 265.5 %reduce-scatter.2.cloned.1.call-start = ((), (), s32[]{:S(2)}) async-start(), calls=%async_computation.4 | async-start | bytes 7864320 | tf_op jit(solution)/shard_map/reduce_scatter | solution.py:502
  94.7 16.8 %collective-permute-start.3 = (bf16[48,6144]{1,0:T(8,128)(2,1)S(1)}, bf16[48,6144]{1,0:T(8,128)(2,1)S(1)}, u32[]{:S(2)}, u32[]{:S(2)}) collective-permute-start(bf16[48,6144]{1,0:T(8,128)(2,1)S(1)} %get-tuple-element.57), channel_id=1, source_target_pairs={{0,1},{1,2},{2,3},{3,0},{4,5},{5,6},{6,7},{7,4},{8,9},{9,10},{10,1... | collective-permute-start | bytes 1769480 | tf_op jit(solution)/shard_map/ppermute | solution.py:424
  96.3 27.2 %collective-permute-start.4 = (bf16[48,6144]{1,0:T(8,128)(2,1)S(1)}, bf16[48,6144]{1,0:T(8,128)(2,1)S(1)}, u32[]{:S(2)}, u32[]{:S(2)}) collective-permute-start(bf16[48,6144]{1,0:T(8,128)(2,1)S(1)} %get-tuple-element.58), channel_id=1, source_target_pairs={{0,3},{1,0},{2,1},{3,2},{4,7},{5,4},{6,5},{7,6},{8,11},{9,8},{10,9... | collective-permute-start | bytes 1769480 | tf_op jit(solution)/shard_map/ppermute | solution.py:428
  98.0 27.0 %collective-permute-start.5 = (bf16[48,6144]{1,0:T(8,128)(2,1)S(1)}, bf16[48,6144]{1,0:T(8,128)(2,1)S(1)}, u32[]{:S(2)}, u32[]{:S(2)}) collective-permute-start(bf16[48,6144]{1,0:T(8,128)(2,1)S(1)} %get-tuple-element.59), channel_id=1, source_target_pairs={{0,2},{1,3},{2,0},{3,1},{4,6},{5,7},{6,4},{7,5},{8,10},{9,11},{10,... | collective-permute-start | bytes 1769480 | tf_op jit(solution)/shard_map/ppermute | solution.py:432
  128.4 11.5 %collective-permute-start.8 = (bf16[48,3072]{1,0:T(8,128)(2,1)S(1)}, bf16[48,3072]{1,0:T(8,128)(2,1)S(1)}, u32[]{:S(2)}, u32[]{:S(2)}) collective-permute-start(bf16[48,3072]{1,0:T(8,128)(2,1)S(1)} %get-tuple-element.61.a0), channel_id=1, source_target_pairs={{0,16},{8,24},{16,0},{24,8},{1,17},{9,25},{17,1},{25,9},{2,18},{10... | collective-permute-start | bytes 884744 | tf_op jit(solution)/shard_map/ppermute | solution.py:432
  131.4 21.9 %collective-permute-start.7 = (bf16[48,3072]{1,0:T(8,128)(2,1)S(1)}, bf16[48,3072]{1,0:T(8,128)(2,1)S(1)}, u32[]{:S(2)}, u32[]{:S(2)}) collective-permute-start(bf16[48,3072]{1,0:T(8,128)(2,1)S(1)} %get-tuple-element.61.a0), channel_id=1, source_target_pairs={{0,24},{8,0},{16,8},{24,16},{1,25},{9,1},{17,9},{25,17},{2,26},{10... | collective-permute-start | bytes 884744 | tf_op jit(solution)/shard_map/ppermute | solution.py:428
  132.6 20.6 %collective-permute-start.6 = (bf16[48,3072]{1,0:T(8,128)(2,1)S(1)}, bf16[48,3072]{1,0:T(8,128)(2,1)S(1)}, u32[]{:S(2)}, u32[]{:S(2)}) collective-permute-start(bf16[48,3072]{1,0:T(8,128)(2,1)S(1)} %get-tuple-element.61.a0), channel_id=1, source_target_pairs={{0,8},{8,16},{16,24},{24,0},{1,9},{9,17},{17,25},{25,1},{2,10},{10... | collective-permute-start | bytes 884744 | tf_op jit(solution)/shard_map/ppermute | solution.py:424
  133.4 19.8 %collective-permute-start.11 = (bf16[48,3072]{1,0:T(8,128)(2,1)S(1)}, bf16[48,3072]{1,0:T(8,128)(2,1)S(1)}, u32[]{:S(2)}, u32[]{:S(2)}) collective-permute-start(bf16[48,3072]{1,0:T(8,128)(2,1)S(1)} %get-tuple-element.62.b0), channel_id=1, source_target_pairs={{0,64},{32,96},{64,0},{96,32},{1,65},{33,97},{65,1},{97,33},{2,66}... | collective-permute-start | bytes 884744 | tf_op jit(solution)/shard_map/ppermute | solution.py:432
  135.2 18.0 %collective-permute-start.10 = (bf16[48,3072]{1,0:T(8,128)(2,1)S(1)}, bf16[48,3072]{1,0:T(8,128)(2,1)S(1)}, u32[]{:S(2)}, u32[]{:S(2)}) collective-permute-start(bf16[48,3072]{1,0:T(8,128)(2,1)S(1)} %get-tuple-element.62.b0), channel_id=1, source_target_pairs={{0,96},{32,0},{64,32},{96,64},{1,97},{33,1},{65,33},{97,65},{2,98}... | collective-permute-start | bytes 884744 | tf_op jit(solution)/shard_map/ppermute | solution.py:428
  139.9 13.3 %collective-permute-start.9 = (bf16[48,3072]{1,0:T(8,128)(2,1)S(1)}, bf16[48,3072]{1,0:T(8,128)(2,1)S(1)}, u32[]{:S(2)}, u32[]{:S(2)}) collective-permute-start(bf16[48,3072]{1,0:T(8,128)(2,1)S(1)} %get-tuple-element.62.b0), channel_id=1, source_target_pairs={{0,32},{32,64},{64,96},{96,0},{1,33},{33,65},{65,97},{97,1},{2,34}... | collective-permute-start | bytes 884744 | tf_op jit(solution)/shard_map/ppermute | solution.py:424
  159.3 28.7 %collective-permute-start.13 = (bf16[4,48,3072]{2,1,0:T(8,128)(2,1)S(1)}, bf16[4,48,3072]{2,1,0:T(8,128)(2,1)S(1)}, u32[]{:S(2)}, u32[]{:S(2)}) collective-permute-start(bf16[4,48,3072]{2,1,0:T(8,128)(2,1)S(1)} %get-tuple-element.63.refs_0_), channel_id=1, source_target_pairs={{0,96},{32,0},{64,32},{96,64},{1,97},{33,1},{65,33},{97,65},{2,98}... | collective-permute-start | bytes 3538952 | tf_op jit(solution)/shard_map/ppermute | solution.py:428
  162.3 29.5 %collective-permute-start.12 = (bf16[4,48,3072]{2,1,0:T(8,128)(2,1)S(1)}, bf16[4,48,3072]{2,1,0:T(8,128)(2,1)S(1)}, u32[]{:S(2)}, u32[]{:S(2)}) collective-permute-start(bf16[4,48,3072]{2,1,0:T(8,128)(2,1)S(1)} %get-tuple-element.63.refs_0_), channel_id=1, source_target_pairs={{0,32},{32,64},{64,96},{96,0},{1,33},{33,65},{65,97},{97,1},{2,34}... | collective-permute-start | bytes 3538952 | tf_op jit(solution)/shard_map/ppermute | solution.py:424
  162.3 29.6 %collective-permute-start.17 = (bf16[4,48,3072]{2,1,0:T(8,128)(2,1)S(1)}, bf16[4,48,3072]{2,1,0:T(8,128)(2,1)S(1)}, u32[]{:S(2)}, u32[]{:S(2)}) collective-permute-start(bf16[4,48,3072]{2,1,0:T(8,128)(2,1)S(1)} %get-tuple-element.64.refs_5_), channel_id=1, source_target_pairs={{0,24},{8,0},{16,8},{24,16},{1,25},{9,1},{17,9},{25,17},{2,26},{10... | collective-permute-start | bytes 3538952 | tf_op jit(solution)/shard_map/ppermute | solution.py:428
  165.1 29.8 %collective-permute-start.16 = (bf16[4,48,3072]{2,1,0:T(8,128)(2,1)S(1)}, bf16[4,48,3072]{2,1,0:T(8,128)(2,1)S(1)}, u32[]{:S(2)}, u32[]{:S(2)}) collective-permute-start(bf16[4,48,3072]{2,1,0:T(8,128)(2,1)S(1)} %get-tuple-element.64.refs_5_), channel_id=1, source_target_pairs={{0,8},{8,16},{16,24},{24,0},{1,9},{9,17},{17,25},{25,1},{2,10},{10... | collective-permute-start | bytes 3538952 | tf_op jit(solution)/shard_map/ppermute | solution.py:424
  188.1 16.1 %collective-permute-start.15 = (bf16[2,48,3072]{2,1,0:T(8,128)(2,1)S(1)}, bf16[2,48,3072]{2,1,0:T(8,128)(2,1)S(1)}, u32[]{:S(2)}, u32[]{:S(2)}) collective-permute-start(bf16[2,48,3072]{2,1,0:T(8,128)(2,1)S(1)} %slice.17), channel_id=1, source_target_pairs={{0,96},{32,0},{64,32},{96,64},{1,97},{33,1},{65,33},{97,65},{2,98}... | collective-permute-start | bytes 1769480 | tf_op jit(solution)/shard_map/ppermute | solution.py:428
  191.9 15.8 %collective-permute-start.14 = (bf16[2,48,3072]{2,1,0:T(8,128)(2,1)S(1)}, bf16[2,48,3072]{2,1,0:T(8,128)(2,1)S(1)}, u32[]{:S(2)}, u32[]{:S(2)}) collective-permute-start(bf16[2,48,3072]{2,1,0:T(8,128)(2,1)S(1)} %slice.16), channel_id=1, source_target_pairs={{0,32},{32,64},{64,96},{96,0},{1,33},{33,65},{65,97},{97,1},{2,34}... | collective-permute-start | bytes 1769480 | tf_op jit(solution)/shard_map/ppermute | solution.py:424
  192.0 15.7 %collective-permute-start.19 = (bf16[2,48,3072]{2,1,0:T(8,128)(2,1)S(1)}, bf16[2,48,3072]{2,1,0:T(8,128)(2,1)S(1)}, u32[]{:S(2)}, u32[]{:S(2)}) collective-permute-start(bf16[2,48,3072]{2,1,0:T(8,128)(2,1)S(1)} %slice.19), channel_id=1, source_target_pairs={{0,24},{8,0},{16,8},{24,16},{1,25},{9,1},{17,9},{25,17},{2,26},{10... | collective-permute-start | bytes 1769480 | tf_op jit(solution)/shard_map/ppermute | solution.py:428
  194.9 15.5 %collective-permute-start.18 = (bf16[2,48,3072]{2,1,0:T(8,128)(2,1)S(1)}, bf16[2,48,3072]{2,1,0:T(8,128)(2,1)S(1)}, u32[]{:S(2)}, u32[]{:S(2)}) collective-permute-start(bf16[2,48,3072]{2,1,0:T(8,128)(2,1)S(1)} %slice.18), channel_id=1, source_target_pairs={{0,8},{8,16},{16,24},{24,0},{1,9},{9,17},{17,25},{25,1},{2,10},{10... | collective-permute-start | bytes 1769480 | tf_op jit(solution)/shard_map/ppermute | solution.py:424
  241.1 14.8 %collective-permute-start.20 = (bf16[2,48,3072]{2,1,0:T(8,128)(2,1)S(1)}, bf16[2,48,3072]{2,1,0:T(8,128)(2,1)S(1)}, u32[]{:S(2)}, u32[]{:S(2)}) collective-permute-start(bf16[2,48,3072]{2,1,0:T(8,128)(2,1)S(1)} %get-tuple-element.71), channel_id=1, source_target_pairs={{0,32},{32,64},{64,96},{96,0},{1,33},{33,65},{65,97},{97,1},{2,34}... | collective-permute-start | bytes 1769480 | tf_op jit(solution)/shard_map/ppermute | solution.py:424
  241.2 14.7 %collective-permute-start.21 = (bf16[2,48,3072]{2,1,0:T(8,128)(2,1)S(1)}, bf16[2,48,3072]{2,1,0:T(8,128)(2,1)S(1)}, u32[]{:S(2)}, u32[]{:S(2)}) collective-permute-start(bf16[2,48,3072]{2,1,0:T(8,128)(2,1)S(1)} %get-tuple-element.72), channel_id=1, source_target_pairs={{0,96},{32,0},{64,32},{96,64},{1,97},{33,1},{65,33},{97,65},{2,98}... | collective-permute-start | bytes 1769480 | tf_op jit(solution)/shard_map/ppermute | solution.py:428
  244.4 14.2 %collective-permute-start.22 = (bf16[2,48,3072]{2,1,0:T(8,128)(2,1)S(1)}, bf16[2,48,3072]{2,1,0:T(8,128)(2,1)S(1)}, u32[]{:S(2)}, u32[]{:S(2)}) collective-permute-start(bf16[2,48,3072]{2,1,0:T(8,128)(2,1)S(1)} %get-tuple-element.75), channel_id=1, source_target_pairs={{0,8},{8,16},{16,24},{24,0},{1,9},{9,17},{17,25},{25,1},{2,10},{10... | collective-permute-start | bytes 1769480 | tf_op jit(solution)/shard_map/ppermute | solution.py:424
  244.4 14.2 %collective-permute-start.23 = (bf16[2,48,3072]{2,1,0:T(8,128)(2,1)S(1)}, bf16[2,48,3072]{2,1,0:T(8,128)(2,1)S(1)}, u32[]{:S(2)}, u32[]{:S(2)}) collective-permute-start(bf16[2,48,3072]{2,1,0:T(8,128)(2,1)S(1)} %get-tuple-element.76), channel_id=1, source_target_pairs={{0,24},{8,0},{16,8},{24,16},{1,25},{9,1},{17,9},{25,17},{2,26},{10... | collective-permute-start | bytes 1769480 | tf_op jit(solution)/shard_map/ppermute | solution.py:428
  259.2 26.0 %collective-permute-start.24 = (bf16[4,48,3072]{2,1,0:T(8,128)(2,1)S(1)}, bf16[4,48,3072]{2,1,0:T(8,128)(2,1)S(1)}, u32[]{:S(2)}, u32[]{:S(2)}) collective-permute-start(bf16[4,48,3072]{2,1,0:T(8,128)(2,1)S(1)} %get-tuple-element.77), channel_id=1, source_target_pairs={{0,32},{32,64},{64,96},{96,0},{1,33},{33,65},{65,97},{97,1},{2,34}... | collective-permute-start | bytes 3538952 | tf_op jit(solution)/shard_map/ppermute | solution.py:424
  259.3 25.9 %collective-permute-start.25 = (bf16[4,48,3072]{2,1,0:T(8,128)(2,1)S(1)}, bf16[4,48,3072]{2,1,0:T(8,128)(2,1)S(1)}, u32[]{:S(2)}, u32[]{:S(2)}) collective-permute-start(bf16[4,48,3072]{2,1,0:T(8,128)(2,1)S(1)} %get-tuple-element.78), channel_id=1, source_target_pairs={{0,96},{32,0},{64,32},{96,64},{1,97},{33,1},{65,33},{97,65},{2,98}... | collective-permute-start | bytes 3538952 | tf_op jit(solution)/shard_map/ppermute | solution.py:428
  262.5 25.3 %collective-permute-start.26 = (bf16[4,48,3072]{2,1,0:T(8,128)(2,1)S(1)}, bf16[4,48,3072]{2,1,0:T(8,128)(2,1)S(1)}, u32[]{:S(2)}, u32[]{:S(2)}) collective-permute-start(bf16[4,48,3072]{2,1,0:T(8,128)(2,1)S(1)} %get-tuple-element.80), channel_id=1, source_target_pairs={{0,8},{8,16},{16,24},{24,0},{1,9},{9,17},{17,25},{25,1},{2,10},{10... | collective-permute-start | bytes 3538952 | tf_op jit(solution)/shard_map/ppermute | solution.py:424
  262.5 25.3 %collective-permute-start.27 = (bf16[4,48,3072]{2,1,0:T(8,128)(2,1)S(1)}, bf16[4,48,3072]{2,1,0:T(8,128)(2,1)S(1)}, u32[]{:S(2)}, u32[]{:S(2)}) collective-permute-start(bf16[4,48,3072]{2,1,0:T(8,128)(2,1)S(1)} %get-tuple-element.81), channel_id=1, source_target_pairs={{0,24},{8,0},{16,8},{24,16},{1,25},{9,1},{17,9},{25,17},{2,26},{10... | collective-permute-start | bytes 3538952 | tf_op jit(solution)/shard_map/ppermute | solution.py:428
  293.4 10.7 %collective-permute-start.32 = (bf16[48,3072]{1,0:T(8,128)(2,1)S(1)}, bf16[48,3072]{1,0:T(8,128)(2,1)S(1)}, u32[]{:S(2)}, u32[]{:S(2)}) collective-permute-start(bf16[48,3072]{1,0:T(8,128)(2,1)S(1)} %get-tuple-element.91), channel_id=1, source_target_pairs={{0,96},{32,0},{64,32},{96,64},{1,97},{33,1},{65,33},{97,65},{2,98}... | collective-permute-start | bytes 884744 | tf_op jit(solution)/shard_map/ppermute | solution.py:428
  (36 other events, 254.2 us)
Sparse Core Ops, SparseCore 0:
  9.6 74.8 all-gather.7
  86.1 19.8 all-gather.9
  107.7 21.9 all-gather.11
  131.2 21.9 all-gather.13
  155.5 65.2 reduce-scatter.1

commit v3 on v2

--- a/solution.py
+++ b/solution.py
@@ -17,6 +17,12 @@
 JREL = {0: 0, 3: 1, 1: 2, 2: 3}
 
 
+VM = pl.BlockSpec(memory_space=pltpu.VMEM)
+SM = pl.BlockSpec(memory_space=pltpu.SMEM)
+ANY = pl.BlockSpec(memory_space=pl.ANY)
+HBM = pl.BlockSpec(memory_space=pltpu.HBM)
+
+
 def ring(n, k):
     return [(i, (i + k) % n) for i in range(n)]
 
@@ -35,14 +41,14 @@
 
 
 def local_kernel(q_ref, k_ref, v_ref, d_ref, inner_ref, state_ref, cum_ref):
-    steps, heads = d_ref.shape[1], d_ref.shape[2]
+    heads, steps = d_ref.shape[1], d_ref.shape[2]
     row = lax.broadcasted_iota(jnp.int32, (steps, steps), 0)
     col = lax.broadcasted_iota(jnp.int32, (steps, steps), 1)
     later = row >= col
-    decay = d_ref[0]
-    cum = jnp.dot(later.astype(F32), decay, precision=HI, preferred_element_type=F32)
+    upto = (row <= col).astype(F32)
+    turned = jnp.dot(d_ref[0], upto, precision=HI, preferred_element_type=F32)
+    cum = turned.T
     cum_ref[0] = cum
-    turned = cum.T
     final = cum[steps - 1 : steps, :]
     tail = jnp.exp(final - cum)
     ends = jnp.exp(final)
@@ -77,14 +83,14 @@
     return pl.pallas_call(
         local_kernel,
         grid=(seqs,),
-        in_specs=[block, block, block, thin],
+        in_specs=[block, block, block, pl.BlockSpec((1, heads, steps), lambda s: (s, 0, 0))],
         out_specs=[block, pl.BlockSpec((2 * heads, half + DEC, HEAD), lambda s: (s, 0, 0)), thin],
         out_shape=[
             jax.ShapeDtypeStruct((seqs, steps, width), F32),
             jax.ShapeDtypeStruct((seqs * heads * 2, half + DEC, HEAD), BF),
             jax.ShapeDtypeStruct((seqs, steps, heads), F32),
         ],
-        compiler_params=pltpu.CompilerParams(vmem_limit_bytes=48 * 2**20),
+        compiler_params=pltpu.CompilerParams(vmem_limit_bytes=32 * 2**20),
         name="local_attention",
     )(q, k, v, d)
 
@@ -104,12 +110,12 @@
     return pl.pallas_call(
         scan_kernel,
         out_shape=jax.ShapeDtypeStruct((blocks, rows - DEC, width), BF),
-        compiler_params=pltpu.CompilerParams(vmem_limit_bytes=48 * 2**20),
+        compiler_params=pltpu.CompilerParams(vmem_limit_bytes=32 * 2**20),
         name="state_prefix",
     )(arrived)
 
 
-def carry_kernel(q_ref, inner_ref, cum_ref, state_ref, gain_ref, out_ref):
+def carry_kernel(q_ref, inner_ref, cum_ref, state_ref, gain_ref, h0, h1, h2, out_ref, *same):
     shares, slice_len = out_ref.shape[0], out_ref.shape[2]
     heads = cum_ref.shape[2]
     grow = jnp.exp(cum_ref[0])
@@ -124,7 +130,7 @@
             ]
 
 
-def carried(q, inner, cum, state, gain, shares):
+def carried(q, inner, cum, state, gain, shares, held):
     seqs, steps, width = q.shape
     heads = width // HEAD
     block = pl.BlockSpec((1, steps, width), lambda s: (s, 0, 0))
@@ -137,12 +143,16 @@
             pl.BlockSpec((1, steps, heads), lambda s: (s, 0, 0)),
             pl.BlockSpec((heads, HEAD, HEAD), lambda s: (s, 0, 0)),
             pl.BlockSpec((1, width), lambda s: (0, 0)),
-        ],
-        out_specs=pl.BlockSpec((shares, 1, steps // shares, width), lambda s: (0, s, 0, 0)),
-        out_shape=jax.ShapeDtypeStruct((shares, seqs, steps // shares, width), BF),
-        compiler_params=pltpu.CompilerParams(vmem_limit_bytes=48 * 2**20),
+        ]
+        + [ANY] * 3,
+        out_specs=[pl.BlockSpec((shares, 1, steps // shares, width), lambda s: (0, s, 0, 0))]
+        + [ANY] * 3,
+        out_shape=[jax.ShapeDtypeStruct((shares, seqs, steps // shares, width), BF)]
+        + [jax.ShapeDtypeStruct(h.shape, BF) for h in held],
+        input_output_aliases={5: 1, 6: 2, 7: 3},
+        compiler_params=pltpu.CompilerParams(vmem_limit_bytes=32 * 2**20),
         name="carried_norm",
-    )(q, inner, cum, state, gain)
+    )(q, inner, cum, state, gain, *held)
 
 
 def route_kernel(cap, me_ref, routes_ref, place_ref, own_ref):
@@ -172,7 +182,7 @@
 
 
 def call(kernel, name, outs, *args, **kw):
-    limit = kw.pop("vmem", 40)
+    limit = kw.pop("vmem", 16)
     return pl.pallas_call(
         kernel,
         out_shape=[jax.ShapeDtypeStruct(s, d) for s, d in outs],
@@ -180,11 +190,6 @@
         name=name,
         **kw,
     )(*args)
-
-
-VM = pl.BlockSpec(memory_space=pltpu.VMEM)
-SM = pl.BlockSpec(memory_space=pltpu.SMEM)
-ANY = pl.BlockSpec(memory_space=pl.ANY)
 
 
 def route(me, routes, cap):
@@ -242,6 +247,7 @@
         ],
         out_specs=[pl.BlockSpec((size, tile), lambda n: (0, n))] * 4,
         scratch_shapes=[pltpu.VMEM((picks, width), BF)],
+        vmem=40,
     )
 
 
@@ -266,10 +272,11 @@
         cost_estimate=pl.CostEstimate(
             flops=2 * total * model * width, bytes_accessed=4 * model * width, transcendentals=0
         ),
+        vmem=24,
     )[0]
 
 
-def norm_kernel(a, b, c, d, gain, held, o0, o1, same):
+def norm_kernel(a, b, c, d, gain, held, w0, o0, o1, *same):
     x = a[...].astype(F32) + b[...].astype(F32) + c[...].astype(F32) + d[...].astype(F32)
     x = x * lax.rsqrt(jnp.mean(x * x, -1, keepdims=True) + 1e-06) * gain[...]
     half = o0.shape[1]
@@ -277,80 +284,177 @@
     o1[...] = x[:, half:].astype(BF)
 
 
-def stack_kernel(a0, a1, a2, a3, b0, b1, b2, b3, w0, w1, w2, o0, o1, *same):
+def stack_kernel(a0, a1, a2, a3, b0, b1, b2, b3, o0, o1):
     for i, (a, b) in enumerate(((a0, b0), (a1, b1), (a2, b2), (a3, b3))):
         o0[i] = a[...]
         o1[i] = b[...]
 
 
-def expert_kernel(tile, *refs):
-    xa, xb = refs[0:5], refs[5:10]
-    gate, up, down = refs[10:13]
-    oa, ob = refs[13:18], refs[18:23]
-    x, gates, uppers, hidden = refs[23:]
-    rows, half = xa[0].shape[1], xa[0].shape[2]
-
-    def piece(refs, u, v):
-        if u < 3:
-            return refs[u], v
-        return (refs[3], v) if v < 2 else (refs[4], v - 2)
-
-    def pieces(refs, flip):
-        for z in range(4):
-            for y in range(4):
-                ref, i = piece(refs, y, z) if flip else piece(refs, z, y)
-                yield (z * 4 + y) * rows, ref, i
-
-    gates[...] = jnp.zeros_like(gates)
-    uppers[...] = jnp.zeros_like(uppers)
-    for k, (refs_x, flip) in enumerate(((xa, False), (xb, True))):
-
-        @pl.loop(0, half // tile)
-        def _(c):
-            at = pl.ds(pl.multiple_of(c * tile, tile), tile)
-            wide = pl.ds(pl.multiple_of(k * half + c * tile, tile), tile)
-            for row, ref, i in pieces(refs_x, flip):
-                x[row : row + rows, :] = ref[i, :, at]
-            gates[...] += nt(gate[:, wide], x[...])
-            uppers[...] += nt(up[:, wide], x[...])
-
-    g = gates[...]
-    hidden[...] = (g / (1.0 + jnp.exp(-g)) * uppers[...]).T.astype(BF)
-    for k, (refs_o, flip) in enumerate(((oa, False), (ob, True))):
-
-        @pl.loop(0, half // tile)
-        def _(c):
-            at = pl.ds(pl.multiple_of(c * tile, tile), tile)
-            wide = pl.ds(pl.multiple_of(k * half + c * tile, tile), tile)
-            full = mm(hidden[...], down[:, wide]).astype(BF)
-            for row, ref, i in pieces(refs_o, flip):
-                ref[i, :, at] = full[row : row + rows]
-
-
-def expert(xa, xb, gate, up, down, tile=1024):
-    rows, half = xa[0].shape[1], xa[0].shape[2]
-    units = gate.shape[0]
-    total = 16 * rows
-    outs = call(
-        functools.partial(expert_kernel, tile),
-        "expert",
-        [((k, rows, half), BF) for k in (4, 4, 4, 2, 2)] * 2,
-        *xa,
-        *xb,
-        gate,
-        up,
+def pack_kernel(g0, g1, u0, u1, d0, d1, late, gu, down, sems):
+    units = g0.shape[0]
+    copies = []
+    for i, part in enumerate((g0, g1, u0, u1)):
+        copies.append((part, gu.at[pl.ds(i * units, units)]))
+    for i, part in enumerate((d0, d1)):
+        copies.append((part, down.at[pl.ds(i * units, units)]))
+    copies = [pltpu.make_async_copy(a, b, sems.at[i]) for i, (a, b) in enumerate(copies)]
+    for c in copies:
+        c.start()
+    for c in copies:
+        c.wait()
+
+
+def by_y(rows, y):
+    return [((z * 4 + y) * rows, z) for z in range(4)]
+
+
+def near_kernel(tile, a0, a1, a2, b0, b1, b2, gu, acc, x, part):
+    rows, half = a0.shape[1], a0.shape[2]
+    block = 4 * rows
+
+    def fill(refs, at):
+        for k, ref in enumerate(refs):
+            for i in range(4):
+                x[k * block + i * rows : k * block + (i + 1) * rows, :] = ref[i, :, at]
+
+    acc[...] = jnp.zeros_like(acc)
+    part[...] = jnp.zeros_like(part)
+
+    @pl.loop(0, half // tile)
+    def _(c):
+        at = pl.ds(pl.multiple_of(c * tile, tile), tile)
+        fill((a0, a1, a2), at)
+        acc[0 : 3 * block, :] += nt(x[...], gu[:, at])
+
+    @pl.loop(0, half // tile)
+    def _(c):
+        at = pl.ds(pl.multiple_of(c * tile, tile), tile)
+        wide = pl.ds(pl.multiple_of(half + c * tile, tile), tile)
+        fill((b0, b1, b2), at)
+        part[...] += nt(x[...], gu[:, wide])
+
+    for y in range(3):
+        for row, z in by_y(rows, y):
+            at = y * block + z * rows
+            acc[row : row + rows, :] += part[at : at + rows, :]
+
+
+def far_kernel(tile, acc, a3, a4, b3, b4, gu, down, hidden, oa3, oa4, ob3, ob4, x, part, own):
+    rows, half = a3.shape[1], a3.shape[2]
+    block = 4 * rows
+    units = down.shape[0]
+
+    def fill(refs, at):
+        for k, ref in enumerate(refs):
+            for i in range(2):
+                x[(2 * k + i) * rows : (2 * k + i + 1) * rows, :] = ref[i, :, at]
+
+    part[...] = jnp.zeros_like(part)
+
+    @pl.loop(0, half // tile)
+    def _(c):
+        at = pl.ds(pl.multiple_of(c * tile, tile), tile)
+        wide = pl.ds(pl.multiple_of(half + c * tile, tile), tile)
+        fill((a3, a4), at)
+        part[0:block, :] += nt(x[...], gu[:, at])
+        fill((b3, b4), at)
+        part[block : 2 * block, :] += nt(x[...], gu[:, wide])
+
+    own[...] = acc[...]
+    own[3 * block : 4 * block, :] += part[0:block, :]
+    for row, z in by_y(rows, 3):
+        own[row : row + rows, :] += part[block + z * rows : block + (z + 1) * rows, :]
+    g = own[:, :units]
+    hidden[...] = (g / (1.0 + jnp.exp(-g)) * own[:, units:]).astype(BF)
+    by_z = hidden[3 * block : 4 * block, :]
+    across_y = jnp.concatenate([hidden[row : row + rows, :] for row, _ in by_y(rows, 3)])
+
+    @pl.loop(0, half // tile)
+    def _(c):
+        at = pl.ds(pl.multiple_of(c * tile, tile), tile)
+        wide = pl.ds(pl.multiple_of(half + c * tile, tile), tile)
+        for value, cols, outs in ((by_z, at, (oa3, oa4)), (across_y, wide, (ob3, ob4))):
+            full = mm(value, down[:, cols]).astype(BF)
+            for i in range(4):
+                outs[i // 2][i % 2, :, at] = full[i * rows : (i + 1) * rows]
+
+
+def rest_kernel(tile, hidden, down, oa0, oa1, oa2, ob0, ob1, ob2):
+    rows, half = oa0.shape[1], oa0.shape[2]
+    block = 4 * rows
+    by_z = hidden[0 : 3 * block, :]
+    across_y = jnp.concatenate(
+        [hidden[row : row + rows, :] for y in range(3) for row, _ in by_y(rows, y)]
+    )
+
+    @pl.loop(0, half // tile)
+    def _(c):
+        at = pl.ds(pl.multiple_of(c * tile, tile), tile)
+        wide = pl.ds(pl.multiple_of(half + c * tile, tile), tile)
+        for value, cols, outs in ((by_z, at, (oa0, oa1, oa2)), (across_y, wide, (ob0, ob1, ob2))):
+            full = mm(value, down[:, cols]).astype(BF)
+            for k, out in enumerate(outs):
+                for i in range(4):
+                    out[i, :, at] = full[k * block + i * rows : k * block + (i + 1) * rows]
+
+
+def cost(flops):
+    return pl.CostEstimate(flops=flops, bytes_accessed=2**20, transcendentals=0)
+
+
+def near(xs, gu, tile=1024):
+    rows, half = xs[0].shape[1:]
+    return call(
+        functools.partial(near_kernel, tile),
+        "near_rows",
+        [((16 * rows, gu.shape[0]), F32)],
+        *xs,
+        gu,
+        in_specs=[VM] * 7,
+        out_specs=[VM],
+        scratch_shapes=[
+            pltpu.VMEM((12 * rows, tile), BF),
+            pltpu.VMEM((12 * rows, gu.shape[0]), F32),
+        ],
+        cost_estimate=cost(2 * 12 * rows * gu.size),
+        vmem=16,
+    )[0]
+
+
+def far(acc, xs, gu, down, tile=1024):
+    rows, half = xs[0].shape[1:]
+    return call(
+        functools.partial(far_kernel, tile),
+        "far_rows",
+        [((16 * rows, down.shape[0]), BF)] + [((2, rows, half), BF)] * 4,
+        acc,
+        *xs,
+        gu,
         down,
-        in_specs=[VM] * 13,
-        out_specs=[VM] * 10,
+        in_specs=[VM] * 7,
+        out_specs=[VM] * 5,
         scratch_shapes=[
-            pltpu.VMEM((total, tile), BF),
-            pltpu.VMEM((units, total), F32),
-            pltpu.VMEM((units, total), F32),
-            pltpu.VMEM((total, units), BF),
+            pltpu.VMEM((4 * rows, tile), BF),
+            pltpu.VMEM((8 * rows, gu.shape[0]), F32),
+            pltpu.VMEM(acc.shape, F32),
         ],
         vmem=20,
     )
-    return outs[:5], outs[5:]
+
+
+def rest(hidden, down, rows, tile=1024):
+    half = down.shape[1] // 2
+    return call(
+        functools.partial(rest_kernel, tile),
+        "rest_rows",
+        [((4, rows, half), BF)] * 6,
+        hidden,
+        down,
+        in_specs=[VM] * 2,
+        out_specs=[VM] * 6,
+        cost_estimate=cost(2 * 12 * rows * down.size),
+        vmem=16,
+    )
 
 
 def fold_kernel(bl0, ab0, up0, dn0, bl1, ab1, up1, dn1, ob0, oa0, ob1, oa1):
@@ -384,11 +488,11 @@
             o[:, k * half : (k + 1) * half] = mm(pick, total).astype(BF)
 
 
-def home_kernel(me_ref, routes_ref, res, mixed, gain, router, late, hidden_ref, hi_ref, lo_ref):
+def home_kernel(me_ref, routes_ref, res, mixed, gain, router, late, hidden_ref, coef_ref):
     x = res[...].astype(F32) + mixed[...].astype(F32)
     hidden_ref[...] = x
     normed = (x * lax.rsqrt(jnp.mean(x * x, -1, keepdims=True) + 1e-06) * gain[...]).astype(BF)
-    logits = mm(normed, router[...])
+    logits = nt(normed, router[...])
     rows, experts = logits.shape
     labels = lax.broadcasted_iota(jnp.int32, (rows, experts), 1)
     one, two = routes_ref[:, 0:1], routes_ref[:, 1:2]
@@ -396,7 +500,7 @@
     second = jnp.sum(jnp.where(two == labels, logits, 0.0), -1, keepdims=True)
     gate0 = 1.0 / (1.0 + jnp.exp(second - first))
     gate1 = 1.0 / (1.0 + jnp.exp(first - second))
-    cols = hi_ref.shape[1]
+    cols = coef_ref.shape[1] // 2
     place = lax.broadcasted_iota(jnp.int32, (rows, cols), 1)
     a = lax.broadcasted_iota(jnp.int32, (rows, rows), 0)
     b = lax.broadcasted_iota(jnp.int32, (rows, rows), 1)
@@ -409,14 +513,14 @@
         rank = mm(before, jnp.broadcast_to(chosen, (rows, 128)).astype(BF))[:, 0:1].astype(jnp.int32)
         total = total + jnp.where(place == rank + 16 * j, hit0 * gate0 + hit1 * gate1, 0.0)
     hi, lo = split(total)
-    hi_ref[...] = hi
-    lo_ref[...] = lo
-
-
-def final_kernel(hidden, hi, lo, b0, b1, b2, b3, out, back):
-    for i, b in enumerate((b0, b1, b2, b3)):
+    coef_ref[:, :cols] = hi
+    coef_ref[:, cols:] = lo
+
+
+def final_kernel(hidden, coef, b0, b1, b2, b3, out, back):
+    for i, b in enumerate((b0, b1, b2, b3) * 2):
         back[16 * i : 16 * i + 16, :] = b[...]
-    moe = mm(hi[...], back[...]) + mm(lo[...], back[...])
+    moe = mm(coef[...], back[...])
     out[...] = (hidden[...] + moe).astype(BF)
 
 
@@ -460,23 +564,25 @@
     me = lax.axis_index("x").astype(jnp.int32).reshape(1)
 
     weight_out = lax.all_gather(out_weight.T, SEQ, axis=0, tiled=True)
-    gate, up, down = [
-        lax.all_gather(w[0], "core", axis=0, tiled=True)
-        for w in (gate_weight, up_weight, down_weight)
-    ]
+    units = gate_weight.shape[1]
+    weights = (gate_weight[0], up_weight[0], down_weight[0])
+    swapped = [lax.ppermute(w, "core", ring(2, 1)) for w in weights]
     routes = picks.reshape(rows, 2)
     turned = routes.T
     all_routes = jnp.concatenate(
         [turned] + [lax.ppermute(turned, "x", ring(4, -delta)) for delta in (1, 2, 3)], axis=1
     )
 
-    inner, states, cum = local_part(queries, keys, payload_vectors, log_decay)
+    inner, states, cum = local_part(
+        queries, keys, payload_vectors, log_decay.transpose(0, 2, 1)
+    )
     arrived = lax.all_to_all(states, SEQ, 0, 0, tiled=True)
     prefix = lax.all_to_all(scan_states(arrived), SEQ, 0, 0, tiled=True)
     prefix = prefix.reshape(seqs * width // HEAD, HEAD, HEAD)
-    normed = carried(
-        queries, inner, cum, prefix, attn_gain.reshape(1, width), shares
-    ).reshape(shares * rows, width)
+    normed, *swapped = carried(
+        queries, inner, cum, prefix, attn_gain.reshape(1, width), shares, swapped
+    )
+    normed = normed.reshape(shares * rows, width)
 
     place, own_place = route(me, all_routes, cap)
     flat = residual.reshape(rows, model)
@@ -485,26 +591,39 @@
     whole = whole_projection(normed, weight_out)
 
     size = here.shape[0]
-    a0, b0, whole = call(
+    gu, down = call(
+        pack_kernel,
+        "pack",
+        [((4 * units, model), BF), ((2 * units, model), BF)],
+        *[w for pair in zip(weights, swapped) for w in pair],
+        here,
+        in_specs=[ANY] * 6 + [VM],
+        out_specs=[VM, HBM],
+        scratch_shapes=[pltpu.SemaphoreType.DMA((6,))],
+        vmem=8,
+    )
+    a0, b0, whole, gu = call(
         norm_kernel,
         "selected_norm",
-        [((size, half), BF)] * 2 + [(whole.shape, BF)],
+        [((size, half), BF)] * 2 + [(w.shape, BF) for w in (whole, gu)],
         here,
         up_one(to_up, "x"),
         down_one(to_down, "x"),
         across(to_far, "x"),
         gain,
         whole,
-        in_specs=[VM] * 5 + [ANY],
-        out_specs=[VM] * 2 + [ANY],
-        input_output_aliases={5: 2},
+        gu,
+        in_specs=[VM] * 5 + [HBM, VM],
+        out_specs=[VM] * 2 + [HBM, VM],
+        input_output_aliases={5: 2, 6: 3},
+        vmem=16,
     )
     mixed = lax.psum_scatter(whole, "x", scatter_dimension=0, tiled=True)
 
-    a4, b4, gate, up, down = call(
+    a4, b4 = call(
         stack_kernel,
         "stack",
-        [((4, size, half), BF)] * 2 + [(w.shape, BF) for w in (gate, up, down)],
+        [((4, size, half), BF)] * 2,
         a0,
         up_one(a0, "y"),
         down_one(a0, "y"),
@@ -513,20 +632,18 @@
         up_one(b0, "z"),
         down_one(b0, "z"),
         across(b0, "z"),
-        gate,
-        up,
-        down,
-        in_specs=[VM] * 8 + [ANY] * 3,
-        out_specs=[VM] * 2 + [ANY] * 3,
-        input_output_aliases={8: 2, 9: 3, 10: 4},
+        in_specs=[VM] * 8,
+        out_specs=[VM] * 2,
+        vmem=8,
     )
     a_below, a_above = up_one(a4, "z"), down_one(a4, "z")
     b_below, b_above = up_one(b4, "y"), down_one(b4, "y")
     a_far, b_far = far_sides(a_below, a_above, "z"), far_sides(b_below, b_above, "y")
 
-    oa, ob = expert(
-        (a4, a_below, a_above, *a_far), (b4, b_below, b_above, *b_far), gate, up, down
-    )
+    acc = near((a4, a_below, a_above, b4, b_below, b_above), gu)
+    hidden, *ends = far(acc, (*a_far, *b_far), gu, down)
+    body = rest(hidden, down, size)
+    oa, ob = (*body[:3], *ends[:2]), (*body[3:], *ends[2:])
     a_below, a_above, b_below, b_above = call(
         fold_kernel,
         "fold",
@@ -541,6 +658,7 @@
         down_one(ob[4], "y"),
         in_specs=[VM] * 8,
         out_specs=[VM] * 4,
+        vmem=16,
     )
     parts = call(
         phase_kernel,
@@ -554,6 +672,7 @@
         down_one(b_below, "y"),
         in_specs=[VM] * 6,
         out_specs=[VM] * 8,
+        vmem=16,
     )
     s0, s1, s2, s3 = call(
         functools.partial(served_kernel, cap),
@@ -571,35 +690,35 @@
         out_specs=[VM] * 4,
     )
 
-    hidden, hi, lo = call(
+    hidden, coef = call(
         home_kernel,
         "home",
-        [((rows, model), F32), ((rows, 64), BF), ((rows, 64), BF)],
+        [((rows, model), F32), ((rows, 128), BF)],
         me,
         routes,
         flat,
         mixed,
         gain,
-        router_weight,
-        parts[0],
-        in_specs=[SM] + [VM] * 5 + [ANY],
-        out_specs=[VM] * 3,
-        vmem=56,
+        router_weight.T,
+        a_below,
+        in_specs=[SM] + [VM] * 6,
+        out_specs=[VM] * 2,
+        vmem=20,
     )
     out = call(
         final_kernel,
         "combine",
         [((rows, model), BF)],
         hidden,
-        hi,
-        lo,
+        coef,
         s0,
         down_one(s1, "x"),
         up_one(s2, "x"),
         across(s3, "x"),
-        in_specs=[VM] * 7,
+        in_specs=[VM] * 6,
         out_specs=[VM],
-        scratch_shapes=[pltpu.VMEM((64, model), BF)],
+        scratch_shapes=[pltpu.VMEM((128, model), BF)],
+        vmem=16,
     )[0]
     return out.reshape(seqs, slice_len, model)
 

time: 332 us -> 320 us (0.964)
  waiting for transfers between devices: 140 us -> 92.1 us
  local copies, waits for them, and re-layouts: 26.8 us -> 60.5 us
    unnamed x53 -> x103, local copies, waits for them, and re-layouts: 26.3 us -> 54.4 us
    ppermute x14, waiting for transfers between devices: 47.7 us -> 28.7 us  [down_one(): return lax.ppermute(x, axis, ring(4, -1))]
    all_gather x3 -> x0, waiting for transfers between devices: 12.3 us -> none  [shards(): lax.all_gather(w[0], 'core', axis=0, tiled=True)]
    ppermute x14, waiting for transfers between devices: 43.8 us -> 34.3 us  [up_one(): return lax.ppermute(x, axis, ring(4, 1))]
    all_gather x1, waiting for transfers between devices: 16.7 us -> 11.2 us  [shards(): weight_out = lax.all_gather(out_weight.T, SEQ, axis=0, tiled=True)]
    ppermute x14, starting transfers between devices: 37.9 us -> 32.6 us  [down_one(): return lax.ppermute(x, axis, ring(4, -1))]
    pallas_call x11 -> x14, Pallas kernels: 54.2 us -> 58.4 us  [call(): pl.pallas_call(kernel, out_shape=[jax.ShapeDtypeStruct(s, d) for s, d in...]
    ppermute x14, starting transfers between devices: 4.59 us -> 8.69 us  [up_one(): return lax.ppermute(x, axis, ring(4, 1))]
  transfers between devices with their start and end apart: 43 -> 43, of which waited for: 24 -> 20; matrix products, arithmetic and copies ran while one was open for 1% -> 2% of each run, Pallas kernels for 18% -> 16%
where the time goes in v3:
time: 320 us; the launch traced here: 319 us
  waiting for transfers between devices  92.1 us (29%)
  Pallas kernels  66.3 us (21%)
  starting transfers between devices  61 us (19%)
  local copies, waits for them, and re-layouts  60.5 us (19%)
  blocking collectives  24.3 us (8%)
  between operations  13.8 us (4%)
    pallas_call x14, Pallas kernels, call(): pl.pallas_call(kernel, out_shape=[jax.ShapeDtypeStruct(s, d) for s, d in...  58.4 us
    unnamed x103, local copies, waits for them, and re-layouts  54.4 us
    ppermute x14, waiting for transfers between devices, up_one(): return lax.ppermute(x, axis, ring(4, 1))  34.3 us
    ppermute x14, starting transfers between devices, down_one(): return lax.ppermute(x, axis, ring(4, -1))  32.6 us
    ppermute x14, waiting for transfers between devices, down_one(): return lax.ppermute(x, axis, ring(4, -1))  28.7 us
    all_to_all x1, blocking collectives, shards(): arrived = lax.all_to_all(states, SEQ, 0, 0, tiled=True)  24.3 us
    ppermute x6, waiting for transfers between devices, across(): return lax.ppermute(x, axis, ring(4, 2))  12.8 us
    all_gather x1, waiting for transfers between devices, shards(): weight_out = lax.all_gather(out_weight.T, SEQ, axis=0, tiled=True)  11.2 us
  transfers between devices with their start and end apart: 43, of which 20 were waited for; matrix products, arithmetic and copies ran while one was open for 2% of the time, Pallas kernels for 16%

profile of v3, /device:TPU:0, one launch (start us, length us, event | category | flops | bytes accessed | tf_op | source)
XLA Modules:
  0.0 318.7 jit_solution(711612656851351644)
XLA Ops:
  12.3 4.7 %local_attention.1 = (f32[2,256,1024]{2,1,0:T(8,128)S(1)}, bf16[32,80,128]{2,1,0:T(8,128)(2,1)S(1)}, f32[2,256,8]{2,1,0:T(8,128)S(1)}) custom-call(bf16[2,256,1024]{2,1,0:T(8,128)(2,1)S(1)} %copy-done.8, bf16[2,256,1024]{2,1,0:T(8,128)(2,1)S(1)} %copy-done.22, bf16[2,256,1024]{2,1,0:T(8,128)(2,1)S(1)} %copy-done.23, f32[2,8,256]{2,1,0:T(8,128)S(1)} %bitcast.36), custom_call_target="tpu_custom_call" | custom-call | tf_op jit(solution)/shard_map/local_attention/pallas_call | solution.py:83
  18.4 24.3 %all_to_all.10.in_ref = bf16[32,80,128]{2,1,0:T(8,128)(2,1)S(1)} all-to-all(bf16[32,80,128]{2,1,0:T(8,128)(2,1)S(1)} %get-tuple-element.59), channel_id=1, replica_groups=mesh['z'=4,'y'=4,'core'=2,'x'=4] {'z','y','core'}, dimensions={0} | all-to-all | bytes 1310720 | tf_op jit(solution)/shard_map/all_to_all | solution.py:579
  43.7 4.6 %all-to-all-start.1 = ((bf16[32,64,128]{2,1,0:T(8,128)(2,1)}), bf16[32,64,128]{2,1,0:T(8,128)(2,1)}, u32[]{:S(2)}, u32[]{:S(2)}) async-start(bf16[32,64,128]{2,1,0:T(8,128)(2,1)} %copy-done.18), calls=%async_computation.1 | async-start | bytes 1048576 | tf_op jit(solution)/shard_map/all_to_all | solution.py:580
  70.0 3.1 carried_norm.1
  74.0 11.2 %all-gather.2.cloned.1.call-done.weight_ref = bf16[6144,1024]{1,0:T(8,128)(2,1)} async-done(((bf16[192,1024]{1,0:T(8,128)(2,1)}), bf16[6144,1024]{1,0:T(8,128)(2,1)}) %all-gather.2.cloned.1.call-update) | async-done | bytes 12582928 | tf_op jit(solution)/shard_map/all_gather | solution.py:566
  89.6 10.5 %selected_projection.1 = (bf16[48,6144]{1,0:T(8,128)(2,1)}, bf16[48,6144]{1,0:T(8,128)(2,1)}, bf16[48,6144]{1,0:T(8,128)(2,1)}, bf16[48,6144]{1,0:T(8,128)(2,1)S(1)}) custom-call(bf16[192,512]{1,0:T(8,128)(2,1)S(1)} %copy-done.38, bf16[192,128]{1,0:T(8,128)(2,1)S(1)} %copy-done.41, bf16[512,1024]{1,0:T(8,128)(2,1)S(1)} %bitcast.26, ...), custom_call_target="tpu_custom_call" | custom-call | tf_op jit(solution)/shard_map/selected_projection/pallas_call | solution.py:186
  109.0 4.4 %pack.1 = (bf16[1152,6144]{1,0:T(8,128)(2,1)S(1)}, bf16[576,6144]{1,0:T(8,128)(2,1)S(1)}) custom-call(bf16[288,6144]{1,0:T(8,128)(2,1)S(1)} %bitcast.21, bf16[288,6144]{1,0:T(8,128)(2,1)S(1)} %get-tuple-element.65.g1, bf16[288,6144]{1,0:T(8,128)(2,1)S(1)} %bitcast.23, bf16[288,6144]{1,0:T(8,128)(2,1)} %get-tuple-element.66.u1, ...), custom_call_target="tpu_custom_call" | custom-call | tf_op jit(solution)/shard_map/pack/pallas_call | solution.py:186
  113.5 2.9 copy-done.5
  116.4 4.6 %copy-done.4 = bf16[6144,1024]{1,0:T(8,128)(2,1)S(1)} copy-done((bf16[6144,1024]{1,0:T(8,128)(2,1)S(1)}, bf16[6144,1024]{1,0:T(8,128)(2,1)}, u32[]{:S(2)}) %copy-start.4) | copy-done | bytes 12582936
  122.2 8.1 %whole_projection.1.held = bf16[512,6144]{1,0:T(8,128)(2,1)S(1)} custom-call(bf16[512,1024]{1,0:T(8,128)(2,1)S(1)} %bitcast.27, bf16[6144,1024]{1,0:T(8,128)(2,1)S(1)} %copy-done.4), custom_call_target="tpu_custom_call" | custom-call | flops 6442450944 | bytes 25165824 | tf_op jit(solution)/shard_map/whole_projection/pallas_call | solution.py:186
  133.5 5.0 %copy-done = bf16[1152,6144]{1,0:T(8,128)(2,1)} copy-done((bf16[1152,6144]{1,0:T(8,128)(2,1)}, bf16[1152,6144]{1,0:T(8,128)(2,1)S(1)}, u32[]{:S(2)}) %copy-start) | copy-done | bytes 14155800
  138.6 2.7 copy-done.3
  141.2 3.0 collective-permute-start.11
  149.1 3.7 %collective-permute-done.11.a3 = bf16[48,3072]{1,0:T(8,128)(2,1)S(1)} collective-permute-done((bf16[48,3072]{1,0:T(8,128)(2,1)S(1)}, bf16[48,3072]{1,0:T(8,128)(2,1)S(1)}, u32[]{:S(2)}, u32[]{:S(2)}) %collective-permute-start.11) | collective-permute-done | bytes 294944 | tf_op jit(solution)/shard_map/ppermute | solution.py:536
  153.9 3.7 %collective-permute-done.10.a2 = bf16[48,3072]{1,0:T(8,128)(2,1)S(1)} collective-permute-done((bf16[48,3072]{1,0:T(8,128)(2,1)S(1)}, bf16[48,3072]{1,0:T(8,128)(2,1)S(1)}, u32[]{:S(2)}, u32[]{:S(2)}) %collective-permute-start.10) | collective-permute-done | bytes 294944 | tf_op jit(solution)/shard_map/ppermute | solution.py:532
  163.9 2.9 collective-permute-start.18
  167.8 20.4 %collective-permute-done.16.a2 = bf16[4,48,3072]{2,1,0:T(8,128)(2,1)S(1)} collective-permute-done((bf16[4,48,3072]{2,1,0:T(8,128)(2,1)S(1)}, bf16[4,48,3072]{2,1,0:T(8,128)(2,1)S(1)}, u32[]{:S(2)}, u32[]{:S(2)}) %collective-permute-start.16) | collective-permute-done | bytes 1179680 | tf_op jit(solution)/shard_map/ppermute | solution.py:532
  188.3 3.8 %collective-permute-start.20 = (bf16[2,48,3072]{2,1,0:T(8,128)(2,1)S(1)}, bf16[2,48,3072]{2,1,0:T(8,128)(2,1)S(1)}, u32[]{:S(2)}, u32[]{:S(2)}) collective-permute-start(bf16[2,48,3072]{2,1,0:T(8,128)(2,1)S(1)} %slice.17), channel_id=1, source_target_pairs={{0,96},{32,0},{64,32},{96,64},{1,97},{33,1},{65,33},{97,65},{2,98}... | collective-permute-start | bytes 1769480 | tf_op jit(solution)/shard_map/ppermute | solution.py:532
  197.5 5.2 %copy-done.1 = bf16[1152,6144]{1,0:T(8,128)(2,1)S(1)} copy-done((bf16[1152,6144]{1,0:T(8,128)(2,1)S(1)}, bf16[1152,6144]{1,0:T(8,128)(2,1)}, u32[]{:S(2)}) %copy-start.1) | copy-done | bytes 14155800
  206.6 11.0 %near_rows.1.acc = f32[768,1152]{1,0:T(8,128)S(1)} custom-call(bf16[4,48,3072]{2,1,0:T(8,128)(2,1)S(1)} %copy-done.45, bf16[4,48,3072]{2,1,0:T(8,128)(2,1)S(1)} %copy-done.32, bf16[4,48,3072]{2,1,0:T(8,128)(2,1)S(1)} %copy-done.30, bf16[4,48,3072]{2,1,0:T(8,128)(2,1)S(1)} %copy-done.47, bf16[4,48,3072]{2,1,0:T(8,128)(2,1)S(1)} %collective-permute-done.17.b1, ...), custom_call_target="tpu_custom_call" | custom-call | flops 8153726976 | bytes 1048576 | tf_op jit(solution)/shard_map/near_rows/pallas_call | solution.py:186
  221.5 8.3 %far_rows.1 = (bf16[768,576]{1,0:T(8,128)(2,1)S(1)}, bf16[2,48,3072]{2,1,0:T(8,128)(2,1)S(1)}, bf16[2,48,3072]{2,1,0:T(8,128)(2,1)S(1)}, bf16[2,48,3072]{2,1,0:T(8,128)(2,1)S(1)}, bf16[2,48,3072]{2,1,0:T(8,128)(2,1)S(1)}) custom-call(f32[768,1152]{1,0:T(8,128)S(1)} %copy-done.11, bf16[2,48,3072]{2,1,0:T(8,128)(2,1)S(1)} %collective-permute-done.19.a3, ...), custom_call_target="tpu_custom_call" | custom-call | tf_op jit(solution)/shard_map/far_rows/pallas_call | solution.py:186
  229.9 3.3 %collective-permute-start.24 = (bf16[2,48,3072]{2,1,0:T(8,128)(2,1)S(1)}, bf16[2,48,3072]{2,1,0:T(8,128)(2,1)S(1)}, u32[]{:S(2)}, u32[]{:S(2)}) collective-permute-start(bf16[2,48,3072]{2,1,0:T(8,128)(2,1)S(1)} %get-tuple-element.80), channel_id=1, source_target_pairs={{0,96},{32,0},{64,32},{96,64},{1,97},{33,1},{65,33},{97,65},{2,98}... | collective-permute-start | bytes 1769480 | tf_op jit(solution)/shard_map/ppermute | solution.py:532
  233.2 3.2 %collective-permute-start.26 = (bf16[2,48,3072]{2,1,0:T(8,128)(2,1)S(1)}, bf16[2,48,3072]{2,1,0:T(8,128)(2,1)S(1)}, u32[]{:S(2)}, u32[]{:S(2)}) collective-permute-start(bf16[2,48,3072]{2,1,0:T(8,128)(2,1)S(1)} %get-tuple-element.84), channel_id=1, source_target_pairs={{0,24},{8,0},{16,8},{24,16},{1,25},{9,1},{17,9},{25,17},{2,26},{10... | collective-permute-start | bytes 1769480 | tf_op jit(solution)/shard_map/ppermute | solution.py:532
  236.4 6.1 %rest_rows.1 = (bf16[4,48,3072]{2,1,0:T(8,128)(2,1)S(1)}, bf16[4,48,3072]{2,1,0:T(8,128)(2,1)S(1)}, bf16[4,48,3072]{2,1,0:T(8,128)(2,1)S(1)}, bf16[4,48,3072]{2,...) custom-call(bf16[768,576]{1,0:T(8,128)(2,1)S(1)} %get-tuple-element.76.hidden, ...), custom_call_target="tpu_custom_call" | custom-call | flops 4076863488 | bytes 1048576 | tf_op jit(solution)/shard_map/rest_rows/pallas_call | solution.py:186
  245.1 2.7 collective-permute-done.25.up1
  251.9 3.2 collective-permute-start.28
  255.0 20.0 %collective-permute-done.27.u0 = bf16[4,48,3072]{2,1,0:T(8,128)(2,1)S(1)} collective-permute-done((bf16[4,48,3072]{2,1,0:T(8,128)(2,1)S(1)}, bf16[4,48,3072]{2,1,0:T(8,128)(2,1)S(1)}, u32[]{:S(2)}, u32[]{:S(2)}) %collective-permute-start.27) | collective-permute-done | bytes 1179680 | tf_op jit(solution)/shard_map/ppermute | solution.py:528
  277.9 3.2 %collective-permute-start.32 = (bf16[48,3072]{1,0:T(8,128)(2,1)S(1)}, bf16[48,3072]{1,0:T(8,128)(2,1)S(1)}, u32[]{:S(2)}, u32[]{:S(2)}) collective-permute-start(bf16[48,3072]{1,0:T(8,128)(2,1)S(1)} %get-tuple-element.95), channel_id=1, source_target_pairs={{0,24},{8,0},{16,8},{24,16},{1,25},{9,1},{17,9},{25,17},{2,26},{10... | collective-permute-start | bytes 884744 | tf_op jit(solution)/shard_map/ppermute | solution.py:532
  281.7 3.1 collective-permute-start.35
  284.8 5.1 %collective-permute-done.31.a1 = bf16[48,3072]{1,0:T(8,128)(2,1)S(1)} collective-permute-done((bf16[48,3072]{1,0:T(8,128)(2,1)S(1)}, bf16[48,3072]{1,0:T(8,128)(2,1)S(1)}, u32[]{:S(2)}, u32[]{:S(2)}) %collective-permute-start.31) | collective-permute-done | bytes 294944 | tf_op jit(solution)/shard_map/ppermute | solution.py:528
  292.7 5.5 %collective-permute-done.36.b3 = bf16[48,3072]{1,0:T(8,128)(2,1)S(1)} collective-permute-done((bf16[48,3072]{1,0:T(8,128)(2,1)S(1)}, bf16[48,3072]{1,0:T(8,128)(2,1)S(1)}, u32[]{:S(2)}, u32[]{:S(2)}) %collective-permute-start.36) | collective-permute-done | bytes 294944 | tf_op jit(solution)/shard_map/ppermute | solution.py:536
  309.0 2.8 combine.1
  (187 shorter events, 98.6 us)
Async XLA Ops:
  6.5 78.7 %all-gather.2.cloned.1.call-start = ((), (), s32[]{:S(2)}) async-start(), calls=%async_computation.3 | async-start | bytes 12976128 | tf_op jit(solution)/shard_map/all_gather | solution.py:566
  7.3 58.7 %collective-permute-start.3 = (bf16[288,6144]{1,0:T(8,128)(2,1)}, bf16[288,6144]{1,0:T(8,128)(2,1)S(1)}, u32[]{:S(2)}, u32[]{:S(2)}) collective-permute-start(bf16[288,6144]{1,0:T(8,128)(2,1)} %bitcast.20), channel_id=1, source_target_pairs={{0,4},{4,0},{1,5},{5,1},{2,6},{6,2},{3,7},{7,3},{8,12},{12,8},{9,1... | collective-permute-start | bytes 10616840 | tf_op jit(solution)/shard_map/ppermute | solution.py:569
  7.4 58.7 %collective-permute-start.4 = (bf16[288,6144]{1,0:T(8,128)(2,1)}, bf16[288,6144]{1,0:T(8,128)(2,1)}, u32[]{:S(2)}, u32[]{:S(2)}) collective-permute-start(bf16[288,6144]{1,0:T(8,128)(2,1)} %bitcast.22), channel_id=1, source_target_pairs={{0,4},{4,0},{1,5},{5,1},{2,6},{6,2},{3,7},{7,3},{8,12},{12,8},{9,1... | collective-permute-start | bytes 10616840 | tf_op jit(solution)/shard_map/ppermute | solution.py:569
  7.8 58.2 %collective-permute-start.5 = (bf16[288,6144]{1,0:T(8,128)(2,1)}, bf16[288,6144]{1,0:T(8,128)(2,1)}, u32[]{:S(2)}, u32[]{:S(2)}) collective-permute-start(bf16[288,6144]{1,0:T(8,128)(2,1)} %bitcast.24), channel_id=1, source_target_pairs={{0,4},{4,0},{1,5},{5,1},{2,6},{6,2},{3,7},{7,3},{8,12},{12,8},{9,1... | collective-permute-start | bytes 10616840 | tf_op jit(solution)/shard_map/ppermute | solution.py:569
  43.7 22.3 %all-to-all-start.1 = ((bf16[32,64,128]{2,1,0:T(8,128)(2,1)}), bf16[32,64,128]{2,1,0:T(8,128)(2,1)}, u32[]{:S(2)}, u32[]{:S(2)}) async-start(bf16[32,64,128]{2,1,0:T(8,128)(2,1)} %copy-done.18), calls=%async_computation.1 | async-start | bytes 1048576 | tf_op jit(solution)/shard_map/all_to_all | solution.py:580
  48.3 253.3 %reduce-scatter.2.cloned.1.call-start = ((), (), s32[]{:S(2)}) async-start(), calls=%async_computation.4 | async-start | bytes 7864320 | tf_op jit(solution)/shard_map/reduce_scatter | solution.py:621
  100.9 29.3 %collective-permute-start.6 = (bf16[48,6144]{1,0:T(8,128)(2,1)}, bf16[48,6144]{1,0:T(8,128)(2,1)}, u32[]{:S(2)}, u32[]{:S(2)}) collective-permute-start(bf16[48,6144]{1,0:T(8,128)(2,1)} %get-tuple-element.62), channel_id=1, source_target_pairs={{0,1},{1,2},{2,3},{3,0},{4,5},{5,6},{6,7},{7,4},{8,9},{9,10},{10,1... | collective-permute-start | bytes 1769480 | tf_op jit(solution)/shard_map/ppermute | solution.py:528
  102.4 27.9 %collective-permute-start.7 = (bf16[48,6144]{1,0:T(8,128)(2,1)}, bf16[48,6144]{1,0:T(8,128)(2,1)}, u32[]{:S(2)}, u32[]{:S(2)}) collective-permute-start(bf16[48,6144]{1,0:T(8,128)(2,1)} %get-tuple-element.63), channel_id=1, source_target_pairs={{0,3},{1,0},{2,1},{3,2},{4,7},{5,4},{6,5},{7,6},{8,11},{9,8},{10,9... | collective-permute-start | bytes 1769480 | tf_op jit(solution)/shard_map/ppermute | solution.py:532
  104.2 27.3 %collective-permute-start.8 = (bf16[48,6144]{1,0:T(8,128)(2,1)}, bf16[48,6144]{1,0:T(8,128)(2,1)}, u32[]{:S(2)}, u32[]{:S(2)}) collective-permute-start(bf16[48,6144]{1,0:T(8,128)(2,1)} %get-tuple-element.64), channel_id=1, source_target_pairs={{0,2},{1,3},{2,0},{3,1},{4,6},{5,7},{6,4},{7,5},{8,10},{9,11},{10,... | collective-permute-start | bytes 1769480 | tf_op jit(solution)/shard_map/ppermute | solution.py:536
  141.2 11.5 %collective-permute-start.11 = (bf16[48,3072]{1,0:T(8,128)(2,1)S(1)}, bf16[48,3072]{1,0:T(8,128)(2,1)S(1)}, u32[]{:S(2)}, u32[]{:S(2)}) collective-permute-start(bf16[48,3072]{1,0:T(8,128)(2,1)S(1)} %get-tuple-element.70.a0), channel_id=1, source_target_pairs={{0,16},{8,24},{16,0},{24,8},{1,17},{9,25},{17,1},{25,9},{2,18},{10... | collective-permute-start | bytes 884744 | tf_op jit(solution)/shard_map/ppermute | solution.py:536
  144.3 13.3 %collective-permute-start.10 = (bf16[48,3072]{1,0:T(8,128)(2,1)S(1)}, bf16[48,3072]{1,0:T(8,128)(2,1)S(1)}, u32[]{:S(2)}, u32[]{:S(2)}) collective-permute-start(bf16[48,3072]{1,0:T(8,128)(2,1)S(1)} %get-tuple-element.70.a0), channel_id=1, source_target_pairs={{0,24},{8,0},{16,8},{24,16},{1,25},{9,1},{17,9},{25,17},{2,26},{10... | collective-permute-start | bytes 884744 | tf_op jit(solution)/shard_map/ppermute | solution.py:532
  145.5 12.1 %collective-permute-start.9 = (bf16[48,3072]{1,0:T(8,128)(2,1)S(1)}, bf16[48,3072]{1,0:T(8,128)(2,1)S(1)}, u32[]{:S(2)}, u32[]{:S(2)}) collective-permute-start(bf16[48,3072]{1,0:T(8,128)(2,1)S(1)} %get-tuple-element.70.a0), channel_id=1, source_target_pairs={{0,8},{8,16},{16,24},{24,0},{1,9},{9,17},{17,25},{25,1},{2,10},{10... | collective-permute-start | bytes 884744 | tf_op jit(solution)/shard_map/ppermute | solution.py:528
  147.7 12.2 %collective-permute-start.13 = (bf16[48,3072]{1,0:T(8,128)(2,1)S(1)}, bf16[48,3072]{1,0:T(8,128)(2,1)S(1)}, u32[]{:S(2)}, u32[]{:S(2)}) collective-permute-start(bf16[48,3072]{1,0:T(8,128)(2,1)S(1)} %get-tuple-element.71.b0), channel_id=1, source_target_pairs={{0,96},{32,0},{64,32},{96,64},{1,97},{33,1},{65,33},{97,65},{2,98}... | collective-permute-start | bytes 884744 | tf_op jit(solution)/shard_map/ppermute | solution.py:532
  161.8 26.4 %collective-permute-start.16 = (bf16[4,48,3072]{2,1,0:T(8,128)(2,1)S(1)}, bf16[4,48,3072]{2,1,0:T(8,128)(2,1)S(1)}, u32[]{:S(2)}, u32[]{:S(2)}) collective-permute-start(bf16[4,48,3072]{2,1,0:T(8,128)(2,1)S(1)} %get-tuple-element.72.a0), channel_id=1, source_target_pairs={{0,96},{32,0},{64,32},{96,64},{1,97},{33,1},{65,33},{97,65},{2,98}... | collective-permute-start | bytes 3538952 | tf_op jit(solution)/shard_map/ppermute | solution.py:532
  162.7 29.3 %collective-permute-start.15 = (bf16[4,48,3072]{2,1,0:T(8,128)(2,1)S(1)}, bf16[4,48,3072]{2,1,0:T(8,128)(2,1)S(1)}, u32[]{:S(2)}, u32[]{:S(2)}) collective-permute-start(bf16[4,48,3072]{2,1,0:T(8,128)(2,1)S(1)} %get-tuple-element.72.a0), channel_id=1, source_target_pairs={{0,32},{32,64},{64,96},{96,0},{1,33},{33,65},{65,97},{97,1},{2,34}... | collective-permute-start | bytes 3538952 | tf_op jit(solution)/shard_map/ppermute | solution.py:528
  163.9 29.2 %collective-permute-start.18 = (bf16[4,48,3072]{2,1,0:T(8,128)(2,1)S(1)}, bf16[4,48,3072]{2,1,0:T(8,128)(2,1)S(1)}, u32[]{:S(2)}, u32[]{:S(2)}) collective-permute-start(bf16[4,48,3072]{2,1,0:T(8,128)(2,1)S(1)} %get-tuple-element.73.b0), channel_id=1, source_target_pairs={{0,24},{8,0},{16,8},{24,16},{1,25},{9,1},{17,9},{25,17},{2,26},{10... | collective-permute-start | bytes 3538952 | tf_op jit(solution)/shard_map/ppermute | solution.py:532
  166.8 29.8 %collective-permute-start.17 = (bf16[4,48,3072]{2,1,0:T(8,128)(2,1)S(1)}, bf16[4,48,3072]{2,1,0:T(8,128)(2,1)S(1)}, u32[]{:S(2)}, u32[]{:S(2)}) collective-permute-start(bf16[4,48,3072]{2,1,0:T(8,128)(2,1)S(1)} %get-tuple-element.73.b0), channel_id=1, source_target_pairs={{0,8},{8,16},{16,24},{24,0},{1,9},{9,17},{17,25},{25,1},{2,10},{10... | collective-permute-start | bytes 3538952 | tf_op jit(solution)/shard_map/ppermute | solution.py:528
  188.3 31.1 %collective-permute-start.20 = (bf16[2,48,3072]{2,1,0:T(8,128)(2,1)S(1)}, bf16[2,48,3072]{2,1,0:T(8,128)(2,1)S(1)}, u32[]{:S(2)}, u32[]{:S(2)}) collective-permute-start(bf16[2,48,3072]{2,1,0:T(8,128)(2,1)S(1)} %slice.17), channel_id=1, source_target_pairs={{0,96},{32,0},{64,32},{96,64},{1,97},{33,1},{65,33},{97,65},{2,98}... | collective-permute-start | bytes 1769480 | tf_op jit(solution)/shard_map/ppermute | solution.py:532
  193.1 26.3 %collective-permute-start.19 = (bf16[2,48,3072]{2,1,0:T(8,128)(2,1)S(1)}, bf16[2,48,3072]{2,1,0:T(8,128)(2,1)S(1)}, u32[]{:S(2)}, u32[]{:S(2)}) collective-permute-start(bf16[2,48,3072]{2,1,0:T(8,128)(2,1)S(1)} %slice.16), channel_id=1, source_target_pairs={{0,32},{32,64},{64,96},{96,0},{1,33},{33,65},{65,97},{97,1},{2,34}... | collective-permute-start | bytes 1769480 | tf_op jit(solution)/shard_map/ppermute | solution.py:528
  194.0 25.4 %collective-permute-start.22 = (bf16[2,48,3072]{2,1,0:T(8,128)(2,1)}, bf16[2,48,3072]{2,1,0:T(8,128)(2,1)S(1)}, u32[]{:S(2)}, u32[]{:S(2)}) collective-permute-start(bf16[2,48,3072]{2,1,0:T(8,128)(2,1)} %slice.19), channel_id=1, source_target_pairs={{0,24},{8,0},{16,8},{24,16},{1,25},{9,1},{17,9},{25,17},{2,26},{10... | collective-permute-start | bytes 1769480 | tf_op jit(solution)/shard_map/ppermute | solution.py:532
  197.5 21.9 %collective-permute-start.21 = (bf16[2,48,3072]{2,1,0:T(8,128)(2,1)}, bf16[2,48,3072]{2,1,0:T(8,128)(2,1)S(1)}, u32[]{:S(2)}, u32[]{:S(2)}) collective-permute-start(bf16[2,48,3072]{2,1,0:T(8,128)(2,1)} %slice.18), channel_id=1, source_target_pairs={{0,8},{8,16},{16,24},{24,0},{1,9},{9,17},{17,25},{25,1},{2,10},{10... | collective-permute-start | bytes 1769480 | tf_op jit(solution)/shard_map/ppermute | solution.py:528
  229.8 15.3 %collective-permute-start.23 = (bf16[2,48,3072]{2,1,0:T(8,128)(2,1)S(1)}, bf16[2,48,3072]{2,1,0:T(8,128)(2,1)S(1)}, u32[]{:S(2)}, u32[]{:S(2)}) collective-permute-start(bf16[2,48,3072]{2,1,0:T(8,128)(2,1)S(1)} %get-tuple-element.79), channel_id=1, source_target_pairs={{0,32},{32,64},{64,96},{96,0},{1,33},{33,65},{65,97},{97,1},{2,34}... | collective-permute-start | bytes 1769480 | tf_op jit(solution)/shard_map/ppermute | solution.py:528
  229.9 15.3 %collective-permute-start.24 = (bf16[2,48,3072]{2,1,0:T(8,128)(2,1)S(1)}, bf16[2,48,3072]{2,1,0:T(8,128)(2,1)S(1)}, u32[]{:S(2)}, u32[]{:S(2)}) collective-permute-start(bf16[2,48,3072]{2,1,0:T(8,128)(2,1)S(1)} %get-tuple-element.80), channel_id=1, source_target_pairs={{0,96},{32,0},{64,32},{96,64},{1,97},{33,1},{65,33},{97,65},{2,98}... | collective-permute-start | bytes 1769480 | tf_op jit(solution)/shard_map/ppermute | solution.py:532
  233.2 14.7 %collective-permute-start.25 = (bf16[2,48,3072]{2,1,0:T(8,128)(2,1)S(1)}, bf16[2,48,3072]{2,1,0:T(8,128)(2,1)S(1)}, u32[]{:S(2)}, u32[]{:S(2)}) collective-permute-start(bf16[2,48,3072]{2,1,0:T(8,128)(2,1)S(1)} %get-tuple-element.83), channel_id=1, source_target_pairs={{0,8},{8,16},{16,24},{24,0},{1,9},{9,17},{17,25},{25,1},{2,10},{10... | collective-permute-start | bytes 1769480 | tf_op jit(solution)/shard_map/ppermute | solution.py:528
  233.2 14.7 %collective-permute-start.26 = (bf16[2,48,3072]{2,1,0:T(8,128)(2,1)S(1)}, bf16[2,48,3072]{2,1,0:T(8,128)(2,1)S(1)}, u32[]{:S(2)}, u32[]{:S(2)}) collective-permute-start(bf16[2,48,3072]{2,1,0:T(8,128)(2,1)S(1)} %get-tuple-element.84), channel_id=1, source_target_pairs={{0,24},{8,0},{16,8},{24,16},{1,25},{9,1},{17,9},{25,17},{2,26},{10... | collective-permute-start | bytes 1769480 | tf_op jit(solution)/shard_map/ppermute | solution.py:532
  248.5 26.5 %collective-permute-start.27 = (bf16[4,48,3072]{2,1,0:T(8,128)(2,1)S(1)}, bf16[4,48,3072]{2,1,0:T(8,128)(2,1)S(1)}, u32[]{:S(2)}, u32[]{:S(2)}) collective-permute-start(bf16[4,48,3072]{2,1,0:T(8,128)(2,1)S(1)} %get-tuple-element.89), channel_id=1, source_target_pairs={{0,32},{32,64},{64,96},{96,0},{1,33},{33,65},{65,97},{97,1},{2,34}... | collective-permute-start | bytes 3538952 | tf_op jit(solution)/shard_map/ppermute | solution.py:528
  248.6 26.5 %collective-permute-start.29 = (bf16[4,48,3072]{2,1,0:T(8,128)(2,1)S(1)}, bf16[4,48,3072]{2,1,0:T(8,128)(2,1)S(1)}, u32[]{:S(2)}, u32[]{:S(2)}) collective-permute-start(bf16[4,48,3072]{2,1,0:T(8,128)(2,1)S(1)} %get-tuple-element.91), channel_id=1, source_target_pairs={{0,8},{8,16},{16,24},{24,0},{1,9},{9,17},{17,25},{25,1},{2,10},{10... | collective-permute-start | bytes 3538952 | tf_op jit(solution)/shard_map/ppermute | solution.py:528
  249.8 25.3 %collective-permute-start.30 = (bf16[4,48,3072]{2,1,0:T(8,128)(2,1)S(1)}, bf16[4,48,3072]{2,1,0:T(8,128)(2,1)S(1)}, u32[]{:S(2)}, u32[]{:S(2)}) collective-permute-start(bf16[4,48,3072]{2,1,0:T(8,128)(2,1)S(1)} %get-tuple-element.92), channel_id=1, source_target_pairs={{0,24},{8,0},{16,8},{24,16},{1,25},{9,1},{17,9},{25,17},{2,26},{10... | collective-permute-start | bytes 3538952 | tf_op jit(solution)/shard_map/ppermute | solution.py:532
  251.9 25.1 %collective-permute-start.28 = (bf16[4,48,3072]{2,1,0:T(8,128)(2,1)S(1)}, bf16[4,48,3072]{2,1,0:T(8,128)(2,1)S(1)}, u32[]{:S(2)}, u32[]{:S(2)}) collective-permute-start(bf16[4,48,3072]{2,1,0:T(8,128)(2,1)S(1)} %get-tuple-element.85.late), channel_id=1, source_target_pairs={{0,96},{32,0},{64,32},{96,64},{1,97},{33,1},{65,33},{97,65},{2,98}... | collective-permute-start | bytes 3538952 | tf_op jit(solution)/shard_map/ppermute | solution.py:532
  277.8 12.2 %collective-permute-start.31 = (bf16[48,3072]{1,0:T(8,128)(2,1)S(1)}, bf16[48,3072]{1,0:T(8,128)(2,1)S(1)}, u32[]{:S(2)}, u32[]{:S(2)}) collective-permute-start(bf16[48,3072]{1,0:T(8,128)(2,1)S(1)} %get-tuple-element.94), channel_id=1, source_target_pairs={{0,8},{8,16},{16,24},{24,0},{1,9},{9,17},{17,25},{25,1},{2,10},{10... | collective-permute-start | bytes 884744 | tf_op jit(solution)/shard_map/ppermute | solution.py:528
  277.9 14.0 %collective-permute-start.32 = (bf16[48,3072]{1,0:T(8,128)(2,1)S(1)}, bf16[48,3072]{1,0:T(8,128)(2,1)S(1)}, u32[]{:S(2)}, u32[]{:S(2)}) collective-permute-start(bf16[48,3072]{1,0:T(8,128)(2,1)S(1)} %get-tuple-element.95), channel_id=1, source_target_pairs={{0,24},{8,0},{16,8},{24,16},{1,25},{9,1},{17,9},{25,17},{2,26},{10... | collective-permute-start | bytes 884744 | tf_op jit(solution)/shard_map/ppermute | solution.py:532
  281.1 11.6 %collective-permute-start.34 = (bf16[48,3072]{1,0:T(8,128)(2,1)S(1)}, bf16[48,3072]{1,0:T(8,128)(2,1)S(1)}, u32[]{:S(2)}, u32[]{:S(2)}) collective-permute-start(bf16[48,3072]{1,0:T(8,128)(2,1)S(1)} %get-tuple-element.98), channel_id=1, source_target_pairs={{0,32},{32,64},{64,96},{96,0},{1,33},{33,65},{65,97},{97,1},{2,34}... | collective-permute-start | bytes 884744 | tf_op jit(solution)/shard_map/ppermute | solution.py:528
  (62 other events, 503.7 us)
Sparse Core Ops, SparseCore 0:
  9.6 75.5 all-gather.1
  141.4 62.4 reduce-scatter.1

commit v4 on v3

--- a/solution.py
+++ b/solution.py
@@ -90,7 +90,7 @@
             jax.ShapeDtypeStruct((seqs * heads * 2, half + DEC, HEAD), BF),
             jax.ShapeDtypeStruct((seqs, steps, heads), F32),
         ],
-        compiler_params=pltpu.CompilerParams(vmem_limit_bytes=32 * 2**20),
+        compiler_params=pltpu.CompilerParams(vmem_limit_bytes=60 * 2**20),
         name="local_attention",
     )(q, k, v, d)
 
@@ -115,7 +115,7 @@
     )(arrived)
 
 
-def carry_kernel(q_ref, inner_ref, cum_ref, state_ref, gain_ref, h0, h1, h2, out_ref, *same):
+def carry_kernel(q_ref, inner_ref, cum_ref, state_ref, gain_ref, out_ref):
     shares, slice_len = out_ref.shape[0], out_ref.shape[2]
     heads = cum_ref.shape[2]
     grow = jnp.exp(cum_ref[0])
@@ -130,7 +130,7 @@
             ]
 
 
-def carried(q, inner, cum, state, gain, shares, held):
+def carried(q, inner, cum, state, gain, shares):
     seqs, steps, width = q.shape
     heads = width // HEAD
     block = pl.BlockSpec((1, steps, width), lambda s: (s, 0, 0))
@@ -143,42 +143,12 @@
             pl.BlockSpec((1, steps, heads), lambda s: (s, 0, 0)),
             pl.BlockSpec((heads, HEAD, HEAD), lambda s: (s, 0, 0)),
             pl.BlockSpec((1, width), lambda s: (0, 0)),
-        ]
-        + [ANY] * 3,
-        out_specs=[pl.BlockSpec((shares, 1, steps // shares, width), lambda s: (0, s, 0, 0))]
-        + [ANY] * 3,
-        out_shape=[jax.ShapeDtypeStruct((shares, seqs, steps // shares, width), BF)]
-        + [jax.ShapeDtypeStruct(h.shape, BF) for h in held],
-        input_output_aliases={5: 1, 6: 2, 7: 3},
+        ],
+        out_specs=pl.BlockSpec((shares, 1, steps // shares, width), lambda s: (0, s, 0, 0)),
+        out_shape=jax.ShapeDtypeStruct((shares, seqs, steps // shares, width), BF),
         compiler_params=pltpu.CompilerParams(vmem_limit_bytes=32 * 2**20),
         name="carried_norm",
-    )(q, inner, cum, state, gain, *held)
-
-
-def route_kernel(cap, me_ref, routes_ref, place_ref, own_ref):
-    flight, rows = routes_ref.shape[1] // 128, 128
-    total = routes_ref.shape[1]
-    me = me_ref[0]
-    a = lax.broadcasted_iota(jnp.int32, (total, total), 0)
-    b = lax.broadcasted_iota(jnp.int32, (total, total), 1)
-    before = ((a < b) & (a // rows == b // rows)).astype(BF)
-    first, second = routes_ref[0:1, :], routes_ref[1:2, :]
-    home = lax.broadcasted_iota(jnp.int32, (1, total), 1) // rows
-    slots = lax.broadcasted_iota(jnp.int32, (flight * cap, total), 0)
-    for r, off in enumerate(OFFS):
-        expert = lax.rem(me + off, flight)
-        chosen = ((first == expert) | (second == expert)).astype(F32)
-        rank = mm(jnp.broadcast_to(chosen, (8, total)).astype(BF), before)[0:1].astype(jnp.int32)
-        start = jnp.zeros((1, total), jnp.int32)
-        for delta in range(flight):
-            start = jnp.where(home == delta, cap * JREL[(delta - off) % 4], start)
-        target = jnp.where(chosen > 0.0, start + rank, -1)
-        hits = (slots == target).astype(F32).astype(BF)
-        span = slice(r * flight * cap, (r + 1) * flight * cap)
-        own_ref[span, :] = hits[:, :rows]
-        for delta in range(flight):
-            at = pl.multiple_of(lax.rem(me + delta, flight) * rows, rows)
-            place_ref[span, pl.ds(at, rows)] = hits[:, delta * rows : (delta + 1) * rows]
+    )(q, inner, cum, state, gain)
 
 
 def call(kernel, name, outs, *args, **kw):
@@ -192,16 +162,39 @@
     )(*args)
 
 
+def route_kernel(cap, me_ref, r0, r1, r2, r3, place_ref, own_ref):
+    homes = (r0, r1, r2, r3)
+    flight, rows = len(homes), r0.shape[1]
+    me = me_ref[0]
+    a = lax.broadcasted_iota(jnp.int32, (rows, rows), 0)
+    b = lax.broadcasted_iota(jnp.int32, (rows, rows), 1)
+    before = (a < b).astype(F32).astype(BF)
+    slots = lax.broadcasted_iota(jnp.int32, (flight * cap, rows), 0)
+    for r, off in enumerate(OFFS):
+        expert = lax.rem(me + off, flight)
+        span = slice(r * flight * cap, (r + 1) * flight * cap)
+        for delta, home in enumerate(homes):
+            hit = (home[0:1, :] == expert) | (home[1:2, :] == expert)
+            chosen = hit.astype(F32)
+            rank = mm(jnp.broadcast_to(chosen, (8, rows)).astype(BF), before)[0:1]
+            start = cap * JREL[(delta - off) % 4]
+            target = jnp.where(chosen > 0.0, rank.astype(jnp.int32) + start, -1)
+            hits = (slots == target).astype(F32).astype(BF)
+            at = pl.multiple_of(lax.rem(me + delta, flight) * rows, rows)
+            place_ref[span, pl.ds(at, rows)] = hits
+            if delta == 0:
+                own_ref[span, :] = hits
+
+
 def route(me, routes, cap):
-    total = routes.shape[1]
-    flight = total // 128
+    flight, rows = len(routes), routes[0].shape[1]
     return call(
         functools.partial(route_kernel, cap),
         "route",
-        [((flight * flight * cap, n), BF) for n in (total, 128)],
+        [((flight * flight * cap, n), BF) for n in (flight * rows, rows)],
         me,
-        routes,
-        in_specs=[SM, VM],
+        *routes,
+        in_specs=[SM] + [VM] * flight,
         out_specs=[VM, VM],
     )
 
@@ -216,7 +209,7 @@
     def _():
         picked[...] = mm(place_ref[...], normed_ref[...]).astype(BF)
 
-    full = nt(picked[...], weight_ref[...]) + mm(own_ref[...], res_ref[...])
+    full = nt(weight_ref[...], picked[...]).T + mm(own_ref[...], res_ref[...])
     full = full.astype(BF)
     size = o0.shape[0]
     for i, o in enumerate((o0, o1, o2, o3)):
@@ -247,15 +240,15 @@
         ],
         out_specs=[pl.BlockSpec((size, tile), lambda n: (0, n))] * 4,
         scratch_shapes=[pltpu.VMEM((picks, width), BF)],
-        vmem=40,
-    )
-
-
-def whole_kernel(normed_ref, weight_ref, out_ref):
+        vmem=54,
+    )
+
+
+def whole_kernel(normed_ref, weight_ref, late, out_ref):
     out_ref[...] = nt(normed_ref[...], weight_ref[...]).astype(BF)
 
 
-def whole_projection(normed, weight, tile=1024):
+def whole_projection(normed, weight, late, tile=1024):
     total, (model, width) = normed.shape[0], weight.shape
     return call(
         whole_kernel,
@@ -263,20 +256,23 @@
         [((total, model), BF)],
         normed,
         weight,
+        late,
         grid=(model // tile,),
         in_specs=[
             pl.BlockSpec(normed.shape, lambda n: (0, 0)),
             pl.BlockSpec((tile, width), lambda n: (n, 0)),
+            VM,
         ],
         out_specs=[pl.BlockSpec((total, tile), lambda n: (0, n))],
         cost_estimate=pl.CostEstimate(
             flops=2 * total * model * width, bytes_accessed=4 * model * width, transcendentals=0
         ),
-        vmem=24,
+        vmem=58,
     )[0]
 
 
-def norm_kernel(a, b, c, d, gain, held, w0, o0, o1, *same):
+def norm_kernel(a, b, c, d, gain, o0, o1, ready):
+    ready[...] = jnp.zeros_like(ready)
     x = a[...].astype(F32) + b[...].astype(F32) + c[...].astype(F32) + d[...].astype(F32)
     x = x * lax.rsqrt(jnp.mean(x * x, -1, keepdims=True) + 1e-06) * gain[...]
     half = o0.shape[1]
@@ -284,176 +280,220 @@
     o1[...] = x[:, half:].astype(BF)
 
 
+def hold_kernel(held, late, same):
+    pass
+
+
 def stack_kernel(a0, a1, a2, a3, b0, b1, b2, b3, o0, o1):
     for i, (a, b) in enumerate(((a0, b0), (a1, b1), (a2, b2), (a3, b3))):
         o0[i] = a[...]
         o1[i] = b[...]
 
 
-def pack_kernel(g0, g1, u0, u1, d0, d1, late, gu, down, sems):
-    units = g0.shape[0]
-    copies = []
-    for i, part in enumerate((g0, g1, u0, u1)):
-        copies.append((part, gu.at[pl.ds(i * units, units)]))
-    for i, part in enumerate((d0, d1)):
-        copies.append((part, down.at[pl.ds(i * units, units)]))
-    copies = [pltpu.make_async_copy(a, b, sems.at[i]) for i, (a, b) in enumerate(copies)]
-    for c in copies:
-        c.start()
-    for c in copies:
-        c.wait()
-
-
 def by_y(rows, y):
     return [((z * 4 + y) * rows, z) for z in range(4)]
 
 
-def near_kernel(tile, a0, a1, a2, b0, b1, b2, gu, acc, x, part):
-    rows, half = a0.shape[1], a0.shape[2]
+def fetch(parts, buf, sems, chunk, slot):
+    units, tile = parts[0].shape[0], buf.shape[2]
+    cols = pl.ds(pl.multiple_of(chunk * tile, tile), tile)
+    return [
+        pltpu.make_async_copy(
+            part.at[:, cols], buf.at[slot, pl.ds(i * units, units)], sems.at[slot, i]
+        )
+        for i, part in enumerate(parts)
+    ]
+
+
+def streamed(parts, buf, sems, chunks, body):
+    @pl.loop(0, chunks)
+    def _(c):
+        slot = lax.rem(c, 2)
+
+        @pl.when(c + 1 < chunks)
+        def _():
+            for copy in fetch(parts, buf, sems, c + 1, 1 - slot):
+                copy.start()
+
+        for copy in fetch(parts, buf, sems, c, slot):
+            copy.wait()
+        body(c, buf[slot])
+
+
+def first_chunk(parts, buf, sems):
+    for copy in fetch(parts, buf, sems, 0, 0):
+        copy.start()
+
+
+def gate_up(refs_a, refs_b, parts, x, part, buf, sems):
+    tile = buf.shape[2]
+    rows, half = refs_a[0].shape[1:]
+    each = half // tile
+    part[...] = jnp.zeros_like(part)
+
+    def body(c, weights):
+        for k, refs in enumerate((refs_a, refs_b)):
+
+            @pl.when(c // each == k)
+            def _():
+                at = pl.ds(pl.multiple_of((c - k * each) * tile, tile), tile)
+                row = 0
+                for ref in refs:
+                    for i in range(ref.shape[0]):
+                        x[row : row + rows, :] = ref[i, :, at]
+                        row += rows
+
+        part[c // each] += nt(x[...], weights)
+
+    streamed(parts, buf, sems, 2 * each, body)
+
+
+def down_product(value, parts, buf, sems, outs_a, outs_b):
+    tile = buf.shape[2]
+    rows, half = outs_a[0].shape[1:]
+    each = half // tile
+
+    def body(c, weights):
+        full = mm(value[c // each], weights).astype(BF)
+        for k, outs in enumerate((outs_a, outs_b)):
+
+            @pl.when(c // each == k)
+            def _():
+                at = pl.ds(pl.multiple_of((c - k * each) * tile, tile), tile)
+                row = 0
+                for out in outs:
+                    for i in range(out.shape[0]):
+                        out[i, :, at] = full[row : row + rows]
+                        row += rows
+
+    streamed(parts, buf, sems, 2 * each, body)
+
+
+def near_kernel(*refs):
+    a, b, parts = refs[0:3], refs[3:6], refs[6:8]
+    acc, x, part, buf, sems = refs[8:]
+    rows = a[0].shape[1]
     block = 4 * rows
-
-    def fill(refs, at):
-        for k, ref in enumerate(refs):
-            for i in range(4):
-                x[k * block + i * rows : k * block + (i + 1) * rows, :] = ref[i, :, at]
-
-    acc[...] = jnp.zeros_like(acc)
-    part[...] = jnp.zeros_like(part)
-
-    @pl.loop(0, half // tile)
-    def _(c):
-        at = pl.ds(pl.multiple_of(c * tile, tile), tile)
-        fill((a0, a1, a2), at)
-        acc[0 : 3 * block, :] += nt(x[...], gu[:, at])
-
-    @pl.loop(0, half // tile)
-    def _(c):
-        at = pl.ds(pl.multiple_of(c * tile, tile), tile)
-        wide = pl.ds(pl.multiple_of(half + c * tile, tile), tile)
-        fill((b0, b1, b2), at)
-        part[...] += nt(x[...], gu[:, wide])
-
+    first_chunk(parts, buf, sems)
+    gate_up(a, b, parts, x, part, buf, sems)
+    acc[0 : 3 * block, :] = part[0]
+    acc[3 * block :, :] = jnp.zeros((block, acc.shape[1]), F32)
     for y in range(3):
         for row, z in by_y(rows, y):
             at = y * block + z * rows
-            acc[row : row + rows, :] += part[at : at + rows, :]
-
-
-def far_kernel(tile, acc, a3, a4, b3, b4, gu, down, hidden, oa3, oa4, ob3, ob4, x, part, own):
-    rows, half = a3.shape[1], a3.shape[2]
+            acc[row : row + rows, :] += part[1, at : at + rows, :]
+
+
+def far_kernel(*refs):
+    acc, a, b, parts, downs = refs[0], refs[1:3], refs[3:5], refs[5:7], refs[7:8]
+    hidden, oa, ob = refs[8], refs[9:11], refs[11:13]
+    x, part, own, value, buf, sems, dbuf, dsems = refs[13:]
+    rows = a[0].shape[1]
     block = 4 * rows
-    units = down.shape[0]
-
-    def fill(refs, at):
-        for k, ref in enumerate(refs):
-            for i in range(2):
-                x[(2 * k + i) * rows : (2 * k + i + 1) * rows, :] = ref[i, :, at]
-
-    part[...] = jnp.zeros_like(part)
-
-    @pl.loop(0, half // tile)
-    def _(c):
-        at = pl.ds(pl.multiple_of(c * tile, tile), tile)
-        wide = pl.ds(pl.multiple_of(half + c * tile, tile), tile)
-        fill((a3, a4), at)
-        part[0:block, :] += nt(x[...], gu[:, at])
-        fill((b3, b4), at)
-        part[block : 2 * block, :] += nt(x[...], gu[:, wide])
-
+    units = own.shape[1] // 2
+    first_chunk(parts, buf, sems)
+    first_chunk(downs, dbuf, dsems)
+    gate_up(a, b, parts, x, part, buf, sems)
     own[...] = acc[...]
-    own[3 * block : 4 * block, :] += part[0:block, :]
+    own[3 * block :, :] += part[0]
     for row, z in by_y(rows, 3):
-        own[row : row + rows, :] += part[block + z * rows : block + (z + 1) * rows, :]
+        own[row : row + rows, :] += part[1, z * rows : (z + 1) * rows, :]
     g = own[:, :units]
     hidden[...] = (g / (1.0 + jnp.exp(-g)) * own[:, units:]).astype(BF)
-    by_z = hidden[3 * block : 4 * block, :]
-    across_y = jnp.concatenate([hidden[row : row + rows, :] for row, _ in by_y(rows, 3)])
-
-    @pl.loop(0, half // tile)
-    def _(c):
-        at = pl.ds(pl.multiple_of(c * tile, tile), tile)
-        wide = pl.ds(pl.multiple_of(half + c * tile, tile), tile)
-        for value, cols, outs in ((by_z, at, (oa3, oa4)), (across_y, wide, (ob3, ob4))):
-            full = mm(value, down[:, cols]).astype(BF)
-            for i in range(4):
-                outs[i // 2][i % 2, :, at] = full[i * rows : (i + 1) * rows]
-
-
-def rest_kernel(tile, hidden, down, oa0, oa1, oa2, ob0, ob1, ob2):
-    rows, half = oa0.shape[1], oa0.shape[2]
+    value[0] = hidden[3 * block :, :]
+    for row, z in by_y(rows, 3):
+        value[1, z * rows : (z + 1) * rows, :] = hidden[row : row + rows, :]
+    down_product(value, downs, dbuf, dsems, oa, ob)
+
+
+def rest_kernel(*refs):
+    hidden, downs, oa, ob = refs[0], refs[1:2], refs[2:5], refs[5:8]
+    value, dbuf, dsems = refs[8:]
+    rows = oa[0].shape[1]
     block = 4 * rows
-    by_z = hidden[0 : 3 * block, :]
-    across_y = jnp.concatenate(
-        [hidden[row : row + rows, :] for y in range(3) for row, _ in by_y(rows, y)]
-    )
-
-    @pl.loop(0, half // tile)
-    def _(c):
-        at = pl.ds(pl.multiple_of(c * tile, tile), tile)
-        wide = pl.ds(pl.multiple_of(half + c * tile, tile), tile)
-        for value, cols, outs in ((by_z, at, (oa0, oa1, oa2)), (across_y, wide, (ob0, ob1, ob2))):
-            full = mm(value, down[:, cols]).astype(BF)
-            for k, out in enumerate(outs):
-                for i in range(4):
-                    out[i, :, at] = full[k * block + i * rows : k * block + (i + 1) * rows]
+    first_chunk(downs, dbuf, dsems)
+    value[0] = hidden[: 3 * block, :]
+    for y in range(3):
+        for row, z in by_y(rows, y):
+            at = y * block + z * rows
+            value[1, at : at + rows, :] = hidden[row : row + rows, :]
+    down_product(value, downs, dbuf, dsems, oa, ob)
 
 
 def cost(flops):
     return pl.CostEstimate(flops=flops, bytes_accessed=2**20, transcendentals=0)
 
 
-def near(xs, gu, tile=1024):
-    rows, half = xs[0].shape[1:]
+TILE = 1024
+
+
+def streams(parts):
+    units, count = parts[0].shape[0], len(parts)
+    return [
+        pltpu.VMEM((2, count * units, TILE), BF),
+        pltpu.SemaphoreType.DMA((2, count)),
+    ]
+
+
+def near(xs, parts):
+    rows = xs[0].shape[1]
+    units = len(parts) * parts[0].shape[0]
     return call(
-        functools.partial(near_kernel, tile),
+        near_kernel,
         "near_rows",
-        [((16 * rows, gu.shape[0]), F32)],
+        [((16 * rows, units), F32)],
         *xs,
-        gu,
-        in_specs=[VM] * 7,
+        *parts,
+        in_specs=[VM] * 6 + [HBM] * len(parts),
         out_specs=[VM],
         scratch_shapes=[
-            pltpu.VMEM((12 * rows, tile), BF),
-            pltpu.VMEM((12 * rows, gu.shape[0]), F32),
+            pltpu.VMEM((12 * rows, TILE), BF),
+            pltpu.VMEM((2, 12 * rows, units), F32),
+            *streams(parts),
         ],
-        cost_estimate=cost(2 * 12 * rows * gu.size),
-        vmem=16,
+        cost_estimate=cost(2 * 12 * rows * len(parts) * parts[0].size),
+        vmem=46,
     )[0]
 
 
-def far(acc, xs, gu, down, tile=1024):
+def far(acc, xs, parts, downs):
     rows, half = xs[0].shape[1:]
+    units = len(downs) * downs[0].shape[0]
     return call(
-        functools.partial(far_kernel, tile),
+        far_kernel,
         "far_rows",
-        [((16 * rows, down.shape[0]), BF)] + [((2, rows, half), BF)] * 4,
+        [((16 * rows, units), BF)] + [((2, rows, half), BF)] * 4,
         acc,
         *xs,
-        gu,
-        down,
-        in_specs=[VM] * 7,
+        *parts,
+        *downs,
+        in_specs=[VM] * 5 + [HBM] * (len(parts) + len(downs)),
         out_specs=[VM] * 5,
         scratch_shapes=[
-            pltpu.VMEM((4 * rows, tile), BF),
-            pltpu.VMEM((8 * rows, gu.shape[0]), F32),
+            pltpu.VMEM((4 * rows, TILE), BF),
+            pltpu.VMEM((2, 4 * rows, 2 * units), F32),
             pltpu.VMEM(acc.shape, F32),
+            pltpu.VMEM((2, 4 * rows, units), BF),
+            *streams(parts),
+            *streams(downs),
         ],
-        vmem=20,
-    )
-
-
-def rest(hidden, down, rows, tile=1024):
-    half = down.shape[1] // 2
+        vmem=48,
+    )
+
+
+def rest(hidden, downs, rows):
+    half = downs[0].shape[1] // 2
     return call(
-        functools.partial(rest_kernel, tile),
+        rest_kernel,
         "rest_rows",
         [((4, rows, half), BF)] * 6,
         hidden,
-        down,
-        in_specs=[VM] * 2,
+        *downs,
+        in_specs=[VM] + [HBM] * len(downs),
         out_specs=[VM] * 6,
-        cost_estimate=cost(2 * 12 * rows * down.size),
-        vmem=16,
+        scratch_shapes=[pltpu.VMEM((2, 12 * rows, hidden.shape[1]), BF), *streams(downs)],
+        cost_estimate=cost(2 * 12 * rows * len(downs) * downs[0].size),
+        vmem=46,
     )
 
 
@@ -564,14 +604,13 @@
     me = lax.axis_index("x").astype(jnp.int32).reshape(1)
 
     weight_out = lax.all_gather(out_weight.T, SEQ, axis=0, tiled=True)
-    units = gate_weight.shape[1]
-    weights = (gate_weight[0], up_weight[0], down_weight[0])
-    swapped = [lax.ppermute(w, "core", ring(2, 1)) for w in weights]
+    gate, up, down = [
+        lax.all_gather(w[0], "core", axis=0, tiled=True)
+        for w in (gate_weight, up_weight, down_weight)
+    ]
     routes = picks.reshape(rows, 2)
     turned = routes.T
-    all_routes = jnp.concatenate(
-        [turned] + [lax.ppermute(turned, "x", ring(4, -delta)) for delta in (1, 2, 3)], axis=1
-    )
+    all_routes = [turned] + [lax.ppermute(turned, "x", ring(4, -delta)) for delta in (1, 2, 3)]
 
     inner, states, cum = local_part(
         queries, keys, payload_vectors, log_decay.transpose(0, 2, 1)
@@ -579,8 +618,8 @@
     arrived = lax.all_to_all(states, SEQ, 0, 0, tiled=True)
     prefix = lax.all_to_all(scan_states(arrived), SEQ, 0, 0, tiled=True)
     prefix = prefix.reshape(seqs * width // HEAD, HEAD, HEAD)
-    normed, *swapped = carried(
-        queries, inner, cum, prefix, attn_gain.reshape(1, width), shares, swapped
+    normed = carried(
+        queries, inner, cum, prefix, attn_gain.reshape(1, width), shares
     )
     normed = normed.reshape(shares * rows, width)
 
@@ -588,36 +627,33 @@
     flat = residual.reshape(rows, model)
     gain = norm_gain.reshape(1, model)
     to_up, to_down, to_far, here = selected(place, own_place, normed, weight_out, flat)
-    whole = whole_projection(normed, weight_out)
+    whole = whole_projection(normed, weight_out, here)
 
     size = here.shape[0]
-    gu, down = call(
-        pack_kernel,
-        "pack",
-        [((4 * units, model), BF), ((2 * units, model), BF)],
-        *[w for pair in zip(weights, swapped) for w in pair],
-        here,
-        in_specs=[ANY] * 6 + [VM],
-        out_specs=[VM, HBM],
-        scratch_shapes=[pltpu.SemaphoreType.DMA((6,))],
-        vmem=8,
-    )
-    a0, b0, whole, gu = call(
+    a0, b0, ready = call(
         norm_kernel,
         "selected_norm",
-        [((size, half), BF)] * 2 + [(w.shape, BF) for w in (whole, gu)],
+        [((size, half), BF)] * 2 + [((8, 128), F32)],
         here,
         up_one(to_up, "x"),
         down_one(to_down, "x"),
         across(to_far, "x"),
         gain,
+        in_specs=[VM] * 5,
+        out_specs=[VM] * 3,
+    )
+
+    whole = call(
+        hold_kernel,
+        "hold",
+        [(whole.shape, BF)],
         whole,
-        gu,
-        in_specs=[VM] * 5 + [HBM, VM],
-        out_specs=[VM] * 2 + [HBM, VM],
-        input_output_aliases={5: 2, 6: 3},
-        vmem=16,
-    )
+        ready,
+        in_specs=[ANY, VM],
+        out_specs=[ANY],
+        input_output_aliases={0: 0},
+        vmem=61,
+    )[0]
     mixed = lax.psum_scatter(whole, "x", scatter_dimension=0, tiled=True)
 
     a4, b4 = call(
@@ -634,15 +670,16 @@
         across(b0, "z"),
         in_specs=[VM] * 8,
         out_specs=[VM] * 2,
-        vmem=8,
+        vmem=16,
     )
     a_below, a_above = up_one(a4, "z"), down_one(a4, "z")
     b_below, b_above = up_one(b4, "y"), down_one(b4, "y")
     a_far, b_far = far_sides(a_below, a_above, "z"), far_sides(b_below, b_above, "y")
 
-    acc = near((a4, a_below, a_above, b4, b_below, b_above), gu)
-    hidden, *ends = far(acc, (*a_far, *b_far), gu, down)
-    body = rest(hidden, down, size)
+    gate_up_parts, downs = (gate, up), (down,)
+    acc = near((a4, a_below, a_above, b4, b_below, b_above), gate_up_parts)
+    hidden, *ends = far(acc, (*a_far, *b_far), gate_up_parts, downs)
+    body = rest(hidden, downs, size)
     oa, ob = (*body[:3], *ends[:2]), (*body[3:], *ends[2:])
     a_below, a_above, b_below, b_above = call(
         fold_kernel,

time: 320 us -> 320 us (level)
  local copies, waits for them, and re-layouts: 60.5 us -> 22 us
  Pallas kernels: 66.3 us -> 84.6 us
  starting transfers between devices: 61 us -> 71.7 us
  waiting for transfers between devices: 92.1 us -> 101 us
    unnamed x103 -> x55, local copies, waits for them, and re-layouts: 54.4 us -> 15.6 us
    ppermute x14, waiting for transfers between devices: 28.7 us -> 5.14 us  [down_one(): return lax.ppermute(x, axis, ring(4, -1))]
    pallas_call x14, Pallas kernels: 58.4 us -> 74.3 us  [call(): pl.pallas_call(kernel, out_shape=[jax.ShapeDtypeStruct(s, d) for s, d in...]
    ppermute x14, waiting for transfers between devices: 34.3 us -> 46.9 us  [up_one(): return lax.ppermute(x, axis, ring(4, 1))]
    ppermute x6, waiting for transfers between devices: 12.8 us -> 22.3 us  [across(): return lax.ppermute(x, axis, ring(4, 2))]
    ppermute x6, starting transfers between devices: 8.24 us -> 16.6 us  [across(): return lax.ppermute(x, axis, ring(4, 2))]
    all_gather x1, waiting for transfers between devices: 11.2 us -> 16.5 us  [shards(): weight_out = lax.all_gather(out_weight.T, SEQ, axis=0, tiled=True)]
  transfers between devices with their start and end apart: 43 -> 43, of which waited for: 20 -> 18; matrix products, arithmetic and copies ran while one was open for 2% -> 2% of each run, Pallas kernels for 16% -> 26%
where the time goes in v4:
time: 320 us; the launch traced here: 319 us
  waiting for transfers between devices  101 us (32%)
  Pallas kernels  84.6 us (26%)
  starting transfers between devices  71.7 us (22%)
  blocking collectives  25.9 us (8%)
  local copies, waits for them, and re-layouts  22 us (7%)
  between operations  13.4 us (4%)
    pallas_call x14, Pallas kernels, call(): pl.pallas_call(kernel, out_shape=[jax.ShapeDtypeStruct(s, d) for s, d in...  74.3 us
    ppermute x14, waiting for transfers between devices, up_one(): return lax.ppermute(x, axis, ring(4, 1))  46.9 us
    ppermute x14, starting transfers between devices, down_one(): return lax.ppermute(x, axis, ring(4, -1))  35.7 us
    all_to_all x1, blocking collectives, shards(): arrived = lax.all_to_all(states, SEQ, 0, 0, tiled=True)  25.9 us
    ppermute x6, waiting for transfers between devices, across(): return lax.ppermute(x, axis, ring(4, 2))  22.3 us
    ppermute x6, starting transfers between devices, across(): return lax.ppermute(x, axis, ring(4, 2))  16.6 us
    all_gather x1, waiting for transfers between devices, shards(): weight_out = lax.all_gather(out_weight.T, SEQ, axis=0, tiled=True)  16.5 us
    unnamed x55, local copies, waits for them, and re-layouts  15.6 us
  transfers between devices with their start and end apart: 43, of which 18 were waited for; matrix products, arithmetic and copies ran while one was open for 2% of the time, Pallas kernels for 26%

profile of v4, /device:TPU:0, one launch (start us, length us, event | category | flops | bytes accessed | tf_op | source)
XLA Modules:
  0.0 318.6 jit_solution(9114681634851216155)
XLA Ops:
  9.3 7.1 %local_attention.1 = (f32[2,256,1024]{2,1,0:T(8,128)}, bf16[32,80,128]{2,1,0:T(8,128)(2,1)}, f32[2,256,8]{2,1,0:T(8,128)}) custom-call(bf16[2,256,1024]{2,1,0:T(8,128)(2,1)} %q_ref.3, bf16[2,256,1024]{2,1,0:T(8,128)(2,1)} %k_ref.1, bf16[2,256,1024]{2,1,0:T(8,128)(2,1)} %v_ref.1, f32[2,8,256]{2,1,0:T(8,128)} %bitcast.36), custom_call_target="tpu_custom_call" | custom-call | tf_op jit(solution)/shard_map/local_attention/pallas_call | solution.py:83
  16.4 25.9 %all_to_all.10.in_ref = bf16[32,80,128]{2,1,0:T(8,128)(2,1)S(1)} all-to-all(bf16[32,80,128]{2,1,0:T(8,128)(2,1)} %get-tuple-element.50), channel_id=1, replica_groups=mesh['z'=4,'y'=4,'core'=2,'x'=4] {'z','y','core'}, dimensions={0} | all-to-all | bytes 1310720 | tf_op jit(solution)/shard_map/all_to_all | solution.py:618
  43.3 4.6 %all-to-all-start.1 = ((bf16[32,64,128]{2,1,0:T(8,128)(2,1)}), bf16[32,64,128]{2,1,0:T(8,128)(2,1)}, u32[]{:S(2)}, u32[]{:S(2)}) async-start(bf16[32,64,128]{2,1,0:T(8,128)(2,1)} %copy-done.4), calls=%async_computation.1 | async-start | bytes 1048576 | tf_op jit(solution)/shard_map/all_to_all | solution.py:619
  48.1 2.9 collective-permute-start
  60.6 3.8 %all-to-all-done.1 = bf16[32,64,128]{2,1,0:T(8,128)(2,1)} async-done(((bf16[32,64,128]{2,1,0:T(8,128)(2,1)}), bf16[32,64,128]{2,1,0:T(8,128)(2,1)}, u32[]{:S(2)}, u32[]{:S(2)}) %all-to-all-start.1) | async-done | bytes 524320 | tf_op jit(solution)/shard_map/all_to_all | solution.py:619
  64.4 3.1 carried_norm.1
  68.5 16.5 %all-gather.8.cloned.1.call-done.weight_ref = bf16[6144,1024]{1,0:T(8,128)(2,1)} async-done(((bf16[192,1024]{1,0:T(8,128)(2,1)}), bf16[6144,1024]{1,0:T(8,128)(2,1)}) %all-gather.8.cloned.1.call-update) | async-done | bytes 12582928 | tf_op jit(solution)/shard_map/all_gather | solution.py:606
  85.0 10.6 %selected_projection.1 = (bf16[48,6144]{1,0:T(8,128)(2,1)}, bf16[48,6144]{1,0:T(8,128)(2,1)}, bf16[48,6144]{1,0:T(8,128)(2,1)}, bf16[48,6144]{1,0:T(8,128)(2,1)}) custom-call(bf16[192,512]{1,0:T(8,128)(2,1)} %copy-done.17, bf16[192,128]{1,0:T(8,128)(2,1)} %copy-done.19, bf16[512,1024]{1,0:T(8,128)(2,1)} %bitcast.18, ...), custom_call_target="tpu_custom_call" | custom-call | tf_op jit(solution)/shard_map/selected_projection/pallas_call | solution.py:156
  100.7 13.2 %whole_projection.1.held = bf16[512,6144]{1,0:T(8,128)(2,1)} custom-call(bf16[512,1024]{1,0:T(8,128)(2,1)} %bitcast.19, bf16[6144,1024]{1,0:T(8,128)(2,1)} %all-gather.8.cloned.1.call-done.weight_ref, bf16[48,6144]{1,0:T(8,128)(2,1)} %get-tuple-element.53.late.a), custom_call_target="tpu_custom_call" | custom-call | flops 6442450944 | bytes 25165824 | tf_op jit(solution)/shard_map/whole_projection/pallas_call | solution.py:156
  113.9 12.2 %collective-permute-done.5.d = bf16[48,6144]{1,0:T(8,128)(2,1)S(1)} collective-permute-done((bf16[48,6144]{1,0:T(8,128)(2,1)}, bf16[48,6144]{1,0:T(8,128)(2,1)S(1)}, u32[]{:S(2)}, u32[]{:S(2)}) %collective-permute-start.5) | collective-permute-done | bytes 589856 | tf_op jit(solution)/shard_map/ppermute | solution.py:576
  133.2 3.1 collective-permute-start.10
  138.4 8.3 %collective-permute-start.11 = (bf16[48,3072]{1,0:T(8,128)(2,1)S(1)}, bf16[48,3072]{1,0:T(8,128)(2,1)S(1)}, u32[]{:S(2)}, u32[]{:S(2)}) collective-permute-start(bf16[48,3072]{1,0:T(8,128)(2,1)S(1)} %get-tuple-element.59.b0), channel_id=1, source_target_pairs={{0,64},{32,96},{64,0},{96,32},{1,65},{33,97},{65,1},{97,33},{2,66}... | collective-permute-start | bytes 884744 | tf_op jit(solution)/shard_map/ppermute | solution.py:576
  146.7 7.4 %collective-permute-done.11.b3 = bf16[48,3072]{1,0:T(8,128)(2,1)S(1)} collective-permute-done((bf16[48,3072]{1,0:T(8,128)(2,1)S(1)}, bf16[48,3072]{1,0:T(8,128)(2,1)S(1)}, u32[]{:S(2)}, u32[]{:S(2)}) %collective-permute-start.11) | collective-permute-done | bytes 294944 | tf_op jit(solution)/shard_map/ppermute | solution.py:576
  154.3 2.6 collective-permute-start.12
  158.3 3.2 %collective-permute-start.15 = (bf16[4,48,3072]{2,1,0:T(8,128)(2,1)S(1)}, bf16[4,48,3072]{2,1,0:T(8,128)(2,1)S(1)}, u32[]{:S(2)}, u32[]{:S(2)}) collective-permute-start(bf16[4,48,3072]{2,1,0:T(8,128)(2,1)S(1)} %get-tuple-element.61.refs_3_), channel_id=1, source_target_pairs={{0,24},{8,0},{16,8},{24,16},{1,25},{9,1},{17,9},{25,17},{2,26},{10... | collective-permute-start | bytes 3538952 | tf_op jit(solution)/shard_map/ppermute | solution.py:572
  162.5 17.4 %collective-permute-done.12.refs_1_ = bf16[4,48,3072]{2,1,0:T(8,128)(2,1)S(1)} collective-permute-done((bf16[4,48,3072]{2,1,0:T(8,128)(2,1)S(1)}, bf16[4,48,3072]{2,1,0:T(8,128)(2,1)S(1)}, u32[]{:S(2)}, u32[]{:S(2)}) %collective-permute-start.12) | collective-permute-done | bytes 1179680 | tf_op jit(solution)/shard_map/ppermute | solution.py:568
  188.5 2.9 collective-permute-start.19
  199.2 14.9 %near_rows.1.refs_0_ = f32[768,1152]{1,0:T(8,128)} custom-call(bf16[4,48,3072]{2,1,0:T(8,128)(2,1)S(1)} %copy-done.23, bf16[4,48,3072]{2,1,0:T(8,128)(2,1)S(1)} %copy-done.9, bf16[4,48,3072]{2,1,0:T(8,128)(2,1)S(1)} %copy-done.11, bf16[4,48,3072]{2,1,0:T(8,128)(2,1)S(1)} %copy-done.25, bf16[4,48,3072]{2,1,0:T(8,128)(2,1)S(1)} %copy-done.13, ...), custom_call_target="tpu_custom_call" | custom-call | flops 8153726976 | bytes 1048576 | tf_op jit(solution)/shard_map/near_rows/pallas_call | solution.py:156
  214.2 17.6 %far_rows.1 = (bf16[768,576]{1,0:T(8,128)(2,1)S(1)}, bf16[2,48,3072]{2,1,0:T(8,128)(2,1)S(1)}, bf16[2,48,3072]{2,1,0:T(8,128)(2,1)S(1)}, bf16[2,48,3072]{2,1,0:T(8,128)(2,1)S(1)}, bf16[2,48,3072]{2,1,0:T(8,128)(2,1)S(1)}) custom-call(f32[768,1152]{1,0:T(8,128)} %near_rows.1.refs_0_, bf16[2,48,3072]{2,1,0:T(8,128)(2,1)S(1)} %collective-permute-done.16.refs_1_, ...), custom_call_target="tpu_custom_call" | custom-call | tf_op jit(solution)/shard_map/far_rows/pallas_call | solution.py:156
  232.5 2.6 collective-permute-start.21
  235.1 3.2 %collective-permute-start.23 = (bf16[2,48,3072]{2,1,0:T(8,128)(2,1)S(1)}, bf16[2,48,3072]{2,1,0:T(8,128)(2,1)S(1)}, u32[]{:S(2)}, u32[]{:S(2)}) collective-permute-start(bf16[2,48,3072]{2,1,0:T(8,128)(2,1)S(1)} %get-tuple-element.70), channel_id=1, source_target_pairs={{0,24},{8,0},{16,8},{24,16},{1,25},{9,1},{17,9},{25,17},{2,26},{10... | collective-permute-start | bytes 1769480 | tf_op jit(solution)/shard_map/ppermute | solution.py:572
  238.3 8.7 %rest_rows.1 = (bf16[4,48,3072]{2,1,0:T(8,128)(2,1)S(1)}, bf16[4,48,3072]{2,1,0:T(8,128)(2,1)S(1)}, bf16[4,48,3072]{2,1,0:T(8,128)(2,1)S(1)}, bf16[4,48,3072]{2,...) custom-call(bf16[768,576]{1,0:T(8,128)(2,1)S(1)} %get-tuple-element.62.refs_0_, ...), custom_call_target="tpu_custom_call" | custom-call | flops 4076863488 | bytes 1048576 | tf_op jit(solution)/shard_map/rest_rows/pallas_call | solution.py:156
  247.0 3.1 collective-permute-done.22.up1
  250.9 3.2 %collective-permute-start.25 = (bf16[4,48,3072]{2,1,0:T(8,128)(2,1)S(1)}, bf16[4,48,3072]{2,1,0:T(8,128)(2,1)S(1)}, u32[]{:S(2)}, u32[]{:S(2)}) collective-permute-start(bf16[4,48,3072]{2,1,0:T(8,128)(2,1)S(1)} %get-tuple-element.71.late), channel_id=1, source_target_pairs={{0,96},{32,0},{64,32},{96,64},{1,97},{33,1},{65,33},{97,65},{2,98}... | collective-permute-start | bytes 3538952 | tf_op jit(solution)/shard_map/ppermute | solution.py:572
  254.1 3.5 %collective-permute-start.27 = (bf16[4,48,3072]{2,1,0:T(8,128)(2,1)S(1)}, bf16[4,48,3072]{2,1,0:T(8,128)(2,1)S(1)}, u32[]{:S(2)}, u32[]{:S(2)}) collective-permute-start(bf16[4,48,3072]{2,1,0:T(8,128)(2,1)S(1)} %get-tuple-element.78), channel_id=1, source_target_pairs={{0,24},{8,0},{16,8},{24,16},{1,25},{9,1},{17,9},{25,17},{2,26},{10... | collective-permute-start | bytes 3538952 | tf_op jit(solution)/shard_map/ppermute | solution.py:572
  257.6 11.0 %collective-permute-done.24.u0 = bf16[4,48,3072]{2,1,0:T(8,128)(2,1)S(1)} collective-permute-done((bf16[4,48,3072]{2,1,0:T(8,128)(2,1)S(1)}, bf16[4,48,3072]{2,1,0:T(8,128)(2,1)S(1)}, u32[]{:S(2)}, u32[]{:S(2)}) %collective-permute-start.24) | collective-permute-done | bytes 1179680 | tf_op jit(solution)/shard_map/ppermute | solution.py:568
  270.2 7.9 %collective-permute-done.26.u1 = bf16[4,48,3072]{2,1,0:T(8,128)(2,1)S(1)} collective-permute-done((bf16[4,48,3072]{2,1,0:T(8,128)(2,1)S(1)}, bf16[4,48,3072]{2,1,0:T(8,128)(2,1)S(1)}, u32[]{:S(2)}, u32[]{:S(2)}) %collective-permute-start.26) | collective-permute-done | bytes 1179680 | tf_op jit(solution)/shard_map/ppermute | solution.py:568
  284.5 3.2 %collective-permute-start.32 = (bf16[48,3072]{1,0:T(8,128)(2,1)S(1)}, bf16[48,3072]{1,0:T(8,128)(2,1)S(1)}, u32[]{:S(2)}, u32[]{:S(2)}) collective-permute-start(bf16[48,3072]{1,0:T(8,128)(2,1)S(1)} %get-tuple-element.85), channel_id=1, source_target_pairs={{0,96},{32,0},{64,32},{96,64},{1,97},{33,1},{65,33},{97,65},{2,98}... | collective-permute-start | bytes 884744 | tf_op jit(solution)/shard_map/ppermute | solution.py:572
  292.4 2.7 collective-permute-done.32.b2
  297.3 2.6 collective-permute-start.34
  304.7 4.5 %collective-permute-done.35.b2 = bf16[16,6144]{1,0:T(8,128)(2,1)} collective-permute-done((bf16[16,6144]{1,0:T(8,128)(2,1)}, bf16[16,6144]{1,0:T(8,128)(2,1)}, u32[]{:S(2)}, u32[]{:S(2)}) %collective-permute-start.35) | collective-permute-done | bytes 196640 | tf_op jit(solution)/shard_map/ppermute | solution.py:568
  309.2 2.8 combine.1
  (140 shorter events, 68.3 us)
Async XLA Ops:
  6.5 78.4 %all-gather.8.cloned.1.call-start = ((), (), s32[]{:S(2)}) async-start(), calls=%async_computation.3 | async-start | bytes 12976128 | tf_op jit(solution)/shard_map/all_gather | solution.py:606
  7.3 184.2 %all-gather.10.cloned.1.call-start = ((), (), s32[]{:S(2)}) async-start(), calls=%async_computation.5 | async-start | bytes 10616832 | tf_op jit(solution)/shard_map/all_gather | solution.py:608
  8.0 183.5 %all-gather.12.cloned.1.call-start = ((), (), s32[]{:S(2)}) async-start(), calls=%async_computation.6 | async-start | bytes 10616832 | tf_op jit(solution)/shard_map/all_gather | solution.py:608
  8.7 205.4 %all-gather.14.cloned.1.call-start = ((), (), s32[]{:S(2)}) async-start(), calls=%async_computation.7 | async-start | bytes 10616832 | tf_op jit(solution)/shard_map/all_gather | solution.py:608
  43.3 21.1 %all-to-all-start.1 = ((bf16[32,64,128]{2,1,0:T(8,128)(2,1)}), bf16[32,64,128]{2,1,0:T(8,128)(2,1)}, u32[]{:S(2)}, u32[]{:S(2)}) async-start(bf16[32,64,128]{2,1,0:T(8,128)(2,1)} %copy-done.4), calls=%async_computation.1 | async-start | bytes 1048576 | tf_op jit(solution)/shard_map/all_to_all | solution.py:619
  47.9 253.4 %reduce-scatter.2.cloned.1.call-start = ((), (), s32[]{:S(2)}) async-start(), calls=%async_computation.4 | async-start | bytes 7864320 | tf_op jit(solution)/shard_map/reduce_scatter | solution.py:657
  95.6 18.4 %collective-permute-start.3 = (bf16[48,6144]{1,0:T(8,128)(2,1)}, bf16[48,6144]{1,0:T(8,128)(2,1)S(1)}, u32[]{:S(2)}, u32[]{:S(2)}) collective-permute-start(bf16[48,6144]{1,0:T(8,128)(2,1)} %get-tuple-element.54), channel_id=1, source_target_pairs={{0,1},{1,2},{2,3},{3,0},{4,5},{5,6},{6,7},{7,4},{8,9},{9,10},{10,1... | collective-permute-start | bytes 1769480 | tf_op jit(solution)/shard_map/ppermute | solution.py:568
  97.1 16.8 %collective-permute-start.4 = (bf16[48,6144]{1,0:T(8,128)(2,1)}, bf16[48,6144]{1,0:T(8,128)(2,1)S(1)}, u32[]{:S(2)}, u32[]{:S(2)}) collective-permute-start(bf16[48,6144]{1,0:T(8,128)(2,1)} %get-tuple-element.55), channel_id=1, source_target_pairs={{0,3},{1,0},{2,1},{3,2},{4,7},{5,4},{6,5},{7,6},{8,11},{9,8},{10,9... | collective-permute-start | bytes 1769480 | tf_op jit(solution)/shard_map/ppermute | solution.py:572
  98.9 27.3 %collective-permute-start.5 = (bf16[48,6144]{1,0:T(8,128)(2,1)}, bf16[48,6144]{1,0:T(8,128)(2,1)S(1)}, u32[]{:S(2)}, u32[]{:S(2)}) collective-permute-start(bf16[48,6144]{1,0:T(8,128)(2,1)} %get-tuple-element.56), channel_id=1, source_target_pairs={{0,2},{1,3},{2,0},{3,1},{4,6},{5,7},{6,4},{7,5},{8,10},{9,11},{10,... | collective-permute-start | bytes 1769480 | tf_op jit(solution)/shard_map/ppermute | solution.py:576
  128.1 10.3 %collective-permute-start.6 = (bf16[48,3072]{1,0:T(8,128)(2,1)S(1)}, bf16[48,3072]{1,0:T(8,128)(2,1)S(1)}, u32[]{:S(2)}, u32[]{:S(2)}) collective-permute-start(bf16[48,3072]{1,0:T(8,128)(2,1)S(1)} %get-tuple-element.58.a0), channel_id=1, source_target_pairs={{0,8},{8,16},{16,24},{24,0},{1,9},{9,17},{17,25},{25,1},{2,10},{10... | collective-permute-start | bytes 884744 | tf_op jit(solution)/shard_map/ppermute | solution.py:568
  129.6 17.0 %collective-permute-start.7 = (bf16[48,3072]{1,0:T(8,128)(2,1)S(1)}, bf16[48,3072]{1,0:T(8,128)(2,1)S(1)}, u32[]{:S(2)}, u32[]{:S(2)}) collective-permute-start(bf16[48,3072]{1,0:T(8,128)(2,1)S(1)} %get-tuple-element.58.a0), channel_id=1, source_target_pairs={{0,24},{8,0},{16,8},{24,16},{1,25},{9,1},{17,9},{25,17},{2,26},{10... | collective-permute-start | bytes 884744 | tf_op jit(solution)/shard_map/ppermute | solution.py:572
  131.4 15.3 %collective-permute-start.8 = (bf16[48,3072]{1,0:T(8,128)(2,1)S(1)}, bf16[48,3072]{1,0:T(8,128)(2,1)S(1)}, u32[]{:S(2)}, u32[]{:S(2)}) collective-permute-start(bf16[48,3072]{1,0:T(8,128)(2,1)S(1)} %get-tuple-element.58.a0), channel_id=1, source_target_pairs={{0,16},{8,24},{16,0},{24,8},{1,17},{9,25},{17,1},{25,9},{2,18},{10... | collective-permute-start | bytes 884744 | tf_op jit(solution)/shard_map/ppermute | solution.py:576
  133.1 13.6 %collective-permute-start.9 = (bf16[48,3072]{1,0:T(8,128)(2,1)S(1)}, bf16[48,3072]{1,0:T(8,128)(2,1)S(1)}, u32[]{:S(2)}, u32[]{:S(2)}) collective-permute-start(bf16[48,3072]{1,0:T(8,128)(2,1)S(1)} %get-tuple-element.59.b0), channel_id=1, source_target_pairs={{0,32},{32,64},{64,96},{96,0},{1,33},{33,65},{65,97},{97,1},{2,34}... | collective-permute-start | bytes 884744 | tf_op jit(solution)/shard_map/ppermute | solution.py:568
  133.2 13.5 %collective-permute-start.10 = (bf16[48,3072]{1,0:T(8,128)(2,1)S(1)}, bf16[48,3072]{1,0:T(8,128)(2,1)S(1)}, u32[]{:S(2)}, u32[]{:S(2)}) collective-permute-start(bf16[48,3072]{1,0:T(8,128)(2,1)S(1)} %get-tuple-element.59.b0), channel_id=1, source_target_pairs={{0,96},{32,0},{64,32},{96,64},{1,97},{33,1},{65,33},{97,65},{2,98}... | collective-permute-start | bytes 884744 | tf_op jit(solution)/shard_map/ppermute | solution.py:572
  138.4 15.8 %collective-permute-start.11 = (bf16[48,3072]{1,0:T(8,128)(2,1)S(1)}, bf16[48,3072]{1,0:T(8,128)(2,1)S(1)}, u32[]{:S(2)}, u32[]{:S(2)}) collective-permute-start(bf16[48,3072]{1,0:T(8,128)(2,1)S(1)} %get-tuple-element.59.b0), channel_id=1, source_target_pairs={{0,64},{32,96},{64,0},{96,32},{1,65},{33,97},{65,1},{97,33},{2,66}... | collective-permute-start | bytes 884744 | tf_op jit(solution)/shard_map/ppermute | solution.py:576
  154.3 25.6 %collective-permute-start.12 = (bf16[4,48,3072]{2,1,0:T(8,128)(2,1)S(1)}, bf16[4,48,3072]{2,1,0:T(8,128)(2,1)S(1)}, u32[]{:S(2)}, u32[]{:S(2)}) collective-permute-start(bf16[4,48,3072]{2,1,0:T(8,128)(2,1)S(1)} %get-tuple-element.60.refs_0_), channel_id=1, source_target_pairs={{0,32},{32,64},{64,96},{96,0},{1,33},{33,65},{65,97},{97,1},{2,34}... | collective-permute-start | bytes 3538952 | tf_op jit(solution)/shard_map/ppermute | solution.py:568
  156.9 25.8 %collective-permute-start.13 = (bf16[4,48,3072]{2,1,0:T(8,128)(2,1)S(1)}, bf16[4,48,3072]{2,1,0:T(8,128)(2,1)S(1)}, u32[]{:S(2)}, u32[]{:S(2)}) collective-permute-start(bf16[4,48,3072]{2,1,0:T(8,128)(2,1)S(1)} %get-tuple-element.60.refs_0_), channel_id=1, source_target_pairs={{0,96},{32,0},{64,32},{96,64},{1,97},{33,1},{65,33},{97,65},{2,98}... | collective-permute-start | bytes 3538952 | tf_op jit(solution)/shard_map/ppermute | solution.py:572
  158.2 27.7 %collective-permute-start.14 = (bf16[4,48,3072]{2,1,0:T(8,128)(2,1)S(1)}, bf16[4,48,3072]{2,1,0:T(8,128)(2,1)S(1)}, u32[]{:S(2)}, u32[]{:S(2)}) collective-permute-start(bf16[4,48,3072]{2,1,0:T(8,128)(2,1)S(1)} %get-tuple-element.61.refs_3_), channel_id=1, source_target_pairs={{0,8},{8,16},{16,24},{24,0},{1,9},{9,17},{17,25},{25,1},{2,10},{10... | collective-permute-start | bytes 3538952 | tf_op jit(solution)/shard_map/ppermute | solution.py:568
  158.3 28.7 %collective-permute-start.15 = (bf16[4,48,3072]{2,1,0:T(8,128)(2,1)S(1)}, bf16[4,48,3072]{2,1,0:T(8,128)(2,1)S(1)}, u32[]{:S(2)}, u32[]{:S(2)}) collective-permute-start(bf16[4,48,3072]{2,1,0:T(8,128)(2,1)S(1)} %get-tuple-element.61.refs_3_), channel_id=1, source_target_pairs={{0,24},{8,0},{16,8},{24,16},{1,25},{9,1},{17,9},{25,17},{2,26},{10... | collective-permute-start | bytes 3538952 | tf_op jit(solution)/shard_map/ppermute | solution.py:572
  180.9 33.3 %collective-permute-start.16 = (bf16[2,48,3072]{2,1,0:T(8,128)(2,1)}, bf16[2,48,3072]{2,1,0:T(8,128)(2,1)S(1)}, u32[]{:S(2)}, u32[]{:S(2)}) collective-permute-start(bf16[2,48,3072]{2,1,0:T(8,128)(2,1)} %slice.16), channel_id=1, source_target_pairs={{0,32},{32,64},{64,96},{96,0},{1,33},{33,65},{65,97},{97,1},{2,34}... | collective-permute-start | bytes 1769480 | tf_op jit(solution)/shard_map/ppermute | solution.py:568
  184.7 29.5 %collective-permute-start.17 = (bf16[2,48,3072]{2,1,0:T(8,128)(2,1)}, bf16[2,48,3072]{2,1,0:T(8,128)(2,1)S(1)}, u32[]{:S(2)}, u32[]{:S(2)}) collective-permute-start(bf16[2,48,3072]{2,1,0:T(8,128)(2,1)} %slice.17), channel_id=1, source_target_pairs={{0,96},{32,0},{64,32},{96,64},{1,97},{33,1},{65,33},{97,65},{2,98}... | collective-permute-start | bytes 1769480 | tf_op jit(solution)/shard_map/ppermute | solution.py:572
  186.9 27.2 %collective-permute-start.18 = (bf16[2,48,3072]{2,1,0:T(8,128)(2,1)}, bf16[2,48,3072]{2,1,0:T(8,128)(2,1)S(1)}, u32[]{:S(2)}, u32[]{:S(2)}) collective-permute-start(bf16[2,48,3072]{2,1,0:T(8,128)(2,1)} %slice.18), channel_id=1, source_target_pairs={{0,8},{8,16},{16,24},{24,0},{1,9},{9,17},{17,25},{25,1},{2,10},{10... | collective-permute-start | bytes 1769480 | tf_op jit(solution)/shard_map/ppermute | solution.py:568
  188.5 25.6 %collective-permute-start.19 = (bf16[2,48,3072]{2,1,0:T(8,128)(2,1)}, bf16[2,48,3072]{2,1,0:T(8,128)(2,1)S(1)}, u32[]{:S(2)}, u32[]{:S(2)}) collective-permute-start(bf16[2,48,3072]{2,1,0:T(8,128)(2,1)} %slice.19), channel_id=1, source_target_pairs={{0,24},{8,0},{16,8},{24,16},{1,25},{9,1},{17,9},{25,17},{2,26},{10... | collective-permute-start | bytes 1769480 | tf_op jit(solution)/shard_map/ppermute | solution.py:572
  231.8 15.2 %collective-permute-start.20 = (bf16[2,48,3072]{2,1,0:T(8,128)(2,1)S(1)}, bf16[2,48,3072]{2,1,0:T(8,128)(2,1)S(1)}, u32[]{:S(2)}, u32[]{:S(2)}) collective-permute-start(bf16[2,48,3072]{2,1,0:T(8,128)(2,1)S(1)} %get-tuple-element.65), channel_id=1, source_target_pairs={{0,32},{32,64},{64,96},{96,0},{1,33},{33,65},{65,97},{97,1},{2,34}... | collective-permute-start | bytes 1769480 | tf_op jit(solution)/shard_map/ppermute | solution.py:568
  232.5 14.5 %collective-permute-start.21 = (bf16[2,48,3072]{2,1,0:T(8,128)(2,1)S(1)}, bf16[2,48,3072]{2,1,0:T(8,128)(2,1)S(1)}, u32[]{:S(2)}, u32[]{:S(2)}) collective-permute-start(bf16[2,48,3072]{2,1,0:T(8,128)(2,1)S(1)} %get-tuple-element.66), channel_id=1, source_target_pairs={{0,96},{32,0},{64,32},{96,64},{1,97},{33,1},{65,33},{97,65},{2,98}... | collective-permute-start | bytes 1769480 | tf_op jit(solution)/shard_map/ppermute | solution.py:572
  235.1 15.1 %collective-permute-start.22 = (bf16[2,48,3072]{2,1,0:T(8,128)(2,1)S(1)}, bf16[2,48,3072]{2,1,0:T(8,128)(2,1)S(1)}, u32[]{:S(2)}, u32[]{:S(2)}) collective-permute-start(bf16[2,48,3072]{2,1,0:T(8,128)(2,1)S(1)} %get-tuple-element.69), channel_id=1, source_target_pairs={{0,8},{8,16},{16,24},{24,0},{1,9},{9,17},{17,25},{25,1},{2,10},{10... | collective-permute-start | bytes 1769480 | tf_op jit(solution)/shard_map/ppermute | solution.py:568
  235.1 15.1 %collective-permute-start.23 = (bf16[2,48,3072]{2,1,0:T(8,128)(2,1)S(1)}, bf16[2,48,3072]{2,1,0:T(8,128)(2,1)S(1)}, u32[]{:S(2)}, u32[]{:S(2)}) collective-permute-start(bf16[2,48,3072]{2,1,0:T(8,128)(2,1)S(1)} %get-tuple-element.70), channel_id=1, source_target_pairs={{0,24},{8,0},{16,8},{24,16},{1,25},{9,1},{17,9},{25,17},{2,26},{10... | collective-permute-start | bytes 1769480 | tf_op jit(solution)/shard_map/ppermute | solution.py:572
  250.8 17.9 %collective-permute-start.24 = (bf16[4,48,3072]{2,1,0:T(8,128)(2,1)S(1)}, bf16[4,48,3072]{2,1,0:T(8,128)(2,1)S(1)}, u32[]{:S(2)}, u32[]{:S(2)}) collective-permute-start(bf16[4,48,3072]{2,1,0:T(8,128)(2,1)S(1)} %get-tuple-element.75), channel_id=1, source_target_pairs={{0,32},{32,64},{64,96},{96,0},{1,33},{33,65},{65,97},{97,1},{2,34}... | collective-permute-start | bytes 3538952 | tf_op jit(solution)/shard_map/ppermute | solution.py:568
  250.9 19.3 %collective-permute-start.25 = (bf16[4,48,3072]{2,1,0:T(8,128)(2,1)S(1)}, bf16[4,48,3072]{2,1,0:T(8,128)(2,1)S(1)}, u32[]{:S(2)}, u32[]{:S(2)}) collective-permute-start(bf16[4,48,3072]{2,1,0:T(8,128)(2,1)S(1)} %get-tuple-element.71.late), channel_id=1, source_target_pairs={{0,96},{32,0},{64,32},{96,64},{1,97},{33,1},{65,33},{97,65},{2,98}... | collective-permute-start | bytes 3538952 | tf_op jit(solution)/shard_map/ppermute | solution.py:572
  254.1 24.0 %collective-permute-start.26 = (bf16[4,48,3072]{2,1,0:T(8,128)(2,1)S(1)}, bf16[4,48,3072]{2,1,0:T(8,128)(2,1)S(1)}, u32[]{:S(2)}, u32[]{:S(2)}) collective-permute-start(bf16[4,48,3072]{2,1,0:T(8,128)(2,1)S(1)} %get-tuple-element.77), channel_id=1, source_target_pairs={{0,8},{8,16},{16,24},{24,0},{1,9},{9,17},{17,25},{25,1},{2,10},{10... | collective-permute-start | bytes 3538952 | tf_op jit(solution)/shard_map/ppermute | solution.py:568
  254.1 24.0 %collective-permute-start.27 = (bf16[4,48,3072]{2,1,0:T(8,128)(2,1)S(1)}, bf16[4,48,3072]{2,1,0:T(8,128)(2,1)S(1)}, u32[]{:S(2)}, u32[]{:S(2)}) collective-permute-start(bf16[4,48,3072]{2,1,0:T(8,128)(2,1)S(1)} %get-tuple-element.78), channel_id=1, source_target_pairs={{0,24},{8,0},{16,8},{24,16},{1,25},{9,1},{17,9},{25,17},{2,26},{10... | collective-permute-start | bytes 3538952 | tf_op jit(solution)/shard_map/ppermute | solution.py:572
  284.5 10.6 %collective-permute-start.32 = (bf16[48,3072]{1,0:T(8,128)(2,1)S(1)}, bf16[48,3072]{1,0:T(8,128)(2,1)S(1)}, u32[]{:S(2)}, u32[]{:S(2)}) collective-permute-start(bf16[48,3072]{1,0:T(8,128)(2,1)S(1)} %get-tuple-element.85), channel_id=1, source_target_pairs={{0,96},{32,0},{64,32},{96,64},{1,97},{33,1},{65,33},{97,65},{2,98}... | collective-permute-start | bytes 884744 | tf_op jit(solution)/shard_map/ppermute | solution.py:572
  (38 other events, 320.0 us)
Sparse Core Ops, SparseCore 0:
  9.6 75.3 all-gather.7
  86.6 20.0 all-gather.9
  108.3 21.9 all-gather.11
  131.8 21.9 all-gather.13
  156.1 65.2 reduce-scatter.1

commit v5 on v4

--- a/solution.py
+++ b/solution.py
@@ -12,6 +12,7 @@
 F32 = jnp.float32
 HI = lax.Precision.HIGHEST
 SEQ = ("z", "y", "core")
+TILE = 1024
 DEC = 16
 OFFS = (1, 3, 2, 0)
 JREL = {0: 0, 3: 1, 1: 2, 2: 3}
@@ -203,43 +204,50 @@
     return lax.dot_general(a, b, (((1,), (1,)), ((), ())), preferred_element_type=F32)
 
 
-def selected_kernel(place_ref, own_ref, normed_ref, weight_ref, res_ref, o0, o1, o2, o3, picked):
-
-    @pl.when(pl.program_id(0) == 0)
-    def _():
-        picked[...] = mm(place_ref[...], normed_ref[...]).astype(BF)
-
-    full = nt(weight_ref[...], picked[...]).T + mm(own_ref[...], res_ref[...])
-    full = full.astype(BF)
+def selected_kernel(place, own, normed, weight, res, o0, o1, o2, o3, w_here, r_here, sems):
     size = o0.shape[0]
-    for i, o in enumerate((o0, o1, o2, o3)):
-        o[...] = full[i * size : (i + 1) * size]
-
-
-def selected(place, own, normed, weight, res, tile=1024):
-    picks, (model, width) = place.shape[0], weight.shape
-    rows = res.shape[0]
-    size = picks // 4
-    whole = lambda a: pl.BlockSpec(a.shape, lambda n: (0, 0))
+    chunks = weight.shape[0] // TILE
+
+    def copy(c):
+        span = pl.ds(pl.multiple_of(c * TILE, TILE), TILE)
+        return pltpu.make_async_copy(weight.at[span], w_here.at[span], sems.at[c])
+
+    @pl.loop(0, chunks)
+    def _(c):
+        copy(c).start()
+
+    rest = pltpu.make_async_copy(res, r_here, sems.at[chunks])
+    rest.start()
+    picked = mm(place[...], normed[...]).astype(BF)
+    rest.wait()
+
+    @pl.loop(0, chunks)
+    def _(c):
+        span = pl.ds(pl.multiple_of(c * TILE, TILE), TILE)
+        copy(c).wait()
+        full = (nt(picked, w_here[span, :]) + mm(own[...], r_here[:, span])).astype(BF)
+        for i, o in enumerate((o0, o1, o2, o3)):
+            o[:, span] = full[i * size : (i + 1) * size]
+
+
+def selected(place, own, normed, weight, res):
+    picks, model = place.shape[0], weight.shape[0]
     return call(
         selected_kernel,
         "selected_projection",
-        [((size, model), BF)] * 4,
+        [((picks // 4, model), BF)] * 4,
         place,
         own,
         normed,
         weight,
         res,
-        grid=(model // tile,),
-        in_specs=[
-            whole(place),
-            whole(own),
-            whole(normed),
-            pl.BlockSpec((tile, width), lambda n: (n, 0)),
-            pl.BlockSpec((rows, tile), lambda n: (0, n)),
+        in_specs=[VM] * 3 + [ANY] * 2,
+        out_specs=[VM] * 4,
+        scratch_shapes=[
+            pltpu.VMEM(weight.shape, BF),
+            pltpu.VMEM(res.shape, BF),
+            pltpu.SemaphoreType.DMA((model // TILE + 1,)),
         ],
-        out_specs=[pl.BlockSpec((size, tile), lambda n: (0, n))] * 4,
-        scratch_shapes=[pltpu.VMEM((picks, width), BF)],
         vmem=54,
     )
 
@@ -294,106 +302,93 @@
     return [((z * 4 + y) * rows, z) for z in range(4)]
 
 
-def fetch(parts, buf, sems, chunk, slot):
-    units, tile = parts[0].shape[0], buf.shape[2]
-    cols = pl.ds(pl.multiple_of(chunk * tile, tile), tile)
-    return [
-        pltpu.make_async_copy(
-            part.at[:, cols], buf.at[slot, pl.ds(i * units, units)], sems.at[slot, i]
-        )
-        for i, part in enumerate(parts)
-    ]
-
-
-def streamed(parts, buf, sems, chunks, body):
-    @pl.loop(0, chunks)
+def gate_up(refs_a, refs_b, gu, x, part, arrive):
+    rows, half = refs_a[0].shape[1:]
+    each = half // TILE
+    part[...] = jnp.zeros_like(part)
+
+    @pl.loop(0, 2 * each)
     def _(c):
-        slot = lax.rem(c, 2)
-
-        @pl.when(c + 1 < chunks)
-        def _():
-            for copy in fetch(parts, buf, sems, c + 1, 1 - slot):
-                copy.start()
-
-        for copy in fetch(parts, buf, sems, c, slot):
-            copy.wait()
-        body(c, buf[slot])
-
-
-def first_chunk(parts, buf, sems):
-    for copy in fetch(parts, buf, sems, 0, 0):
-        copy.start()
-
-
-def gate_up(refs_a, refs_b, parts, x, part, buf, sems):
-    tile = buf.shape[2]
-    rows, half = refs_a[0].shape[1:]
-    each = half // tile
-    part[...] = jnp.zeros_like(part)
-
-    def body(c, weights):
         for k, refs in enumerate((refs_a, refs_b)):
 
             @pl.when(c // each == k)
             def _():
-                at = pl.ds(pl.multiple_of((c - k * each) * tile, tile), tile)
+                at = pl.ds(pl.multiple_of((c - k * each) * TILE, TILE), TILE)
                 row = 0
                 for ref in refs:
                     for i in range(ref.shape[0]):
                         x[row : row + rows, :] = ref[i, :, at]
                         row += rows
 
-        part[c // each] += nt(x[...], weights)
-
-    streamed(parts, buf, sems, 2 * each, body)
-
-
-def down_product(value, parts, buf, sems, outs_a, outs_b):
-    tile = buf.shape[2]
+        arrive(c)
+        wide = pl.ds(pl.multiple_of(c * TILE, TILE), TILE)
+        units = gu[0].shape[0]
+        for i, w in enumerate(gu):
+            part[c // each, :, i * units : (i + 1) * units] += nt(x[...], w[:, wide])
+
+
+def down_product(value, down, outs_a, outs_b):
     rows, half = outs_a[0].shape[1:]
-    each = half // tile
-
-    def body(c, weights):
-        full = mm(value[c // each], weights).astype(BF)
+    each = half // TILE
+
+    @pl.loop(0, 2 * each)
+    def _(c):
+        wide = pl.ds(pl.multiple_of(c * TILE, TILE), TILE)
+        full = mm(value[c // each], down[:, wide]).astype(BF)
         for k, outs in enumerate((outs_a, outs_b)):
 
             @pl.when(c // each == k)
             def _():
-                at = pl.ds(pl.multiple_of((c - k * each) * tile, tile), tile)
+                at = pl.ds(pl.multiple_of((c - k * each) * TILE, TILE), TILE)
                 row = 0
                 for out in outs:
                     for i in range(out.shape[0]):
                         out[i, :, at] = full[row : row + rows]
                         row += rows
 
-    streamed(parts, buf, sems, 2 * each, body)
-
-
-def near_kernel(*refs):
-    a, b, parts = refs[0:3], refs[3:6], refs[6:8]
-    acc, x, part, buf, sems = refs[8:]
-    rows = a[0].shape[1]
+
+def near_kernel(
+    a0, a1, a2, b0, b1, b2, gate, up, down, acc, gate_here, up_here, down_here, x, part, sems, last
+):
+    rows = a0.shape[1]
     block = 4 * rows
-    first_chunk(parts, buf, sems)
-    gate_up(a, b, parts, x, part, buf, sems)
+    chunks = gate.shape[1] // TILE
+
+    def copies(c):
+        cols = pl.ds(pl.multiple_of(c * TILE, TILE), TILE)
+        pairs = ((gate, gate_here), (up, up_here))
+        return [
+            pltpu.make_async_copy(a.at[:, cols], b.at[:, cols], sems.at[c, i])
+            for i, (a, b) in enumerate(pairs)
+        ]
+
+    @pl.loop(0, chunks)
+    def _(c):
+        for copy in copies(c):
+            copy.start()
+
+    whole = pltpu.make_async_copy(down, down_here, last)
+    whole.start()
+
+    def arrive(c):
+        for copy in copies(c):
+            copy.wait()
+
+    gate_up((a0, a1, a2), (b0, b1, b2), (gate_here, up_here), x, part, arrive)
     acc[0 : 3 * block, :] = part[0]
     acc[3 * block :, :] = jnp.zeros((block, acc.shape[1]), F32)
     for y in range(3):
         for row, z in by_y(rows, y):
             at = y * block + z * rows
             acc[row : row + rows, :] += part[1, at : at + rows, :]
-
-
-def far_kernel(*refs):
-    acc, a, b, parts, downs = refs[0], refs[1:3], refs[3:5], refs[5:7], refs[7:8]
-    hidden, oa, ob = refs[8], refs[9:11], refs[11:13]
-    x, part, own, value, buf, sems, dbuf, dsems = refs[13:]
-    rows = a[0].shape[1]
+    whole.wait()
+
+
+def far_kernel(acc, a3, a4, b3, b4, gate, up, down, hidden, oa3, oa4, ob3, ob4, x, part, own, value):
+    rows = a3.shape[1]
     block = 4 * rows
-    units = own.shape[1] // 2
-    first_chunk(parts, buf, sems)
-    first_chunk(downs, dbuf, dsems)
-    gate_up(a, b, parts, x, part, buf, sems)
+    units = down.shape[0]
+    gate_up((a3, a4), (b3, b4), (gate, up), x, part, lambda c: None)
     own[...] = acc[...]
     own[3 * block :, :] += part[0]
     for row, z in by_y(rows, 3):
@@ -403,97 +398,85 @@
     value[0] = hidden[3 * block :, :]
     for row, z in by_y(rows, 3):
         value[1, z * rows : (z + 1) * rows, :] = hidden[row : row + rows, :]
-    down_product(value, downs, dbuf, dsems, oa, ob)
-
-
-def rest_kernel(*refs):
-    hidden, downs, oa, ob = refs[0], refs[1:2], refs[2:5], refs[5:8]
-    value, dbuf, dsems = refs[8:]
-    rows = oa[0].shape[1]
+    down_product(value, down, (oa3, oa4), (ob3, ob4))
+
+
+def rest_kernel(hidden, down, oa0, oa1, oa2, ob0, ob1, ob2, value):
+    rows = oa0.shape[1]
     block = 4 * rows
-    first_chunk(downs, dbuf, dsems)
     value[0] = hidden[: 3 * block, :]
     for y in range(3):
         for row, z in by_y(rows, y):
             at = y * block + z * rows
             value[1, at : at + rows, :] = hidden[row : row + rows, :]
-    down_product(value, downs, dbuf, dsems, oa, ob)
+    down_product(value, down, (oa0, oa1, oa2), (ob0, ob1, ob2))
 
 
 def cost(flops):
     return pl.CostEstimate(flops=flops, bytes_accessed=2**20, transcendentals=0)
 
 
-TILE = 1024
-
-
-def streams(parts):
-    units, count = parts[0].shape[0], len(parts)
-    return [
-        pltpu.VMEM((2, count * units, TILE), BF),
-        pltpu.SemaphoreType.DMA((2, count)),
-    ]
-
-
-def near(xs, parts):
+def near(xs, gate, up, down):
     rows = xs[0].shape[1]
-    units = len(parts) * parts[0].shape[0]
+    units, model = gate.shape
     return call(
         near_kernel,
         "near_rows",
-        [((16 * rows, units), F32)],
+        [((16 * rows, 2 * units), F32)] + [((units, model), BF)] * 3,
         *xs,
-        *parts,
-        in_specs=[VM] * 6 + [HBM] * len(parts),
-        out_specs=[VM],
+        gate,
+        up,
+        down,
+        in_specs=[VM] * 6 + [ANY] * 3,
+        out_specs=[VM] * 4,
         scratch_shapes=[
             pltpu.VMEM((12 * rows, TILE), BF),
-            pltpu.VMEM((2, 12 * rows, units), F32),
-            *streams(parts),
+            pltpu.VMEM((2, 12 * rows, 2 * units), F32),
+            pltpu.SemaphoreType.DMA((model // TILE, 2)),
+            pltpu.SemaphoreType.DMA,
         ],
-        cost_estimate=cost(2 * 12 * rows * len(parts) * parts[0].size),
-        vmem=46,
-    )[0]
-
-
-def far(acc, xs, parts, downs):
+        cost_estimate=cost(4 * 12 * rows * gate.size),
+        vmem=24,
+    )
+
+
+def far(acc, xs, gate, up, down):
     rows, half = xs[0].shape[1:]
-    units = len(downs) * downs[0].shape[0]
+    units = down.shape[0]
     return call(
         far_kernel,
         "far_rows",
         [((16 * rows, units), BF)] + [((2, rows, half), BF)] * 4,
         acc,
         *xs,
-        *parts,
-        *downs,
-        in_specs=[VM] * 5 + [HBM] * (len(parts) + len(downs)),
+        gate,
+        up,
+        down,
+        in_specs=[VM] * 8,
         out_specs=[VM] * 5,
         scratch_shapes=[
             pltpu.VMEM((4 * rows, TILE), BF),
             pltpu.VMEM((2, 4 * rows, 2 * units), F32),
             pltpu.VMEM(acc.shape, F32),
             pltpu.VMEM((2, 4 * rows, units), BF),
-            *streams(parts),
-            *streams(downs),
         ],
-        vmem=48,
-    )
-
-
-def rest(hidden, downs, rows):
-    half = downs[0].shape[1] // 2
+        vmem=16,
+    )
+
+
+def rest(hidden, down, rows):
+    half = down.shape[1] // 2
     return call(
         rest_kernel,
         "rest_rows",
         [((4, rows, half), BF)] * 6,
         hidden,
-        *downs,
-        in_specs=[VM] + [HBM] * len(downs),
+        down,
+        in_specs=[VM] * 2,
         out_specs=[VM] * 6,
-        scratch_shapes=[pltpu.VMEM((2, 12 * rows, hidden.shape[1]), BF), *streams(downs)],
-        cost_estimate=cost(2 * 12 * rows * len(downs) * downs[0].size),
-        vmem=46,
+        scratch_shapes=[pltpu.VMEM((2, 12 * rows, hidden.shape[1]), BF)],
+        cost_estimate=cost(2 * 12 * rows * down.size),
+        vmem=12,
     )
 
 
@@ -676,10 +659,9 @@
     b_below, b_above = up_one(b4, "y"), down_one(b4, "y")
     a_far, b_far = far_sides(a_below, a_above, "z"), far_sides(b_below, b_above, "y")
 
-    gate_up_parts, downs = (gate, up), (down,)
-    acc = near((a4, a_below, a_above, b4, b_below, b_above), gate_up_parts)
-    hidden, *ends = far(acc, (*a_far, *b_far), gate_up_parts, downs)
-    body = rest(hidden, downs, size)
+    acc, gate, up, down = near((a4, a_below, a_above, b4, b_below, b_above), gate, up, down)
+    hidden, *ends = far(acc, (*a_far, *b_far), gate, up, down)
+    body = rest(hidden, down, size)
     oa, ob = (*body[:3], *ends[:2]), (*body[3:], *ends[2:])
     a_below, a_above, b_below, b_above = call(
         fold_kernel,

time: 320 us -> 327 us (1.022)
  local copies, waits for them, and re-layouts: 22 us -> 28.7 us
    unnamed x55 -> x61, local copies, waits for them, and re-layouts: 15.6 us -> 22.3 us
  transfers between devices with their start and end apart: 43 -> 43, of which waited for: 18 -> 20; matrix products, arithmetic and copies ran while one was open for 2% -> 2% of each run, Pallas kernels for 26% -> 24%
where the time goes in v5:
time: 327 us; the launch traced here: 326 us
  waiting for transfers between devices  103 us (31%)
  Pallas kernels  82.2 us (25%)
  starting transfers between devices  71.8 us (22%)
  local copies, waits for them, and re-layouts  28.7 us (9%)
  blocking collectives  25.9 us (8%)
  between operations  13.4 us (4%)
    pallas_call x14, Pallas kernels, call(): pl.pallas_call(kernel, out_shape=[jax.ShapeDtypeStruct(s, d) for s, d in...  71.8 us
    ppermute x14, waiting for transfers between devices, up_one(): return lax.ppermute(x, axis, ring(4, 1))  49.4 us
    ppermute x14, starting transfers between devices, down_one(): return lax.ppermute(x, axis, ring(4, -1))  36.8 us
    all_to_all x1, blocking collectives, shards(): arrived = lax.all_to_all(states, SEQ, 0, 0, tiled=True)  25.9 us
    ppermute x6, waiting for transfers between devices, across(): return lax.ppermute(x, axis, ring(4, 2))  22.7 us
    unnamed x61, local copies, waits for them, and re-layouts  22.3 us
    all_gather x1, waiting for transfers between devices, shards(): weight_out = lax.all_gather(out_weight.T, SEQ, axis=0, tiled=True)  16.4 us
    ppermute x6, starting transfers between devices, across(): return lax.ppermute(x, axis, ring(4, 2))  16.3 us
  transfers between devices with their start and end apart: 43, of which 20 were waited for; matrix products, arithmetic and copies ran while one was open for 2% of the time, Pallas kernels for 24%

profile of v5, /device:TPU:0, one launch (start us, length us, event | category | flops | bytes accessed | tf_op | source)
XLA Modules:
  0.0 325.5 jit_solution(2292036803103039224)
XLA Ops:
  9.3 7.1 %local_attention.1 = (f32[2,256,1024]{2,1,0:T(8,128)}, bf16[32,80,128]{2,1,0:T(8,128)(2,1)}, f32[2,256,8]{2,1,0:T(8,128)}) custom-call(bf16[2,256,1024]{2,1,0:T(8,128)(2,1)} %q_ref.3, bf16[2,256,1024]{2,1,0:T(8,128)(2,1)} %k_ref.1, bf16[2,256,1024]{2,1,0:T(8,128)(2,1)} %v_ref.1, f32[2,8,256]{2,1,0:T(8,128)} %bitcast.30), custom_call_target="tpu_custom_call" | custom-call | tf_op jit(solution)/shard_map/local_attention/pallas_call | solution.py:84
  16.5 25.9 %all_to_all.10.in_ref = bf16[32,80,128]{2,1,0:T(8,128)(2,1)S(1)} all-to-all(bf16[32,80,128]{2,1,0:T(8,128)(2,1)} %get-tuple-element.54), channel_id=1, replica_groups=mesh['z'=4,'y'=4,'core'=2,'x'=4] {'z','y','core'}, dimensions={0} | all-to-all | bytes 1310720 | tf_op jit(solution)/shard_map/all_to_all | solution.py:601
  43.3 4.6 %all-to-all-start.1 = ((bf16[32,64,128]{2,1,0:T(8,128)(2,1)}), bf16[32,64,128]{2,1,0:T(8,128)(2,1)}, u32[]{:S(2)}, u32[]{:S(2)}) async-start(bf16[32,64,128]{2,1,0:T(8,128)(2,1)} %copy-done.7), calls=%async_computation.1 | async-start | bytes 1048576 | tf_op jit(solution)/shard_map/all_to_all | solution.py:602
  48.1 2.9 collective-permute-start
  60.6 3.9 %all-to-all-done.1 = bf16[32,64,128]{2,1,0:T(8,128)(2,1)} async-done(((bf16[32,64,128]{2,1,0:T(8,128)(2,1)}), bf16[32,64,128]{2,1,0:T(8,128)(2,1)}, u32[]{:S(2)}, u32[]{:S(2)}) %all-to-all-start.1) | async-done | bytes 524320 | tf_op jit(solution)/shard_map/all_to_all | solution.py:602
  64.5 3.1 carried_norm.1
  68.6 16.4 %all-gather.8.cloned.1.call-done.weight.weight_ref = bf16[6144,1024]{1,0:T(8,128)(2,1)} async-done(((bf16[192,1024]{1,0:T(8,128)(2,1)}), bf16[6144,1024]{1,0:T(8,128)(2,1)}) %all-gather.8.cloned.1.call-update) | async-done | bytes 12582928 | tf_op jit(solution)/shard_map/all_gather | solution.py:589
  85.0 13.4 %selected_projection.1 = (bf16[48,6144]{1,0:T(8,128)(2,1)}, bf16[48,6144]{1,0:T(8,128)(2,1)}, bf16[48,6144]{1,0:T(8,128)(2,1)}, bf16[48,6144]{1,0:T(8,128)(2,1)}) custom-call(bf16[192,512]{1,0:T(8,128)(2,1)} %copy-done.20, bf16[192,128]{1,0:T(8,128)(2,1)} %copy-done.22, bf16[512,1024]{1,0:T(8,128)(2,1)} %bitcast.18, ...), custom_call_target="tpu_custom_call" | custom-call | tf_op jit(solution)/shard_map/selected_projection/pallas_call | solution.py:157
  103.5 12.6 %whole_projection.1.held = bf16[512,6144]{1,0:T(8,128)(2,1)} custom-call(bf16[512,1024]{1,0:T(8,128)(2,1)} %bitcast.19, bf16[6144,1024]{1,0:T(8,128)(2,1)} %all-gather.8.cloned.1.call-done.weight.weight_ref, bf16[48,6144]{1,0:T(8,128)(2,1)} %get-tuple-element.57.late.a), custom_call_target="tpu_custom_call" | custom-call | flops 6442450944 | bytes 25165824 | tf_op jit(solution)/shard_map/whole_projection/pallas_call | solution.py:157
  116.4 12.6 %collective-permute-done.5.d = bf16[48,6144]{1,0:T(8,128)(2,1)S(1)} collective-permute-done((bf16[48,6144]{1,0:T(8,128)(2,1)}, bf16[48,6144]{1,0:T(8,128)(2,1)S(1)}, u32[]{:S(2)}, u32[]{:S(2)}) %collective-permute-start.5) | collective-permute-done | bytes 589856 | tf_op jit(solution)/shard_map/ppermute | solution.py:559
  136.0 3.2 collective-permute-start.10
  141.2 8.3 %collective-permute-start.11 = (bf16[48,3072]{1,0:T(8,128)(2,1)S(1)}, bf16[48,3072]{1,0:T(8,128)(2,1)S(1)}, u32[]{:S(2)}, u32[]{:S(2)}) collective-permute-start(bf16[48,3072]{1,0:T(8,128)(2,1)S(1)} %get-tuple-element.63.b0), channel_id=1, source_target_pairs={{0,64},{32,96},{64,0},{96,32},{1,65},{33,97},{65,1},{97,33},{2,66}... | collective-permute-start | bytes 884744 | tf_op jit(solution)/shard_map/ppermute | solution.py:559
  149.5 7.4 %collective-permute-done.11.b3 = bf16[48,3072]{1,0:T(8,128)(2,1)S(1)} collective-permute-done((bf16[48,3072]{1,0:T(8,128)(2,1)S(1)}, bf16[48,3072]{1,0:T(8,128)(2,1)S(1)}, u32[]{:S(2)}, u32[]{:S(2)}) %collective-permute-start.11) | collective-permute-done | bytes 294944 | tf_op jit(solution)/shard_map/ppermute | solution.py:559
  161.1 3.2 collective-permute-start.15
  165.4 17.1 %collective-permute-done.12.a1 = bf16[4,48,3072]{2,1,0:T(8,128)(2,1)S(1)} collective-permute-done((bf16[4,48,3072]{2,1,0:T(8,128)(2,1)S(1)}, bf16[4,48,3072]{2,1,0:T(8,128)(2,1)S(1)}, u32[]{:S(2)}, u32[]{:S(2)}) %collective-permute-start.12) | collective-permute-done | bytes 1179680 | tf_op jit(solution)/shard_map/ppermute | solution.py:551
  191.0 2.9 collective-permute-start.19
  201.7 18.6 %near_rows.1 = (f32[768,1152]{1,0:T(8,128)S(1)}, bf16[576,6144]{1,0:T(8,128)(2,1)S(1)}, bf16[576,6144]{1,0:T(8,128)(2,1)S(1)}, bf16[576,6144]{1,0:T(8,128)(2,1)}) custom-call(bf16[4,48,3072]{2,1,0:T(8,128)(2,1)S(1)} %copy-done.26, bf16[4,48,3072]{2,1,0:T(8,128)(2,1)S(1)} %copy-done.12, bf16[4,48,3072]{2,1,0:T(8,128)(2,1)S(1)} %copy-done.14, ...), custom_call_target="tpu_custom_call" | custom-call | flops 8153726976 | bytes 1048576 | tf_op jit(solution)/shard_map/near_rows/pallas_call | solution.py:157
  222.1 3.0 copy-done
  227.1 10.8 %far_rows.1 = (bf16[768,576]{1,0:T(8,128)(2,1)S(1)}, bf16[2,48,3072]{2,1,0:T(8,128)(2,1)S(1)}, bf16[2,48,3072]{2,1,0:T(8,128)(2,1)S(1)}, bf16[2,48,3072]{2,1,0:T(8,128)(2,1)S(1)}, bf16[2,48,3072]{2,1,0:T(8,128)(2,1)S(1)}) custom-call(f32[768,1152]{1,0:T(8,128)S(1)} %copy-done.5, bf16[2,48,3072]{2,1,0:T(8,128)(2,1)S(1)} %collective-permute-done.16.a3, ...), custom_call_target="tpu_custom_call" | custom-call | tf_op jit(solution)/shard_map/far_rows/pallas_call | solution.py:157
  238.5 2.8 collective-permute-start.21
  241.2 3.2 collective-permute-start.23
  244.5 7.3 %rest_rows.1 = (bf16[4,48,3072]{2,1,0:T(8,128)(2,1)S(1)}, bf16[4,48,3072]{2,1,0:T(8,128)(2,1)S(1)}, bf16[4,48,3072]{2,1,0:T(8,128)(2,1)S(1)}, bf16[4,48,3072]{2,...) custom-call(bf16[768,576]{1,0:T(8,128)(2,1)S(1)} %get-tuple-element.70.hidden, ...), custom_call_target="tpu_custom_call" | custom-call | flops 4076863488 | bytes 1048576 | tf_op jit(solution)/shard_map/rest_rows/pallas_call | solution.py:157
  253.0 3.8 %collective-permute-done.22.up1 = bf16[2,48,3072]{2,1,0:T(8,128)(2,1)S(1)} collective-permute-done((bf16[2,48,3072]{2,1,0:T(8,128)(2,1)S(1)}, bf16[2,48,3072]{2,1,0:T(8,128)(2,1)S(1)}, u32[]{:S(2)}, u32[]{:S(2)}) %collective-permute-start.22) | collective-permute-done | bytes 589856 | tf_op jit(solution)/shard_map/ppermute | solution.py:551
  257.5 3.2 collective-permute-start.25
  260.7 3.5 %collective-permute-start.27 = (bf16[4,48,3072]{2,1,0:T(8,128)(2,1)S(1)}, bf16[4,48,3072]{2,1,0:T(8,128)(2,1)S(1)}, u32[]{:S(2)}, u32[]{:S(2)}) collective-permute-start(bf16[4,48,3072]{2,1,0:T(8,128)(2,1)S(1)} %get-tuple-element.86), channel_id=1, source_target_pairs={{0,24},{8,0},{16,8},{24,16},{1,25},{9,1},{17,9},{25,17},{2,26},{10... | collective-permute-start | bytes 3538952 | tf_op jit(solution)/shard_map/ppermute | solution.py:555
  264.2 11.5 %collective-permute-done.24.u0 = bf16[4,48,3072]{2,1,0:T(8,128)(2,1)S(1)} collective-permute-done((bf16[4,48,3072]{2,1,0:T(8,128)(2,1)S(1)}, bf16[4,48,3072]{2,1,0:T(8,128)(2,1)S(1)}, u32[]{:S(2)}, u32[]{:S(2)}) %collective-permute-start.24) | collective-permute-done | bytes 1179680 | tf_op jit(solution)/shard_map/ppermute | solution.py:551
  276.3 8.4 %collective-permute-done.26.u1 = bf16[4,48,3072]{2,1,0:T(8,128)(2,1)S(1)} collective-permute-done((bf16[4,48,3072]{2,1,0:T(8,128)(2,1)S(1)}, bf16[4,48,3072]{2,1,0:T(8,128)(2,1)S(1)}, u32[]{:S(2)}, u32[]{:S(2)}) %collective-permute-start.26) | collective-permute-done | bytes 1179680 | tf_op jit(solution)/shard_map/ppermute | solution.py:551
  291.1 3.2 collective-permute-start.32
  299.1 2.7 collective-permute-done.32.b2
  303.9 3.0 collective-permute-start.34
  311.7 4.5 %collective-permute-done.35.b2 = bf16[16,6144]{1,0:T(8,128)(2,1)} collective-permute-done((bf16[16,6144]{1,0:T(8,128)(2,1)}, bf16[16,6144]{1,0:T(8,128)(2,1)}, u32[]{:S(2)}, u32[]{:S(2)}) %collective-permute-start.35) | collective-permute-done | bytes 196640 | tf_op jit(solution)/shard_map/ppermute | solution.py:551
  316.2 2.8 combine.1
  (146 shorter events, 75.0 us)
Async XLA Ops:
  6.5 78.5 %all-gather.8.cloned.1.call-start = ((), (), s32[]{:S(2)}) async-start(), calls=%async_computation.3 | async-start | bytes 12976128 | tf_op jit(solution)/shard_map/all_gather | solution.py:589
  7.3 186.7 %all-gather.10.cloned.1.call-start = ((), (), s32[]{:S(2)}) async-start(), calls=%async_computation.5 | async-start | bytes 10616832 | tf_op jit(solution)/shard_map/all_gather | solution.py:591
  8.0 186.0 %all-gather.12.cloned.1.call-start = ((), (), s32[]{:S(2)}) async-start(), calls=%async_computation.6 | async-start | bytes 10616832 | tf_op jit(solution)/shard_map/all_gather | solution.py:591
  8.7 185.2 %all-gather.14.cloned.1.call-start = ((), (), s32[]{:S(2)}) async-start(), calls=%async_computation.7 | async-start | bytes 10616832 | tf_op jit(solution)/shard_map/all_gather | solution.py:591
  43.3 21.1 %all-to-all-start.1 = ((bf16[32,64,128]{2,1,0:T(8,128)(2,1)}), bf16[32,64,128]{2,1,0:T(8,128)(2,1)}, u32[]{:S(2)}, u32[]{:S(2)}) async-start(bf16[32,64,128]{2,1,0:T(8,128)(2,1)} %copy-done.7), calls=%async_computation.1 | async-start | bytes 1048576 | tf_op jit(solution)/shard_map/all_to_all | solution.py:602
  48.0 260.4 %reduce-scatter.2.cloned.1.call-start = ((), (), s32[]{:S(2)}) async-start(), calls=%async_computation.4 | async-start | bytes 7864320 | tf_op jit(solution)/shard_map/reduce_scatter | solution.py:640
  98.4 17.7 %collective-permute-start.3 = (bf16[48,6144]{1,0:T(8,128)(2,1)}, bf16[48,6144]{1,0:T(8,128)(2,1)S(1)}, u32[]{:S(2)}, u32[]{:S(2)}) collective-permute-start(bf16[48,6144]{1,0:T(8,128)(2,1)} %get-tuple-element.58), channel_id=1, source_target_pairs={{0,1},{1,2},{2,3},{3,0},{4,5},{5,6},{6,7},{7,4},{8,9},{9,10},{10,1... | collective-permute-start | bytes 1769480 | tf_op jit(solution)/shard_map/ppermute | solution.py:551
  100.0 16.4 %collective-permute-start.4 = (bf16[48,6144]{1,0:T(8,128)(2,1)}, bf16[48,6144]{1,0:T(8,128)(2,1)S(1)}, u32[]{:S(2)}, u32[]{:S(2)}) collective-permute-start(bf16[48,6144]{1,0:T(8,128)(2,1)} %get-tuple-element.59), channel_id=1, source_target_pairs={{0,3},{1,0},{2,1},{3,2},{4,7},{5,4},{6,5},{7,6},{8,11},{9,8},{10,9... | collective-permute-start | bytes 1769480 | tf_op jit(solution)/shard_map/ppermute | solution.py:555
  101.7 27.3 %collective-permute-start.5 = (bf16[48,6144]{1,0:T(8,128)(2,1)}, bf16[48,6144]{1,0:T(8,128)(2,1)S(1)}, u32[]{:S(2)}, u32[]{:S(2)}) collective-permute-start(bf16[48,6144]{1,0:T(8,128)(2,1)} %get-tuple-element.60), channel_id=1, source_target_pairs={{0,2},{1,3},{2,0},{3,1},{4,6},{5,7},{6,4},{7,5},{8,10},{9,11},{10,... | collective-permute-start | bytes 1769480 | tf_op jit(solution)/shard_map/ppermute | solution.py:559
  130.9 10.3 %collective-permute-start.6 = (bf16[48,3072]{1,0:T(8,128)(2,1)S(1)}, bf16[48,3072]{1,0:T(8,128)(2,1)S(1)}, u32[]{:S(2)}, u32[]{:S(2)}) collective-permute-start(bf16[48,3072]{1,0:T(8,128)(2,1)S(1)} %get-tuple-element.62.a0), channel_id=1, source_target_pairs={{0,8},{8,16},{16,24},{24,0},{1,9},{9,17},{17,25},{25,1},{2,10},{10... | collective-permute-start | bytes 884744 | tf_op jit(solution)/shard_map/ppermute | solution.py:551
  132.4 17.0 %collective-permute-start.7 = (bf16[48,3072]{1,0:T(8,128)(2,1)S(1)}, bf16[48,3072]{1,0:T(8,128)(2,1)S(1)}, u32[]{:S(2)}, u32[]{:S(2)}) collective-permute-start(bf16[48,3072]{1,0:T(8,128)(2,1)S(1)} %get-tuple-element.62.a0), channel_id=1, source_target_pairs={{0,24},{8,0},{16,8},{24,16},{1,25},{9,1},{17,9},{25,17},{2,26},{10... | collective-permute-start | bytes 884744 | tf_op jit(solution)/shard_map/ppermute | solution.py:555
  134.2 15.3 %collective-permute-start.8 = (bf16[48,3072]{1,0:T(8,128)(2,1)S(1)}, bf16[48,3072]{1,0:T(8,128)(2,1)S(1)}, u32[]{:S(2)}, u32[]{:S(2)}) collective-permute-start(bf16[48,3072]{1,0:T(8,128)(2,1)S(1)} %get-tuple-element.62.a0), channel_id=1, source_target_pairs={{0,16},{8,24},{16,0},{24,8},{1,17},{9,25},{17,1},{25,9},{2,18},{10... | collective-permute-start | bytes 884744 | tf_op jit(solution)/shard_map/ppermute | solution.py:559
  136.0 13.5 %collective-permute-start.9 = (bf16[48,3072]{1,0:T(8,128)(2,1)S(1)}, bf16[48,3072]{1,0:T(8,128)(2,1)S(1)}, u32[]{:S(2)}, u32[]{:S(2)}) collective-permute-start(bf16[48,3072]{1,0:T(8,128)(2,1)S(1)} %get-tuple-element.63.b0), channel_id=1, source_target_pairs={{0,32},{32,64},{64,96},{96,0},{1,33},{33,65},{65,97},{97,1},{2,34}... | collective-permute-start | bytes 884744 | tf_op jit(solution)/shard_map/ppermute | solution.py:551
  136.0 13.5 %collective-permute-start.10 = (bf16[48,3072]{1,0:T(8,128)(2,1)S(1)}, bf16[48,3072]{1,0:T(8,128)(2,1)S(1)}, u32[]{:S(2)}, u32[]{:S(2)}) collective-permute-start(bf16[48,3072]{1,0:T(8,128)(2,1)S(1)} %get-tuple-element.63.b0), channel_id=1, source_target_pairs={{0,96},{32,0},{64,32},{96,64},{1,97},{33,1},{65,33},{97,65},{2,98}... | collective-permute-start | bytes 884744 | tf_op jit(solution)/shard_map/ppermute | solution.py:555
  141.2 15.8 %collective-permute-start.11 = (bf16[48,3072]{1,0:T(8,128)(2,1)S(1)}, bf16[48,3072]{1,0:T(8,128)(2,1)S(1)}, u32[]{:S(2)}, u32[]{:S(2)}) collective-permute-start(bf16[48,3072]{1,0:T(8,128)(2,1)S(1)} %get-tuple-element.63.b0), channel_id=1, source_target_pairs={{0,64},{32,96},{64,0},{96,32},{1,65},{33,97},{65,1},{97,33},{2,66}... | collective-permute-start | bytes 884744 | tf_op jit(solution)/shard_map/ppermute | solution.py:559
  157.1 25.3 %collective-permute-start.12 = (bf16[4,48,3072]{2,1,0:T(8,128)(2,1)S(1)}, bf16[4,48,3072]{2,1,0:T(8,128)(2,1)S(1)}, u32[]{:S(2)}, u32[]{:S(2)}) collective-permute-start(bf16[4,48,3072]{2,1,0:T(8,128)(2,1)S(1)} %get-tuple-element.64.a0), channel_id=1, source_target_pairs={{0,32},{32,64},{64,96},{96,0},{1,33},{33,65},{65,97},{97,1},{2,34}... | collective-permute-start | bytes 3538952 | tf_op jit(solution)/shard_map/ppermute | solution.py:551
  159.6 25.4 %collective-permute-start.13 = (bf16[4,48,3072]{2,1,0:T(8,128)(2,1)S(1)}, bf16[4,48,3072]{2,1,0:T(8,128)(2,1)S(1)}, u32[]{:S(2)}, u32[]{:S(2)}) collective-permute-start(bf16[4,48,3072]{2,1,0:T(8,128)(2,1)S(1)} %get-tuple-element.64.a0), channel_id=1, source_target_pairs={{0,96},{32,0},{64,32},{96,64},{1,97},{33,1},{65,33},{97,65},{2,98}... | collective-permute-start | bytes 3538952 | tf_op jit(solution)/shard_map/ppermute | solution.py:555
  161.1 27.5 %collective-permute-start.14 = (bf16[4,48,3072]{2,1,0:T(8,128)(2,1)S(1)}, bf16[4,48,3072]{2,1,0:T(8,128)(2,1)S(1)}, u32[]{:S(2)}, u32[]{:S(2)}) collective-permute-start(bf16[4,48,3072]{2,1,0:T(8,128)(2,1)S(1)} %get-tuple-element.65.b0), channel_id=1, source_target_pairs={{0,8},{8,16},{16,24},{24,0},{1,9},{9,17},{17,25},{25,1},{2,10},{10... | collective-permute-start | bytes 3538952 | tf_op jit(solution)/shard_map/ppermute | solution.py:551
  161.1 28.4 %collective-permute-start.15 = (bf16[4,48,3072]{2,1,0:T(8,128)(2,1)S(1)}, bf16[4,48,3072]{2,1,0:T(8,128)(2,1)S(1)}, u32[]{:S(2)}, u32[]{:S(2)}) collective-permute-start(bf16[4,48,3072]{2,1,0:T(8,128)(2,1)S(1)} %get-tuple-element.65.b0), channel_id=1, source_target_pairs={{0,24},{8,0},{16,8},{24,16},{1,25},{9,1},{17,9},{25,17},{2,26},{10... | collective-permute-start | bytes 3538952 | tf_op jit(solution)/shard_map/ppermute | solution.py:555
  183.4 38.6 %collective-permute-start.16 = (bf16[2,48,3072]{2,1,0:T(8,128)(2,1)}, bf16[2,48,3072]{2,1,0:T(8,128)(2,1)S(1)}, u32[]{:S(2)}, u32[]{:S(2)}) collective-permute-start(bf16[2,48,3072]{2,1,0:T(8,128)(2,1)} %slice.16), channel_id=1, source_target_pairs={{0,32},{32,64},{64,96},{96,0},{1,33},{33,65},{65,97},{97,1},{2,34}... | collective-permute-start | bytes 1769480 | tf_op jit(solution)/shard_map/ppermute | solution.py:551
  186.9 35.2 %collective-permute-start.17 = (bf16[2,48,3072]{2,1,0:T(8,128)(2,1)}, bf16[2,48,3072]{2,1,0:T(8,128)(2,1)S(1)}, u32[]{:S(2)}, u32[]{:S(2)}) collective-permute-start(bf16[2,48,3072]{2,1,0:T(8,128)(2,1)} %slice.17), channel_id=1, source_target_pairs={{0,96},{32,0},{64,32},{96,64},{1,97},{33,1},{65,33},{97,65},{2,98}... | collective-permute-start | bytes 1769480 | tf_op jit(solution)/shard_map/ppermute | solution.py:555
  189.5 32.6 %collective-permute-start.18 = (bf16[2,48,3072]{2,1,0:T(8,128)(2,1)}, bf16[2,48,3072]{2,1,0:T(8,128)(2,1)S(1)}, u32[]{:S(2)}, u32[]{:S(2)}) collective-permute-start(bf16[2,48,3072]{2,1,0:T(8,128)(2,1)} %slice.18), channel_id=1, source_target_pairs={{0,8},{8,16},{16,24},{24,0},{1,9},{9,17},{17,25},{25,1},{2,10},{10... | collective-permute-start | bytes 1769480 | tf_op jit(solution)/shard_map/ppermute | solution.py:551
  191.0 31.1 %collective-permute-start.19 = (bf16[2,48,3072]{2,1,0:T(8,128)(2,1)}, bf16[2,48,3072]{2,1,0:T(8,128)(2,1)S(1)}, u32[]{:S(2)}, u32[]{:S(2)}) collective-permute-start(bf16[2,48,3072]{2,1,0:T(8,128)(2,1)} %slice.19), channel_id=1, source_target_pairs={{0,24},{8,0},{16,8},{24,16},{1,25},{9,1},{17,9},{25,17},{2,26},{10... | collective-permute-start | bytes 1769480 | tf_op jit(solution)/shard_map/ppermute | solution.py:555
  237.9 15.0 %collective-permute-start.20 = (bf16[2,48,3072]{2,1,0:T(8,128)(2,1)S(1)}, bf16[2,48,3072]{2,1,0:T(8,128)(2,1)S(1)}, u32[]{:S(2)}, u32[]{:S(2)}) collective-permute-start(bf16[2,48,3072]{2,1,0:T(8,128)(2,1)S(1)} %get-tuple-element.73), channel_id=1, source_target_pairs={{0,32},{32,64},{64,96},{96,0},{1,33},{33,65},{65,97},{97,1},{2,34}... | collective-permute-start | bytes 1769480 | tf_op jit(solution)/shard_map/ppermute | solution.py:551
  238.5 14.5 %collective-permute-start.21 = (bf16[2,48,3072]{2,1,0:T(8,128)(2,1)S(1)}, bf16[2,48,3072]{2,1,0:T(8,128)(2,1)S(1)}, u32[]{:S(2)}, u32[]{:S(2)}) collective-permute-start(bf16[2,48,3072]{2,1,0:T(8,128)(2,1)S(1)} %get-tuple-element.74), channel_id=1, source_target_pairs={{0,96},{32,0},{64,32},{96,64},{1,97},{33,1},{65,33},{97,65},{2,98}... | collective-permute-start | bytes 1769480 | tf_op jit(solution)/shard_map/ppermute | solution.py:555
  241.2 15.5 %collective-permute-start.22 = (bf16[2,48,3072]{2,1,0:T(8,128)(2,1)S(1)}, bf16[2,48,3072]{2,1,0:T(8,128)(2,1)S(1)}, u32[]{:S(2)}, u32[]{:S(2)}) collective-permute-start(bf16[2,48,3072]{2,1,0:T(8,128)(2,1)S(1)} %get-tuple-element.77), channel_id=1, source_target_pairs={{0,8},{8,16},{16,24},{24,0},{1,9},{9,17},{17,25},{25,1},{2,10},{10... | collective-permute-start | bytes 1769480 | tf_op jit(solution)/shard_map/ppermute | solution.py:551
  241.2 15.5 %collective-permute-start.23 = (bf16[2,48,3072]{2,1,0:T(8,128)(2,1)S(1)}, bf16[2,48,3072]{2,1,0:T(8,128)(2,1)S(1)}, u32[]{:S(2)}, u32[]{:S(2)}) collective-permute-start(bf16[2,48,3072]{2,1,0:T(8,128)(2,1)S(1)} %get-tuple-element.78), channel_id=1, source_target_pairs={{0,24},{8,0},{16,8},{24,16},{1,25},{9,1},{17,9},{25,17},{2,26},{10... | collective-permute-start | bytes 1769480 | tf_op jit(solution)/shard_map/ppermute | solution.py:555
  257.4 18.3 %collective-permute-start.24 = (bf16[4,48,3072]{2,1,0:T(8,128)(2,1)S(1)}, bf16[4,48,3072]{2,1,0:T(8,128)(2,1)S(1)}, u32[]{:S(2)}, u32[]{:S(2)}) collective-permute-start(bf16[4,48,3072]{2,1,0:T(8,128)(2,1)S(1)} %get-tuple-element.83), channel_id=1, source_target_pairs={{0,32},{32,64},{64,96},{96,0},{1,33},{33,65},{65,97},{97,1},{2,34}... | collective-permute-start | bytes 3538952 | tf_op jit(solution)/shard_map/ppermute | solution.py:551
  257.5 18.8 %collective-permute-start.25 = (bf16[4,48,3072]{2,1,0:T(8,128)(2,1)S(1)}, bf16[4,48,3072]{2,1,0:T(8,128)(2,1)S(1)}, u32[]{:S(2)}, u32[]{:S(2)}) collective-permute-start(bf16[4,48,3072]{2,1,0:T(8,128)(2,1)S(1)} %get-tuple-element.79.late), channel_id=1, source_target_pairs={{0,96},{32,0},{64,32},{96,64},{1,97},{33,1},{65,33},{97,65},{2,98}... | collective-permute-start | bytes 3538952 | tf_op jit(solution)/shard_map/ppermute | solution.py:555
  260.7 24.0 %collective-permute-start.26 = (bf16[4,48,3072]{2,1,0:T(8,128)(2,1)S(1)}, bf16[4,48,3072]{2,1,0:T(8,128)(2,1)S(1)}, u32[]{:S(2)}, u32[]{:S(2)}) collective-permute-start(bf16[4,48,3072]{2,1,0:T(8,128)(2,1)S(1)} %get-tuple-element.85), channel_id=1, source_target_pairs={{0,8},{8,16},{16,24},{24,0},{1,9},{9,17},{17,25},{25,1},{2,10},{10... | collective-permute-start | bytes 3538952 | tf_op jit(solution)/shard_map/ppermute | solution.py:551
  260.7 24.0 %collective-permute-start.27 = (bf16[4,48,3072]{2,1,0:T(8,128)(2,1)S(1)}, bf16[4,48,3072]{2,1,0:T(8,128)(2,1)S(1)}, u32[]{:S(2)}, u32[]{:S(2)}) collective-permute-start(bf16[4,48,3072]{2,1,0:T(8,128)(2,1)S(1)} %get-tuple-element.86), channel_id=1, source_target_pairs={{0,24},{8,0},{16,8},{24,16},{1,25},{9,1},{17,9},{25,17},{2,26},{10... | collective-permute-start | bytes 3538952 | tf_op jit(solution)/shard_map/ppermute | solution.py:555
  291.1 10.6 %collective-permute-start.32 = (bf16[48,3072]{1,0:T(8,128)(2,1)S(1)}, bf16[48,3072]{1,0:T(8,128)(2,1)S(1)}, u32[]{:S(2)}, u32[]{:S(2)}) collective-permute-start(bf16[48,3072]{1,0:T(8,128)(2,1)S(1)} %get-tuple-element.93), channel_id=1, source_target_pairs={{0,96},{32,0},{64,32},{96,64},{1,97},{33,1},{65,33},{97,65},{2,98}... | collective-permute-start | bytes 884744 | tf_op jit(solution)/shard_map/ppermute | solution.py:555
  (41 other events, 327.1 us)
Sparse Core Ops, SparseCore 0:
  9.6 75.3 all-gather.7
  86.6 20.0 all-gather.9
  108.4 21.9 all-gather.11
  131.9 21.9 all-gather.13
  156.1 65.2 reduce-scatter.1

commit v6 on v5

--- a/solution.py
+++ b/solution.py
@@ -204,34 +204,35 @@
     return lax.dot_general(a, b, (((1,), (1,)), ((), ())), preferred_element_type=F32)
 
 
-def selected_kernel(place, own, normed, weight, res, o0, o1, o2, o3, w_here, r_here, sems):
+def selected_kernel(place, own, normed, weight, res, o0, o1, o2, o3, w_here, sems):
     size = o0.shape[0]
     chunks = weight.shape[0] // TILE
 
     def copy(c):
+        slot = lax.rem(c, AHEAD + 1)
         span = pl.ds(pl.multiple_of(c * TILE, TILE), TILE)
-        return pltpu.make_async_copy(weight.at[span], w_here.at[span], sems.at[c])
+        return pltpu.make_async_copy(weight.at[span], w_here.at[slot], sems.at[slot])
+
+    for c in range(AHEAD):
+        copy(c).start()
+    picked = mm(place[...], normed[...]).astype(BF)
 
     @pl.loop(0, chunks)
     def _(c):
-        copy(c).start()
-
-    rest = pltpu.make_async_copy(res, r_here, sems.at[chunks])
-    rest.start()
-    picked = mm(place[...], normed[...]).astype(BF)
-    rest.wait()
-
-    @pl.loop(0, chunks)
-    def _(c):
+        @pl.when(c + AHEAD < chunks)
+        def _():
+            copy(c + AHEAD).start()
+
         span = pl.ds(pl.multiple_of(c * TILE, TILE), TILE)
         copy(c).wait()
-        full = (nt(picked, w_here[span, :]) + mm(own[...], r_here[:, span])).astype(BF)
+        full = nt(picked, w_here[lax.rem(c, AHEAD + 1)]) + mm(own[...], res[:, span])
+        full = full.astype(BF)
         for i, o in enumerate((o0, o1, o2, o3)):
             o[:, span] = full[i * size : (i + 1) * size]
 
 
 def selected(place, own, normed, weight, res):
-    picks, model = place.shape[0], weight.shape[0]
+    picks, (model, width) = place.shape[0], weight.shape
     return call(
         selected_kernel,
         "selected_projection",
@@ -241,14 +242,13 @@
         normed,
         weight,
         res,
-        in_specs=[VM] * 3 + [ANY] * 2,
+        in_specs=[VM] * 3 + [ANY, VM],
         out_specs=[VM] * 4,
         scratch_shapes=[
-            pltpu.VMEM(weight.shape, BF),
-            pltpu.VMEM(res.shape, BF),
-            pltpu.SemaphoreType.DMA((model // TILE + 1,)),
+            pltpu.VMEM((AHEAD + 1, TILE, width), BF),
+            pltpu.SemaphoreType.DMA((AHEAD + 1,)),
         ],
-        vmem=54,
+        vmem=48,
     )
 
 
@@ -302,13 +302,69 @@
     return [((z * 4 + y) * rows, z) for z in range(4)]
 
 
-def gate_up(refs_a, refs_b, gu, x, part, arrive):
+AHEAD = 2
+
+
+class Stream:
+    def __init__(self, source, spans, buf, sems):
+        self.source, self.spans, self.buf, self.sems = source, spans, buf, sems
+        self.chunks = source.shape[1] // TILE
+
+    def copies(self, c):
+        slot = lax.rem(c, AHEAD + 1)
+        cols = pl.ds(pl.multiple_of(c * TILE, TILE), TILE)
+        made, at = [], 0
+        for i, (start, size) in enumerate(self.spans):
+            made.append(
+                pltpu.make_async_copy(
+                    self.source.at[pl.ds(start, size), cols],
+                    self.buf.at[slot, pl.ds(at, size)],
+                    self.sems.at[slot, i],
+                )
+            )
+            at += size
+        return made
+
+    def start(self, c):
+        for copy in self.copies(c):
+            copy.start()
+
+    def begin(self):
+        for c in range(AHEAD):
+            self.start(c)
+
+    def run(self, body, then=None):
+        @pl.loop(0, self.chunks)
+        def _(c):
+            @pl.when(c + AHEAD < self.chunks)
+            def _():
+                self.start(c + AHEAD)
+
+            if then is not None:
+
+                @pl.when(c + AHEAD >= self.chunks)
+                def _():
+                    then.start(c + AHEAD - self.chunks)
+
+            for copy in self.copies(c):
+                copy.wait()
+            body(c, self.buf[lax.rem(c, AHEAD + 1)])
+
+
+def gate_up_spans(units):
+    return ((0, 2 * units), (3 * units, 2 * units))
+
+
+def down_spans(units):
+    return ((2 * units, units), (5 * units, units))
+
+
+def gate_up(refs_a, refs_b, x, part, stream, then=None):
     rows, half = refs_a[0].shape[1:]
     each = half // TILE
     part[...] = jnp.zeros_like(part)
 
-    @pl.loop(0, 2 * each)
-    def _(c):
+    def body(c, weights):
         for k, refs in enumerate((refs_a, refs_b)):
 
             @pl.when(c // each == k)
@@ -320,21 +376,17 @@
                         x[row : row + rows, :] = ref[i, :, at]
                         row += rows
 
-        arrive(c)
-        wide = pl.ds(pl.multiple_of(c * TILE, TILE), TILE)
-        units = gu[0].shape[0]
-        for i, w in enumerate(gu):
-            part[c // each, :, i * units : (i + 1) * units] += nt(x[...], w[:, wide])
-
-
-def down_product(value, down, outs_a, outs_b):
+        part[c // each] += nt(x[...], weights)
+
+    stream.run(body, then)
+
+
+def down_product(value, stream, outs_a, outs_b):
     rows, half = outs_a[0].shape[1:]
     each = half // TILE
 
-    @pl.loop(0, 2 * each)
-    def _(c):
-        wide = pl.ds(pl.multiple_of(c * TILE, TILE), TILE)
-        full = mm(value[c // each], down[:, wide]).astype(BF)
+    def body(c, weights):
+        full = mm(value[c // each], weights).astype(BF)
         for k, outs in enumerate((outs_a, outs_b)):
 
             @pl.when(c // each == k)
@@ -346,137 +398,129 @@
                         out[i, :, at] = full[row : row + rows]
                         row += rows
 
-
-def near_kernel(
-    a0, a1, a2, b0, b1, b2, gate, up, down, acc, gate_here, up_here, down_here, x, part, sems, last
-):
+    stream.run(body)
+
+
+def near_kernel(a0, a1, a2, b0, b1, b2, weights, acc, x, part, buf, sems):
     rows = a0.shape[1]
     block = 4 * rows
-    chunks = gate.shape[1] // TILE
-
-    def copies(c):
-        cols = pl.ds(pl.multiple_of(c * TILE, TILE), TILE)
-        pairs = ((gate, gate_here), (up, up_here))
-        return [
-            pltpu.make_async_copy(a.at[:, cols], b.at[:, cols], sems.at[c, i])
-            for i, (a, b) in enumerate(pairs)
-        ]
-
-    @pl.loop(0, chunks)
-    def _(c):
-        for copy in copies(c):
-            copy.start()
-
-    whole = pltpu.make_async_copy(down, down_here, last)
-    whole.start()
-
-    def arrive(c):
-        for copy in copies(c):
-            copy.wait()
-
-    gate_up((a0, a1, a2), (b0, b1, b2), (gate_here, up_here), x, part, arrive)
+    stream = Stream(weights, gate_up_spans(weights.shape[0] // 6), buf, sems)
+    stream.begin()
+    gate_up((a0, a1, a2), (b0, b1, b2), x, part, stream)
     acc[0 : 3 * block, :] = part[0]
     acc[3 * block :, :] = jnp.zeros((block, acc.shape[1]), F32)
     for y in range(3):
         for row, z in by_y(rows, y):
             at = y * block + z * rows
             acc[row : row + rows, :] += part[1, at : at + rows, :]
-    whole.wait()
-
-
-def far_kernel(acc, a3, a4, b3, b4, gate, up, down, hidden, oa3, oa4, ob3, ob4, x, part, own, value):
+
+
+def far_kernel(
+    acc, a3, a4, b3, b4, weights, hidden, oa3, oa4, ob3, ob4, x, part, own, value, buf, sems, dbuf, dsems
+):
     rows = a3.shape[1]
     block = 4 * rows
-    units = down.shape[0]
-    gate_up((a3, a4), (b3, b4), (gate, up), x, part, lambda c: None)
+    units = weights.shape[0] // 6
+    stream = Stream(weights, gate_up_spans(units), buf, sems)
+    downs = Stream(weights, down_spans(units), dbuf, dsems)
+    stream.begin()
+    gate_up((a3, a4), (b3, b4), x, part, stream, downs)
     own[...] = acc[...]
     own[3 * block :, :] += part[0]
     for row, z in by_y(rows, 3):
         own[row : row + rows, :] += part[1, z * rows : (z + 1) * rows, :]
-    g = own[:, :units]
-    hidden[...] = (g / (1.0 + jnp.exp(-g)) * own[:, units:]).astype(BF)
+    for core in range(2):
+        g = own[:, 2 * core * units : (2 * core + 1) * units]
+        u = own[:, (2 * core + 1) * units : (2 * core + 2) * units]
+        hidden[:, core * units : (core + 1) * units] = (g / (1.0 + jnp.exp(-g)) * u).astype(BF)
     value[0] = hidden[3 * block :, :]
     for row, z in by_y(rows, 3):
         value[1, z * rows : (z + 1) * rows, :] = hidden[row : row + rows, :]
-    down_product(value, down, (oa3, oa4), (ob3, ob4))
-
-
-def rest_kernel(hidden, down, oa0, oa1, oa2, ob0, ob1, ob2, value):
+    down_product(value, downs, (oa3, oa4), (ob3, ob4))
+
+
+def rest_kernel(hidden, weights, oa0, oa1, oa2, ob0, ob1, ob2, value, dbuf, dsems):
     rows = oa0.shape[1]
     block = 4 * rows
+    downs = Stream(weights, down_spans(weights.shape[0] // 6), dbuf, dsems)
+    downs.begin()
     value[0] = hidden[: 3 * block, :]
     for y in range(3):
         for row, z in by_y(rows, y):
             at = y * block + z * rows
             value[1, at : at + rows, :] = hidden[row : row + rows, :]
-    down_product(value, down, (oa0, oa1, oa2), (ob0, ob1, ob2))
+    down_product(value, downs, (oa0, oa1, oa2), (ob0, ob1, ob2))
 
 
 def cost(flops):
     return pl.CostEstimate(flops=flops, bytes_accessed=2**20, transcendentals=0)
 
 
-def near(xs, gate, up, down):
+def slots(rows, parts):
+    return [
+        pltpu.VMEM((AHEAD + 1, rows, TILE), BF),
+        pltpu.SemaphoreType.DMA((AHEAD + 1, parts)),
+    ]
+
+
+def near(xs, weights):
     rows = xs[0].shape[1]
-    units, model = gate.shape
+    wide = weights.shape[0] * 2 // 3
     return call(
         near_kernel,
         "near_rows",
-        [((16 * rows, 2 * units), F32)] + [((units, model), BF)] * 3,
+        [((16 * rows, wide), F32)],
         *xs,
-        gate,
-        up,
-        down,
-        in_specs=[VM] * 6 + [ANY] * 3,
-        out_specs=[VM] * 4,
+        weights,
+        in_specs=[VM] * 6 + [ANY],
+        out_specs=[VM],
         scratch_shapes=[
             pltpu.VMEM((12 * rows, TILE), BF),
-            pltpu.VMEM((2, 12 * rows, 2 * units), F32),
-            pltpu.SemaphoreType.DMA((model // TILE, 2)),
-            pltpu.SemaphoreType.DMA,
+            pltpu.VMEM((2, 12 * rows, wide), F32),
+            *slots(wide, 2),
         ],
-        cost_estimate=cost(4 * 12 * rows * gate.size),
-        vmem=24,
-    )
-
-
-def far(acc, xs, gate, up, down):
+        cost_estimate=cost(2 * 12 * rows * wide * weights.shape[1]),
+        vmem=30,
+    )[0]
+
+
+def far(acc, xs, weights):
     rows, half = xs[0].shape[1:]
-    units = down.shape[0]
+    wide = acc.shape[1]
     return call(
         far_kernel,
         "far_rows",
-        [((16 * rows, units), BF)] + [((2, rows, half), BF)] * 4,
+        [((16 * rows, wide // 2), BF)] + [((2, rows, half), BF)] * 4,
         acc,
         *xs,
-        gate,
-        up,
-        down,
-        in_specs=[VM] * 8,
+        weights,
+        in_specs=[VM] * 5 + [ANY],
         out_specs=[VM] * 5,
         scratch_shapes=[
             pltpu.VMEM((4 * rows, TILE), BF),
-            pltpu.VMEM((2, 4 * rows, 2 * units), F32),
+            pltpu.VMEM((2, 4 * rows, wide), F32),
             pltpu.VMEM(acc.shape, F32),
-            pltpu.VMEM((2, 4 * rows, units), BF),
+            pltpu.VMEM((2, 4 * rows, wide // 2), BF),
+            *slots(wide, 2),
+            *slots(wide // 2, 2),
         ],
-        vmem=16,
-    )
-
-
-def rest(hidden, down, rows):
-    half = down.shape[1] // 2
+        vmem=36,
+    )
+
+
+def rest(hidden, weights, rows):
+    wide, half = hidden.shape[1], weights.shape[1] // 2
     return call(
         rest_kernel,
         "rest_rows",
         [((4, rows, half), BF)] * 6,
         hidden,
-        down,
-        in_specs=[VM] * 2,
+        weights,
+        in_specs=[VM, ANY],
         out_specs=[VM] * 6,
-        scratch_shapes=[pltpu.VMEM((2, 12 * rows, hidden.shape[1]), BF)],
-        cost_estimate=cost(2 * 12 * rows * down.size),
-        vmem=12,
+        scratch_shapes=[pltpu.VMEM((2, 12 * rows, wide), BF), *slots(wide, 2)],
+        cost_estimate=cost(2 * 12 * rows * wide * weights.shape[1]),
+        vmem=36,
     )
 
 
@@ -587,10 +631,8 @@
     me = lax.axis_index("x").astype(jnp.int32).reshape(1)
 
     weight_out = lax.all_gather(out_weight.T, SEQ, axis=0, tiled=True)
-    gate, up, down = [
-        lax.all_gather(w[0], "core", axis=0, tiled=True)
-        for w in (gate_weight, up_weight, down_weight)
-    ]
+    weights = jnp.concatenate([gate_weight[0], up_weight[0], down_weight[0]])
+    weights = lax.all_gather(weights, "core", axis=0, tiled=True)
     routes = picks.reshape(rows, 2)
     turned = routes.T
     all_routes = [turned] + [lax.ppermute(turned, "x", ring(4, -delta)) for delta in (1, 2, 3)]
@@ -639,6 +681,7 @@
     )[0]
     mixed = lax.psum_scatter(whole, "x", scatter_dimension=0, tiled=True)
 
+    a_across, b_across = across(a0, "y"), across(b0, "z")
     a4, b4 = call(
         stack_kernel,
         "stack",
@@ -646,11 +689,11 @@
         a0,
         up_one(a0, "y"),
         down_one(a0, "y"),
-        across(a0, "y"),
+        a_across,
         b0,
         up_one(b0, "z"),
         down_one(b0, "z"),
-        across(b0, "z"),
+        b_across,
         in_specs=[VM] * 8,
         out_specs=[VM] * 2,
         vmem=16,
@@ -659,9 +702,9 @@
     b_below, b_above = up_one(b4, "y"), down_one(b4, "y")
     a_far, b_far = far_sides(a_below, a_above, "z"), far_sides(b_below, b_above, "y")
 
-    acc, gate, up, down = near((a4, a_below, a_above, b4, b_below, b_above), gate, up, down)
-    hidden, *ends = far(acc, (*a_far, *b_far), gate, up, down)
-    body = rest(hidden, down, size)
+    acc = near((a4, a_below, a_above, b4, b_below, b_above), weights)
+    hidden, *ends = far(acc, (*a_far, *b_far), weights)
+    body = rest(hidden, weights, size)
     oa, ob = (*body[:3], *ends[:2]), (*body[3:], *ends[2:])
     a_below, a_above, b_below, b_above = call(
         fold_kernel,

time: 327 us -> 315 us (0.963)
  other arithmetic: 0 us -> 9.48 us
  waiting for transfers between devices: 103 us -> 95.6 us
  blocking collectives: 25.9 us -> 21.8 us
  Pallas kernels: 82.2 us -> 78.2 us
  local copies, waits for them, and re-layouts: 28.7 us -> 24.9 us
    ppermute x6, waiting for transfers between devices: 22.7 us -> 11.9 us  [across(): return lax.ppermute(x, axis, ring(4, 2))]
    concatenate x0 -> x1, other arithmetic: none -> 9.48 us  [shards(): weights = jnp.concatenate([gate_weight[0], up_weight[0], down_weight[0]])]
    ppermute x14, waiting for transfers between devices: 4.89 us -> 13.5 us  [down_one(): return lax.ppermute(x, axis, ring(4, -1))]
    all_gather x1, waiting for transfers between devices: 16.4 us -> 9.01 us  [shards(): weight_out = lax.all_gather(out_weight.T, SEQ, axis=0, tiled=True)]
    all_to_all x1, blocking collectives: 25.9 us -> 21.8 us  [shards(): arrived = lax.all_to_all(states, SEQ, 0, 0, tiled=True)]
    pallas_call x14, Pallas kernels: 71.8 us -> 68 us  [call(): pl.pallas_call(kernel, out_shape=[jax.ShapeDtypeStruct(s, d) for s, d in...]
    ppermute x14, starting transfers between devices: 9.37 us -> 5.98 us  [up_one(): return lax.ppermute(x, axis, ring(4, 1))]
    ppermute x14, starting transfers between devices: 36.8 us -> 40.1 us  [down_one(): return lax.ppermute(x, axis, ring(4, -1))]
  transfers between devices with their start and end apart: 43 -> 41, of which waited for: 20 -> 19; matrix products, arithmetic and copies ran while one was open for 2% -> 4% of each run, Pallas kernels for 24% -> 24%
where the time goes in v6:
time: 315 us; the launch traced here: 314 us
  waiting for transfers between devices  95.6 us (30%)
  Pallas kernels  78.2 us (25%)
  starting transfers between devices  70.5 us (22%)
  local copies, waits for them, and re-layouts  24.9 us (8%)
  blocking collectives  21.8 us (7%)
  between operations  13.4 us (4%)
  other arithmetic  9.48 us (3%)
    pallas_call x14, Pallas kernels, call(): pl.pallas_call(kernel, out_shape=[jax.ShapeDtypeStruct(s, d) for s, d in...  68 us
    ppermute x14, waiting for transfers between devices, up_one(): return lax.ppermute(x, axis, ring(4, 1))  48.8 us
    ppermute x14, starting transfers between devices, down_one(): return lax.ppermute(x, axis, ring(4, -1))  40.1 us
    all_to_all x1, blocking collectives, shards(): arrived = lax.all_to_all(states, SEQ, 0, 0, tiled=True)  21.8 us
    unnamed x65, local copies, waits for them, and re-layouts  21.1 us
    ppermute x6, starting transfers between devices, across(): return lax.ppermute(x, axis, ring(4, 2))  15.9 us
    ppermute x14, waiting for transfers between devices, down_one(): return lax.ppermute(x, axis, ring(4, -1))  13.5 us
    ppermute x6, waiting for transfers between devices, across(): return lax.ppermute(x, axis, ring(4, 2))  11.9 us
  transfers between devices with their start and end apart: 41, of which 19 were waited for; matrix products, arithmetic and copies ran while one was open for 4% of the time, Pallas kernels for 24%

profile of v6, /device:TPU:0, one launch (start us, length us, event | category | flops | bytes accessed | tf_op | source)
XLA Modules:
  0.0 313.8 jit_solution(10158443669000831695)
XLA Ops:
  7.3 9.5 %pad_maximum_fusion = bf16[864,6144]{1,0:T(8,128)(2,1)} fusion(bf16[288,6144]{1,0:T(8,128)(2,1)} %bitcast.30, bf16[288,6144]{1,0:T(8,128)(2,1)} %bitcast.31, bf16[288,6144]{1,0:T(8,128)(2,1)} %bitcast.32), kind=kLoop, calls=%fused_computation | loop fusion | flops 31850496 | bytes 21233664 | tf_op jit(solution)/shard_map/concatenate | solution.py:634
  16.8 7.1 %local_attention.1 = (f32[2,256,1024]{2,1,0:T(8,128)}, bf16[32,80,128]{2,1,0:T(8,128)(2,1)}, f32[2,256,8]{2,1,0:T(8,128)}) custom-call(bf16[2,256,1024]{2,1,0:T(8,128)(2,1)} %q_ref.3, bf16[2,256,1024]{2,1,0:T(8,128)(2,1)} %k_ref.1, bf16[2,256,1024]{2,1,0:T(8,128)(2,1)} %v_ref.1, f32[2,8,256]{2,1,0:T(8,128)} %bitcast.34), custom_call_target="tpu_custom_call" | custom-call | tf_op jit(solution)/shard_map/local_attention/pallas_call | solution.py:84
  24.0 21.8 %all_to_all.10.in_ref = bf16[32,80,128]{2,1,0:T(8,128)(2,1)S(1)} all-to-all(bf16[32,80,128]{2,1,0:T(8,128)(2,1)} %get-tuple-element.50), channel_id=1, replica_groups=mesh['z'=4,'y'=4,'core'=2,'x'=4] {'z','y','core'}, dimensions={0} | all-to-all | bytes 1310720 | tf_op jit(solution)/shard_map/all_to_all | solution.py:643
  46.7 3.9 %all-to-all-start.1 = ((bf16[32,64,128]{2,1,0:T(8,128)(2,1)}), bf16[32,64,128]{2,1,0:T(8,128)(2,1)S(1)}, u32[]{:S(2)}, u32[]{:S(2)}) async-start(bf16[32,64,128]{2,1,0:T(8,128)(2,1)} %state_prefix.1), calls=%async_computation.1 | async-start | bytes 1048576 | tf_op jit(solution)/shard_map/all_to_all | solution.py:644
  50.7 2.8 collective-permute-start
  56.9 2.8 collective-permute-done.1
  61.4 6.8 %all-to-all-done.1 = bf16[32,64,128]{2,1,0:T(8,128)(2,1)S(1)} async-done(((bf16[32,64,128]{2,1,0:T(8,128)(2,1)}), bf16[32,64,128]{2,1,0:T(8,128)(2,1)S(1)}, u32[]{:S(2)}, u32[]{:S(2)}) %all-to-all-start.1) | async-done | bytes 524320 | tf_op jit(solution)/shard_map/all_to_all | solution.py:644
  74.7 9.0 %all-gather.3.cloned.1.call-done.weight.weight_ref = bf16[6144,1024]{1,0:T(8,128)(2,1)} async-done(((bf16[192,1024]{1,0:T(8,128)(2,1)}), bf16[6144,1024]{1,0:T(8,128)(2,1)}) %all-gather.3.cloned.1.call-update) | async-done | bytes 12582928 | tf_op jit(solution)/shard_map/all_gather | solution.py:633
  85.0 8.1 %selected_projection.1 = (bf16[48,6144]{1,0:T(8,128)(2,1)}, bf16[48,6144]{1,0:T(8,128)(2,1)S(1)}, bf16[48,6144]{1,0:T(8,128)(2,1)S(1)}, bf16[48,6144]{1,0:T(8,128)(2,1)S(1)}) custom-call(bf16[192,512]{1,0:T(8,128)(2,1)S(1)} %copy-done.27, bf16[192,128]{1,0:T(8,128)(2,1)S(1)} %get-tuple-element.52.own, bf16[512,1024]{1,0:T(8,128)(2,1)S(1)} %bitcast.19, ...), custom_call_target="tpu_custom_call" | custom-call | tf_op jit(solution)/shard_map/selected_projection/pallas_call | solution.py:157
  98.9 14.8 %whole_projection.1.held = bf16[512,6144]{1,0:T(8,128)(2,1)} custom-call(bf16[512,1024]{1,0:T(8,128)(2,1)} %bitcast.18, bf16[6144,1024]{1,0:T(8,128)(2,1)} %all-gather.3.cloned.1.call-done.weight.weight_ref, bf16[48,6144]{1,0:T(8,128)(2,1)} %copy-done.18), custom_call_target="tpu_custom_call" | custom-call | flops 6442450944 | bytes 25165824 | tf_op jit(solution)/shard_map/whole_projection/pallas_call | solution.py:157
  113.8 8.8 %collective-permute-done.4.c = bf16[48,6144]{1,0:T(8,128)(2,1)S(1)} collective-permute-done((bf16[48,6144]{1,0:T(8,128)(2,1)S(1)}, bf16[48,6144]{1,0:T(8,128)(2,1)S(1)}, u32[]{:S(2)}, u32[]{:S(2)}) %collective-permute-start.4) | collective-permute-done | bytes 589856 | tf_op jit(solution)/shard_map/ppermute | solution.py:599
  133.7 3.2 %collective-permute-start.10 = (bf16[48,3072]{1,0:T(8,128)(2,1)S(1)}, bf16[48,3072]{1,0:T(8,128)(2,1)S(1)}, u32[]{:S(2)}, u32[]{:S(2)}) collective-permute-start(bf16[48,3072]{1,0:T(8,128)(2,1)S(1)} %copy-done.24), channel_id=1, source_target_pairs={{0,96},{32,0},{64,32},{96,64},{1,97},{33,1},{65,33},{97,65},{2,98}... | collective-permute-start | bytes 884744 | tf_op jit(solution)/shard_map/ppermute | solution.py:599
  138.8 8.4 %collective-permute-start.11 = (bf16[48,3072]{1,0:T(8,128)(2,1)S(1)}, bf16[48,3072]{1,0:T(8,128)(2,1)S(1)}, u32[]{:S(2)}, u32[]{:S(2)}) collective-permute-start(bf16[48,3072]{1,0:T(8,128)(2,1)S(1)} %copy-done.24), channel_id=1, source_target_pairs={{0,64},{32,96},{64,0},{96,32},{1,65},{33,97},{65,1},{97,33},{2,66}... | collective-permute-start | bytes 884744 | tf_op jit(solution)/shard_map/ppermute | solution.py:603
  147.2 7.4 %collective-permute-done.11.b3 = bf16[48,3072]{1,0:T(8,128)(2,1)S(1)} collective-permute-done((bf16[48,3072]{1,0:T(8,128)(2,1)S(1)}, bf16[48,3072]{1,0:T(8,128)(2,1)S(1)}, u32[]{:S(2)}, u32[]{:S(2)}) %collective-permute-start.11) | collective-permute-done | bytes 294944 | tf_op jit(solution)/shard_map/ppermute | solution.py:603
  155.7 3.2 %collective-permute-start.13 = (bf16[4,48,3072]{2,1,0:T(8,128)(2,1)S(1)}, bf16[4,48,3072]{2,1,0:T(8,128)(2,1)S(1)}, u32[]{:S(2)}, u32[]{:S(2)}) collective-permute-start(bf16[4,48,3072]{2,1,0:T(8,128)(2,1)S(1)} %get-tuple-element.60.a0), channel_id=1, source_target_pairs={{0,96},{32,0},{64,32},{96,64},{1,97},{33,1},{65,33},{97,65},{2,98}... | collective-permute-start | bytes 3538952 | tf_op jit(solution)/shard_map/ppermute | solution.py:599
  158.9 3.2 %collective-permute-start.15 = (bf16[4,48,3072]{2,1,0:T(8,128)(2,1)S(1)}, bf16[4,48,3072]{2,1,0:T(8,128)(2,1)S(1)}, u32[]{:S(2)}, u32[]{:S(2)}) collective-permute-start(bf16[4,48,3072]{2,1,0:T(8,128)(2,1)S(1)} %get-tuple-element.61.b0), channel_id=1, source_target_pairs={{0,24},{8,0},{16,8},{24,16},{1,25},{9,1},{17,9},{25,17},{2,26},{10... | collective-permute-start | bytes 3538952 | tf_op jit(solution)/shard_map/ppermute | solution.py:599
  162.1 18.1 %collective-permute-done.12.a1 = bf16[4,48,3072]{2,1,0:T(8,128)(2,1)S(1)} collective-permute-done((bf16[4,48,3072]{2,1,0:T(8,128)(2,1)S(1)}, bf16[4,48,3072]{2,1,0:T(8,128)(2,1)S(1)}, u32[]{:S(2)}, u32[]{:S(2)}) %collective-permute-start.12) | collective-permute-done | bytes 1179680 | tf_op jit(solution)/shard_map/ppermute | solution.py:595
  183.5 2.8 collective-permute-start.17
  190.1 3.2 %collective-permute-start.19 = (bf16[2,48,3072]{2,1,0:T(8,128)(2,1)}, bf16[2,48,3072]{2,1,0:T(8,128)(2,1)}, u32[]{:S(2)}, u32[]{:S(2)}) collective-permute-start(bf16[2,48,3072]{2,1,0:T(8,128)(2,1)} %slice.19), channel_id=1, source_target_pairs={{0,24},{8,0},{16,8},{24,16},{1,25},{9,1},{17,9},{25,17},{2,26},{10... | collective-permute-start | bytes 1769480 | tf_op jit(solution)/shard_map/ppermute | solution.py:599
  199.7 13.2 %near_rows.1.acc = f32[768,1152]{1,0:T(8,128)S(1)} custom-call(bf16[4,48,3072]{2,1,0:T(8,128)(2,1)S(1)} %copy-done.15, bf16[4,48,3072]{2,1,0:T(8,128)(2,1)S(1)} %collective-permute-done.12.a1, bf16[4,48,3072]{2,1,0:T(8,128)(2,1)S(1)} %copy-done.5, bf16[4,48,3072]{2,1,0:T(8,128)(2,1)S(1)} %copy-done.17, bf16[4,48,3072]{2,1,0:T(8,128)(2,1)S(1)} %copy-done.7, ...), custom_call_target="tpu_custom_call" | custom-call | flops 8153726976 | bytes 1048576 | tf_op jit(solution)/shard_map/near_rows/pallas_call | solution.py:157
  212.9 14.1 %far_rows.1 = (bf16[768,576]{1,0:T(8,128)(2,1)S(1)}, bf16[2,48,3072]{2,1,0:T(8,128)(2,1)S(1)}, bf16[2,48,3072]{2,1,0:T(8,128)(2,1)S(1)}, bf16[2,48,3072]{2,1,0:T(8,128)(2,1)S(1)}, bf16[2,48,3072]{2,1,0:T(8,128)(2,1)S(1)}) custom-call(f32[768,1152]{1,0:T(8,128)S(1)} %near_rows.1.acc, bf16[2,48,3072]{2,1,0:T(8,128)(2,1)} %collective-permute-done.16.a3, ...), custom_call_target="tpu_custom_call" | custom-call | tf_op jit(solution)/shard_map/far_rows/pallas_call | solution.py:157
  227.1 3.2 %collective-permute-start.21 = (bf16[2,48,3072]{2,1,0:T(8,128)(2,1)S(1)}, bf16[2,48,3072]{2,1,0:T(8,128)(2,1)S(1)}, u32[]{:S(2)}, u32[]{:S(2)}) collective-permute-start(bf16[2,48,3072]{2,1,0:T(8,128)(2,1)S(1)} %get-tuple-element.66), channel_id=1, source_target_pairs={{0,96},{32,0},{64,32},{96,64},{1,97},{33,1},{65,33},{97,65},{2,98}... | collective-permute-start | bytes 1769480 | tf_op jit(solution)/shard_map/ppermute | solution.py:599
  230.3 3.2 %collective-permute-start.23 = (bf16[2,48,3072]{2,1,0:T(8,128)(2,1)S(1)}, bf16[2,48,3072]{2,1,0:T(8,128)(2,1)S(1)}, u32[]{:S(2)}, u32[]{:S(2)}) collective-permute-start(bf16[2,48,3072]{2,1,0:T(8,128)(2,1)S(1)} %get-tuple-element.70), channel_id=1, source_target_pairs={{0,24},{8,0},{16,8},{24,16},{1,25},{9,1},{17,9},{25,17},{2,26},{10... | collective-permute-start | bytes 1769480 | tf_op jit(solution)/shard_map/ppermute | solution.py:599
  233.6 8.5 %rest_rows.1 = (bf16[4,48,3072]{2,1,0:T(8,128)(2,1)S(1)}, bf16[4,48,3072]{2,1,0:T(8,128)(2,1)S(1)}, bf16[4,48,3072]{2,1,0:T(8,128)(2,1)S(1)}, bf16[4,48,3072]{2,...) custom-call(bf16[768,576]{1,0:T(8,128)(2,1)S(1)} %get-tuple-element.62.hidden, ...), custom_call_target="tpu_custom_call" | custom-call | flops 4076863488 | bytes 1048576 | tf_op jit(solution)/shard_map/rest_rows/pallas_call | solution.py:157
  242.2 3.2 %collective-permute-done.22.up1 = bf16[2,48,3072]{2,1,0:T(8,128)(2,1)S(1)} collective-permute-done((bf16[2,48,3072]{2,1,0:T(8,128)(2,1)S(1)}, bf16[2,48,3072]{2,1,0:T(8,128)(2,1)S(1)}, u32[]{:S(2)}, u32[]{:S(2)}) %collective-permute-start.22) | collective-permute-done | bytes 589856 | tf_op jit(solution)/shard_map/ppermute | solution.py:595
  246.1 3.2 %collective-permute-start.25 = (bf16[4,48,3072]{2,1,0:T(8,128)(2,1)S(1)}, bf16[4,48,3072]{2,1,0:T(8,128)(2,1)S(1)}, u32[]{:S(2)}, u32[]{:S(2)}) collective-permute-start(bf16[4,48,3072]{2,1,0:T(8,128)(2,1)S(1)} %get-tuple-element.71.late), channel_id=1, source_target_pairs={{0,96},{32,0},{64,32},{96,64},{1,97},{33,1},{65,33},{97,65},{2,98}... | collective-permute-start | bytes 3538952 | tf_op jit(solution)/shard_map/ppermute | solution.py:599
  249.3 3.5 %collective-permute-start.27 = (bf16[4,48,3072]{2,1,0:T(8,128)(2,1)S(1)}, bf16[4,48,3072]{2,1,0:T(8,128)(2,1)S(1)}, u32[]{:S(2)}, u32[]{:S(2)}) collective-permute-start(bf16[4,48,3072]{2,1,0:T(8,128)(2,1)S(1)} %get-tuple-element.78), channel_id=1, source_target_pairs={{0,24},{8,0},{16,8},{24,16},{1,25},{9,1},{17,9},{25,17},{2,26},{10... | collective-permute-start | bytes 3538952 | tf_op jit(solution)/shard_map/ppermute | solution.py:599
  252.8 11.0 %collective-permute-done.24.u0 = bf16[4,48,3072]{2,1,0:T(8,128)(2,1)S(1)} collective-permute-done((bf16[4,48,3072]{2,1,0:T(8,128)(2,1)S(1)}, bf16[4,48,3072]{2,1,0:T(8,128)(2,1)S(1)}, u32[]{:S(2)}, u32[]{:S(2)}) %collective-permute-start.24) | collective-permute-done | bytes 1179680 | tf_op jit(solution)/shard_map/ppermute | solution.py:595
  263.8 9.5 %collective-permute-done.26.u1 = bf16[4,48,3072]{2,1,0:T(8,128)(2,1)S(1)} collective-permute-done((bf16[4,48,3072]{2,1,0:T(8,128)(2,1)S(1)}, bf16[4,48,3072]{2,1,0:T(8,128)(2,1)S(1)}, u32[]{:S(2)}, u32[]{:S(2)}) %collective-permute-start.26) | collective-permute-done | bytes 1179680 | tf_op jit(solution)/shard_map/ppermute | solution.py:595
  279.7 3.2 %collective-permute-start.32 = (bf16[48,3072]{1,0:T(8,128)(2,1)S(1)}, bf16[48,3072]{1,0:T(8,128)(2,1)S(1)}, u32[]{:S(2)}, u32[]{:S(2)}) collective-permute-start(bf16[48,3072]{1,0:T(8,128)(2,1)S(1)} %get-tuple-element.85), channel_id=1, source_target_pairs={{0,96},{32,0},{64,32},{96,64},{1,97},{33,1},{65,33},{97,65},{2,98}... | collective-permute-start | bytes 884744 | tf_op jit(solution)/shard_map/ppermute | solution.py:599
  300.2 4.2 %collective-permute-done.35.b2 = bf16[16,6144]{1,0:T(8,128)(2,1)} collective-permute-done((bf16[16,6144]{1,0:T(8,128)(2,1)}, bf16[16,6144]{1,0:T(8,128)(2,1)}, u32[]{:S(2)}, u32[]{:S(2)}) %collective-permute-start.35) | collective-permute-done | bytes 196640 | tf_op jit(solution)/shard_map/ppermute | solution.py:595
  304.4 2.8 combine.1
  (145 shorter events, 72.4 us)
Async XLA Ops:
  6.5 77.2 %all-gather.3.cloned.1.call-start = ((), (), s32[]{:S(2)}) async-start(), calls=%async_computation.3 | async-start | bytes 12976128 | tf_op jit(solution)/shard_map/all_gather | solution.py:633
  7.3 186.1 %all-gather.5.cloned.1.call-start = ((), (), s32[]{:S(2)}) async-start(), calls=%async_computation.5 | async-start | bytes 31850496 | tf_op jit(solution)/shard_map/all_gather | solution.py:635
  46.7 21.5 %all-to-all-start.1 = ((bf16[32,64,128]{2,1,0:T(8,128)(2,1)}), bf16[32,64,128]{2,1,0:T(8,128)(2,1)S(1)}, u32[]{:S(2)}, u32[]{:S(2)}) async-start(bf16[32,64,128]{2,1,0:T(8,128)(2,1)} %state_prefix.1), calls=%async_computation.1 | async-start | bytes 1048576 | tf_op jit(solution)/shard_map/all_to_all | solution.py:644
  50.6 246.3 %reduce-scatter.2.cloned.1.call-start = ((), (), s32[]{:S(2)}) async-start(), calls=%async_computation.4 | async-start | bytes 7864320 | tf_op jit(solution)/shard_map/reduce_scatter | solution.py:682
  93.9 19.9 %collective-permute-start.3 = (bf16[48,6144]{1,0:T(8,128)(2,1)}, bf16[48,6144]{1,0:T(8,128)(2,1)S(1)}, u32[]{:S(2)}, u32[]{:S(2)}) collective-permute-start(bf16[48,6144]{1,0:T(8,128)(2,1)} %get-tuple-element.54), channel_id=1, source_target_pairs={{0,1},{1,2},{2,3},{3,0},{4,5},{5,6},{6,7},{7,4},{8,9},{9,10},{10,1... | collective-permute-start | bytes 1769480 | tf_op jit(solution)/shard_map/ppermute | solution.py:595
  95.4 27.2 %collective-permute-start.4 = (bf16[48,6144]{1,0:T(8,128)(2,1)S(1)}, bf16[48,6144]{1,0:T(8,128)(2,1)S(1)}, u32[]{:S(2)}, u32[]{:S(2)}) collective-permute-start(bf16[48,6144]{1,0:T(8,128)(2,1)S(1)} %get-tuple-element.55), channel_id=1, source_target_pairs={{0,3},{1,0},{2,1},{3,2},{4,7},{5,4},{6,5},{7,6},{8,11},{9,8},{10,9... | collective-permute-start | bytes 1769480 | tf_op jit(solution)/shard_map/ppermute | solution.py:599
  97.1 27.2 %collective-permute-start.5 = (bf16[48,6144]{1,0:T(8,128)(2,1)S(1)}, bf16[48,6144]{1,0:T(8,128)(2,1)S(1)}, u32[]{:S(2)}, u32[]{:S(2)}) collective-permute-start(bf16[48,6144]{1,0:T(8,128)(2,1)S(1)} %get-tuple-element.56), channel_id=1, source_target_pairs={{0,2},{1,3},{2,0},{3,1},{4,6},{5,7},{6,4},{7,5},{8,10},{9,11},{10,... | collective-permute-start | bytes 1769480 | tf_op jit(solution)/shard_map/ppermute | solution.py:603
  128.6 10.1 %collective-permute-start.6 = (bf16[48,3072]{1,0:T(8,128)(2,1)S(1)}, bf16[48,3072]{1,0:T(8,128)(2,1)S(1)}, u32[]{:S(2)}, u32[]{:S(2)}) collective-permute-start(bf16[48,3072]{1,0:T(8,128)(2,1)S(1)} %copy-done.22), channel_id=1, source_target_pairs={{0,8},{8,16},{16,24},{24,0},{1,9},{9,17},{17,25},{25,1},{2,10},{10... | collective-permute-start | bytes 884744 | tf_op jit(solution)/shard_map/ppermute | solution.py:595
  130.1 17.1 %collective-permute-start.7 = (bf16[48,3072]{1,0:T(8,128)(2,1)S(1)}, bf16[48,3072]{1,0:T(8,128)(2,1)S(1)}, u32[]{:S(2)}, u32[]{:S(2)}) collective-permute-start(bf16[48,3072]{1,0:T(8,128)(2,1)S(1)} %copy-done.22), channel_id=1, source_target_pairs={{0,24},{8,0},{16,8},{24,16},{1,25},{9,1},{17,9},{25,17},{2,26},{10... | collective-permute-start | bytes 884744 | tf_op jit(solution)/shard_map/ppermute | solution.py:599
  131.9 15.3 %collective-permute-start.8 = (bf16[48,3072]{1,0:T(8,128)(2,1)S(1)}, bf16[48,3072]{1,0:T(8,128)(2,1)S(1)}, u32[]{:S(2)}, u32[]{:S(2)}) collective-permute-start(bf16[48,3072]{1,0:T(8,128)(2,1)S(1)} %copy-done.22), channel_id=1, source_target_pairs={{0,16},{8,24},{16,0},{24,8},{1,17},{9,25},{17,1},{25,9},{2,18},{10... | collective-permute-start | bytes 884744 | tf_op jit(solution)/shard_map/ppermute | solution.py:603
  133.7 13.5 %collective-permute-start.9 = (bf16[48,3072]{1,0:T(8,128)(2,1)S(1)}, bf16[48,3072]{1,0:T(8,128)(2,1)S(1)}, u32[]{:S(2)}, u32[]{:S(2)}) collective-permute-start(bf16[48,3072]{1,0:T(8,128)(2,1)S(1)} %copy-done.24), channel_id=1, source_target_pairs={{0,32},{32,64},{64,96},{96,0},{1,33},{33,65},{65,97},{97,1},{2,34}... | collective-permute-start | bytes 884744 | tf_op jit(solution)/shard_map/ppermute | solution.py:595
  133.7 13.5 %collective-permute-start.10 = (bf16[48,3072]{1,0:T(8,128)(2,1)S(1)}, bf16[48,3072]{1,0:T(8,128)(2,1)S(1)}, u32[]{:S(2)}, u32[]{:S(2)}) collective-permute-start(bf16[48,3072]{1,0:T(8,128)(2,1)S(1)} %copy-done.24), channel_id=1, source_target_pairs={{0,96},{32,0},{64,32},{96,64},{1,97},{33,1},{65,33},{97,65},{2,98}... | collective-permute-start | bytes 884744 | tf_op jit(solution)/shard_map/ppermute | solution.py:599
  138.8 15.8 %collective-permute-start.11 = (bf16[48,3072]{1,0:T(8,128)(2,1)S(1)}, bf16[48,3072]{1,0:T(8,128)(2,1)S(1)}, u32[]{:S(2)}, u32[]{:S(2)}) collective-permute-start(bf16[48,3072]{1,0:T(8,128)(2,1)S(1)} %copy-done.24), channel_id=1, source_target_pairs={{0,64},{32,96},{64,0},{96,32},{1,65},{33,97},{65,1},{97,33},{2,66}... | collective-permute-start | bytes 884744 | tf_op jit(solution)/shard_map/ppermute | solution.py:603
  154.8 25.4 %collective-permute-start.12 = (bf16[4,48,3072]{2,1,0:T(8,128)(2,1)S(1)}, bf16[4,48,3072]{2,1,0:T(8,128)(2,1)S(1)}, u32[]{:S(2)}, u32[]{:S(2)}) collective-permute-start(bf16[4,48,3072]{2,1,0:T(8,128)(2,1)S(1)} %get-tuple-element.60.a0), channel_id=1, source_target_pairs={{0,32},{32,64},{64,96},{96,0},{1,33},{33,65},{65,97},{97,1},{2,34}... | collective-permute-start | bytes 3538952 | tf_op jit(solution)/shard_map/ppermute | solution.py:595
  155.7 25.8 %collective-permute-start.13 = (bf16[4,48,3072]{2,1,0:T(8,128)(2,1)S(1)}, bf16[4,48,3072]{2,1,0:T(8,128)(2,1)S(1)}, u32[]{:S(2)}, u32[]{:S(2)}) collective-permute-start(bf16[4,48,3072]{2,1,0:T(8,128)(2,1)S(1)} %get-tuple-element.60.a0), channel_id=1, source_target_pairs={{0,96},{32,0},{64,32},{96,64},{1,97},{33,1},{65,33},{97,65},{2,98}... | collective-permute-start | bytes 3538952 | tf_op jit(solution)/shard_map/ppermute | solution.py:599
  158.9 27.4 %collective-permute-start.14 = (bf16[4,48,3072]{2,1,0:T(8,128)(2,1)S(1)}, bf16[4,48,3072]{2,1,0:T(8,128)(2,1)S(1)}, u32[]{:S(2)}, u32[]{:S(2)}) collective-permute-start(bf16[4,48,3072]{2,1,0:T(8,128)(2,1)S(1)} %get-tuple-element.61.b0), channel_id=1, source_target_pairs={{0,8},{8,16},{16,24},{24,0},{1,9},{9,17},{17,25},{25,1},{2,10},{10... | collective-permute-start | bytes 3538952 | tf_op jit(solution)/shard_map/ppermute | solution.py:595
  158.9 29.3 %collective-permute-start.15 = (bf16[4,48,3072]{2,1,0:T(8,128)(2,1)S(1)}, bf16[4,48,3072]{2,1,0:T(8,128)(2,1)S(1)}, u32[]{:S(2)}, u32[]{:S(2)}) collective-permute-start(bf16[4,48,3072]{2,1,0:T(8,128)(2,1)S(1)} %get-tuple-element.61.b0), channel_id=1, source_target_pairs={{0,24},{8,0},{16,8},{24,16},{1,25},{9,1},{17,9},{25,17},{2,26},{10... | collective-permute-start | bytes 3538952 | tf_op jit(solution)/shard_map/ppermute | solution.py:599
  181.1 31.8 %collective-permute-start.16 = (bf16[2,48,3072]{2,1,0:T(8,128)(2,1)}, bf16[2,48,3072]{2,1,0:T(8,128)(2,1)}, u32[]{:S(2)}, u32[]{:S(2)}) collective-permute-start(bf16[2,48,3072]{2,1,0:T(8,128)(2,1)} %slice.16), channel_id=1, source_target_pairs={{0,32},{32,64},{64,96},{96,0},{1,33},{33,65},{65,97},{97,1},{2,34}... | collective-permute-start | bytes 1769480 | tf_op jit(solution)/shard_map/ppermute | solution.py:595
  183.5 29.4 %collective-permute-start.17 = (bf16[2,48,3072]{2,1,0:T(8,128)(2,1)}, bf16[2,48,3072]{2,1,0:T(8,128)(2,1)}, u32[]{:S(2)}, u32[]{:S(2)}) collective-permute-start(bf16[2,48,3072]{2,1,0:T(8,128)(2,1)} %slice.17), channel_id=1, source_target_pairs={{0,96},{32,0},{64,32},{96,64},{1,97},{33,1},{65,33},{97,65},{2,98}... | collective-permute-start | bytes 1769480 | tf_op jit(solution)/shard_map/ppermute | solution.py:599
  188.2 24.7 %collective-permute-start.18 = (bf16[2,48,3072]{2,1,0:T(8,128)(2,1)}, bf16[2,48,3072]{2,1,0:T(8,128)(2,1)}, u32[]{:S(2)}, u32[]{:S(2)}) collective-permute-start(bf16[2,48,3072]{2,1,0:T(8,128)(2,1)} %slice.18), channel_id=1, source_target_pairs={{0,8},{8,16},{16,24},{24,0},{1,9},{9,17},{17,25},{25,1},{2,10},{10... | collective-permute-start | bytes 1769480 | tf_op jit(solution)/shard_map/ppermute | solution.py:595
  190.1 22.8 %collective-permute-start.19 = (bf16[2,48,3072]{2,1,0:T(8,128)(2,1)}, bf16[2,48,3072]{2,1,0:T(8,128)(2,1)}, u32[]{:S(2)}, u32[]{:S(2)}) collective-permute-start(bf16[2,48,3072]{2,1,0:T(8,128)(2,1)} %slice.19), channel_id=1, source_target_pairs={{0,24},{8,0},{16,8},{24,16},{1,25},{9,1},{17,9},{25,17},{2,26},{10... | collective-permute-start | bytes 1769480 | tf_op jit(solution)/shard_map/ppermute | solution.py:599
  227.0 15.1 %collective-permute-start.20 = (bf16[2,48,3072]{2,1,0:T(8,128)(2,1)S(1)}, bf16[2,48,3072]{2,1,0:T(8,128)(2,1)S(1)}, u32[]{:S(2)}, u32[]{:S(2)}) collective-permute-start(bf16[2,48,3072]{2,1,0:T(8,128)(2,1)S(1)} %get-tuple-element.65), channel_id=1, source_target_pairs={{0,32},{32,64},{64,96},{96,0},{1,33},{33,65},{65,97},{97,1},{2,34}... | collective-permute-start | bytes 1769480 | tf_op jit(solution)/shard_map/ppermute | solution.py:595
  227.1 15.0 %collective-permute-start.21 = (bf16[2,48,3072]{2,1,0:T(8,128)(2,1)S(1)}, bf16[2,48,3072]{2,1,0:T(8,128)(2,1)S(1)}, u32[]{:S(2)}, u32[]{:S(2)}) collective-permute-start(bf16[2,48,3072]{2,1,0:T(8,128)(2,1)S(1)} %get-tuple-element.66), channel_id=1, source_target_pairs={{0,96},{32,0},{64,32},{96,64},{1,97},{33,1},{65,33},{97,65},{2,98}... | collective-permute-start | bytes 1769480 | tf_op jit(solution)/shard_map/ppermute | solution.py:599
  230.3 15.0 %collective-permute-start.22 = (bf16[2,48,3072]{2,1,0:T(8,128)(2,1)S(1)}, bf16[2,48,3072]{2,1,0:T(8,128)(2,1)S(1)}, u32[]{:S(2)}, u32[]{:S(2)}) collective-permute-start(bf16[2,48,3072]{2,1,0:T(8,128)(2,1)S(1)} %get-tuple-element.69), channel_id=1, source_target_pairs={{0,8},{8,16},{16,24},{24,0},{1,9},{9,17},{17,25},{25,1},{2,10},{10... | collective-permute-start | bytes 1769480 | tf_op jit(solution)/shard_map/ppermute | solution.py:595
  230.3 15.0 %collective-permute-start.23 = (bf16[2,48,3072]{2,1,0:T(8,128)(2,1)S(1)}, bf16[2,48,3072]{2,1,0:T(8,128)(2,1)S(1)}, u32[]{:S(2)}, u32[]{:S(2)}) collective-permute-start(bf16[2,48,3072]{2,1,0:T(8,128)(2,1)S(1)} %get-tuple-element.70), channel_id=1, source_target_pairs={{0,24},{8,0},{16,8},{24,16},{1,25},{9,1},{17,9},{25,17},{2,26},{10... | collective-permute-start | bytes 1769480 | tf_op jit(solution)/shard_map/ppermute | solution.py:599
  246.0 17.8 %collective-permute-start.24 = (bf16[4,48,3072]{2,1,0:T(8,128)(2,1)S(1)}, bf16[4,48,3072]{2,1,0:T(8,128)(2,1)S(1)}, u32[]{:S(2)}, u32[]{:S(2)}) collective-permute-start(bf16[4,48,3072]{2,1,0:T(8,128)(2,1)S(1)} %get-tuple-element.75), channel_id=1, source_target_pairs={{0,32},{32,64},{64,96},{96,0},{1,33},{33,65},{65,97},{97,1},{2,34}... | collective-permute-start | bytes 3538952 | tf_op jit(solution)/shard_map/ppermute | solution.py:595
  246.1 17.8 %collective-permute-start.25 = (bf16[4,48,3072]{2,1,0:T(8,128)(2,1)S(1)}, bf16[4,48,3072]{2,1,0:T(8,128)(2,1)S(1)}, u32[]{:S(2)}, u32[]{:S(2)}) collective-permute-start(bf16[4,48,3072]{2,1,0:T(8,128)(2,1)S(1)} %get-tuple-element.71.late), channel_id=1, source_target_pairs={{0,96},{32,0},{64,32},{96,64},{1,97},{33,1},{65,33},{97,65},{2,98}... | collective-permute-start | bytes 3538952 | tf_op jit(solution)/shard_map/ppermute | solution.py:599
  249.3 24.0 %collective-permute-start.26 = (bf16[4,48,3072]{2,1,0:T(8,128)(2,1)S(1)}, bf16[4,48,3072]{2,1,0:T(8,128)(2,1)S(1)}, u32[]{:S(2)}, u32[]{:S(2)}) collective-permute-start(bf16[4,48,3072]{2,1,0:T(8,128)(2,1)S(1)} %get-tuple-element.77), channel_id=1, source_target_pairs={{0,8},{8,16},{16,24},{24,0},{1,9},{9,17},{17,25},{25,1},{2,10},{10... | collective-permute-start | bytes 3538952 | tf_op jit(solution)/shard_map/ppermute | solution.py:595
  249.3 24.0 %collective-permute-start.27 = (bf16[4,48,3072]{2,1,0:T(8,128)(2,1)S(1)}, bf16[4,48,3072]{2,1,0:T(8,128)(2,1)S(1)}, u32[]{:S(2)}, u32[]{:S(2)}) collective-permute-start(bf16[4,48,3072]{2,1,0:T(8,128)(2,1)S(1)} %get-tuple-element.78), channel_id=1, source_target_pairs={{0,24},{8,0},{16,8},{24,16},{1,25},{9,1},{17,9},{25,17},{2,26},{10... | collective-permute-start | bytes 3538952 | tf_op jit(solution)/shard_map/ppermute | solution.py:599
  275.6 9.3 %collective-permute-start.29 = (bf16[48,3072]{1,0:T(8,128)(2,1)S(1)}, bf16[48,3072]{1,0:T(8,128)(2,1)S(1)}, u32[]{:S(2)}, u32[]{:S(2)}) collective-permute-start(bf16[48,3072]{1,0:T(8,128)(2,1)S(1)} %get-tuple-element.81), channel_id=1, source_target_pairs={{0,24},{8,0},{16,8},{24,16},{1,25},{9,1},{17,9},{25,17},{2,26},{10... | collective-permute-start | bytes 884744 | tf_op jit(solution)/shard_map/ppermute | solution.py:599
  279.7 10.6 %collective-permute-start.32 = (bf16[48,3072]{1,0:T(8,128)(2,1)S(1)}, bf16[48,3072]{1,0:T(8,128)(2,1)S(1)}, u32[]{:S(2)}, u32[]{:S(2)}) collective-permute-start(bf16[48,3072]{1,0:T(8,128)(2,1)S(1)} %get-tuple-element.85), channel_id=1, source_target_pairs={{0,96},{32,0},{64,32},{96,64},{1,97},{33,1},{65,33},{97,65},{2,98}... | collective-permute-start | bytes 884744 | tf_op jit(solution)/shard_map/ppermute | solution.py:599
  295.1 9.3 %collective-permute-start.36 = (bf16[16,6144]{1,0:T(8,128)(2,1)}, bf16[16,6144]{1,0:T(8,128)(2,1)}, u32[]{:S(2)}, u32[]{:S(2)}) collective-permute-start(bf16[16,6144]{1,0:T(8,128)(2,1)} %get-tuple-element.90), channel_id=1, source_target_pairs={{0,2},{1,3},{2,0},{3,1},{4,6},{5,7},{6,4},{7,5},{8,10},{9,11},{10,... | collective-permute-start | bytes 589832 | tf_op jit(solution)/shard_map/ppermute | solution.py:603
  (41 other events, 424.7 us)
Sparse Core Ops, SparseCore 0:
  9.6 74.1 all-gather.2
  85.4 38.2 all-gather.4
  127.8 63.5 reduce-scatter.1

commit v7 on v6

--- a/solution.py
+++ b/solution.py
@@ -204,7 +204,7 @@
     return lax.dot_general(a, b, (((1,), (1,)), ((), ())), preferred_element_type=F32)
 
 
-def selected_kernel(place, own, normed, weight, res, o0, o1, o2, o3, w_here, sems):
+def selected_kernel(place, own, normed, weight, res, o0, o1, o2, o3, w_here, r_here, sems, last):
     size = o0.shape[0]
     chunks = weight.shape[0] // TILE
 
@@ -213,9 +213,13 @@
         span = pl.ds(pl.multiple_of(c * TILE, TILE), TILE)
         return pltpu.make_async_copy(weight.at[span], w_here.at[slot], sems.at[slot])
 
-    for c in range(AHEAD):
+    rest = pltpu.make_async_copy(res, r_here, last)
+    copy(0).start()
+    rest.start()
+    for c in range(1, AHEAD):
         copy(c).start()
     picked = mm(place[...], normed[...]).astype(BF)
+    rest.wait()
 
     @pl.loop(0, chunks)
     def _(c):
@@ -225,7 +229,7 @@
 
         span = pl.ds(pl.multiple_of(c * TILE, TILE), TILE)
         copy(c).wait()
-        full = nt(picked, w_here[lax.rem(c, AHEAD + 1)]) + mm(own[...], res[:, span])
+        full = nt(picked, w_here[lax.rem(c, AHEAD + 1)]) + mm(own[...], r_here[:, span])
         full = full.astype(BF)
         for i, o in enumerate((o0, o1, o2, o3)):
             o[:, span] = full[i * size : (i + 1) * size]
@@ -242,11 +246,13 @@
         normed,
         weight,
         res,
-        in_specs=[VM] * 3 + [ANY, VM],
+        in_specs=[VM] * 3 + [ANY] * 2,
         out_specs=[VM] * 4,
         scratch_shapes=[
             pltpu.VMEM((AHEAD + 1, TILE, width), BF),
+            pltpu.VMEM(res.shape, BF),
             pltpu.SemaphoreType.DMA((AHEAD + 1,)),
+            pltpu.SemaphoreType.DMA,
         ],
         vmem=48,
     )
@@ -279,8 +285,7 @@
     )[0]
 
 
-def norm_kernel(a, b, c, d, gain, o0, o1, ready):
-    ready[...] = jnp.zeros_like(ready)
+def norm_kernel(a, b, c, d, gain, held, o0, o1, same):
     x = a[...].astype(F32) + b[...].astype(F32) + c[...].astype(F32) + d[...].astype(F32)
     x = x * lax.rsqrt(jnp.mean(x * x, -1, keepdims=True) + 1e-06) * gain[...]
     half = o0.shape[1]
@@ -288,11 +293,14 @@
     o1[...] = x[:, half:].astype(BF)
 
 
-def hold_kernel(held, late, same):
-    pass
-
-
-def stack_kernel(a0, a1, a2, a3, b0, b1, b2, b3, o0, o1):
+def forward_kernel(a_below, b_below, a_above, b_above, a_up, b_up, a_down, b_down):
+    a_up[...] = a_below[0:2]
+    b_up[...] = b_below[0:2]
+    a_down[...] = a_above[2:4]
+    b_down[...] = b_above[2:4]
+
+
+def stack_kernel(a0, b0, a3, b3, a1, b1, a2, b2, held, o0, o1, same):
     for i, (a, b) in enumerate(((a0, b0), (a1, b1), (a2, b2), (a3, b3))):
         o0[i] = a[...]
         o1[i] = b[...]
@@ -359,13 +367,14 @@
     return ((2 * units, units), (5 * units, units))
 
 
-def gate_up(refs_a, refs_b, x, part, stream, then=None):
+def gate_up(refs_a, refs_b, x, part_a, part_b, stream, then=None):
     rows, half = refs_a[0].shape[1:]
     each = half // TILE
-    part[...] = jnp.zeros_like(part)
+    part_a[...] = jnp.zeros_like(part_a)
+    part_b[...] = jnp.zeros_like(part_b)
 
     def body(c, weights):
-        for k, refs in enumerate((refs_a, refs_b)):
+        for k, (refs, part) in enumerate(((refs_a, part_a), (refs_b, part_b))):
 
             @pl.when(c // each == k)
             def _():
@@ -375,8 +384,7 @@
                     for i in range(ref.shape[0]):
                         x[row : row + rows, :] = ref[i, :, at]
                         row += rows
-
-        part[c // each] += nt(x[...], weights)
+                part[...] += nt(x[...], weights)
 
     stream.run(body, then)
 
@@ -401,22 +409,21 @@
     stream.run(body)
 
 
-def near_kernel(a0, a1, a2, b0, b1, b2, weights, acc, x, part, buf, sems):
+def near_kernel(a0, b0, a1, b1, a2, b2, weights, acc, x, part, buf, sems):
     rows = a0.shape[1]
     block = 4 * rows
     stream = Stream(weights, gate_up_spans(weights.shape[0] // 6), buf, sems)
     stream.begin()
-    gate_up((a0, a1, a2), (b0, b1, b2), x, part, stream)
-    acc[0 : 3 * block, :] = part[0]
+    gate_up((a0, a1, a2), (b0, b1, b2), x, acc.at[pl.ds(0, 3 * block)], part, stream)
     acc[3 * block :, :] = jnp.zeros((block, acc.shape[1]), F32)
     for y in range(3):
         for row, z in by_y(rows, y):
             at = y * block + z * rows
-            acc[row : row + rows, :] += part[1, at : at + rows, :]
+            acc[row : row + rows, :] += part[at : at + rows, :]
 
 
 def far_kernel(
-    acc, a3, a4, b3, b4, weights, hidden, oa3, oa4, ob3, ob4, x, part, own, value, buf, sems, dbuf, dsems
+    acc, a3, b3, a4, b4, weights, hidden, oa3, oa4, ob3, ob4, x, part, own, value, buf, sems, dbuf, dsems
 ):
     rows = a3.shape[1]
     block = 4 * rows
@@ -424,7 +431,7 @@
     stream = Stream(weights, gate_up_spans(units), buf, sems)
     downs = Stream(weights, down_spans(units), dbuf, dsems)
     stream.begin()
-    gate_up((a3, a4), (b3, b4), x, part, stream, downs)
+    gate_up((a3, a4), (b3, b4), x, part.at[0], part.at[1], stream, downs)
     own[...] = acc[...]
     own[3 * block :, :] += part[0]
     for row, z in by_y(rows, 3):
@@ -476,7 +483,7 @@
         out_specs=[VM],
         scratch_shapes=[
             pltpu.VMEM((12 * rows, TILE), BF),
-            pltpu.VMEM((2, 12 * rows, wide), F32),
+            pltpu.VMEM((12 * rows, wide), F32),
             *slots(wide, 2),
         ],
         cost_estimate=cost(2 * 12 * rows * wide * weights.shape[1]),
@@ -504,7 +511,7 @@
             *slots(wide, 2),
             *slots(wide // 2, 2),
         ],
-        vmem=36,
+        vmem=32,
     )
 
 
@@ -520,11 +527,11 @@
         out_specs=[VM] * 6,
         scratch_shapes=[pltpu.VMEM((2, 12 * rows, wide), BF), *slots(wide, 2)],
         cost_estimate=cost(2 * 12 * rows * wide * weights.shape[1]),
-        vmem=36,
-    )
-
-
-def fold_kernel(bl0, ab0, up0, dn0, bl1, ab1, up1, dn1, ob0, oa0, ob1, oa1):
+        vmem=32,
+    )
+
+
+def fold_kernel(bl0, ab0, bl1, ab1, up0, up1, dn0, dn1, ob0, oa0, ob1, oa1):
     for below, above, up, down, o_below, o_above in (
         (bl0, ab0, up0, dn0, ob0, oa0),
         (bl1, ab1, up1, dn1, ob1, oa1),
@@ -535,14 +542,14 @@
         o_below[2:4] = (below[2:4].astype(F32) + down[...].astype(F32)).astype(BF)
 
 
-def phase_kernel(m0, u0, d0, m1, u1, d1, *outs):
+def phase_kernel(m0, m1, u0, u1, d0, d1, *outs):
     for k, (m, u, d) in enumerate(((m0, u0, d0), (m1, u1, d1))):
         total = m[...].astype(F32) + u[...].astype(F32) + d[...].astype(F32)
         for i in range(4):
             outs[4 * k + i][...] = total[i].astype(BF)
 
 
-def served_kernel(cap, a0, a1, a2, a3, b0, b1, b2, b3, o0, o1, o2, o3):
+def served_kernel(cap, a0, b0, a3, b3, a1, b1, a2, b2, o0, o1, o2, o3):
     half = a0.shape[1]
     rows = a0.shape[0]
     padded = o0.shape[0]
@@ -603,10 +610,6 @@
     return lax.ppermute(x, axis, ring(4, 2))
 
 
-def far_sides(below, above, axis):
-    return up_one(below[:2], axis), down_one(above[2:], axis)
-
-
 def shards(
     queries,
     keys,
@@ -655,55 +658,60 @@
     whole = whole_projection(normed, weight_out, here)
 
     size = here.shape[0]
-    a0, b0, ready = call(
+    a0, b0, whole = call(
         norm_kernel,
         "selected_norm",
-        [((size, half), BF)] * 2 + [((8, 128), F32)],
+        [((size, half), BF)] * 2 + [(whole.shape, BF)],
         here,
         up_one(to_up, "x"),
         down_one(to_down, "x"),
         across(to_far, "x"),
         gain,
-        in_specs=[VM] * 5,
-        out_specs=[VM] * 3,
-    )
-
-    whole = call(
-        hold_kernel,
-        "hold",
-        [(whole.shape, BF)],
         whole,
-        ready,
-        in_specs=[ANY, VM],
-        out_specs=[ANY],
-        input_output_aliases={0: 0},
-        vmem=61,
-    )[0]
+        in_specs=[VM] * 5 + [ANY],
+        out_specs=[VM] * 2 + [ANY],
+        input_output_aliases={5: 2},
+        vmem=58,
+    )
+
     mixed = lax.psum_scatter(whole, "x", scatter_dimension=0, tiled=True)
 
-    a_across, b_across = across(a0, "y"), across(b0, "z")
-    a4, b4 = call(
+    a4, b4, weights = call(
         stack_kernel,
         "stack",
-        [((4, size, half), BF)] * 2,
+        [((4, size, half), BF)] * 2 + [(weights.shape, BF)],
         a0,
+        b0,
+        across(a0, "y"),
+        across(b0, "z"),
         up_one(a0, "y"),
+        up_one(b0, "z"),
         down_one(a0, "y"),
-        a_across,
-        b0,
-        up_one(b0, "z"),
         down_one(b0, "z"),
-        b_across,
-        in_specs=[VM] * 8,
-        out_specs=[VM] * 2,
-        vmem=16,
-    )
-    a_below, a_above = up_one(a4, "z"), down_one(a4, "z")
-    b_below, b_above = up_one(b4, "y"), down_one(b4, "y")
-    a_far, b_far = far_sides(a_below, a_above, "z"), far_sides(b_below, b_above, "y")
-
-    acc = near((a4, a_below, a_above, b4, b_below, b_above), weights)
-    hidden, *ends = far(acc, (*a_far, *b_far), weights)
+        weights,
+        in_specs=[VM] * 8 + [ANY],
+        out_specs=[VM] * 2 + [ANY],
+        input_output_aliases={8: 2},
+        vmem=50,
+    )
+    a_below, b_below = up_one(a4, "z"), up_one(b4, "y")
+    a_above, b_above = down_one(a4, "z"), down_one(b4, "y")
+    a_up, b_up, a_down, b_down = call(
+        forward_kernel,
+        "forward",
+        [((2, size, half), BF)] * 4,
+        a_below,
+        b_below,
+        a_above,
+        b_above,
+        in_specs=[VM] * 4,
+        out_specs=[VM] * 4,
+        vmem=8,
+    )
+    ends_in = (up_one(a_up, "z"), up_one(b_up, "y"), down_one(a_down, "z"), down_one(b_down, "y"))
+
+    acc = near((a4, b4, a_below, b_below, a_above, b_above), weights)
+    hidden, *ends = far(acc, ends_in, weights)
     body = rest(hidden, weights, size)
     oa, ob = (*body[:3], *ends[:2]), (*body[3:], *ends[2:])
     a_below, a_above, b_below, b_above = call(
@@ -712,11 +720,11 @@
         [((4, size, half), BF)] * 4,
         oa[1],
         oa[2],
-        up_one(oa[3], "z"),
-        down_one(oa[4], "z"),
         ob[1],
         ob[2],
+        up_one(oa[3], "z"),
         up_one(ob[3], "y"),
+        down_one(oa[4], "z"),
         down_one(ob[4], "y"),
         in_specs=[VM] * 8,
         out_specs=[VM] * 4,
@@ -727,10 +735,10 @@
         "phase",
         [((size, half), BF)] * 8,
         oa[0],
+        ob[0],
         up_one(a_above, "z"),
+        up_one(b_above, "y"),
         down_one(a_below, "z"),
-        ob[0],
-        up_one(b_above, "y"),
         down_one(b_below, "y"),
         in_specs=[VM] * 6,
         out_specs=[VM] * 8,
@@ -741,13 +749,13 @@
         "served",
         [((16, model), BF)] * 4,
         parts[0],
+        parts[4],
+        across(parts[3], "y"),
+        across(parts[7], "z"),
         up_one(parts[2], "y"),
+        up_one(parts[6], "z"),
         down_one(parts[1], "y"),
-        across(parts[3], "y"),
-        parts[4],
-        up_one(parts[6], "z"),
         down_one(parts[5], "z"),
-        across(parts[7], "z"),
         in_specs=[VM] * 8,
         out_specs=[VM] * 4,
     )

time: 315 us -> 304 us (0.965)
  local copies, waits for them, and re-layouts: 24.9 us -> 9.84 us
  waiting for transfers between devices: 95.6 us -> 103 us
  starting transfers between devices: 70.5 us -> 64.8 us
    ppermute x14, waiting for transfers between devices: 13.5 us -> 41.5 us  [down_one(): return lax.ppermute(x, axis, ring(4, -1))]
    ppermute x14, waiting for transfers between devices: 48.8 us -> 32.8 us  [up_one(): return lax.ppermute(x, axis, ring(4, 1))]
    unnamed x65 -> x41, local copies, waits for them, and re-layouts: 21.1 us -> 9.59 us
    ppermute x6, starting transfers between devices: 15.9 us -> 8.83 us  [across(): return lax.ppermute(x, axis, ring(4, 2))]
    ppermute x6, waiting for transfers between devices: 11.9 us -> 6.57 us  [across(): return lax.ppermute(x, axis, ring(4, 2))]
    ppermute x14, starting transfers between devices: 5.98 us -> 9.92 us  [up_one(): return lax.ppermute(x, axis, ring(4, 1))]
    ppermute x14, starting transfers between devices: 40.1 us -> 36.4 us  [down_one(): return lax.ppermute(x, axis, ring(4, -1))]
    slice x4 -> x0, local copies, waits for them, and re-layouts: 3.51 us -> none  [far_sides(): return (up_one(below[:2], axis), down_one(above[2:], axis))]
  transfers between devices with their start and end apart: 41 -> 41, of which waited for: 19 -> 21; matrix products, arithmetic and copies ran while one was open for 4% -> 3% of each run, Pallas kernels for 24% -> 26%
where the time goes in v7:
time: 304 us; the launch traced here: 303 us
  waiting for transfers between devices  103 us (34%)
  Pallas kernels  80.4 us (26%)
  starting transfers between devices  64.8 us (21%)
  blocking collectives  21.8 us (7%)
  between operations  13.4 us (4%)
  local copies, waits for them, and re-layouts  9.84 us (3%)
  other arithmetic  9.24 us (3%)
    pallas_call x14, Pallas kernels, call(): pl.pallas_call(kernel, out_shape=[jax.ShapeDtypeStruct(s, d) for s, d in...  70.3 us
    ppermute x14, waiting for transfers between devices, down_one(): return lax.ppermute(x, axis, ring(4, -1))  41.5 us
    ppermute x14, starting transfers between devices, down_one(): return lax.ppermute(x, axis, ring(4, -1))  36.4 us
    ppermute x14, waiting for transfers between devices, up_one(): return lax.ppermute(x, axis, ring(4, 1))  32.8 us
    all_to_all x1, blocking collectives, shards(): arrived = lax.all_to_all(states, SEQ, 0, 0, tiled=True)  21.8 us
    all_gather x1, waiting for transfers between devices, shards(): weight_out = lax.all_gather(out_weight.T, SEQ, axis=0, tiled=True)  11.2 us
    ppermute x14, starting transfers between devices, up_one(): return lax.ppermute(x, axis, ring(4, 1))  9.92 us
    unnamed x41, local copies, waits for them, and re-layouts  9.59 us
  transfers between devices with their start and end apart: 41, of which 21 were waited for; matrix products, arithmetic and copies ran while one was open for 3% of the time, Pallas kernels for 26%

profile of v7, /device:TPU:0, one launch (start us, length us, event | category | flops | bytes accessed | tf_op | source)
XLA Modules:
  0.0 302.9 jit_solution(8302257308351892674)
XLA Ops:
  7.3 9.2 %pad_maximum_fusion = bf16[864,6144]{1,0:T(8,128)(2,1)} fusion(bf16[288,6144]{1,0:T(8,128)(2,1)} %bitcast.30, bf16[288,6144]{1,0:T(8,128)(2,1)} %bitcast.31, bf16[288,6144]{1,0:T(8,128)(2,1)} %bitcast.32), kind=kLoop, calls=%fused_computation | loop fusion | flops 31850496 | bytes 21233664 | tf_op jit(solution)/shard_map/concatenate | solution.py:637
  16.6 7.1 %local_attention.1 = (f32[2,256,1024]{2,1,0:T(8,128)}, bf16[32,80,128]{2,1,0:T(8,128)(2,1)}, f32[2,256,8]{2,1,0:T(8,128)}) custom-call(bf16[2,256,1024]{2,1,0:T(8,128)(2,1)} %q_ref.3, bf16[2,256,1024]{2,1,0:T(8,128)(2,1)} %k_ref.1, bf16[2,256,1024]{2,1,0:T(8,128)(2,1)} %v_ref.1, f32[2,8,256]{2,1,0:T(8,128)} %bitcast.34), custom_call_target="tpu_custom_call" | custom-call | tf_op jit(solution)/shard_map/local_attention/pallas_call | solution.py:84
  23.7 21.8 %all_to_all.10.in_ref = bf16[32,80,128]{2,1,0:T(8,128)(2,1)S(1)} all-to-all(bf16[32,80,128]{2,1,0:T(8,128)(2,1)} %get-tuple-element.57), channel_id=1, replica_groups=mesh['z'=4,'y'=4,'core'=2,'x'=4] {'z','y','core'}, dimensions={0} | all-to-all | bytes 1310720 | tf_op jit(solution)/shard_map/all_to_all | solution.py:646
  46.4 3.9 %all-to-all-start.1 = ((bf16[32,64,128]{2,1,0:T(8,128)(2,1)}), bf16[32,64,128]{2,1,0:T(8,128)(2,1)S(1)}, u32[]{:S(2)}, u32[]{:S(2)}) async-start(bf16[32,64,128]{2,1,0:T(8,128)(2,1)} %state_prefix.1), calls=%async_computation.1 | async-start | bytes 1048576 | tf_op jit(solution)/shard_map/all_to_all | solution.py:647
  60.1 7.8 %all-to-all-done.1 = bf16[32,64,128]{2,1,0:T(8,128)(2,1)S(1)} async-done(((bf16[32,64,128]{2,1,0:T(8,128)(2,1)}), bf16[32,64,128]{2,1,0:T(8,128)(2,1)S(1)}, u32[]{:S(2)}, u32[]{:S(2)}) %all-to-all-start.1) | async-done | bytes 524320 | tf_op jit(solution)/shard_map/all_to_all | solution.py:647
  72.7 11.2 %all-gather.3.cloned.1.call-done.weight.weight_ref = bf16[6144,1024]{1,0:T(8,128)(2,1)} async-done(((bf16[192,1024]{1,0:T(8,128)(2,1)}), bf16[6144,1024]{1,0:T(8,128)(2,1)}) %all-gather.3.cloned.1.call-update) | async-done | bytes 12582928 | tf_op jit(solution)/shard_map/all_gather | solution.py:636
  86.1 7.1 %selected_projection.1 = (bf16[48,6144]{1,0:T(8,128)(2,1)S(1)}, bf16[48,6144]{1,0:T(8,128)(2,1)S(1)}, bf16[48,6144]{1,0:T(8,128)(2,1)S(1)}, bf16[48,6144]{1,0:T(8,128)(2,1)S(1)}) custom-call(bf16[192,512]{1,0:T(8,128)(2,1)S(1)} %copy-done.13, bf16[192,128]{1,0:T(8,128)(2,1)S(1)} %get-tuple-element.54.own, bf16[512,1024]{1,0:T(8,128)(2,1)S(1)} %bitcast.19, ...), custom_call_target="tpu_custom_call" | custom-call | tf_op jit(solution)/shard_map/selected_projection/pallas_call | solution.py:157
  99.1 14.8 %whole_projection.1.held = bf16[512,6144]{1,0:T(8,128)(2,1)} custom-call(bf16[512,1024]{1,0:T(8,128)(2,1)} %bitcast.18, bf16[6144,1024]{1,0:T(8,128)(2,1)} %all-gather.3.cloned.1.call-done.weight.weight_ref, bf16[48,6144]{1,0:T(8,128)(2,1)} %copy-done.7), custom_call_target="tpu_custom_call" | custom-call | flops 6442450944 | bytes 25165824 | tf_op jit(solution)/shard_map/whole_projection/pallas_call | solution.py:157
  113.9 8.8 %collective-permute-done.4.c = bf16[48,6144]{1,0:T(8,128)(2,1)S(1)} collective-permute-done((bf16[48,6144]{1,0:T(8,128)(2,1)S(1)}, bf16[48,6144]{1,0:T(8,128)(2,1)S(1)}, u32[]{:S(2)}, u32[]{:S(2)}) %collective-permute-start.4) | collective-permute-done | bytes 589856 | tf_op jit(solution)/shard_map/ppermute | solution.py:606
  125.2 3.0 selected_norm.1
  129.1 2.7 collective-permute-start.10
  136.2 7.9 %collective-permute-done.10.a2 = bf16[48,3072]{1,0:T(8,128)(2,1)S(1)} collective-permute-done((bf16[48,3072]{1,0:T(8,128)(2,1)S(1)}, bf16[48,3072]{1,0:T(8,128)(2,1)S(1)}, u32[]{:S(2)}, u32[]{:S(2)}) %collective-permute-start.10) | collective-permute-done | bytes 294944 | tf_op jit(solution)/shard_map/ppermute | solution.py:606
  144.1 3.4 %collective-permute-done.8.a1 = bf16[48,3072]{1,0:T(8,128)(2,1)S(1)} collective-permute-done((bf16[48,3072]{1,0:T(8,128)(2,1)S(1)}, bf16[48,3072]{1,0:T(8,128)(2,1)S(1)}, u32[]{:S(2)}, u32[]{:S(2)}) %collective-permute-start.8) | collective-permute-done | bytes 294944 | tf_op jit(solution)/shard_map/ppermute | solution.py:602
  147.5 4.9 %collective-permute-done.7.b3 = bf16[48,3072]{1,0:T(8,128)(2,1)} collective-permute-done((bf16[48,3072]{1,0:T(8,128)(2,1)S(1)}, bf16[48,3072]{1,0:T(8,128)(2,1)}, u32[]{:S(2)}, u32[]{:S(2)}) %collective-permute-start.7) | collective-permute-done | bytes 294944 | tf_op jit(solution)/shard_map/ppermute | solution.py:610
  156.7 5.5 %collective-permute-start.15 = (bf16[4,48,3072]{2,1,0:T(8,128)(2,1)}, bf16[4,48,3072]{2,1,0:T(8,128)(2,1)S(1)}, u32[]{:S(2)}, u32[]{:S(2)}) collective-permute-start(bf16[4,48,3072]{2,1,0:T(8,128)(2,1)} %get-tuple-element.66.b0), channel_id=1, source_target_pairs={{0,24},{8,0},{16,8},{24,16},{1,25},{9,1},{17,9},{25,17},{2,26},{10... | collective-permute-start | bytes 3538952 | tf_op jit(solution)/shard_map/ppermute | solution.py:606
  162.2 14.0 %collective-permute-done.14.a2.a_above = bf16[4,48,3072]{2,1,0:T(8,128)(2,1)S(1)} collective-permute-done((bf16[4,48,3072]{2,1,0:T(8,128)(2,1)S(1)}, bf16[4,48,3072]{2,1,0:T(8,128)(2,1)S(1)}, u32[]{:S(2)}, u32[]{:S(2)}) %collective-permute-start.14) | collective-permute-done | bytes 1179680 | tf_op jit(solution)/shard_map/ppermute | solution.py:606
  176.2 4.3 %collective-permute-done.12.a1.a_below = bf16[4,48,3072]{2,1,0:T(8,128)(2,1)S(1)} collective-permute-done((bf16[4,48,3072]{2,1,0:T(8,128)(2,1)S(1)}, bf16[4,48,3072]{2,1,0:T(8,128)(2,1)S(1)}, u32[]{:S(2)}, u32[]{:S(2)}) %collective-permute-start.12) | collective-permute-done | bytes 1179680 | tf_op jit(solution)/shard_map/ppermute | solution.py:602
  180.4 3.0 %collective-permute-done.13.b1.b_below = bf16[4,48,3072]{2,1,0:T(8,128)(2,1)S(1)} collective-permute-done((bf16[4,48,3072]{2,1,0:T(8,128)(2,1)}, bf16[4,48,3072]{2,1,0:T(8,128)(2,1)S(1)}, u32[]{:S(2)}, u32[]{:S(2)}) %collective-permute-start.13) | collective-permute-done | bytes 1179680 | tf_op jit(solution)/shard_map/ppermute | solution.py:602
  183.8 3.1 %collective-permute-start.18 = (bf16[2,48,3072]{2,1,0:T(8,128)(2,1)S(1)}, bf16[2,48,3072]{2,1,0:T(8,128)(2,1)S(1)}, u32[]{:S(2)}, u32[]{:S(2)}) collective-permute-start(bf16[2,48,3072]{2,1,0:T(8,128)(2,1)S(1)} %get-tuple-element.70), channel_id=1, source_target_pairs={{0,96},{32,0},{64,32},{96,64},{1,97},{33,1},{65,33},{97,65},{2,98}... | collective-permute-start | bytes 1769480 | tf_op jit(solution)/shard_map/ppermute | solution.py:606
  186.9 3.2 %collective-permute-start.19 = (bf16[2,48,3072]{2,1,0:T(8,128)(2,1)S(1)}, bf16[2,48,3072]{2,1,0:T(8,128)(2,1)S(1)}, u32[]{:S(2)}, u32[]{:S(2)}) collective-permute-start(bf16[2,48,3072]{2,1,0:T(8,128)(2,1)S(1)} %get-tuple-element.71), channel_id=1, source_target_pairs={{0,24},{8,0},{16,8},{24,16},{1,25},{9,1},{17,9},{25,17},{2,26},{10... | collective-permute-start | bytes 1769480 | tf_op jit(solution)/shard_map/ppermute | solution.py:606
  190.2 13.6 %near_rows.1.acc = f32[768,1152]{1,0:T(8,128)S(1)} custom-call(bf16[4,48,3072]{2,1,0:T(8,128)(2,1)S(1)} %get-tuple-element.65.a0, bf16[4,48,3072]{2,1,0:T(8,128)(2,1)S(1)} %copy-done.6, bf16[4,48,3072]{2,1,0:T(8,128)(2,1)S(1)} %collective-permute-done.12.a1.a_below, bf16[4,48,3072]{2,1,0:T(8,128)(2,1)S(1)} %collective-permute-done.13.b1.b_below, ...), custom_call_target="tpu_custom_call" | custom-call | flops 8153726976 | bytes 1048576 | tf_op jit(solution)/shard_map/near_rows/pallas_call | solution.py:157
  203.8 13.1 %far_rows.1 = (bf16[768,576]{1,0:T(8,128)(2,1)S(1)}, bf16[2,48,3072]{2,1,0:T(8,128)(2,1)S(1)}, bf16[2,48,3072]{2,1,0:T(8,128)(2,1)S(1)}, bf16[2,48,3072]{2,1,0:T(8,128)(2,1)S(1)}, bf16[2,48,3072]{2,1,0:T(8,128)(2,1)S(1)}) custom-call(f32[768,1152]{1,0:T(8,128)S(1)} %near_rows.1.acc, bf16[2,48,3072]{2,1,0:T(8,128)(2,1)S(1)} %collective-permute-done.16.a3, ...), custom_call_target="tpu_custom_call" | custom-call | tf_op jit(solution)/shard_map/far_rows/pallas_call | solution.py:157
  217.0 3.1 %collective-permute-start.22 = (bf16[2,48,3072]{2,1,0:T(8,128)(2,1)S(1)}, bf16[2,48,3072]{2,1,0:T(8,128)(2,1)S(1)}, u32[]{:S(2)}, u32[]{:S(2)}) collective-permute-start(bf16[2,48,3072]{2,1,0:T(8,128)(2,1)S(1)} %get-tuple-element.79), channel_id=1, source_target_pairs={{0,96},{32,0},{64,32},{96,64},{1,97},{33,1},{65,33},{97,65},{2,98}... | collective-permute-start | bytes 1769480 | tf_op jit(solution)/shard_map/ppermute | solution.py:606
  220.2 3.2 %collective-permute-start.23 = (bf16[2,48,3072]{2,1,0:T(8,128)(2,1)S(1)}, bf16[2,48,3072]{2,1,0:T(8,128)(2,1)S(1)}, u32[]{:S(2)}, u32[]{:S(2)}) collective-permute-start(bf16[2,48,3072]{2,1,0:T(8,128)(2,1)S(1)} %get-tuple-element.80), channel_id=1, source_target_pairs={{0,24},{8,0},{16,8},{24,16},{1,25},{9,1},{17,9},{25,17},{2,26},{10... | collective-permute-start | bytes 1769480 | tf_op jit(solution)/shard_map/ppermute | solution.py:606
  223.4 8.6 %rest_rows.1 = (bf16[4,48,3072]{2,1,0:T(8,128)(2,1)S(1)}, bf16[4,48,3072]{2,1,0:T(8,128)(2,1)S(1)}, bf16[4,48,3072]{2,1,0:T(8,128)(2,1)S(1)}, bf16[4,48,3072]{2,...) custom-call(bf16[768,576]{1,0:T(8,128)(2,1)S(1)} %get-tuple-element.72.hidden, ...), custom_call_target="tpu_custom_call" | custom-call | flops 4076863488 | bytes 1048576 | tf_op jit(solution)/shard_map/rest_rows/pallas_call | solution.py:157
  232.0 4.7 %collective-permute-done.23.dn1 = bf16[2,48,3072]{2,1,0:T(8,128)(2,1)S(1)} collective-permute-done((bf16[2,48,3072]{2,1,0:T(8,128)(2,1)S(1)}, bf16[2,48,3072]{2,1,0:T(8,128)(2,1)S(1)}, u32[]{:S(2)}, u32[]{:S(2)}) %collective-permute-start.23) | collective-permute-done | bytes 589856 | tf_op jit(solution)/shard_map/ppermute | solution.py:606
  237.5 3.8 %collective-permute-start.27 = (bf16[4,48,3072]{2,1,0:T(8,128)(2,1)S(1)}, bf16[4,48,3072]{2,1,0:T(8,128)(2,1)S(1)}, u32[]{:S(2)}, u32[]{:S(2)}) collective-permute-start(bf16[4,48,3072]{2,1,0:T(8,128)(2,1)S(1)} %get-tuple-element.88), channel_id=1, source_target_pairs={{0,24},{8,0},{16,8},{24,16},{1,25},{9,1},{17,9},{25,17},{2,26},{10... | collective-permute-start | bytes 3538952 | tf_op jit(solution)/shard_map/ppermute | solution.py:606
  241.3 3.1 %collective-permute-start.26 = (bf16[4,48,3072]{2,1,0:T(8,128)(2,1)S(1)}, bf16[4,48,3072]{2,1,0:T(8,128)(2,1)S(1)}, u32[]{:S(2)}, u32[]{:S(2)}) collective-permute-start(bf16[4,48,3072]{2,1,0:T(8,128)(2,1)S(1)} %get-tuple-element.81.late), channel_id=1, source_target_pairs={{0,96},{32,0},{64,32},{96,64},{1,97},{33,1},{65,33},{97,65},{2,98}... | collective-permute-start | bytes 3538952 | tf_op jit(solution)/shard_map/ppermute | solution.py:606
  244.3 16.8 %collective-permute-done.24.u0 = bf16[4,48,3072]{2,1,0:T(8,128)(2,1)S(1)} collective-permute-done((bf16[4,48,3072]{2,1,0:T(8,128)(2,1)S(1)}, bf16[4,48,3072]{2,1,0:T(8,128)(2,1)S(1)}, u32[]{:S(2)}, u32[]{:S(2)}) %collective-permute-start.24) | collective-permute-done | bytes 1179680 | tf_op jit(solution)/shard_map/ppermute | solution.py:602
  274.6 2.8 collective-permute-start.33
  289.6 4.0 %collective-permute-done.35.b2 = bf16[16,6144]{1,0:T(8,128)(2,1)} collective-permute-done((bf16[16,6144]{1,0:T(8,128)(2,1)}, bf16[16,6144]{1,0:T(8,128)(2,1)}, u32[]{:S(2)}, u32[]{:S(2)}) %collective-permute-start.35) | collective-permute-done | bytes 196640 | tf_op jit(solution)/shard_map/ppermute | solution.py:602
  293.5 2.8 combine.1
  (117 shorter events, 63.0 us)
Async XLA Ops:
  6.5 77.4 %all-gather.3.cloned.1.call-start = ((), (), s32[]{:S(2)}) async-start(), calls=%async_computation.3 | async-start | bytes 12976128 | tf_op jit(solution)/shard_map/all_gather | solution.py:636
  7.3 136.8 %all-gather.5.cloned.1.call-start = ((), (), s32[]{:S(2)}) async-start(), calls=%async_computation.5 | async-start | bytes 31850496 | tf_op jit(solution)/shard_map/all_gather | solution.py:638
  46.4 21.5 %all-to-all-start.1 = ((bf16[32,64,128]{2,1,0:T(8,128)(2,1)}), bf16[32,64,128]{2,1,0:T(8,128)(2,1)S(1)}, u32[]{:S(2)}, u32[]{:S(2)}) async-start(bf16[32,64,128]{2,1,0:T(8,128)(2,1)} %state_prefix.1), calls=%async_computation.1 | async-start | bytes 1048576 | tf_op jit(solution)/shard_map/all_to_all | solution.py:647
  50.3 235.9 %reduce-scatter.2.cloned.1.call-start = ((), (), s32[]{:S(2)}) async-start(), calls=%async_computation.4 | async-start | bytes 7864320 | tf_op jit(solution)/shard_map/reduce_scatter | solution.py:677
  94.1 19.8 %collective-permute-start.3 = (bf16[48,6144]{1,0:T(8,128)(2,1)S(1)}, bf16[48,6144]{1,0:T(8,128)(2,1)S(1)}, u32[]{:S(2)}, u32[]{:S(2)}) collective-permute-start(bf16[48,6144]{1,0:T(8,128)(2,1)S(1)} %get-tuple-element.59), channel_id=1, source_target_pairs={{0,1},{1,2},{2,3},{3,0},{4,5},{5,6},{6,7},{7,4},{8,9},{9,10},{10,1... | collective-permute-start | bytes 1769480 | tf_op jit(solution)/shard_map/ppermute | solution.py:602
  95.6 27.2 %collective-permute-start.4 = (bf16[48,6144]{1,0:T(8,128)(2,1)S(1)}, bf16[48,6144]{1,0:T(8,128)(2,1)S(1)}, u32[]{:S(2)}, u32[]{:S(2)}) collective-permute-start(bf16[48,6144]{1,0:T(8,128)(2,1)S(1)} %get-tuple-element.60), channel_id=1, source_target_pairs={{0,3},{1,0},{2,1},{3,2},{4,7},{5,4},{6,5},{7,6},{8,11},{9,8},{10,9... | collective-permute-start | bytes 1769480 | tf_op jit(solution)/shard_map/ppermute | solution.py:606
  97.3 27.0 %collective-permute-start.5 = (bf16[48,6144]{1,0:T(8,128)(2,1)S(1)}, bf16[48,6144]{1,0:T(8,128)(2,1)S(1)}, u32[]{:S(2)}, u32[]{:S(2)}) collective-permute-start(bf16[48,6144]{1,0:T(8,128)(2,1)S(1)} %get-tuple-element.61), channel_id=1, source_target_pairs={{0,2},{1,3},{2,0},{3,1},{4,6},{5,7},{6,4},{7,5},{8,10},{9,11},{10,... | collective-permute-start | bytes 1769480 | tf_op jit(solution)/shard_map/ppermute | solution.py:610
  129.1 15.0 %collective-permute-start.10 = (bf16[48,3072]{1,0:T(8,128)(2,1)S(1)}, bf16[48,3072]{1,0:T(8,128)(2,1)S(1)}, u32[]{:S(2)}, u32[]{:S(2)}) collective-permute-start(bf16[48,3072]{1,0:T(8,128)(2,1)S(1)} %copy-done.9), channel_id=1, source_target_pairs={{0,24},{8,0},{16,8},{24,16},{1,25},{9,1},{17,9},{25,17},{2,26},{10... | collective-permute-start | bytes 884744 | tf_op jit(solution)/shard_map/ppermute | solution.py:606
  131.9 15.6 %collective-permute-start.8 = (bf16[48,3072]{1,0:T(8,128)(2,1)S(1)}, bf16[48,3072]{1,0:T(8,128)(2,1)S(1)}, u32[]{:S(2)}, u32[]{:S(2)}) collective-permute-start(bf16[48,3072]{1,0:T(8,128)(2,1)S(1)} %copy-done.9), channel_id=1, source_target_pairs={{0,8},{8,16},{16,24},{24,0},{1,9},{9,17},{17,25},{25,1},{2,10},{10... | collective-permute-start | bytes 884744 | tf_op jit(solution)/shard_map/ppermute | solution.py:602
  131.9 15.6 %collective-permute-start.6 = (bf16[48,3072]{1,0:T(8,128)(2,1)S(1)}, bf16[48,3072]{1,0:T(8,128)(2,1)S(1)}, u32[]{:S(2)}, u32[]{:S(2)}) collective-permute-start(bf16[48,3072]{1,0:T(8,128)(2,1)S(1)} %copy-done.9), channel_id=1, source_target_pairs={{0,16},{8,24},{16,0},{24,8},{1,17},{9,25},{17,1},{25,9},{2,18},{10... | collective-permute-start | bytes 884744 | tf_op jit(solution)/shard_map/ppermute | solution.py:610
  134.2 13.3 %collective-permute-start.11 = (bf16[48,3072]{1,0:T(8,128)(2,1)S(1)}, bf16[48,3072]{1,0:T(8,128)(2,1)S(1)}, u32[]{:S(2)}, u32[]{:S(2)}) collective-permute-start(bf16[48,3072]{1,0:T(8,128)(2,1)S(1)} %copy-done.10), channel_id=1, source_target_pairs={{0,96},{32,0},{64,32},{96,64},{1,97},{33,1},{65,33},{97,65},{2,98}... | collective-permute-start | bytes 884744 | tf_op jit(solution)/shard_map/ppermute | solution.py:606
  135.0 12.5 %collective-permute-start.9 = (bf16[48,3072]{1,0:T(8,128)(2,1)S(1)}, bf16[48,3072]{1,0:T(8,128)(2,1)}, u32[]{:S(2)}, u32[]{:S(2)}) collective-permute-start(bf16[48,3072]{1,0:T(8,128)(2,1)S(1)} %copy-done.10), channel_id=1, source_target_pairs={{0,32},{32,64},{64,96},{96,0},{1,33},{33,65},{65,97},{97,1},{2,34}... | collective-permute-start | bytes 884744 | tf_op jit(solution)/shard_map/ppermute | solution.py:602
  154.6 21.5 %collective-permute-start.14 = (bf16[4,48,3072]{2,1,0:T(8,128)(2,1)S(1)}, bf16[4,48,3072]{2,1,0:T(8,128)(2,1)S(1)}, u32[]{:S(2)}, u32[]{:S(2)}) collective-permute-start(bf16[4,48,3072]{2,1,0:T(8,128)(2,1)S(1)} %get-tuple-element.65.a0), channel_id=1, source_target_pairs={{0,96},{32,0},{64,32},{96,64},{1,97},{33,1},{65,33},{97,65},{2,98}... | collective-permute-start | bytes 3538952 | tf_op jit(solution)/shard_map/ppermute | solution.py:606
  154.6 25.8 %collective-permute-start.12 = (bf16[4,48,3072]{2,1,0:T(8,128)(2,1)S(1)}, bf16[4,48,3072]{2,1,0:T(8,128)(2,1)S(1)}, u32[]{:S(2)}, u32[]{:S(2)}) collective-permute-start(bf16[4,48,3072]{2,1,0:T(8,128)(2,1)S(1)} %get-tuple-element.65.a0), channel_id=1, source_target_pairs={{0,32},{32,64},{64,96},{96,0},{1,33},{33,65},{65,97},{97,1},{2,34}... | collective-permute-start | bytes 3538952 | tf_op jit(solution)/shard_map/ppermute | solution.py:602
  156.7 23.8 %collective-permute-start.15 = (bf16[4,48,3072]{2,1,0:T(8,128)(2,1)}, bf16[4,48,3072]{2,1,0:T(8,128)(2,1)S(1)}, u32[]{:S(2)}, u32[]{:S(2)}) collective-permute-start(bf16[4,48,3072]{2,1,0:T(8,128)(2,1)} %get-tuple-element.66.b0), channel_id=1, source_target_pairs={{0,24},{8,0},{16,8},{24,16},{1,25},{9,1},{17,9},{25,17},{2,26},{10... | collective-permute-start | bytes 3538952 | tf_op jit(solution)/shard_map/ppermute | solution.py:606
  162.2 21.3 %collective-permute-start.13 = (bf16[4,48,3072]{2,1,0:T(8,128)(2,1)}, bf16[4,48,3072]{2,1,0:T(8,128)(2,1)S(1)}, u32[]{:S(2)}, u32[]{:S(2)}) collective-permute-start(bf16[4,48,3072]{2,1,0:T(8,128)(2,1)} %get-tuple-element.66.b0), channel_id=1, source_target_pairs={{0,8},{8,16},{16,24},{24,0},{1,9},{9,17},{17,25},{25,1},{2,10},{10... | collective-permute-start | bytes 3538952 | tf_op jit(solution)/shard_map/ppermute | solution.py:602
  183.6 20.1 %collective-permute-start.16 = (bf16[2,48,3072]{2,1,0:T(8,128)(2,1)S(1)}, bf16[2,48,3072]{2,1,0:T(8,128)(2,1)S(1)}, u32[]{:S(2)}, u32[]{:S(2)}) collective-permute-start(bf16[2,48,3072]{2,1,0:T(8,128)(2,1)S(1)} %get-tuple-element.68), channel_id=1, source_target_pairs={{0,32},{32,64},{64,96},{96,0},{1,33},{33,65},{65,97},{97,1},{2,34}... | collective-permute-start | bytes 1769480 | tf_op jit(solution)/shard_map/ppermute | solution.py:602
  183.7 20.1 %collective-permute-start.17 = (bf16[2,48,3072]{2,1,0:T(8,128)(2,1)S(1)}, bf16[2,48,3072]{2,1,0:T(8,128)(2,1)S(1)}, u32[]{:S(2)}, u32[]{:S(2)}) collective-permute-start(bf16[2,48,3072]{2,1,0:T(8,128)(2,1)S(1)} %get-tuple-element.69), channel_id=1, source_target_pairs={{0,8},{8,16},{16,24},{24,0},{1,9},{9,17},{17,25},{25,1},{2,10},{10... | collective-permute-start | bytes 1769480 | tf_op jit(solution)/shard_map/ppermute | solution.py:602
  183.8 20.0 %collective-permute-start.18 = (bf16[2,48,3072]{2,1,0:T(8,128)(2,1)S(1)}, bf16[2,48,3072]{2,1,0:T(8,128)(2,1)S(1)}, u32[]{:S(2)}, u32[]{:S(2)}) collective-permute-start(bf16[2,48,3072]{2,1,0:T(8,128)(2,1)S(1)} %get-tuple-element.70), channel_id=1, source_target_pairs={{0,96},{32,0},{64,32},{96,64},{1,97},{33,1},{65,33},{97,65},{2,98}... | collective-permute-start | bytes 1769480 | tf_op jit(solution)/shard_map/ppermute | solution.py:606
  186.9 16.9 %collective-permute-start.19 = (bf16[2,48,3072]{2,1,0:T(8,128)(2,1)S(1)}, bf16[2,48,3072]{2,1,0:T(8,128)(2,1)S(1)}, u32[]{:S(2)}, u32[]{:S(2)}) collective-permute-start(bf16[2,48,3072]{2,1,0:T(8,128)(2,1)S(1)} %get-tuple-element.71), channel_id=1, source_target_pairs={{0,24},{8,0},{16,8},{24,16},{1,25},{9,1},{17,9},{25,17},{2,26},{10... | collective-permute-start | bytes 1769480 | tf_op jit(solution)/shard_map/ppermute | solution.py:606
  216.9 15.1 %collective-permute-start.20 = (bf16[2,48,3072]{2,1,0:T(8,128)(2,1)S(1)}, bf16[2,48,3072]{2,1,0:T(8,128)(2,1)S(1)}, u32[]{:S(2)}, u32[]{:S(2)}) collective-permute-start(bf16[2,48,3072]{2,1,0:T(8,128)(2,1)S(1)} %get-tuple-element.77), channel_id=1, source_target_pairs={{0,32},{32,64},{64,96},{96,0},{1,33},{33,65},{65,97},{97,1},{2,34}... | collective-permute-start | bytes 1769480 | tf_op jit(solution)/shard_map/ppermute | solution.py:602
  217.0 15.0 %collective-permute-start.21 = (bf16[2,48,3072]{2,1,0:T(8,128)(2,1)S(1)}, bf16[2,48,3072]{2,1,0:T(8,128)(2,1)S(1)}, u32[]{:S(2)}, u32[]{:S(2)}) collective-permute-start(bf16[2,48,3072]{2,1,0:T(8,128)(2,1)S(1)} %get-tuple-element.78), channel_id=1, source_target_pairs={{0,8},{8,16},{16,24},{24,0},{1,9},{9,17},{17,25},{25,1},{2,10},{10... | collective-permute-start | bytes 1769480 | tf_op jit(solution)/shard_map/ppermute | solution.py:602
  217.0 15.0 %collective-permute-start.22 = (bf16[2,48,3072]{2,1,0:T(8,128)(2,1)S(1)}, bf16[2,48,3072]{2,1,0:T(8,128)(2,1)S(1)}, u32[]{:S(2)}, u32[]{:S(2)}) collective-permute-start(bf16[2,48,3072]{2,1,0:T(8,128)(2,1)S(1)} %get-tuple-element.79), channel_id=1, source_target_pairs={{0,96},{32,0},{64,32},{96,64},{1,97},{33,1},{65,33},{97,65},{2,98}... | collective-permute-start | bytes 1769480 | tf_op jit(solution)/shard_map/ppermute | solution.py:606
  220.2 16.5 %collective-permute-start.23 = (bf16[2,48,3072]{2,1,0:T(8,128)(2,1)S(1)}, bf16[2,48,3072]{2,1,0:T(8,128)(2,1)S(1)}, u32[]{:S(2)}, u32[]{:S(2)}) collective-permute-start(bf16[2,48,3072]{2,1,0:T(8,128)(2,1)S(1)} %get-tuple-element.80), channel_id=1, source_target_pairs={{0,24},{8,0},{16,8},{24,16},{1,25},{9,1},{17,9},{25,17},{2,26},{10... | collective-permute-start | bytes 1769480 | tf_op jit(solution)/shard_map/ppermute | solution.py:606
  237.3 23.8 %collective-permute-start.24 = (bf16[4,48,3072]{2,1,0:T(8,128)(2,1)S(1)}, bf16[4,48,3072]{2,1,0:T(8,128)(2,1)S(1)}, u32[]{:S(2)}, u32[]{:S(2)}) collective-permute-start(bf16[4,48,3072]{2,1,0:T(8,128)(2,1)S(1)} %get-tuple-element.86), channel_id=1, source_target_pairs={{0,32},{32,64},{64,96},{96,0},{1,33},{33,65},{65,97},{97,1},{2,34}... | collective-permute-start | bytes 3538952 | tf_op jit(solution)/shard_map/ppermute | solution.py:602
  237.4 24.3 %collective-permute-start.25 = (bf16[4,48,3072]{2,1,0:T(8,128)(2,1)S(1)}, bf16[4,48,3072]{2,1,0:T(8,128)(2,1)S(1)}, u32[]{:S(2)}, u32[]{:S(2)}) collective-permute-start(bf16[4,48,3072]{2,1,0:T(8,128)(2,1)S(1)} %get-tuple-element.87), channel_id=1, source_target_pairs={{0,8},{8,16},{16,24},{24,0},{1,9},{9,17},{17,25},{25,1},{2,10},{10... | collective-permute-start | bytes 3538952 | tf_op jit(solution)/shard_map/ppermute | solution.py:602
  237.5 24.9 %collective-permute-start.27 = (bf16[4,48,3072]{2,1,0:T(8,128)(2,1)S(1)}, bf16[4,48,3072]{2,1,0:T(8,128)(2,1)S(1)}, u32[]{:S(2)}, u32[]{:S(2)}) collective-permute-start(bf16[4,48,3072]{2,1,0:T(8,128)(2,1)S(1)} %get-tuple-element.88), channel_id=1, source_target_pairs={{0,24},{8,0},{16,8},{24,16},{1,25},{9,1},{17,9},{25,17},{2,26},{10... | collective-permute-start | bytes 3538952 | tf_op jit(solution)/shard_map/ppermute | solution.py:606
  241.3 23.1 %collective-permute-start.26 = (bf16[4,48,3072]{2,1,0:T(8,128)(2,1)S(1)}, bf16[4,48,3072]{2,1,0:T(8,128)(2,1)S(1)}, u32[]{:S(2)}, u32[]{:S(2)}) collective-permute-start(bf16[4,48,3072]{2,1,0:T(8,128)(2,1)S(1)} %get-tuple-element.81.late), channel_id=1, source_target_pairs={{0,96},{32,0},{64,32},{96,64},{1,97},{33,1},{65,33},{97,65},{2,98}... | collective-permute-start | bytes 3538952 | tf_op jit(solution)/shard_map/ppermute | solution.py:606
  265.2 9.3 %collective-permute-start.28 = (bf16[48,3072]{1,0:T(8,128)(2,1)S(1)}, bf16[48,3072]{1,0:T(8,128)(2,1)S(1)}, u32[]{:S(2)}, u32[]{:S(2)}) collective-permute-start(bf16[48,3072]{1,0:T(8,128)(2,1)S(1)} %get-tuple-element.91), channel_id=1, source_target_pairs={{0,16},{8,24},{16,0},{24,8},{1,17},{9,25},{17,1},{25,9},{2,18},{10... | collective-permute-start | bytes 884744 | tf_op jit(solution)/shard_map/ppermute | solution.py:610
  266.8 10.6 %collective-permute-start.29 = (bf16[48,3072]{1,0:T(8,128)(2,1)S(1)}, bf16[48,3072]{1,0:T(8,128)(2,1)S(1)}, u32[]{:S(2)}, u32[]{:S(2)}) collective-permute-start(bf16[48,3072]{1,0:T(8,128)(2,1)S(1)} %get-tuple-element.92), channel_id=1, source_target_pairs={{0,64},{32,96},{64,0},{96,32},{1,65},{33,97},{65,1},{97,33},{2,66}... | collective-permute-start | bytes 884744 | tf_op jit(solution)/shard_map/ppermute | solution.py:610
  268.7 8.6 %collective-permute-start.30 = (bf16[48,3072]{1,0:T(8,128)(2,1)S(1)}, bf16[48,3072]{1,0:T(8,128)(2,1)S(1)}, u32[]{:S(2)}, u32[]{:S(2)}) collective-permute-start(bf16[48,3072]{1,0:T(8,128)(2,1)S(1)} %get-tuple-element.93), channel_id=1, source_target_pairs={{0,8},{8,16},{16,24},{24,0},{1,9},{9,17},{17,25},{25,1},{2,10},{10... | collective-permute-start | bytes 884744 | tf_op jit(solution)/shard_map/ppermute | solution.py:602
  284.2 9.3 %collective-permute-start.35 = (bf16[16,6144]{1,0:T(8,128)(2,1)}, bf16[16,6144]{1,0:T(8,128)(2,1)}, u32[]{:S(2)}, u32[]{:S(2)}) collective-permute-start(bf16[16,6144]{1,0:T(8,128)(2,1)} %get-tuple-element.99), channel_id=1, source_target_pairs={{0,1},{1,2},{2,3},{3,0},{4,5},{5,6},{6,7},{7,4},{8,9},{9,10},{10,1... | collective-permute-start | bytes 589832 | tf_op jit(solution)/shard_map/ppermute | solution.py:602
  (29 other events, 338.6 us)
Sparse Core Ops, SparseCore 0:
  9.6 74.3 all-gather.2
  85.6 38.2 all-gather.4
  128.3 63.3 reduce-scatter.1

commit v8 on v7

--- a/solution.py
+++ b/solution.py
@@ -204,7 +204,11 @@
     return lax.dot_general(a, b, (((1,), (1,)), ((), ())), preferred_element_type=F32)
 
 
-def selected_kernel(place, own, normed, weight, res, o0, o1, o2, o3, w_here, r_here, sems, last):
+def pick_kernel(place, normed, out):
+    out[...] = mm(place[...], normed[...]).astype(BF)
+
+
+def selected_kernel(picked, own, weight, res, o0, o1, o2, o3, w_here, r_here, sems, last):
     size = o0.shape[0]
     chunks = weight.shape[0] // TILE
 
@@ -218,7 +222,6 @@
     rest.start()
     for c in range(1, AHEAD):
         copy(c).start()
-    picked = mm(place[...], normed[...]).astype(BF)
     rest.wait()
 
     @pl.loop(0, chunks)
@@ -229,24 +232,23 @@
 
         span = pl.ds(pl.multiple_of(c * TILE, TILE), TILE)
         copy(c).wait()
-        full = nt(picked, w_here[lax.rem(c, AHEAD + 1)]) + mm(own[...], r_here[:, span])
+        full = nt(picked[...], w_here[lax.rem(c, AHEAD + 1)]) + mm(own[...], r_here[:, span])
         full = full.astype(BF)
         for i, o in enumerate((o0, o1, o2, o3)):
             o[:, span] = full[i * size : (i + 1) * size]
 
 
-def selected(place, own, normed, weight, res):
-    picks, (model, width) = place.shape[0], weight.shape
+def selected(picked, own, weight, res):
+    picks, (model, width) = picked.shape[0], weight.shape
     return call(
         selected_kernel,
         "selected_projection",
         [((picks // 4, model), BF)] * 4,
-        place,
+        picked,
         own,
-        normed,
         weight,
         res,
-        in_specs=[VM] * 3 + [ANY] * 2,
+        in_specs=[VM] * 2 + [ANY] * 2,
         out_specs=[VM] * 4,
         scratch_shapes=[
             pltpu.VMEM((AHEAD + 1, TILE, width), BF),
@@ -258,34 +260,36 @@
     )
 
 
-def whole_kernel(normed_ref, weight_ref, late, out_ref):
+def whole_kernel(normed_ref, weight_ref, out_ref, done_ref):
     out_ref[...] = nt(normed_ref[...], weight_ref[...]).astype(BF)
-
-
-def whole_projection(normed, weight, late, tile=1024):
+    done_ref[...] = jnp.zeros_like(done_ref)
+
+
+def whole_projection(normed, weight, tile=1024):
     total, (model, width) = normed.shape[0], weight.shape
     return call(
         whole_kernel,
         "whole_projection",
-        [((total, model), BF)],
+        [((total, model), BF), ((8, 128), F32)],
         normed,
         weight,
-        late,
         grid=(model // tile,),
         in_specs=[
             pl.BlockSpec(normed.shape, lambda n: (0, 0)),
             pl.BlockSpec((tile, width), lambda n: (n, 0)),
-            VM,
         ],
-        out_specs=[pl.BlockSpec((total, tile), lambda n: (0, n))],
+        out_specs=[
+            pl.BlockSpec((total, tile), lambda n: (0, n)),
+            pl.BlockSpec((8, 128), lambda n: (0, 0)),
+        ],
         cost_estimate=pl.CostEstimate(
             flops=2 * total * model * width, bytes_accessed=4 * model * width, transcendentals=0
         ),
         vmem=58,
-    )[0]
-
-
-def norm_kernel(a, b, c, d, gain, held, o0, o1, same):
+    )
+
+
+def norm_kernel(a, b, c, d, gain, done, o0, o1):
     x = a[...].astype(F32) + b[...].astype(F32) + c[...].astype(F32) + d[...].astype(F32)
     x = x * lax.rsqrt(jnp.mean(x * x, -1, keepdims=True) + 1e-06) * gain[...]
     half = o0.shape[1]
@@ -300,7 +304,7 @@
     b_down[...] = b_above[2:4]
 
 
-def stack_kernel(a0, b0, a3, b3, a1, b1, a2, b2, held, o0, o1, same):
+def stack_kernel(a0, b0, a3, b3, a1, b1, a2, b2, h0, h1, o0, o1, *same):
     for i, (a, b) in enumerate(((a0, b0), (a1, b1), (a2, b2), (a3, b3))):
         o0[i] = a[...]
         o1[i] = b[...]
@@ -654,32 +658,38 @@
     place, own_place = route(me, all_routes, cap)
     flat = residual.reshape(rows, model)
     gain = norm_gain.reshape(1, model)
-    to_up, to_down, to_far, here = selected(place, own_place, normed, weight_out, flat)
-    whole = whole_projection(normed, weight_out, here)
+    picked = call(
+        pick_kernel,
+        "pick",
+        [((place.shape[0], width), BF)],
+        place,
+        normed,
+        in_specs=[VM] * 2,
+        out_specs=[VM],
+        vmem=8,
+    )[0]
+    to_up, to_down, to_far, here = selected(picked, own_place, weight_out, flat)
+    whole, done = whole_projection(normed, weight_out)
 
     size = here.shape[0]
-    a0, b0, whole = call(
+    a0, b0 = call(
         norm_kernel,
         "selected_norm",
-        [((size, half), BF)] * 2 + [(whole.shape, BF)],
+        [((size, half), BF)] * 2,
         here,
+        across(to_far, "x"),
         up_one(to_up, "x"),
         down_one(to_down, "x"),
-        across(to_far, "x"),
         gain,
-        whole,
-        in_specs=[VM] * 5 + [ANY],
-        out_specs=[VM] * 2 + [ANY],
-        input_output_aliases={5: 2},
-        vmem=58,
-    )
-
-    mixed = lax.psum_scatter(whole, "x", scatter_dimension=0, tiled=True)
-
-    a4, b4, weights = call(
+        done,
+        in_specs=[VM] * 6,
+        out_specs=[VM] * 2,
+    )
+
+    a4, b4, weights, whole = call(
         stack_kernel,
         "stack",
-        [((4, size, half), BF)] * 2 + [(weights.shape, BF)],
+        [((4, size, half), BF)] * 2 + [(weights.shape, BF), (whole.shape, BF)],
         a0,
         b0,
         across(a0, "y"),
@@ -689,11 +699,13 @@
         down_one(a0, "y"),
         down_one(b0, "z"),
         weights,
-        in_specs=[VM] * 8 + [ANY],
-        out_specs=[VM] * 2 + [ANY],
-        input_output_aliases={8: 2},
-        vmem=50,
-    )
+        whole,
+        in_specs=[VM] * 8 + [ANY] * 2,
+        out_specs=[VM] * 2 + [ANY] * 2,
+        input_output_aliases={8: 2, 9: 3},
+        vmem=54,
+    )
+    mixed = lax.psum_scatter(whole, "x", scatter_dimension=0, tiled=True)
     a_below, b_below = up_one(a4, "z"), up_one(b4, "y")
     a_above, b_above = down_one(a4, "z"), down_one(b4, "y")
     a_up, b_up, a_down, b_down = call(

time: 304 us -> 304 us (level)
    ppermute x14, waiting for transfers between devices: 32.8 us -> 43.9 us  [up_one(): return lax.ppermute(x, axis, ring(4, 1))]
    ppermute x14, waiting for transfers between devices: 41.5 us -> 34.3 us  [down_one(): return lax.ppermute(x, axis, ring(4, -1))]
    unnamed x41 -> x43, local copies, waits for them, and re-layouts: 9.59 us -> 6.79 us
    pallas_call x14 -> x15, Pallas kernels: 70.3 us -> 69.9 us  [call(): pl.pallas_call(kernel, out_shape=[jax.ShapeDtypeStruct(s, d) for s, d in...]
  transfers between devices with their start and end apart: 41 -> 41, of which waited for: 21 -> 20; matrix products, arithmetic and copies ran while one was open for 3% -> 3% of each run, Pallas kernels for 26% -> 24%
where the time goes in v8:
time: 304 us; the launch traced here: 303 us
  waiting for transfers between devices  106 us (35%)
  Pallas kernels  80.1 us (26%)
  starting transfers between devices  65.7 us (22%)
  blocking collectives  21.8 us (7%)
  between operations  13.5 us (4%)
  other arithmetic  9.28 us (3%)
  local copies, waits for them, and re-layouts  7.04 us (2%)
    pallas_call x15, Pallas kernels, call(): pl.pallas_call(kernel, out_shape=[jax.ShapeDtypeStruct(s, d) for s, d in...  69.9 us
    ppermute x14, waiting for transfers between devices, up_one(): return lax.ppermute(x, axis, ring(4, 1))  43.9 us
    ppermute x14, starting transfers between devices, down_one(): return lax.ppermute(x, axis, ring(4, -1))  37.6 us
    ppermute x14, waiting for transfers between devices, down_one(): return lax.ppermute(x, axis, ring(4, -1))  34.3 us
    all_to_all x1, blocking collectives, shards(): arrived = lax.all_to_all(states, SEQ, 0, 0, tiled=True)  21.8 us
    all_gather x1, waiting for transfers between devices, shards(): weight_out = lax.all_gather(out_weight.T, SEQ, axis=0, tiled=True)  10.8 us
    ppermute x14, starting transfers between devices, up_one(): return lax.ppermute(x, axis, ring(4, 1))  9.76 us
    concatenate x1, other arithmetic, shards(): weights = jnp.concatenate([gate_weight[0], up_weight[0], down_weight[0]])  9.28 us
  transfers between devices with their start and end apart: 41, of which 20 were waited for; matrix products, arithmetic and copies ran while one was open for 3% of the time, Pallas kernels for 24%

profile of v8, /device:TPU:0, one launch (start us, length us, event | category | flops | bytes accessed | tf_op | source)
XLA Modules:
  0.0 303.0 jit_solution(6860895178709803722)
XLA Ops:
  7.3 9.3 %pad_maximum_fusion = bf16[864,6144]{1,0:T(8,128)(2,1)} fusion(bf16[288,6144]{1,0:T(8,128)(2,1)} %bitcast.30, bf16[288,6144]{1,0:T(8,128)(2,1)} %bitcast.31, bf16[288,6144]{1,0:T(8,128)(2,1)} %bitcast.32), kind=kLoop, calls=%fused_computation | loop fusion | flops 31850496 | bytes 21233664 | tf_op jit(solution)/shard_map/concatenate | solution.py:641
  16.6 7.1 %local_attention.1 = (f32[2,256,1024]{2,1,0:T(8,128)}, bf16[32,80,128]{2,1,0:T(8,128)(2,1)}, f32[2,256,8]{2,1,0:T(8,128)}) custom-call(bf16[2,256,1024]{2,1,0:T(8,128)(2,1)} %q_ref.3, bf16[2,256,1024]{2,1,0:T(8,128)(2,1)} %k_ref.1, bf16[2,256,1024]{2,1,0:T(8,128)(2,1)} %v_ref.1, f32[2,8,256]{2,1,0:T(8,128)} %bitcast.34), custom_call_target="tpu_custom_call" | custom-call | tf_op jit(solution)/shard_map/local_attention/pallas_call | solution.py:84
  23.8 21.8 %all_to_all.10.in_ref = bf16[32,80,128]{2,1,0:T(8,128)(2,1)S(1)} all-to-all(bf16[32,80,128]{2,1,0:T(8,128)(2,1)} %get-tuple-element.58), channel_id=1, replica_groups=mesh['z'=4,'y'=4,'core'=2,'x'=4] {'z','y','core'}, dimensions={0} | all-to-all | bytes 1310720 | tf_op jit(solution)/shard_map/all_to_all | solution.py:650
  46.5 3.9 %all-to-all-start.1 = ((bf16[32,64,128]{2,1,0:T(8,128)(2,1)}), bf16[32,64,128]{2,1,0:T(8,128)(2,1)S(1)}, u32[]{:S(2)}, u32[]{:S(2)}) async-start(bf16[32,64,128]{2,1,0:T(8,128)(2,1)} %state_prefix.1), calls=%async_computation.1 | async-start | bytes 1048576 | tf_op jit(solution)/shard_map/all_to_all | solution.py:651
  60.1 7.8 %all-to-all-done.1 = bf16[32,64,128]{2,1,0:T(8,128)(2,1)S(1)} async-done(((bf16[32,64,128]{2,1,0:T(8,128)(2,1)}), bf16[32,64,128]{2,1,0:T(8,128)(2,1)S(1)}, u32[]{:S(2)}, u32[]{:S(2)}) %all-to-all-start.1) | async-done | bytes 524320 | tf_op jit(solution)/shard_map/all_to_all | solution.py:651
  73.2 10.8 %all-gather.3.cloned.1.call-done.weight.weight_ref = bf16[6144,1024]{1,0:T(8,128)(2,1)} async-done(((bf16[192,1024]{1,0:T(8,128)(2,1)}), bf16[6144,1024]{1,0:T(8,128)(2,1)}) %all-gather.3.cloned.1.call-update) | async-done | bytes 12582928 | tf_op jit(solution)/shard_map/all_gather | solution.py:640
  84.0 8.0 %selected_projection.1 = (bf16[48,6144]{1,0:T(8,128)(2,1)S(1)}, bf16[48,6144]{1,0:T(8,128)(2,1)S(1)}, bf16[48,6144]{1,0:T(8,128)(2,1)}, bf16[48,6144]{1,0:T(8,128)(2,1)S(1)}) custom-call(bf16[192,1024]{1,0:T(8,128)(2,1)S(1)} %pick.1.picked, bf16[192,128]{1,0:T(8,128)(2,1)S(1)} %get-tuple-element.59.own, ...), custom_call_target="tpu_custom_call" | custom-call | tf_op jit(solution)/shard_map/selected_projection/pallas_call | solution.py:157
  91.9 3.1 %collective-permute-start.3 = (bf16[48,6144]{1,0:T(8,128)(2,1)}, bf16[48,6144]{1,0:T(8,128)(2,1)S(1)}, u32[]{:S(2)}, u32[]{:S(2)}) collective-permute-start(bf16[48,6144]{1,0:T(8,128)(2,1)} %get-tuple-element.61), channel_id=1, source_target_pairs={{0,2},{1,3},{2,0},{3,1},{4,6},{5,7},{6,4},{7,5},{8,10},{9,11},{10,... | collective-permute-start | bytes 1769480 | tf_op jit(solution)/shard_map/ppermute | solution.py:614
  98.2 14.7 %whole_projection.1 = (bf16[512,6144]{1,0:T(8,128)(2,1)}, f32[8,128]{1,0:T(8,128)}) custom-call(bf16[512,1024]{1,0:T(8,128)(2,1)} %bitcast.19, bf16[6144,1024]{1,0:T(8,128)(2,1)} %all-gather.3.cloned.1.call-done.weight.weight_ref), custom_call_target="tpu_custom_call" | custom-call | flops 6442450944 | bytes 25165824 | tf_op jit(solution)/shard_map/whole_projection/pallas_call | solution.py:157
  112.9 9.0 %collective-permute-done.4.c = bf16[48,6144]{1,0:T(8,128)(2,1)S(1)} collective-permute-done((bf16[48,6144]{1,0:T(8,128)(2,1)S(1)}, bf16[48,6144]{1,0:T(8,128)(2,1)S(1)}, u32[]{:S(2)}, u32[]{:S(2)}) %collective-permute-start.4) | collective-permute-done | bytes 589856 | tf_op jit(solution)/shard_map/ppermute | solution.py:606
  130.3 8.4 %collective-permute-done.10.a2 = bf16[48,3072]{1,0:T(8,128)(2,1)S(1)} collective-permute-done((bf16[48,3072]{1,0:T(8,128)(2,1)S(1)}, bf16[48,3072]{1,0:T(8,128)(2,1)S(1)}, u32[]{:S(2)}, u32[]{:S(2)}) %collective-permute-start.10) | collective-permute-done | bytes 294944 | tf_op jit(solution)/shard_map/ppermute | solution.py:610
  138.8 3.4 %collective-permute-done.8.a1 = bf16[48,3072]{1,0:T(8,128)(2,1)S(1)} collective-permute-done((bf16[48,3072]{1,0:T(8,128)(2,1)S(1)}, bf16[48,3072]{1,0:T(8,128)(2,1)S(1)}, u32[]{:S(2)}, u32[]{:S(2)}) %collective-permute-start.8) | collective-permute-done | bytes 294944 | tf_op jit(solution)/shard_map/ppermute | solution.py:606
  142.2 4.9 %collective-permute-done.7.b3 = bf16[48,3072]{1,0:T(8,128)(2,1)} collective-permute-done((bf16[48,3072]{1,0:T(8,128)(2,1)S(1)}, bf16[48,3072]{1,0:T(8,128)(2,1)}, u32[]{:S(2)}, u32[]{:S(2)}) %collective-permute-start.7) | collective-permute-done | bytes 294944 | tf_op jit(solution)/shard_map/ppermute | solution.py:614
  147.2 3.2 %stack.1 = (bf16[4,48,3072]{2,1,0:T(8,128)(2,1)}, bf16[4,48,3072]{2,1,0:T(8,128)(2,1)}, bf16[1728,6144]{1,0:T(8,128)(2,1)}, bf16[512,6144]{1,0:T(8,128)(2,1)}) custom-call(bf16[48,3072]{1,0:T(8,128)(2,1)} %copy-done.8, bf16[48,3072]{1,0:T(8,128)(2,1)} %copy-done.9, bf16[48,3072]{1,0:T(8,128)(2,1)} %copy-done.18, ...), custom_call_target="tpu_custom_call", output_to_operand_aliasing={{2}: (8, {}), {3}: (9, {})} | custom-call | tf_op jit(solution)/shard_map/stack/pallas_call | solution.py:157
  153.6 4.9 %collective-permute-start.15 = (bf16[4,48,3072]{2,1,0:T(8,128)(2,1)}, bf16[4,48,3072]{2,1,0:T(8,128)(2,1)S(1)}, u32[]{:S(2)}, u32[]{:S(2)}) collective-permute-start(bf16[4,48,3072]{2,1,0:T(8,128)(2,1)} %get-tuple-element.70.b0), channel_id=1, source_target_pairs={{0,24},{8,0},{16,8},{24,16},{1,25},{9,1},{17,9},{25,17},{2,26},{10... | collective-permute-start | bytes 3538952 | tf_op jit(solution)/shard_map/ppermute | solution.py:610
  158.6 15.2 %collective-permute-done.14.a2.a_above = bf16[4,48,3072]{2,1,0:T(8,128)(2,1)S(1)} collective-permute-done((bf16[4,48,3072]{2,1,0:T(8,128)(2,1)S(1)}, bf16[4,48,3072]{2,1,0:T(8,128)(2,1)S(1)}, u32[]{:S(2)}, u32[]{:S(2)}) %collective-permute-start.14) | collective-permute-done | bytes 1179680 | tf_op jit(solution)/shard_map/ppermute | solution.py:610
  173.7 3.4 %collective-permute-done.12.a1.a_below = bf16[4,48,3072]{2,1,0:T(8,128)(2,1)S(1)} collective-permute-done((bf16[4,48,3072]{2,1,0:T(8,128)(2,1)S(1)}, bf16[4,48,3072]{2,1,0:T(8,128)(2,1)S(1)}, u32[]{:S(2)}, u32[]{:S(2)}) %collective-permute-start.12) | collective-permute-done | bytes 1179680 | tf_op jit(solution)/shard_map/ppermute | solution.py:606
  177.2 4.7 %collective-permute-done.15.b2.b_above = bf16[4,48,3072]{2,1,0:T(8,128)(2,1)S(1)} collective-permute-done((bf16[4,48,3072]{2,1,0:T(8,128)(2,1)}, bf16[4,48,3072]{2,1,0:T(8,128)(2,1)S(1)}, u32[]{:S(2)}, u32[]{:S(2)}) %collective-permute-start.15) | collective-permute-done | bytes 1179680 | tf_op jit(solution)/shard_map/ppermute | solution.py:610
  181.9 3.3 %collective-permute-done.13.b1.b_below = bf16[4,48,3072]{2,1,0:T(8,128)(2,1)S(1)} collective-permute-done((bf16[4,48,3072]{2,1,0:T(8,128)(2,1)}, bf16[4,48,3072]{2,1,0:T(8,128)(2,1)S(1)}, u32[]{:S(2)}, u32[]{:S(2)}) %collective-permute-start.13) | collective-permute-done | bytes 1179680 | tf_op jit(solution)/shard_map/ppermute | solution.py:606
  185.7 3.0 collective-permute-start.18
  188.7 3.2 %collective-permute-start.19 = (bf16[2,48,3072]{2,1,0:T(8,128)(2,1)S(1)}, bf16[2,48,3072]{2,1,0:T(8,128)(2,1)S(1)}, u32[]{:S(2)}, u32[]{:S(2)}) collective-permute-start(bf16[2,48,3072]{2,1,0:T(8,128)(2,1)S(1)} %get-tuple-element.75), channel_id=1, source_target_pairs={{0,24},{8,0},{16,8},{24,16},{1,25},{9,1},{17,9},{25,17},{2,26},{10... | collective-permute-start | bytes 1769480 | tf_op jit(solution)/shard_map/ppermute | solution.py:610
  191.9 13.5 %near_rows.1.acc = f32[768,1152]{1,0:T(8,128)S(1)} custom-call(bf16[4,48,3072]{2,1,0:T(8,128)(2,1)S(1)} %copy-done.5, bf16[4,48,3072]{2,1,0:T(8,128)(2,1)S(1)} %copy-done.6, bf16[4,48,3072]{2,1,0:T(8,128)(2,1)S(1)} %collective-permute-done.12.a1.a_below, bf16[4,48,3072]{2,1,0:T(8,128)(2,1)S(1)} %collective-permute-done.13.b1.b_below, ...), custom_call_target="tpu_custom_call" | custom-call | flops 8153726976 | bytes 1048576 | tf_op jit(solution)/shard_map/near_rows/pallas_call | solution.py:157
  205.4 13.2 %far_rows.1 = (bf16[768,576]{1,0:T(8,128)(2,1)S(1)}, bf16[2,48,3072]{2,1,0:T(8,128)(2,1)S(1)}, bf16[2,48,3072]{2,1,0:T(8,128)(2,1)S(1)}, bf16[2,48,3072]{2,1,0:T(8,128)(2,1)S(1)}, bf16[2,48,3072]{2,1,0:T(8,128)(2,1)S(1)}) custom-call(f32[768,1152]{1,0:T(8,128)S(1)} %near_rows.1.acc, bf16[2,48,3072]{2,1,0:T(8,128)(2,1)S(1)} %collective-permute-done.16.a3, ...), custom_call_target="tpu_custom_call" | custom-call | tf_op jit(solution)/shard_map/far_rows/pallas_call | solution.py:157
  218.8 3.1 %collective-permute-start.22 = (bf16[2,48,3072]{2,1,0:T(8,128)(2,1)S(1)}, bf16[2,48,3072]{2,1,0:T(8,128)(2,1)S(1)}, u32[]{:S(2)}, u32[]{:S(2)}) collective-permute-start(bf16[2,48,3072]{2,1,0:T(8,128)(2,1)S(1)} %get-tuple-element.83), channel_id=1, source_target_pairs={{0,96},{32,0},{64,32},{96,64},{1,97},{33,1},{65,33},{97,65},{2,98}... | collective-permute-start | bytes 1769480 | tf_op jit(solution)/shard_map/ppermute | solution.py:610
  221.9 3.2 %collective-permute-start.23 = (bf16[2,48,3072]{2,1,0:T(8,128)(2,1)S(1)}, bf16[2,48,3072]{2,1,0:T(8,128)(2,1)S(1)}, u32[]{:S(2)}, u32[]{:S(2)}) collective-permute-start(bf16[2,48,3072]{2,1,0:T(8,128)(2,1)S(1)} %get-tuple-element.84), channel_id=1, source_target_pairs={{0,24},{8,0},{16,8},{24,16},{1,25},{9,1},{17,9},{25,17},{2,26},{10... | collective-permute-start | bytes 1769480 | tf_op jit(solution)/shard_map/ppermute | solution.py:610
  225.2 8.6 %rest_rows.1 = (bf16[4,48,3072]{2,1,0:T(8,128)(2,1)S(1)}, bf16[4,48,3072]{2,1,0:T(8,128)(2,1)S(1)}, bf16[4,48,3072]{2,1,0:T(8,128)(2,1)S(1)}, bf16[4,48,3072]{2,...) custom-call(bf16[768,576]{1,0:T(8,128)(2,1)S(1)} %get-tuple-element.76.hidden, ...), custom_call_target="tpu_custom_call" | custom-call | flops 4076863488 | bytes 1048576 | tf_op jit(solution)/shard_map/rest_rows/pallas_call | solution.py:157
  234.6 3.2 %collective-permute-start.27 = (bf16[4,48,3072]{2,1,0:T(8,128)(2,1)S(1)}, bf16[4,48,3072]{2,1,0:T(8,128)(2,1)S(1)}, u32[]{:S(2)}, u32[]{:S(2)}) collective-permute-start(bf16[4,48,3072]{2,1,0:T(8,128)(2,1)S(1)} %get-tuple-element.92), channel_id=1, source_target_pairs={{0,24},{8,0},{16,8},{24,16},{1,25},{9,1},{17,9},{25,17},{2,26},{10... | collective-permute-start | bytes 3538952 | tf_op jit(solution)/shard_map/ppermute | solution.py:610
  237.8 3.2 %collective-permute-start.26 = (bf16[4,48,3072]{2,1,0:T(8,128)(2,1)S(1)}, bf16[4,48,3072]{2,1,0:T(8,128)(2,1)S(1)}, u32[]{:S(2)}, u32[]{:S(2)}) collective-permute-start(bf16[4,48,3072]{2,1,0:T(8,128)(2,1)S(1)} %get-tuple-element.85.late), channel_id=1, source_target_pairs={{0,96},{32,0},{64,32},{96,64},{1,97},{33,1},{65,33},{97,65},{2,98}... | collective-permute-start | bytes 3538952 | tf_op jit(solution)/shard_map/ppermute | solution.py:610
  240.9 20.3 %collective-permute-done.24.u0 = bf16[4,48,3072]{2,1,0:T(8,128)(2,1)S(1)} collective-permute-done((bf16[4,48,3072]{2,1,0:T(8,128)(2,1)S(1)}, bf16[4,48,3072]{2,1,0:T(8,128)(2,1)S(1)}, u32[]{:S(2)}, u32[]{:S(2)}) %collective-permute-start.24) | collective-permute-done | bytes 1179680 | tf_op jit(solution)/shard_map/ppermute | solution.py:606
  267.5 3.4 %collective-permute-start.31 = (bf16[48,3072]{1,0:T(8,128)(2,1)S(1)}, bf16[48,3072]{1,0:T(8,128)(2,1)S(1)}, u32[]{:S(2)}, u32[]{:S(2)}) collective-permute-start(bf16[48,3072]{1,0:T(8,128)(2,1)S(1)} %get-tuple-element.98), channel_id=1, source_target_pairs={{0,32},{32,64},{64,96},{96,0},{1,33},{33,65},{65,97},{97,1},{2,34}... | collective-permute-start | bytes 884744 | tf_op jit(solution)/shard_map/ppermute | solution.py:606
  272.2 3.7 %collective-permute-start.33 = (bf16[48,3072]{1,0:T(8,128)(2,1)S(1)}, bf16[48,3072]{1,0:T(8,128)(2,1)S(1)}, u32[]{:S(2)}, u32[]{:S(2)}) collective-permute-start(bf16[48,3072]{1,0:T(8,128)(2,1)S(1)} %get-tuple-element.100), channel_id=1, source_target_pairs={{0,96},{32,0},{64,32},{96,64},{1,97},{33,1},{65,33},{97,65},{2,98}... | collective-permute-start | bytes 884744 | tf_op jit(solution)/shard_map/ppermute | solution.py:610
  289.1 4.5 %collective-permute-done.35.b2 = bf16[16,6144]{1,0:T(8,128)(2,1)} collective-permute-done((bf16[16,6144]{1,0:T(8,128)(2,1)}, bf16[16,6144]{1,0:T(8,128)(2,1)}, u32[]{:S(2)}, u32[]{:S(2)}) %collective-permute-start.35) | collective-permute-done | bytes 196640 | tf_op jit(solution)/shard_map/ppermute | solution.py:606
  (120 shorter events, 56.6 us)
Async XLA Ops:
  6.5 77.4 %all-gather.3.cloned.1.call-start = ((), (), s32[]{:S(2)}) async-start(), calls=%async_computation.3 | async-start | bytes 12976128 | tf_op jit(solution)/shard_map/all_gather | solution.py:640
  7.3 131.5 %all-gather.5.cloned.1.call-start = ((), (), s32[]{:S(2)}) async-start(), calls=%async_computation.4 | async-start | bytes 31850496 | tf_op jit(solution)/shard_map/all_gather | solution.py:642
  46.5 21.5 %all-to-all-start.1 = ((bf16[32,64,128]{2,1,0:T(8,128)(2,1)}), bf16[32,64,128]{2,1,0:T(8,128)(2,1)S(1)}, u32[]{:S(2)}, u32[]{:S(2)}) async-start(bf16[32,64,128]{2,1,0:T(8,128)(2,1)} %state_prefix.1), calls=%async_computation.1 | async-start | bytes 1048576 | tf_op jit(solution)/shard_map/all_to_all | solution.py:651
  50.4 235.4 %reduce-scatter.2.cloned.1.call-start = ((), (), s32[]{:S(2)}) async-start(), calls=%async_computation.5 | async-start | bytes 7864320 | tf_op jit(solution)/shard_map/reduce_scatter | solution.py:708
  91.9 21.0 %collective-permute-start.3 = (bf16[48,6144]{1,0:T(8,128)(2,1)}, bf16[48,6144]{1,0:T(8,128)(2,1)S(1)}, u32[]{:S(2)}, u32[]{:S(2)}) collective-permute-start(bf16[48,6144]{1,0:T(8,128)(2,1)} %get-tuple-element.61), channel_id=1, source_target_pairs={{0,2},{1,3},{2,0},{3,1},{4,6},{5,7},{6,4},{7,5},{8,10},{9,11},{10,... | collective-permute-start | bytes 1769480 | tf_op jit(solution)/shard_map/ppermute | solution.py:614
  95.0 26.9 %collective-permute-start.4 = (bf16[48,6144]{1,0:T(8,128)(2,1)S(1)}, bf16[48,6144]{1,0:T(8,128)(2,1)S(1)}, u32[]{:S(2)}, u32[]{:S(2)}) collective-permute-start(bf16[48,6144]{1,0:T(8,128)(2,1)S(1)} %get-tuple-element.62), channel_id=1, source_target_pairs={{0,1},{1,2},{2,3},{3,0},{4,5},{5,6},{6,7},{7,4},{8,9},{9,10},{10,1... | collective-permute-start | bytes 1769480 | tf_op jit(solution)/shard_map/ppermute | solution.py:606
  95.6 26.4 %collective-permute-start.5 = (bf16[48,6144]{1,0:T(8,128)(2,1)S(1)}, bf16[48,6144]{1,0:T(8,128)(2,1)S(1)}, u32[]{:S(2)}, u32[]{:S(2)}) collective-permute-start(bf16[48,6144]{1,0:T(8,128)(2,1)S(1)} %get-tuple-element.63), channel_id=1, source_target_pairs={{0,3},{1,0},{2,1},{3,2},{4,7},{5,4},{6,5},{7,6},{8,11},{9,8},{10,9... | collective-permute-start | bytes 1769480 | tf_op jit(solution)/shard_map/ppermute | solution.py:610
  123.2 15.6 %collective-permute-start.10 = (bf16[48,3072]{1,0:T(8,128)(2,1)S(1)}, bf16[48,3072]{1,0:T(8,128)(2,1)S(1)}, u32[]{:S(2)}, u32[]{:S(2)}) collective-permute-start(bf16[48,3072]{1,0:T(8,128)(2,1)S(1)} %get-tuple-element.65.a0), channel_id=1, source_target_pairs={{0,24},{8,0},{16,8},{24,16},{1,25},{9,1},{17,9},{25,17},{2,26},{10... | collective-permute-start | bytes 884744 | tf_op jit(solution)/shard_map/ppermute | solution.py:610
  126.0 16.1 %collective-permute-start.8 = (bf16[48,3072]{1,0:T(8,128)(2,1)S(1)}, bf16[48,3072]{1,0:T(8,128)(2,1)S(1)}, u32[]{:S(2)}, u32[]{:S(2)}) collective-permute-start(bf16[48,3072]{1,0:T(8,128)(2,1)S(1)} %get-tuple-element.65.a0), channel_id=1, source_target_pairs={{0,8},{8,16},{16,24},{24,0},{1,9},{9,17},{17,25},{25,1},{2,10},{10... | collective-permute-start | bytes 884744 | tf_op jit(solution)/shard_map/ppermute | solution.py:606
  126.0 16.1 %collective-permute-start.6 = (bf16[48,3072]{1,0:T(8,128)(2,1)S(1)}, bf16[48,3072]{1,0:T(8,128)(2,1)S(1)}, u32[]{:S(2)}, u32[]{:S(2)}) collective-permute-start(bf16[48,3072]{1,0:T(8,128)(2,1)S(1)} %get-tuple-element.65.a0), channel_id=1, source_target_pairs={{0,16},{8,24},{16,0},{24,8},{1,17},{9,25},{17,1},{25,9},{2,18},{10... | collective-permute-start | bytes 884744 | tf_op jit(solution)/shard_map/ppermute | solution.py:614
  128.3 13.9 %collective-permute-start.11 = (bf16[48,3072]{1,0:T(8,128)(2,1)S(1)}, bf16[48,3072]{1,0:T(8,128)(2,1)S(1)}, u32[]{:S(2)}, u32[]{:S(2)}) collective-permute-start(bf16[48,3072]{1,0:T(8,128)(2,1)S(1)} %get-tuple-element.66.b0), channel_id=1, source_target_pairs={{0,96},{32,0},{64,32},{96,64},{1,97},{33,1},{65,33},{97,65},{2,98}... | collective-permute-start | bytes 884744 | tf_op jit(solution)/shard_map/ppermute | solution.py:610
  129.1 13.1 %collective-permute-start.9 = (bf16[48,3072]{1,0:T(8,128)(2,1)S(1)}, bf16[48,3072]{1,0:T(8,128)(2,1)}, u32[]{:S(2)}, u32[]{:S(2)}) collective-permute-start(bf16[48,3072]{1,0:T(8,128)(2,1)S(1)} %get-tuple-element.66.b0), channel_id=1, source_target_pairs={{0,32},{32,64},{64,96},{96,0},{1,33},{33,65},{65,97},{97,1},{2,34}... | collective-permute-start | bytes 884744 | tf_op jit(solution)/shard_map/ppermute | solution.py:606
  151.6 22.1 %collective-permute-start.14 = (bf16[4,48,3072]{2,1,0:T(8,128)(2,1)S(1)}, bf16[4,48,3072]{2,1,0:T(8,128)(2,1)S(1)}, u32[]{:S(2)}, u32[]{:S(2)}) collective-permute-start(bf16[4,48,3072]{2,1,0:T(8,128)(2,1)S(1)} %copy-done.5), channel_id=1, source_target_pairs={{0,96},{32,0},{64,32},{96,64},{1,97},{33,1},{65,33},{97,65},{2,98}... | collective-permute-start | bytes 3538952 | tf_op jit(solution)/shard_map/ppermute | solution.py:610
  151.6 25.6 %collective-permute-start.12 = (bf16[4,48,3072]{2,1,0:T(8,128)(2,1)S(1)}, bf16[4,48,3072]{2,1,0:T(8,128)(2,1)S(1)}, u32[]{:S(2)}, u32[]{:S(2)}) collective-permute-start(bf16[4,48,3072]{2,1,0:T(8,128)(2,1)S(1)} %copy-done.5), channel_id=1, source_target_pairs={{0,32},{32,64},{64,96},{96,0},{1,33},{33,65},{65,97},{97,1},{2,34}... | collective-permute-start | bytes 3538952 | tf_op jit(solution)/shard_map/ppermute | solution.py:606
  153.6 28.3 %collective-permute-start.15 = (bf16[4,48,3072]{2,1,0:T(8,128)(2,1)}, bf16[4,48,3072]{2,1,0:T(8,128)(2,1)S(1)}, u32[]{:S(2)}, u32[]{:S(2)}) collective-permute-start(bf16[4,48,3072]{2,1,0:T(8,128)(2,1)} %get-tuple-element.70.b0), channel_id=1, source_target_pairs={{0,24},{8,0},{16,8},{24,16},{1,25},{9,1},{17,9},{25,17},{2,26},{10... | collective-permute-start | bytes 3538952 | tf_op jit(solution)/shard_map/ppermute | solution.py:610
  158.6 26.6 %collective-permute-start.13 = (bf16[4,48,3072]{2,1,0:T(8,128)(2,1)}, bf16[4,48,3072]{2,1,0:T(8,128)(2,1)S(1)}, u32[]{:S(2)}, u32[]{:S(2)}) collective-permute-start(bf16[4,48,3072]{2,1,0:T(8,128)(2,1)} %get-tuple-element.70.b0), channel_id=1, source_target_pairs={{0,8},{8,16},{16,24},{24,0},{1,9},{9,17},{17,25},{25,1},{2,10},{10... | collective-permute-start | bytes 3538952 | tf_op jit(solution)/shard_map/ppermute | solution.py:606
  185.4 20.0 %collective-permute-start.16 = (bf16[2,48,3072]{2,1,0:T(8,128)(2,1)S(1)}, bf16[2,48,3072]{2,1,0:T(8,128)(2,1)S(1)}, u32[]{:S(2)}, u32[]{:S(2)}) collective-permute-start(bf16[2,48,3072]{2,1,0:T(8,128)(2,1)S(1)} %get-tuple-element.72), channel_id=1, source_target_pairs={{0,32},{32,64},{64,96},{96,0},{1,33},{33,65},{65,97},{97,1},{2,34}... | collective-permute-start | bytes 1769480 | tf_op jit(solution)/shard_map/ppermute | solution.py:606
  185.7 19.7 %collective-permute-start.17 = (bf16[2,48,3072]{2,1,0:T(8,128)(2,1)S(1)}, bf16[2,48,3072]{2,1,0:T(8,128)(2,1)S(1)}, u32[]{:S(2)}, u32[]{:S(2)}) collective-permute-start(bf16[2,48,3072]{2,1,0:T(8,128)(2,1)S(1)} %get-tuple-element.73), channel_id=1, source_target_pairs={{0,8},{8,16},{16,24},{24,0},{1,9},{9,17},{17,25},{25,1},{2,10},{10... | collective-permute-start | bytes 1769480 | tf_op jit(solution)/shard_map/ppermute | solution.py:606
  185.7 19.7 %collective-permute-start.18 = (bf16[2,48,3072]{2,1,0:T(8,128)(2,1)S(1)}, bf16[2,48,3072]{2,1,0:T(8,128)(2,1)S(1)}, u32[]{:S(2)}, u32[]{:S(2)}) collective-permute-start(bf16[2,48,3072]{2,1,0:T(8,128)(2,1)S(1)} %get-tuple-element.74), channel_id=1, source_target_pairs={{0,96},{32,0},{64,32},{96,64},{1,97},{33,1},{65,33},{97,65},{2,98}... | collective-permute-start | bytes 1769480 | tf_op jit(solution)/shard_map/ppermute | solution.py:610
  188.7 16.7 %collective-permute-start.19 = (bf16[2,48,3072]{2,1,0:T(8,128)(2,1)S(1)}, bf16[2,48,3072]{2,1,0:T(8,128)(2,1)S(1)}, u32[]{:S(2)}, u32[]{:S(2)}) collective-permute-start(bf16[2,48,3072]{2,1,0:T(8,128)(2,1)S(1)} %get-tuple-element.75), channel_id=1, source_target_pairs={{0,24},{8,0},{16,8},{24,16},{1,25},{9,1},{17,9},{25,17},{2,26},{10... | collective-permute-start | bytes 1769480 | tf_op jit(solution)/shard_map/ppermute | solution.py:610
  218.6 15.1 %collective-permute-start.20 = (bf16[2,48,3072]{2,1,0:T(8,128)(2,1)S(1)}, bf16[2,48,3072]{2,1,0:T(8,128)(2,1)S(1)}, u32[]{:S(2)}, u32[]{:S(2)}) collective-permute-start(bf16[2,48,3072]{2,1,0:T(8,128)(2,1)S(1)} %get-tuple-element.81), channel_id=1, source_target_pairs={{0,32},{32,64},{64,96},{96,0},{1,33},{33,65},{65,97},{97,1},{2,34}... | collective-permute-start | bytes 1769480 | tf_op jit(solution)/shard_map/ppermute | solution.py:606
  218.7 15.0 %collective-permute-start.21 = (bf16[2,48,3072]{2,1,0:T(8,128)(2,1)S(1)}, bf16[2,48,3072]{2,1,0:T(8,128)(2,1)S(1)}, u32[]{:S(2)}, u32[]{:S(2)}) collective-permute-start(bf16[2,48,3072]{2,1,0:T(8,128)(2,1)S(1)} %get-tuple-element.82), channel_id=1, source_target_pairs={{0,8},{8,16},{16,24},{24,0},{1,9},{9,17},{17,25},{25,1},{2,10},{10... | collective-permute-start | bytes 1769480 | tf_op jit(solution)/shard_map/ppermute | solution.py:606
  218.8 15.0 %collective-permute-start.22 = (bf16[2,48,3072]{2,1,0:T(8,128)(2,1)S(1)}, bf16[2,48,3072]{2,1,0:T(8,128)(2,1)S(1)}, u32[]{:S(2)}, u32[]{:S(2)}) collective-permute-start(bf16[2,48,3072]{2,1,0:T(8,128)(2,1)S(1)} %get-tuple-element.83), channel_id=1, source_target_pairs={{0,96},{32,0},{64,32},{96,64},{1,97},{33,1},{65,33},{97,65},{2,98}... | collective-permute-start | bytes 1769480 | tf_op jit(solution)/shard_map/ppermute | solution.py:610
  221.9 11.8 %collective-permute-start.23 = (bf16[2,48,3072]{2,1,0:T(8,128)(2,1)S(1)}, bf16[2,48,3072]{2,1,0:T(8,128)(2,1)S(1)}, u32[]{:S(2)}, u32[]{:S(2)}) collective-permute-start(bf16[2,48,3072]{2,1,0:T(8,128)(2,1)S(1)} %get-tuple-element.84), channel_id=1, source_target_pairs={{0,24},{8,0},{16,8},{24,16},{1,25},{9,1},{17,9},{25,17},{2,26},{10... | collective-permute-start | bytes 1769480 | tf_op jit(solution)/shard_map/ppermute | solution.py:610
  234.4 26.8 %collective-permute-start.24 = (bf16[4,48,3072]{2,1,0:T(8,128)(2,1)S(1)}, bf16[4,48,3072]{2,1,0:T(8,128)(2,1)S(1)}, u32[]{:S(2)}, u32[]{:S(2)}) collective-permute-start(bf16[4,48,3072]{2,1,0:T(8,128)(2,1)S(1)} %get-tuple-element.90), channel_id=1, source_target_pairs={{0,32},{32,64},{64,96},{96,0},{1,33},{33,65},{65,97},{97,1},{2,34}... | collective-permute-start | bytes 3538952 | tf_op jit(solution)/shard_map/ppermute | solution.py:606
  234.5 26.8 %collective-permute-start.25 = (bf16[4,48,3072]{2,1,0:T(8,128)(2,1)S(1)}, bf16[4,48,3072]{2,1,0:T(8,128)(2,1)S(1)}, u32[]{:S(2)}, u32[]{:S(2)}) collective-permute-start(bf16[4,48,3072]{2,1,0:T(8,128)(2,1)S(1)} %get-tuple-element.91), channel_id=1, source_target_pairs={{0,8},{8,16},{16,24},{24,0},{1,9},{9,17},{17,25},{25,1},{2,10},{10... | collective-permute-start | bytes 3538952 | tf_op jit(solution)/shard_map/ppermute | solution.py:606
  234.6 27.0 %collective-permute-start.27 = (bf16[4,48,3072]{2,1,0:T(8,128)(2,1)S(1)}, bf16[4,48,3072]{2,1,0:T(8,128)(2,1)S(1)}, u32[]{:S(2)}, u32[]{:S(2)}) collective-permute-start(bf16[4,48,3072]{2,1,0:T(8,128)(2,1)S(1)} %get-tuple-element.92), channel_id=1, source_target_pairs={{0,24},{8,0},{16,8},{24,16},{1,25},{9,1},{17,9},{25,17},{2,26},{10... | collective-permute-start | bytes 3538952 | tf_op jit(solution)/shard_map/ppermute | solution.py:610
  237.8 25.1 %collective-permute-start.26 = (bf16[4,48,3072]{2,1,0:T(8,128)(2,1)S(1)}, bf16[4,48,3072]{2,1,0:T(8,128)(2,1)S(1)}, u32[]{:S(2)}, u32[]{:S(2)}) collective-permute-start(bf16[4,48,3072]{2,1,0:T(8,128)(2,1)S(1)} %get-tuple-element.85.late), channel_id=1, source_target_pairs={{0,96},{32,0},{64,32},{96,64},{1,97},{33,1},{65,33},{97,65},{2,98}... | collective-permute-start | bytes 3538952 | tf_op jit(solution)/shard_map/ppermute | solution.py:610
  263.9 12.0 %collective-permute-start.29 = (bf16[48,3072]{1,0:T(8,128)(2,1)S(1)}, bf16[48,3072]{1,0:T(8,128)(2,1)S(1)}, u32[]{:S(2)}, u32[]{:S(2)}) collective-permute-start(bf16[48,3072]{1,0:T(8,128)(2,1)S(1)} %get-tuple-element.96), channel_id=1, source_target_pairs={{0,64},{32,96},{64,0},{96,32},{1,65},{33,97},{65,1},{97,33},{2,66}... | collective-permute-start | bytes 884744 | tf_op jit(solution)/shard_map/ppermute | solution.py:614
  265.6 10.3 %collective-permute-start.30 = (bf16[48,3072]{1,0:T(8,128)(2,1)S(1)}, bf16[48,3072]{1,0:T(8,128)(2,1)S(1)}, u32[]{:S(2)}, u32[]{:S(2)}) collective-permute-start(bf16[48,3072]{1,0:T(8,128)(2,1)S(1)} %get-tuple-element.97), channel_id=1, source_target_pairs={{0,8},{8,16},{16,24},{24,0},{1,9},{9,17},{17,25},{25,1},{2,10},{10... | collective-permute-start | bytes 884744 | tf_op jit(solution)/shard_map/ppermute | solution.py:606
  284.3 9.3 %collective-permute-start.35 = (bf16[16,6144]{1,0:T(8,128)(2,1)}, bf16[16,6144]{1,0:T(8,128)(2,1)}, u32[]{:S(2)}, u32[]{:S(2)}) collective-permute-start(bf16[16,6144]{1,0:T(8,128)(2,1)} %get-tuple-element.103), channel_id=1, source_target_pairs={{0,1},{1,2},{2,3},{3,0},{4,5},{5,6},{6,7},{7,4},{8,9},{9,10},{10,1... | collective-permute-start | bytes 589832 | tf_op jit(solution)/shard_map/ppermute | solution.py:606
  284.3 9.3 %collective-permute-start.36 = (bf16[16,6144]{1,0:T(8,128)(2,1)}, bf16[16,6144]{1,0:T(8,128)(2,1)}, u32[]{:S(2)}, u32[]{:S(2)}) collective-permute-start(bf16[16,6144]{1,0:T(8,128)(2,1)} %get-tuple-element.104), channel_id=1, source_target_pairs={{0,2},{1,3},{2,0},{3,1},{4,6},{5,7},{6,4},{7,5},{8,10},{9,11},{10,... | collective-permute-start | bytes 589832 | tf_op jit(solution)/shard_map/ppermute | solution.py:614
  (30 other events, 404.0 us)
Sparse Core Ops, SparseCore 0:
  9.6 74.3 all-gather.2
  85.6 38.2 all-gather.4
  150.5 64.3 reduce-scatter.1

commit v9 on v8

--- a/solution.py
+++ b/solution.py
@@ -116,7 +116,7 @@
     )(arrived)
 
 
-def carry_kernel(q_ref, inner_ref, cum_ref, state_ref, gain_ref, out_ref):
+def carry_kernel(q_ref, inner_ref, cum_ref, state_ref, gain_ref, held, out_ref, same):
     shares, slice_len = out_ref.shape[0], out_ref.shape[2]
     heads = cum_ref.shape[2]
     grow = jnp.exp(cum_ref[0])
@@ -131,7 +131,7 @@
             ]
 
 
-def carried(q, inner, cum, state, gain, shares):
+def carried(q, inner, cum, state, gain, shares, held):
     seqs, steps, width = q.shape
     heads = width // HEAD
     block = pl.BlockSpec((1, steps, width), lambda s: (s, 0, 0))
@@ -144,12 +144,20 @@
             pl.BlockSpec((1, steps, heads), lambda s: (s, 0, 0)),
             pl.BlockSpec((heads, HEAD, HEAD), lambda s: (s, 0, 0)),
             pl.BlockSpec((1, width), lambda s: (0, 0)),
+            ANY,
         ],
-        out_specs=pl.BlockSpec((shares, 1, steps // shares, width), lambda s: (0, s, 0, 0)),
-        out_shape=jax.ShapeDtypeStruct((shares, seqs, steps // shares, width), BF),
-        compiler_params=pltpu.CompilerParams(vmem_limit_bytes=32 * 2**20),
+        out_specs=[
+            pl.BlockSpec((shares, 1, steps // shares, width), lambda s: (0, s, 0, 0)),
+            ANY,
+        ],
+        out_shape=[
+            jax.ShapeDtypeStruct((shares, seqs, steps // shares, width), BF),
+            jax.ShapeDtypeStruct(held.shape, BF),
+        ],
+        input_output_aliases={5: 1},
+        compiler_params=pltpu.CompilerParams(vmem_limit_bytes=56 * 2**20),
         name="carried_norm",
-    )(q, inner, cum, state, gain)
+    )(q, inner, cum, state, gain, held)
 
 
 def call(kernel, name, outs, *args, **kw):
@@ -304,7 +312,7 @@
     b_down[...] = b_above[2:4]
 
 
-def stack_kernel(a0, b0, a3, b3, a1, b1, a2, b2, h0, h1, o0, o1, *same):
+def stack_kernel(a0, b0, a3, b3, a1, b1, a2, b2, held, o0, o1, same):
     for i, (a, b) in enumerate(((a0, b0), (a1, b1), (a2, b2), (a3, b3))):
         o0[i] = a[...]
         o1[i] = b[...]
@@ -318,18 +326,18 @@
 
 
 class Stream:
-    def __init__(self, source, spans, buf, sems):
-        self.source, self.spans, self.buf, self.sems = source, spans, buf, sems
-        self.chunks = source.shape[1] // TILE
+    def __init__(self, sources, spans, buf, sems):
+        self.sources, self.spans, self.buf, self.sems = sources, spans, buf, sems
+        self.chunks = sources[0].shape[1] // TILE
 
     def copies(self, c):
         slot = lax.rem(c, AHEAD + 1)
         cols = pl.ds(pl.multiple_of(c * TILE, TILE), TILE)
         made, at = [], 0
-        for i, (start, size) in enumerate(self.spans):
+        for i, (source, (start, size)) in enumerate(zip(self.sources, self.spans)):
             made.append(
                 pltpu.make_async_copy(
-                    self.source.at[pl.ds(start, size), cols],
+                    source.at[pl.ds(start, size), cols],
                     self.buf.at[slot, pl.ds(at, size)],
                     self.sems.at[slot, i],
                 )
@@ -345,33 +353,23 @@
         for c in range(AHEAD):
             self.start(c)
 
-    def run(self, body, then=None):
+    def run(self, body):
         @pl.loop(0, self.chunks)
         def _(c):
             @pl.when(c + AHEAD < self.chunks)
             def _():
                 self.start(c + AHEAD)
 
-            if then is not None:
-
-                @pl.when(c + AHEAD >= self.chunks)
-                def _():
-                    then.start(c + AHEAD - self.chunks)
-
             for copy in self.copies(c):
                 copy.wait()
             body(c, self.buf[lax.rem(c, AHEAD + 1)])
 
 
-def gate_up_spans(units):
-    return ((0, 2 * units), (3 * units, 2 * units))
-
-
 def down_spans(units):
-    return ((2 * units, units), (5 * units, units))
-
-
-def gate_up(refs_a, refs_b, x, part_a, part_b, stream, then=None):
+    return ((2 * units, units), (2 * units, units))
+
+
+def gate_up(refs_a, refs_b, x, part_a, part_b, stream):
     rows, half = refs_a[0].shape[1:]
     each = half // TILE
     part_a[...] = jnp.zeros_like(part_a)
@@ -388,9 +386,12 @@
                     for i in range(ref.shape[0]):
                         x[row : row + rows, :] = ref[i, :, at]
                         row += rows
-                part[...] += nt(x[...], weights)
-
-    stream.run(body, then)
+                at = 0
+                for w in weights:
+                    part[:, at : at + w.shape[0]] += nt(x[...], w)
+                    at += w.shape[0]
+
+    stream.run(body)
 
 
 def down_product(value, stream, outs_a, outs_b):
@@ -413,11 +414,44 @@
     stream.run(body)
 
 
-def near_kernel(a0, b0, a1, b1, a2, b2, weights, acc, x, part, buf, sems):
+class Resident:
+    def __init__(self, places, sources=(), sems=None):
+        self.places, self.sources, self.sems = places, sources, sems
+        self.chunks = places[0].shape[1] // TILE
+
+    def copies(self, c):
+        cols = pl.ds(pl.multiple_of(c * TILE, TILE), TILE)
+        return [
+            pltpu.make_async_copy(ref.at[pl.ds(start, size), cols], place.at[pl.ds(at, size), cols], self.sems.at[c, i])
+            for i, (ref, start, size, place, at) in enumerate(self.sources)
+        ]
+
+    def start(self, c):
+        for copy in self.copies(c):
+            copy.start()
+
+    def run(self, body):
+        @pl.loop(0, self.chunks)
+        def _(c):
+            if self.sources:
+
+                @pl.when(c + AHEAD < self.chunks)
+                def _():
+                    self.start(c + AHEAD)
+
+                for copy in self.copies(c):
+                    copy.wait()
+            cols = pl.ds(pl.multiple_of(c * TILE, TILE), TILE)
+            body(c, [place[:, cols] for place in self.places])
+
+
+def near_kernel(a0, b0, a1, b1, a2, b2, mine, other, acc, w0, w1, x, part, sems):
     rows = a0.shape[1]
     block = 4 * rows
-    stream = Stream(weights, gate_up_spans(weights.shape[0] // 6), buf, sems)
-    stream.begin()
+    wide = w0.shape[0]
+    stream = Resident((w0, w1), ((mine, 0, wide, w0, 0), (other, 0, wide, w1, 0)), sems)
+    for c in range(AHEAD):
+        stream.start(c)
     gate_up((a0, a1, a2), (b0, b1, b2), x, acc.at[pl.ds(0, 3 * block)], part, stream)
     acc[3 * block :, :] = jnp.zeros((block, acc.shape[1]), F32)
     for y in range(3):
@@ -427,15 +461,14 @@
 
 
 def far_kernel(
-    acc, a3, b3, a4, b4, weights, hidden, oa3, oa4, ob3, ob4, x, part, own, value, buf, sems, dbuf, dsems
+    acc, a3, b3, a4, b4, w0, w1, mine, other, hidden, oa3, oa4, ob3, ob4, x, part, own, value, dbuf, dsems
 ):
     rows = a3.shape[1]
     block = 4 * rows
-    units = weights.shape[0] // 6
-    stream = Stream(weights, gate_up_spans(units), buf, sems)
-    downs = Stream(weights, down_spans(units), dbuf, dsems)
-    stream.begin()
-    gate_up((a3, a4), (b3, b4), x, part.at[0], part.at[1], stream, downs)
+    units = mine.shape[0] // 3
+    downs = Stream((mine, other), down_spans(units), dbuf, dsems)
+    downs.begin()
+    gate_up((a3, a4), (b3, b4), x, part.at[0], part.at[1], Resident((w0, w1)))
     own[...] = acc[...]
     own[3 * block :, :] += part[0]
     for row, z in by_y(rows, 3):
@@ -450,10 +483,10 @@
     down_product(value, downs, (oa3, oa4), (ob3, ob4))
 
 
-def rest_kernel(hidden, weights, oa0, oa1, oa2, ob0, ob1, ob2, value, dbuf, dsems):
+def rest_kernel(hidden, mine, other, oa0, oa1, oa2, ob0, ob1, ob2, value, dbuf, dsems):
     rows = oa0.shape[1]
     block = 4 * rows
-    downs = Stream(weights, down_spans(weights.shape[0] // 6), dbuf, dsems)
+    downs = Stream((mine, other), down_spans(mine.shape[0] // 3), dbuf, dsems)
     downs.begin()
     value[0] = hidden[: 3 * block, :]
     for y in range(3):
@@ -474,28 +507,30 @@
     ]
 
 
-def near(xs, weights):
+def near(xs, mine, other):
     rows = xs[0].shape[1]
-    wide = weights.shape[0] * 2 // 3
+    units, model = mine.shape[0] // 3, mine.shape[1]
+    wide = 4 * units
     return call(
         near_kernel,
         "near_rows",
-        [((16 * rows, wide), F32)],
+        [((16 * rows, wide), F32)] + [((2 * units, model), BF)] * 2,
         *xs,
-        weights,
-        in_specs=[VM] * 6 + [ANY],
-        out_specs=[VM],
+        mine,
+        other,
+        in_specs=[VM] * 6 + [ANY] * 2,
+        out_specs=[VM] * 3,
         scratch_shapes=[
             pltpu.VMEM((12 * rows, TILE), BF),
             pltpu.VMEM((12 * rows, wide), F32),
-            *slots(wide, 2),
+            pltpu.SemaphoreType.DMA((model // TILE, 2)),
         ],
-        cost_estimate=cost(2 * 12 * rows * wide * weights.shape[1]),
-        vmem=30,
-    )[0]
-
-
-def far(acc, xs, weights):
+        cost_estimate=cost(2 * 12 * rows * wide * model),
+        vmem=14,
+    )
+
+
+def far(acc, xs, w0, w1, mine, other):
     rows, half = xs[0].shape[1:]
     wide = acc.shape[1]
     return call(
@@ -504,34 +539,37 @@
         [((16 * rows, wide // 2), BF)] + [((2, rows, half), BF)] * 4,
         acc,
         *xs,
-        weights,
-        in_specs=[VM] * 5 + [ANY],
+        w0,
+        w1,
+        mine,
+        other,
+        in_specs=[VM] * 7 + [ANY] * 2,
         out_specs=[VM] * 5,
         scratch_shapes=[
             pltpu.VMEM((4 * rows, TILE), BF),
             pltpu.VMEM((2, 4 * rows, wide), F32),
             pltpu.VMEM(acc.shape, F32),
             pltpu.VMEM((2, 4 * rows, wide // 2), BF),
-            *slots(wide, 2),
             *slots(wide // 2, 2),
         ],
-        vmem=32,
-    )
-
-
-def rest(hidden, weights, rows):
-    wide, half = hidden.shape[1], weights.shape[1] // 2
+        vmem=24,
+    )
+
+
+def rest(hidden, mine, other, rows):
+    wide, half = hidden.shape[1], mine.shape[1] // 2
     return call(
         rest_kernel,
         "rest_rows",
         [((4, rows, half), BF)] * 6,
         hidden,
-        weights,
-        in_specs=[VM, ANY],
+        mine,
+        other,
+        in_specs=[VM, ANY, ANY],
         out_specs=[VM] * 6,
         scratch_shapes=[pltpu.VMEM((2, 12 * rows, wide), BF), *slots(wide, 2)],
-        cost_estimate=cost(2 * 12 * rows * wide * weights.shape[1]),
-        vmem=32,
+        cost_estimate=cost(2 * 12 * rows * wide * mine.shape[1]),
+        vmem=44,
     )
 
 
@@ -639,7 +677,7 @@
 
     weight_out = lax.all_gather(out_weight.T, SEQ, axis=0, tiled=True)
     weights = jnp.concatenate([gate_weight[0], up_weight[0], down_weight[0]])
-    weights = lax.all_gather(weights, "core", axis=0, tiled=True)
+    other = lax.ppermute(weights, "core", ring(2, 1))
     routes = picks.reshape(rows, 2)
     turned = routes.T
     all_routes = [turned] + [lax.ppermute(turned, "x", ring(4, -delta)) for delta in (1, 2, 3)]
@@ -650,8 +688,8 @@
     arrived = lax.all_to_all(states, SEQ, 0, 0, tiled=True)
     prefix = lax.all_to_all(scan_states(arrived), SEQ, 0, 0, tiled=True)
     prefix = prefix.reshape(seqs * width // HEAD, HEAD, HEAD)
-    normed = carried(
-        queries, inner, cum, prefix, attn_gain.reshape(1, width), shares
+    normed, other = carried(
+        queries, inner, cum, prefix, attn_gain.reshape(1, width), shares, other
     )
     normed = normed.reshape(shares * rows, width)
 
@@ -686,10 +724,10 @@
         out_specs=[VM] * 2,
     )
 
-    a4, b4, weights, whole = call(
+    a4, b4, whole = call(
         stack_kernel,
         "stack",
-        [((4, size, half), BF)] * 2 + [(weights.shape, BF), (whole.shape, BF)],
+        [((4, size, half), BF)] * 2 + [(whole.shape, BF)],
         a0,
         b0,
         across(a0, "y"),
@@ -698,12 +736,11 @@
         up_one(b0, "z"),
         down_one(a0, "y"),
         down_one(b0, "z"),
-        weights,
         whole,
-        in_specs=[VM] * 8 + [ANY] * 2,
-        out_specs=[VM] * 2 + [ANY] * 2,
-        input_output_aliases={8: 2, 9: 3},
-        vmem=54,
+        in_specs=[VM] * 8 + [ANY],
+        out_specs=[VM] * 2 + [ANY],
+        input_output_aliases={8: 2},
+        vmem=50,
     )
     mixed = lax.psum_scatter(whole, "x", scatter_dimension=0, tiled=True)
     a_below, b_below = up_one(a4, "z"), up_one(b4, "y")
@@ -722,9 +759,9 @@
     )
     ends_in = (up_one(a_up, "z"), up_one(b_up, "y"), down_one(a_down, "z"), down_one(b_down, "y"))
 
-    acc = near((a4, b4, a_below, b_below, a_above, b_above), weights)
-    hidden, *ends = far(acc, ends_in, weights)
-    body = rest(hidden, weights, size)
+    acc, w0, w1 = near((a4, b4, a_below, b_below, a_above, b_above), weights, other)
+    hidden, *ends = far(acc, ends_in, w0, w1, weights, other)
+    body = rest(hidden, weights, other, size)
     oa, ob = (*body[:3], *ends[:2]), (*body[3:], *ends[2:])
     a_below, a_above, b_below, b_above = call(
         fold_kernel,

time: 304 us -> 300 us (0.987)
    ppermute x14, waiting for transfers between devices: 34.3 us -> 10.4 us  [down_one(): return lax.ppermute(x, axis, ring(4, -1))]
    ppermute x14, waiting for transfers between devices: 43.9 us -> 65.3 us  [up_one(): return lax.ppermute(x, axis, ring(4, 1))]
    unnamed x43 -> x25, local copies, waits for them, and re-layouts: 6.79 us -> 4.93 us
  transfers between devices with their start and end apart: 41 -> 41, of which waited for: 20 -> 23; matrix products, arithmetic and copies ran while one was open for 3% -> 3% of each run, Pallas kernels for 24% -> 23%
where the time goes in v9:
time: 300 us
  waiting for transfers between devices  103 us (34%)
  Pallas kernels  80.3 us (27%)
  starting transfers between devices  66.2 us (22%)
  blocking collectives  21.7 us (7%)
  between operations  13.6 us (5%)
  other arithmetic  9.37 us (3%)
  local copies, waits for them, and re-layouts  5.16 us (2%)
    pallas_call x15, Pallas kernels, call(): pl.pallas_call(kernel, out_shape=[jax.ShapeDtypeStruct(s, d) for s, d in...  67.6 us
    ppermute x14, waiting for transfers between devices, up_one(): return lax.ppermute(x, axis, ring(4, 1))  65.3 us
    ppermute x14, starting transfers between devices, down_one(): return lax.ppermute(x, axis, ring(4, -1))  37.4 us
    all_to_all x1, blocking collectives, shards(): arrived = lax.all_to_all(states, SEQ, 0, 0, tiled=True)  21.7 us
    ppermute x6, starting transfers between devices, across(): return lax.ppermute(x, axis, ring(4, 2))  11.2 us
    ppermute x14, waiting for transfers between devices, down_one(): return lax.ppermute(x, axis, ring(4, -1))  10.4 us
    concatenate x1, other arithmetic, shards(): weights = jnp.concatenate([gate_weight[0], up_weight[0], down_weight[0]])  9.37 us
    ppermute x14, starting transfers between devices, up_one(): return lax.ppermute(x, axis, ring(4, 1))  9.21 us
  transfers between devices with their start and end apart: 41, of which 23 were waited for; matrix products, arithmetic and copies ran while one was open for 3% of the time, Pallas kernels for 23%

profile of v9, /device:TPU:0, one launch (start us, length us, event | category | flops | bytes accessed | tf_op | source)
XLA Modules:
  0.0 299.6 jit_solution(17144125792971644392)
XLA Ops:
  7.3 9.4 %pad_maximum_fusion.mine = bf16[864,6144]{1,0:T(8,128)(2,1)} fusion(bf16[288,6144]{1,0:T(8,128)(2,1)} %bitcast.28, bf16[288,6144]{1,0:T(8,128)(2,1)} %bitcast.29, bf16[288,6144]{1,0:T(8,128)(2,1)} %bitcast.30), kind=kLoop, calls=%fused_computation | loop fusion | flops 31850496 | bytes 21233664 | tf_op jit(solution)/shard_map/concatenate | solution.py:679
  16.6 7.1 %local_attention.1 = (f32[2,256,1024]{2,1,0:T(8,128)}, bf16[32,80,128]{2,1,0:T(8,128)(2,1)}, f32[2,256,8]{2,1,0:T(8,128)}) custom-call(bf16[2,256,1024]{2,1,0:T(8,128)(2,1)} %q_ref.3, bf16[2,256,1024]{2,1,0:T(8,128)(2,1)} %k_ref.1, bf16[2,256,1024]{2,1,0:T(8,128)(2,1)} %v_ref.1, f32[2,8,256]{2,1,0:T(8,128)} %bitcast.33), custom_call_target="tpu_custom_call" | custom-call | tf_op jit(solution)/shard_map/local_attention/pallas_call | solution.py:84
  23.8 21.7 %all_to_all.10.in_ref = bf16[32,80,128]{2,1,0:T(8,128)(2,1)S(1)} all-to-all(bf16[32,80,128]{2,1,0:T(8,128)(2,1)} %get-tuple-element.62), channel_id=1, replica_groups=mesh['z'=4,'y'=4,'core'=2,'x'=4] {'z','y','core'}, dimensions={0} | all-to-all | bytes 1310720 | tf_op jit(solution)/shard_map/all_to_all | solution.py:688
  46.4 3.9 %all-to-all-start.1 = ((bf16[32,64,128]{2,1,0:T(8,128)(2,1)}), bf16[32,64,128]{2,1,0:T(8,128)(2,1)S(1)}, u32[]{:S(2)}, u32[]{:S(2)}) async-start(bf16[32,64,128]{2,1,0:T(8,128)(2,1)} %state_prefix.1), calls=%async_computation.1 | async-start | bytes 1048576 | tf_op jit(solution)/shard_map/all_to_all | solution.py:689
  50.5 2.8 collective-permute-start
  56.6 2.8 collective-permute-done.1
  60.5 7.5 %all-to-all-done.1 = bf16[32,64,128]{2,1,0:T(8,128)(2,1)S(1)} async-done(((bf16[32,64,128]{2,1,0:T(8,128)(2,1)}), bf16[32,64,128]{2,1,0:T(8,128)(2,1)S(1)}, u32[]{:S(2)}, u32[]{:S(2)}) %all-to-all-start.1) | async-done | bytes 524320 | tf_op jit(solution)/shard_map/all_to_all | solution.py:689
  68.7 4.6 %carried_norm.1 = (bf16[4,2,64,1024]{3,2,1,0:T(8,128)(2,1)}, bf16[864,6144]{1,0:T(8,128)(2,1)}) custom-call(bf16[2,256,1024]{2,1,0:T(8,128)(2,1)} %q_ref.3, f32[2,256,1024]{2,1,0:T(8,128)} %get-tuple-element.60.inner_ref, f32[2,256,8]{2,1,0:T(8,128)} %get-tuple-element.61.cum_ref, bf16[16,128,128]{2,1,0:T(8,128)(2,1)} %bitcast.31, ...), custom_call_target="tpu_custom_call", output_to_operand_aliasing={{1}: (5, {})} | custom-call | tf_op jit(solution)/shard_map/carried_norm/pallas_call | solution.py:138
  75.0 9.0 %all-gather.2.cloned.1.call-done.weight.weight_ref = bf16[6144,1024]{1,0:T(8,128)(2,1)} async-done(((bf16[192,1024]{1,0:T(8,128)(2,1)}), bf16[6144,1024]{1,0:T(8,128)(2,1)}) %all-gather.2.cloned.1.call-update) | async-done | bytes 12582928 | tf_op jit(solution)/shard_map/all_gather | solution.py:678
  84.0 8.0 %selected_projection.1 = (bf16[48,6144]{1,0:T(8,128)(2,1)S(1)}, bf16[48,6144]{1,0:T(8,128)(2,1)S(1)}, bf16[48,6144]{1,0:T(8,128)(2,1)}, bf16[48,6144]{1,0:T(8,128)(2,1)S(1)}) custom-call(bf16[192,1024]{1,0:T(8,128)(2,1)S(1)} %pick.1.picked, bf16[192,128]{1,0:T(8,128)(2,1)S(1)} %get-tuple-element.64.own, ...), custom_call_target="tpu_custom_call" | custom-call | tf_op jit(solution)/shard_map/selected_projection/pallas_call | solution.py:165
  92.0 3.1 %collective-permute-start.4 = (bf16[48,6144]{1,0:T(8,128)(2,1)}, bf16[48,6144]{1,0:T(8,128)(2,1)S(1)}, u32[]{:S(2)}, u32[]{:S(2)}) collective-permute-start(bf16[48,6144]{1,0:T(8,128)(2,1)} %get-tuple-element.66), channel_id=1, source_target_pairs={{0,2},{1,3},{2,0},{3,1},{4,6},{5,7},{6,4},{7,5},{8,10},{9,11},{10,... | collective-permute-start | bytes 1769480 | tf_op jit(solution)/shard_map/ppermute | solution.py:652
  98.3 12.3 %whole_projection.1 = (bf16[512,6144]{1,0:T(8,128)(2,1)}, f32[8,128]{1,0:T(8,128)}) custom-call(bf16[512,1024]{1,0:T(8,128)(2,1)} %bitcast.18, bf16[6144,1024]{1,0:T(8,128)(2,1)} %all-gather.2.cloned.1.call-done.weight.weight_ref), custom_call_target="tpu_custom_call" | custom-call | flops 6442450944 | bytes 25165824 | tf_op jit(solution)/shard_map/whole_projection/pallas_call | solution.py:165
  110.6 11.3 %collective-permute-done.5.c = bf16[48,6144]{1,0:T(8,128)(2,1)S(1)} collective-permute-done((bf16[48,6144]{1,0:T(8,128)(2,1)S(1)}, bf16[48,6144]{1,0:T(8,128)(2,1)S(1)}, u32[]{:S(2)}, u32[]{:S(2)}) %collective-permute-start.5) | collective-permute-done | bytes 589856 | tf_op jit(solution)/shard_map/ppermute | solution.py:644
  123.2 3.1 %collective-permute-start.7 = (bf16[48,3072]{1,0:T(8,128)(2,1)S(1)}, bf16[48,3072]{1,0:T(8,128)(2,1)S(1)}, u32[]{:S(2)}, u32[]{:S(2)}) collective-permute-start(bf16[48,3072]{1,0:T(8,128)(2,1)S(1)} %get-tuple-element.70.a0), channel_id=1, source_target_pairs={{0,16},{8,24},{16,0},{24,8},{1,17},{9,25},{17,1},{25,9},{2,18},{10... | collective-permute-start | bytes 884744 | tf_op jit(solution)/shard_map/ppermute | solution.py:652
  128.5 2.7 collective-permute-start.11
  131.2 3.5 %collective-permute-done.7.a3 = bf16[48,3072]{1,0:T(8,128)(2,1)S(1)} collective-permute-done((bf16[48,3072]{1,0:T(8,128)(2,1)S(1)}, bf16[48,3072]{1,0:T(8,128)(2,1)S(1)}, u32[]{:S(2)}, u32[]{:S(2)}) %collective-permute-start.7) | collective-permute-done | bytes 294944 | tf_op jit(solution)/shard_map/ppermute | solution.py:652
  140.0 3.0 %collective-permute-done.10.b1 = bf16[48,3072]{1,0:T(8,128)(2,1)S(1)} collective-permute-done((bf16[48,3072]{1,0:T(8,128)(2,1)S(1)}, bf16[48,3072]{1,0:T(8,128)(2,1)S(1)}, u32[]{:S(2)}, u32[]{:S(2)}) %collective-permute-start.10) | collective-permute-done | bytes 294944 | tf_op jit(solution)/shard_map/ppermute | solution.py:644
  148.0 3.0 collective-permute-start.16
  151.0 22.6 %collective-permute-done.13.a1.a_below = bf16[4,48,3072]{2,1,0:T(8,128)(2,1)S(1)} collective-permute-done((bf16[4,48,3072]{2,1,0:T(8,128)(2,1)S(1)}, bf16[4,48,3072]{2,1,0:T(8,128)(2,1)S(1)}, u32[]{:S(2)}, u32[]{:S(2)}) %collective-permute-start.13) | collective-permute-done | bytes 1179680 | tf_op jit(solution)/shard_map/ppermute | solution.py:644
  177.6 3.2 %collective-permute-start.19 = (bf16[2,48,3072]{2,1,0:T(8,128)(2,1)S(1)}, bf16[2,48,3072]{2,1,0:T(8,128)(2,1)S(1)}, u32[]{:S(2)}, u32[]{:S(2)}) collective-permute-start(bf16[2,48,3072]{2,1,0:T(8,128)(2,1)S(1)} %get-tuple-element.80), channel_id=1, source_target_pairs={{0,96},{32,0},{64,32},{96,64},{1,97},{33,1},{65,33},{97,65},{2,98}... | collective-permute-start | bytes 1769480 | tf_op jit(solution)/shard_map/ppermute | solution.py:648
  182.9 16.3 %near_rows.1 = (f32[768,1152]{1,0:T(8,128)S(1)}, bf16[576,6144]{1,0:T(8,128)(2,1)S(1)}, bf16[576,6144]{1,0:T(8,128)(2,1)S(1)}) custom-call(bf16[4,48,3072]{2,1,0:T(8,128)(2,1)S(1)} %get-tuple-element.74.a0, bf16[4,48,3072]{2,1,0:T(8,128)(2,1)S(1)} %copy-done.9, bf16[4,48,3072]{2,1,0:T(8,128)(2,1)S(1)} %collective-permute-done.13.a1.a_below, ...), custom_call_target="tpu_custom_call" | custom-call | flops 8153726976 | bytes 1048576 | tf_op jit(solution)/shard_map/near_rows/pallas_call | solution.py:165
  199.2 12.5 %far_rows.1 = (bf16[768,576]{1,0:T(8,128)(2,1)S(1)}, bf16[2,48,3072]{2,1,0:T(8,128)(2,1)S(1)}, bf16[2,48,3072]{2,1,0:T(8,128)(2,1)S(1)}, bf16[2,48,3072]{2,1,0:T(8,128)(2,1)S(1)}, bf16[2,48,3072]{2,1,0:T(8,128)(2,1)S(1)}) custom-call(f32[768,1152]{1,0:T(8,128)S(1)} %get-tuple-element.77.acc, bf16[2,48,3072]{2,1,0:T(8,128)(2,1)S(1)} %collective-permute-done.17.a3, ...), custom_call_target="tpu_custom_call" | custom-call | tf_op jit(solution)/shard_map/far_rows/pallas_call | solution.py:165
  211.9 3.2 %collective-permute-start.23 = (bf16[2,48,3072]{2,1,0:T(8,128)(2,1)S(1)}, bf16[2,48,3072]{2,1,0:T(8,128)(2,1)S(1)}, u32[]{:S(2)}, u32[]{:S(2)}) collective-permute-start(bf16[2,48,3072]{2,1,0:T(8,128)(2,1)S(1)} %get-tuple-element.91), channel_id=1, source_target_pairs={{0,96},{32,0},{64,32},{96,64},{1,97},{33,1},{65,33},{97,65},{2,98}... | collective-permute-start | bytes 1769480 | tf_op jit(solution)/shard_map/ppermute | solution.py:648
  215.0 3.2 %collective-permute-start.24 = (bf16[2,48,3072]{2,1,0:T(8,128)(2,1)S(1)}, bf16[2,48,3072]{2,1,0:T(8,128)(2,1)S(1)}, u32[]{:S(2)}, u32[]{:S(2)}) collective-permute-start(bf16[2,48,3072]{2,1,0:T(8,128)(2,1)S(1)} %get-tuple-element.92), channel_id=1, source_target_pairs={{0,24},{8,0},{16,8},{24,16},{1,25},{9,1},{17,9},{25,17},{2,26},{10... | collective-permute-start | bytes 1769480 | tf_op jit(solution)/shard_map/ppermute | solution.py:648
  218.2 8.5 %rest_rows.1 = (bf16[4,48,3072]{2,1,0:T(8,128)(2,1)S(1)}, bf16[4,48,3072]{2,1,0:T(8,128)(2,1)S(1)}, bf16[4,48,3072]{2,1,0:T(8,128)(2,1)S(1)}, bf16[4,48,3072]{2,...) custom-call(bf16[768,576]{1,0:T(8,128)(2,1)S(1)} %get-tuple-element.84.hidden, ...), custom_call_target="tpu_custom_call" | custom-call | flops 4076863488 | bytes 1048576 | tf_op jit(solution)/shard_map/rest_rows/pallas_call | solution.py:165
  229.2 3.2 %collective-permute-start.27 = (bf16[4,48,3072]{2,1,0:T(8,128)(2,1)S(1)}, bf16[4,48,3072]{2,1,0:T(8,128)(2,1)S(1)}, u32[]{:S(2)}, u32[]{:S(2)}) collective-permute-start(bf16[4,48,3072]{2,1,0:T(8,128)(2,1)S(1)} %get-tuple-element.93.late), channel_id=1, source_target_pairs={{0,96},{32,0},{64,32},{96,64},{1,97},{33,1},{65,33},{97,65},{2,98}... | collective-permute-start | bytes 3538952 | tf_op jit(solution)/shard_map/ppermute | solution.py:648
  232.3 3.1 %collective-permute-start.28 = (bf16[4,48,3072]{2,1,0:T(8,128)(2,1)S(1)}, bf16[4,48,3072]{2,1,0:T(8,128)(2,1)S(1)}, u32[]{:S(2)}, u32[]{:S(2)}) collective-permute-start(bf16[4,48,3072]{2,1,0:T(8,128)(2,1)S(1)} %get-tuple-element.100), channel_id=1, source_target_pairs={{0,24},{8,0},{16,8},{24,16},{1,25},{9,1},{17,9},{25,17},{2,26},{10... | collective-permute-start | bytes 3538952 | tf_op jit(solution)/shard_map/ppermute | solution.py:648
  235.4 18.0 %collective-permute-done.25.u0 = bf16[4,48,3072]{2,1,0:T(8,128)(2,1)S(1)} collective-permute-done((bf16[4,48,3072]{2,1,0:T(8,128)(2,1)S(1)}, bf16[4,48,3072]{2,1,0:T(8,128)(2,1)S(1)}, u32[]{:S(2)}, u32[]{:S(2)}) %collective-permute-start.25) | collective-permute-done | bytes 1179680 | tf_op jit(solution)/shard_map/ppermute | solution.py:644
  254.2 5.0 %collective-permute-done.28.d1 = bf16[4,48,3072]{2,1,0:T(8,128)(2,1)S(1)} collective-permute-done((bf16[4,48,3072]{2,1,0:T(8,128)(2,1)S(1)}, bf16[4,48,3072]{2,1,0:T(8,128)(2,1)S(1)}, u32[]{:S(2)}, u32[]{:S(2)}) %collective-permute-start.28) | collective-permute-done | bytes 1179680 | tf_op jit(solution)/shard_map/ppermute | solution.py:648
  266.2 3.2 %collective-permute-start.33 = (bf16[48,3072]{1,0:T(8,128)(2,1)S(1)}, bf16[48,3072]{1,0:T(8,128)(2,1)S(1)}, u32[]{:S(2)}, u32[]{:S(2)}) collective-permute-start(bf16[48,3072]{1,0:T(8,128)(2,1)S(1)} %get-tuple-element.107), channel_id=1, source_target_pairs={{0,24},{8,0},{16,8},{24,16},{1,25},{9,1},{17,9},{25,17},{2,26},{10... | collective-permute-start | bytes 884744 | tf_op jit(solution)/shard_map/ppermute | solution.py:648
  285.4 4.5 %collective-permute-done.36.b2 = bf16[16,6144]{1,0:T(8,128)(2,1)} collective-permute-done((bf16[16,6144]{1,0:T(8,128)(2,1)}, bf16[16,6144]{1,0:T(8,128)(2,1)}, u32[]{:S(2)}, u32[]{:S(2)}) %collective-permute-start.36) | collective-permute-done | bytes 196640 | tf_op jit(solution)/shard_map/ppermute | solution.py:644
  289.9 2.8 combine.1
  (101 shorter events, 57.9 us)
Async XLA Ops:
  6.5 77.4 %all-gather.2.cloned.1.call-start = ((), (), s32[]{:S(2)}) async-start(), calls=%async_computation.3 | async-start | bytes 12976128 | tf_op jit(solution)/shard_map/all_gather | solution.py:678
  16.6 51.3 %collective-permute-start.3 = (bf16[864,6144]{1,0:T(8,128)(2,1)}, bf16[864,6144]{1,0:T(8,128)(2,1)}, u32[]{:S(2)}, u32[]{:S(2)}) collective-permute-start(bf16[864,6144]{1,0:T(8,128)(2,1)} %pad_maximum_fusion.mine), channel_id=1, source_target_pairs={{0,4},{4,0},{1,5},{5,1},{2,6},{6,2},{3,7},{7,3},{8,12},{12,8},{9,1... | collective-permute-start | bytes 31850504 | tf_op jit(solution)/shard_map/ppermute | solution.py:680
  46.4 21.5 %all-to-all-start.1 = ((bf16[32,64,128]{2,1,0:T(8,128)(2,1)}), bf16[32,64,128]{2,1,0:T(8,128)(2,1)S(1)}, u32[]{:S(2)}, u32[]{:S(2)}) async-start(bf16[32,64,128]{2,1,0:T(8,128)(2,1)} %state_prefix.1), calls=%async_computation.1 | async-start | bytes 1048576 | tf_op jit(solution)/shard_map/all_to_all | solution.py:689
  50.3 231.8 %reduce-scatter.2.cloned.1.call-start = ((), (), s32[]{:S(2)}) async-start(), calls=%async_computation.4 | async-start | bytes 7864320 | tf_op jit(solution)/shard_map/reduce_scatter | solution.py:745
  92.0 18.6 %collective-permute-start.4 = (bf16[48,6144]{1,0:T(8,128)(2,1)}, bf16[48,6144]{1,0:T(8,128)(2,1)S(1)}, u32[]{:S(2)}, u32[]{:S(2)}) collective-permute-start(bf16[48,6144]{1,0:T(8,128)(2,1)} %get-tuple-element.66), channel_id=1, source_target_pairs={{0,2},{1,3},{2,0},{3,1},{4,6},{5,7},{6,4},{7,5},{8,10},{9,11},{10,... | collective-permute-start | bytes 1769480 | tf_op jit(solution)/shard_map/ppermute | solution.py:652
  95.0 26.9 %collective-permute-start.5 = (bf16[48,6144]{1,0:T(8,128)(2,1)S(1)}, bf16[48,6144]{1,0:T(8,128)(2,1)S(1)}, u32[]{:S(2)}, u32[]{:S(2)}) collective-permute-start(bf16[48,6144]{1,0:T(8,128)(2,1)S(1)} %get-tuple-element.67), channel_id=1, source_target_pairs={{0,1},{1,2},{2,3},{3,0},{4,5},{5,6},{6,7},{7,4},{8,9},{9,10},{10,1... | collective-permute-start | bytes 1769480 | tf_op jit(solution)/shard_map/ppermute | solution.py:644
  95.6 26.4 %collective-permute-start.6 = (bf16[48,6144]{1,0:T(8,128)(2,1)S(1)}, bf16[48,6144]{1,0:T(8,128)(2,1)S(1)}, u32[]{:S(2)}, u32[]{:S(2)}) collective-permute-start(bf16[48,6144]{1,0:T(8,128)(2,1)S(1)} %get-tuple-element.68), channel_id=1, source_target_pairs={{0,3},{1,0},{2,1},{3,2},{4,7},{5,4},{6,5},{7,6},{8,11},{9,8},{10,9... | collective-permute-start | bytes 1769480 | tf_op jit(solution)/shard_map/ppermute | solution.py:648
  123.2 11.5 %collective-permute-start.7 = (bf16[48,3072]{1,0:T(8,128)(2,1)S(1)}, bf16[48,3072]{1,0:T(8,128)(2,1)S(1)}, u32[]{:S(2)}, u32[]{:S(2)}) collective-permute-start(bf16[48,3072]{1,0:T(8,128)(2,1)S(1)} %get-tuple-element.70.a0), channel_id=1, source_target_pairs={{0,16},{8,24},{16,0},{24,8},{1,17},{9,25},{17,1},{25,9},{2,18},{10... | collective-permute-start | bytes 884744 | tf_op jit(solution)/shard_map/ppermute | solution.py:652
  126.3 13.7 %collective-permute-start.9 = (bf16[48,3072]{1,0:T(8,128)(2,1)S(1)}, bf16[48,3072]{1,0:T(8,128)(2,1)S(1)}, u32[]{:S(2)}, u32[]{:S(2)}) collective-permute-start(bf16[48,3072]{1,0:T(8,128)(2,1)S(1)} %get-tuple-element.70.a0), channel_id=1, source_target_pairs={{0,8},{8,16},{16,24},{24,0},{1,9},{9,17},{17,25},{25,1},{2,10},{10... | collective-permute-start | bytes 884744 | tf_op jit(solution)/shard_map/ppermute | solution.py:644
  126.9 11.5 %collective-permute-start.8 = (bf16[48,3072]{1,0:T(8,128)(2,1)S(1)}, bf16[48,3072]{1,0:T(8,128)(2,1)S(1)}, u32[]{:S(2)}, u32[]{:S(2)}) collective-permute-start(bf16[48,3072]{1,0:T(8,128)(2,1)S(1)} %get-tuple-element.71.b0), channel_id=1, source_target_pairs={{0,64},{32,96},{64,0},{96,32},{1,65},{33,97},{65,1},{97,33},{2,66}... | collective-permute-start | bytes 884744 | tf_op jit(solution)/shard_map/ppermute | solution.py:652
  128.2 14.8 %collective-permute-start.10 = (bf16[48,3072]{1,0:T(8,128)(2,1)S(1)}, bf16[48,3072]{1,0:T(8,128)(2,1)S(1)}, u32[]{:S(2)}, u32[]{:S(2)}) collective-permute-start(bf16[48,3072]{1,0:T(8,128)(2,1)S(1)} %get-tuple-element.71.b0), channel_id=1, source_target_pairs={{0,32},{32,64},{64,96},{96,0},{1,33},{33,65},{65,97},{97,1},{2,34}... | collective-permute-start | bytes 884744 | tf_op jit(solution)/shard_map/ppermute | solution.py:644
  128.5 14.5 %collective-permute-start.11 = (bf16[48,3072]{1,0:T(8,128)(2,1)S(1)}, bf16[48,3072]{1,0:T(8,128)(2,1)S(1)}, u32[]{:S(2)}, u32[]{:S(2)}) collective-permute-start(bf16[48,3072]{1,0:T(8,128)(2,1)S(1)} %get-tuple-element.70.a0), channel_id=1, source_target_pairs={{0,24},{8,0},{16,8},{24,16},{1,25},{9,1},{17,9},{25,17},{2,26},{10... | collective-permute-start | bytes 884744 | tf_op jit(solution)/shard_map/ppermute | solution.py:648
  144.2 29.4 %collective-permute-start.13 = (bf16[4,48,3072]{2,1,0:T(8,128)(2,1)S(1)}, bf16[4,48,3072]{2,1,0:T(8,128)(2,1)S(1)}, u32[]{:S(2)}, u32[]{:S(2)}) collective-permute-start(bf16[4,48,3072]{2,1,0:T(8,128)(2,1)S(1)} %get-tuple-element.74.a0), channel_id=1, source_target_pairs={{0,32},{32,64},{64,96},{96,0},{1,33},{33,65},{65,97},{97,1},{2,34}... | collective-permute-start | bytes 3538952 | tf_op jit(solution)/shard_map/ppermute | solution.py:644
  144.5 29.3 %collective-permute-start.14 = (bf16[4,48,3072]{2,1,0:T(8,128)(2,1)}, bf16[4,48,3072]{2,1,0:T(8,128)(2,1)S(1)}, u32[]{:S(2)}, u32[]{:S(2)}) collective-permute-start(bf16[4,48,3072]{2,1,0:T(8,128)(2,1)} %get-tuple-element.75.b0), channel_id=1, source_target_pairs={{0,8},{8,16},{16,24},{24,0},{1,9},{9,17},{17,25},{25,1},{2,10},{10... | collective-permute-start | bytes 3538952 | tf_op jit(solution)/shard_map/ppermute | solution.py:644
  145.6 28.3 %collective-permute-start.15 = (bf16[4,48,3072]{2,1,0:T(8,128)(2,1)S(1)}, bf16[4,48,3072]{2,1,0:T(8,128)(2,1)S(1)}, u32[]{:S(2)}, u32[]{:S(2)}) collective-permute-start(bf16[4,48,3072]{2,1,0:T(8,128)(2,1)S(1)} %get-tuple-element.74.a0), channel_id=1, source_target_pairs={{0,96},{32,0},{64,32},{96,64},{1,97},{33,1},{65,33},{97,65},{2,98}... | collective-permute-start | bytes 3538952 | tf_op jit(solution)/shard_map/ppermute | solution.py:648
  148.0 27.8 %collective-permute-start.16 = (bf16[4,48,3072]{2,1,0:T(8,128)(2,1)}, bf16[4,48,3072]{2,1,0:T(8,128)(2,1)S(1)}, u32[]{:S(2)}, u32[]{:S(2)}) collective-permute-start(bf16[4,48,3072]{2,1,0:T(8,128)(2,1)} %get-tuple-element.75.b0), channel_id=1, source_target_pairs={{0,24},{8,0},{16,8},{24,16},{1,25},{9,1},{17,9},{25,17},{2,26},{10... | collective-permute-start | bytes 3538952 | tf_op jit(solution)/shard_map/ppermute | solution.py:648
  176.0 23.2 %collective-permute-start.17 = (bf16[2,48,3072]{2,1,0:T(8,128)(2,1)S(1)}, bf16[2,48,3072]{2,1,0:T(8,128)(2,1)S(1)}, u32[]{:S(2)}, u32[]{:S(2)}) collective-permute-start(bf16[2,48,3072]{2,1,0:T(8,128)(2,1)S(1)} %get-tuple-element.78), channel_id=1, source_target_pairs={{0,32},{32,64},{64,96},{96,0},{1,33},{33,65},{65,97},{97,1},{2,34}... | collective-permute-start | bytes 1769480 | tf_op jit(solution)/shard_map/ppermute | solution.py:644
  176.1 23.1 %collective-permute-start.18 = (bf16[2,48,3072]{2,1,0:T(8,128)(2,1)S(1)}, bf16[2,48,3072]{2,1,0:T(8,128)(2,1)S(1)}, u32[]{:S(2)}, u32[]{:S(2)}) collective-permute-start(bf16[2,48,3072]{2,1,0:T(8,128)(2,1)S(1)} %get-tuple-element.79), channel_id=1, source_target_pairs={{0,8},{8,16},{16,24},{24,0},{1,9},{9,17},{17,25},{25,1},{2,10},{10... | collective-permute-start | bytes 1769480 | tf_op jit(solution)/shard_map/ppermute | solution.py:644
  177.6 21.6 %collective-permute-start.19 = (bf16[2,48,3072]{2,1,0:T(8,128)(2,1)S(1)}, bf16[2,48,3072]{2,1,0:T(8,128)(2,1)S(1)}, u32[]{:S(2)}, u32[]{:S(2)}) collective-permute-start(bf16[2,48,3072]{2,1,0:T(8,128)(2,1)S(1)} %get-tuple-element.80), channel_id=1, source_target_pairs={{0,96},{32,0},{64,32},{96,64},{1,97},{33,1},{65,33},{97,65},{2,98}... | collective-permute-start | bytes 1769480 | tf_op jit(solution)/shard_map/ppermute | solution.py:648
  180.8 18.4 %collective-permute-start.20 = (bf16[2,48,3072]{2,1,0:T(8,128)(2,1)S(1)}, bf16[2,48,3072]{2,1,0:T(8,128)(2,1)S(1)}, u32[]{:S(2)}, u32[]{:S(2)}) collective-permute-start(bf16[2,48,3072]{2,1,0:T(8,128)(2,1)S(1)} %get-tuple-element.81), channel_id=1, source_target_pairs={{0,24},{8,0},{16,8},{24,16},{1,25},{9,1},{17,9},{25,17},{2,26},{10... | collective-permute-start | bytes 1769480 | tf_op jit(solution)/shard_map/ppermute | solution.py:648
  211.7 15.1 %collective-permute-start.21 = (bf16[2,48,3072]{2,1,0:T(8,128)(2,1)S(1)}, bf16[2,48,3072]{2,1,0:T(8,128)(2,1)S(1)}, u32[]{:S(2)}, u32[]{:S(2)}) collective-permute-start(bf16[2,48,3072]{2,1,0:T(8,128)(2,1)S(1)} %get-tuple-element.89), channel_id=1, source_target_pairs={{0,32},{32,64},{64,96},{96,0},{1,33},{33,65},{65,97},{97,1},{2,34}... | collective-permute-start | bytes 1769480 | tf_op jit(solution)/shard_map/ppermute | solution.py:644
  211.8 15.0 %collective-permute-start.22 = (bf16[2,48,3072]{2,1,0:T(8,128)(2,1)S(1)}, bf16[2,48,3072]{2,1,0:T(8,128)(2,1)S(1)}, u32[]{:S(2)}, u32[]{:S(2)}) collective-permute-start(bf16[2,48,3072]{2,1,0:T(8,128)(2,1)S(1)} %get-tuple-element.90), channel_id=1, source_target_pairs={{0,8},{8,16},{16,24},{24,0},{1,9},{9,17},{17,25},{25,1},{2,10},{10... | collective-permute-start | bytes 1769480 | tf_op jit(solution)/shard_map/ppermute | solution.py:644
  211.9 14.9 %collective-permute-start.23 = (bf16[2,48,3072]{2,1,0:T(8,128)(2,1)S(1)}, bf16[2,48,3072]{2,1,0:T(8,128)(2,1)S(1)}, u32[]{:S(2)}, u32[]{:S(2)}) collective-permute-start(bf16[2,48,3072]{2,1,0:T(8,128)(2,1)S(1)} %get-tuple-element.91), channel_id=1, source_target_pairs={{0,96},{32,0},{64,32},{96,64},{1,97},{33,1},{65,33},{97,65},{2,98}... | collective-permute-start | bytes 1769480 | tf_op jit(solution)/shard_map/ppermute | solution.py:648
  215.0 12.7 %collective-permute-start.24 = (bf16[2,48,3072]{2,1,0:T(8,128)(2,1)S(1)}, bf16[2,48,3072]{2,1,0:T(8,128)(2,1)S(1)}, u32[]{:S(2)}, u32[]{:S(2)}) collective-permute-start(bf16[2,48,3072]{2,1,0:T(8,128)(2,1)S(1)} %get-tuple-element.92), channel_id=1, source_target_pairs={{0,24},{8,0},{16,8},{24,16},{1,25},{9,1},{17,9},{25,17},{2,26},{10... | collective-permute-start | bytes 1769480 | tf_op jit(solution)/shard_map/ppermute | solution.py:648
  228.4 25.0 %collective-permute-start.25 = (bf16[4,48,3072]{2,1,0:T(8,128)(2,1)S(1)}, bf16[4,48,3072]{2,1,0:T(8,128)(2,1)S(1)}, u32[]{:S(2)}, u32[]{:S(2)}) collective-permute-start(bf16[4,48,3072]{2,1,0:T(8,128)(2,1)S(1)} %get-tuple-element.98), channel_id=1, source_target_pairs={{0,32},{32,64},{64,96},{96,0},{1,33},{33,65},{65,97},{97,1},{2,34}... | collective-permute-start | bytes 3538952 | tf_op jit(solution)/shard_map/ppermute | solution.py:644
  228.5 25.8 %collective-permute-start.26 = (bf16[4,48,3072]{2,1,0:T(8,128)(2,1)S(1)}, bf16[4,48,3072]{2,1,0:T(8,128)(2,1)S(1)}, u32[]{:S(2)}, u32[]{:S(2)}) collective-permute-start(bf16[4,48,3072]{2,1,0:T(8,128)(2,1)S(1)} %get-tuple-element.99), channel_id=1, source_target_pairs={{0,8},{8,16},{16,24},{24,0},{1,9},{9,17},{17,25},{25,1},{2,10},{10... | collective-permute-start | bytes 3538952 | tf_op jit(solution)/shard_map/ppermute | solution.py:644
  229.2 25.1 %collective-permute-start.27 = (bf16[4,48,3072]{2,1,0:T(8,128)(2,1)S(1)}, bf16[4,48,3072]{2,1,0:T(8,128)(2,1)S(1)}, u32[]{:S(2)}, u32[]{:S(2)}) collective-permute-start(bf16[4,48,3072]{2,1,0:T(8,128)(2,1)S(1)} %get-tuple-element.93.late), channel_id=1, source_target_pairs={{0,96},{32,0},{64,32},{96,64},{1,97},{33,1},{65,33},{97,65},{2,98}... | collective-permute-start | bytes 3538952 | tf_op jit(solution)/shard_map/ppermute | solution.py:648
  232.3 27.0 %collective-permute-start.28 = (bf16[4,48,3072]{2,1,0:T(8,128)(2,1)S(1)}, bf16[4,48,3072]{2,1,0:T(8,128)(2,1)S(1)}, u32[]{:S(2)}, u32[]{:S(2)}) collective-permute-start(bf16[4,48,3072]{2,1,0:T(8,128)(2,1)S(1)} %get-tuple-element.100), channel_id=1, source_target_pairs={{0,24},{8,0},{16,8},{24,16},{1,25},{9,1},{17,9},{25,17},{2,26},{10... | collective-permute-start | bytes 3538952 | tf_op jit(solution)/shard_map/ppermute | solution.py:648
  260.1 9.3 %collective-permute-start.29 = (bf16[48,3072]{1,0:T(8,128)(2,1)S(1)}, bf16[48,3072]{1,0:T(8,128)(2,1)S(1)}, u32[]{:S(2)}, u32[]{:S(2)}) collective-permute-start(bf16[48,3072]{1,0:T(8,128)(2,1)S(1)} %get-tuple-element.103), channel_id=1, source_target_pairs={{0,16},{8,24},{16,0},{24,8},{1,17},{9,25},{17,1},{25,9},{2,18},{10... | collective-permute-start | bytes 884744 | tf_op jit(solution)/shard_map/ppermute | solution.py:652
  262.4 9.2 %collective-permute-start.31 = (bf16[48,3072]{1,0:T(8,128)(2,1)S(1)}, bf16[48,3072]{1,0:T(8,128)(2,1)S(1)}, u32[]{:S(2)}, u32[]{:S(2)}) collective-permute-start(bf16[48,3072]{1,0:T(8,128)(2,1)S(1)} %get-tuple-element.105), channel_id=1, source_target_pairs={{0,8},{8,16},{16,24},{24,0},{1,9},{9,17},{17,25},{25,1},{2,10},{10... | collective-permute-start | bytes 884744 | tf_op jit(solution)/shard_map/ppermute | solution.py:644
  280.6 9.3 %collective-permute-start.36 = (bf16[16,6144]{1,0:T(8,128)(2,1)}, bf16[16,6144]{1,0:T(8,128)(2,1)}, u32[]{:S(2)}, u32[]{:S(2)}) collective-permute-start(bf16[16,6144]{1,0:T(8,128)(2,1)} %get-tuple-element.111), channel_id=1, source_target_pairs={{0,1},{1,2},{2,3},{3,0},{4,5},{5,6},{6,7},{7,4},{8,9},{9,10},{10,1... | collective-permute-start | bytes 589832 | tf_op jit(solution)/shard_map/ppermute | solution.py:644
  280.6 9.3 %collective-permute-start.37 = (bf16[16,6144]{1,0:T(8,128)(2,1)S(1)}, bf16[16,6144]{1,0:T(8,128)(2,1)}, u32[]{:S(2)}, u32[]{:S(2)}) collective-permute-start(bf16[16,6144]{1,0:T(8,128)(2,1)S(1)} %get-tuple-element.112), channel_id=1, source_target_pairs={{0,2},{1,3},{2,0},{3,1},{4,6},{5,7},{6,4},{7,5},{8,10},{9,11},{10,... | collective-permute-start | bytes 589832 | tf_op jit(solution)/shard_map/ppermute | solution.py:652
  (21 other events, 236.3 us)
Sparse Core Ops, SparseCore 0:
  9.6 74.3 all-gather.1
  144.3 62.7 reduce-scatter.1

commit v10 on v9

--- a/solution.py
+++ b/solution.py
@@ -216,16 +216,16 @@
     out[...] = mm(place[...], normed[...]).astype(BF)
 
 
-def selected_kernel(picked, own, weight, res, o0, o1, o2, o3, w_here, r_here, sems, last):
-    size = o0.shape[0]
-    chunks = weight.shape[0] // TILE
+def selected_kernel(first, picked, own, weight, res, o0, o1, o2, o3, w_here, r_here, sems, last):
+    size, half = o0.shape
+    chunks = half // TILE
 
     def copy(c):
         slot = lax.rem(c, AHEAD + 1)
-        span = pl.ds(pl.multiple_of(c * TILE, TILE), TILE)
+        span = pl.ds(pl.multiple_of(first + c * TILE, TILE), TILE)
         return pltpu.make_async_copy(weight.at[span], w_here.at[slot], sems.at[slot])
 
-    rest = pltpu.make_async_copy(res, r_here, last)
+    rest = pltpu.make_async_copy(res.at[:, pl.ds(first, half)], r_here, last)
     copy(0).start()
     rest.start()
     for c in range(1, AHEAD):
@@ -246,12 +246,13 @@
             o[:, span] = full[i * size : (i + 1) * size]
 
 
-def selected(picked, own, weight, res):
+def selected(first, picked, own, weight, res):
     picks, (model, width) = picked.shape[0], weight.shape
+    half = model // 2
     return call(
-        selected_kernel,
+        functools.partial(selected_kernel, first),
         "selected_projection",
-        [((picks // 4, model), BF)] * 4,
+        [((picks // 4, half), BF)] * 4,
         picked,
         own,
         weight,
@@ -260,7 +261,7 @@
         out_specs=[VM] * 4,
         scratch_shapes=[
             pltpu.VMEM((AHEAD + 1, TILE, width), BF),
-            pltpu.VMEM(res.shape, BF),
+            pltpu.VMEM((res.shape[0], half), BF),
             pltpu.SemaphoreType.DMA((AHEAD + 1,)),
             pltpu.SemaphoreType.DMA,
         ],
@@ -297,12 +298,14 @@
     )
 
 
-def norm_kernel(a, b, c, d, gain, done, o0, o1):
-    x = a[...].astype(F32) + b[...].astype(F32) + c[...].astype(F32) + d[...].astype(F32)
-    x = x * lax.rsqrt(jnp.mean(x * x, -1, keepdims=True) + 1e-06) * gain[...]
+def norm_kernel(*refs):
+    gain, _, o0, o1 = refs[8:]
     half = o0.shape[1]
-    o0[...] = x[:, :half].astype(BF)
-    o1[...] = x[:, half:].astype(BF)
+    x = [sum(r[...].astype(F32) for r in refs[4 * k : 4 * k + 4]) for k in range(2)]
+    squares = sum(jnp.sum(v * v, -1, keepdims=True) for v in x)
+    scale = lax.rsqrt(squares / (2 * half) + 1e-06)
+    o0[...] = (x[0] * scale * gain[:, :half]).astype(BF)
+    o1[...] = (x[1] * scale * gain[:, half:]).astype(BF)
 
 
 def forward_kernel(a_below, b_below, a_above, b_above, a_up, b_up, a_down, b_down):
@@ -369,7 +372,7 @@
     return ((2 * units, units), (2 * units, units))
 
 
-def gate_up(refs_a, refs_b, x, part_a, part_b, stream):
+def gate_up(refs_a, refs_b, x, part_a, part_b, stream, turned=False):
     rows, half = refs_a[0].shape[1:]
     each = half // TILE
     part_a[...] = jnp.zeros_like(part_a)
@@ -388,7 +391,11 @@
                         row += rows
                 at = 0
                 for w in weights:
-                    part[:, at : at + w.shape[0]] += nt(x[...], w)
+                    span = slice(at, at + w.shape[0])
+                    if turned:
+                        part[span, :] += nt(w, x[...])
+                    else:
+                        part[:, span] += nt(x[...], w)
                     at += w.shape[0]
 
     stream.run(body)
@@ -468,11 +475,12 @@
     units = mine.shape[0] // 3
     downs = Stream((mine, other), down_spans(units), dbuf, dsems)
     downs.begin()
-    gate_up((a3, a4), (b3, b4), x, part.at[0], part.at[1], Resident((w0, w1)))
+    gate_up((a3, a4), (b3, b4), x, part.at[0], part.at[1], Resident((w0, w1)), turned=True)
     own[...] = acc[...]
-    own[3 * block :, :] += part[0]
+    own[3 * block :, :] += part[0].T
+    across_y = part[1].T
     for row, z in by_y(rows, 3):
-        own[row : row + rows, :] += part[1, z * rows : (z + 1) * rows, :]
+        own[row : row + rows, :] += across_y[z * rows : (z + 1) * rows, :]
     for core in range(2):
         g = own[:, 2 * core * units : (2 * core + 1) * units]
         u = own[:, (2 * core + 1) * units : (2 * core + 2) * units]
@@ -547,12 +555,12 @@
         out_specs=[VM] * 5,
         scratch_shapes=[
             pltpu.VMEM((4 * rows, TILE), BF),
-            pltpu.VMEM((2, 4 * rows, wide), F32),
+            pltpu.VMEM((2, wide, 4 * rows), F32),
             pltpu.VMEM(acc.shape, F32),
             pltpu.VMEM((2, 4 * rows, wide // 2), BF),
             *slots(wide // 2, 2),
         ],
-        vmem=24,
+        vmem=20,
     )
 
 
@@ -706,21 +714,21 @@
         out_specs=[VM],
         vmem=8,
     )[0]
-    to_up, to_down, to_far, here = selected(picked, own_place, weight_out, flat)
+    terms = []
+    for first in (0, half):
+        to_up, to_down, to_far, here = selected(first, picked, own_place, weight_out, flat)
+        terms += [here, across(to_far, "x"), up_one(to_up, "x"), down_one(to_down, "x")]
     whole, done = whole_projection(normed, weight_out)
 
-    size = here.shape[0]
+    size = terms[0].shape[0]
     a0, b0 = call(
         norm_kernel,
         "selected_norm",
         [((size, half), BF)] * 2,
-        here,
-        across(to_far, "x"),
-        up_one(to_up, "x"),
-        down_one(to_down, "x"),
+        *terms,
         gain,
         done,
-        in_specs=[VM] * 6,
+        in_specs=[VM] * 10,
         out_specs=[VM] * 2,
     )
 

time: 300 us -> 298 us (level)
  waiting for transfers between devices: 103 us -> 95 us
  starting transfers between devices: 66.2 us -> 69.9 us
    ppermute x14 -> x15, waiting for transfers between devices: 65.3 us -> 57.1 us  [up_one(): return lax.ppermute(x, axis, ring(4, 1))]
    ppermute x14 -> x15, starting transfers between devices: 37.4 us -> 40.1 us  [down_one(): return lax.ppermute(x, axis, ring(4, -1))]
    ppermute x14 -> x15, starting transfers between devices: 9.21 us -> 9.98 us  [up_one(): return lax.ppermute(x, axis, ring(4, 1))]
    pallas_call x15 -> x16, Pallas kernels: 67.6 us -> 67.8 us  [call(): pl.pallas_call(kernel, out_shape=[jax.ShapeDtypeStruct(s, d) for s, d in...]
    ppermute x6 -> x7, starting transfers between devices: 11.2 us -> 11.4 us  [across(): return lax.ppermute(x, axis, ring(4, 2))]
    ppermute x14 -> x15, waiting for transfers between devices: 10.4 us -> 10.4 us  [down_one(): return lax.ppermute(x, axis, ring(4, -1))]
  transfers between devices with their start and end apart: 41 -> 44, of which waited for: 23 -> 23; matrix products, arithmetic and copies ran while one was open for 3% -> 3% of each run, Pallas kernels for 23% -> 24%
where the time goes in v10:
time: 298 us; the launch traced here: 297 us
  waiting for transfers between devices  95 us (32%)
  Pallas kernels  80.5 us (27%)
  starting transfers between devices  69.9 us (23%)
  blocking collectives  21.7 us (7%)
  between operations  13.7 us (5%)
  other arithmetic  9.33 us (3%)
  local copies, waits for them, and re-layouts  6.74 us (2%)
    pallas_call x16, Pallas kernels, call(): pl.pallas_call(kernel, out_shape=[jax.ShapeDtypeStruct(s, d) for s, d in...  67.8 us
    ppermute x15, waiting for transfers between devices, up_one(): return lax.ppermute(x, axis, ring(4, 1))  57.1 us
    ppermute x15, starting transfers between devices, down_one(): return lax.ppermute(x, axis, ring(4, -1))  40.1 us
    all_to_all x1, blocking collectives, shards(): arrived = lax.all_to_all(states, SEQ, 0, 0, tiled=True)  21.7 us
    ppermute x7, starting transfers between devices, across(): return lax.ppermute(x, axis, ring(4, 2))  11.4 us
    ppermute x15, waiting for transfers between devices, down_one(): return lax.ppermute(x, axis, ring(4, -1))  10.4 us
    ppermute x15, starting transfers between devices, up_one(): return lax.ppermute(x, axis, ring(4, 1))  9.98 us
    concatenate x1, other arithmetic, shards(): weights = jnp.concatenate([gate_weight[0], up_weight[0], down_weight[0]])  9.33 us
  transfers between devices with their start and end apart: 44, of which 23 were waited for; matrix products, arithmetic and copies ran while one was open for 3% of the time, Pallas kernels for 24%

profile of v10, /device:TPU:0, one launch (start us, length us, event | category | flops | bytes accessed | tf_op | source)
XLA Modules:
  0.0 296.9 jit_solution(2138493312721942423)
XLA Ops:
  7.3 9.3 %pad_maximum_fusion.mine = bf16[864,6144]{1,0:T(8,128)(2,1)} fusion(bf16[288,6144]{1,0:T(8,128)(2,1)} %bitcast.29, bf16[288,6144]{1,0:T(8,128)(2,1)} %bitcast.30, bf16[288,6144]{1,0:T(8,128)(2,1)} %bitcast.31), kind=kLoop, calls=%fused_computation | loop fusion | flops 31850496 | bytes 21233664 | tf_op jit(solution)/shard_map/concatenate | solution.py:687
  16.6 7.1 %local_attention.1 = (f32[2,256,1024]{2,1,0:T(8,128)}, bf16[32,80,128]{2,1,0:T(8,128)(2,1)}, f32[2,256,8]{2,1,0:T(8,128)}) custom-call(bf16[2,256,1024]{2,1,0:T(8,128)(2,1)} %q_ref.3, bf16[2,256,1024]{2,1,0:T(8,128)(2,1)} %k_ref.1, bf16[2,256,1024]{2,1,0:T(8,128)(2,1)} %v_ref.1, f32[2,8,256]{2,1,0:T(8,128)} %bitcast.34), custom_call_target="tpu_custom_call" | custom-call | tf_op jit(solution)/shard_map/local_attention/pallas_call | solution.py:84
  23.7 21.7 %all_to_all.10.in_ref = bf16[32,80,128]{2,1,0:T(8,128)(2,1)S(1)} all-to-all(bf16[32,80,128]{2,1,0:T(8,128)(2,1)} %get-tuple-element.66), channel_id=1, replica_groups=mesh['z'=4,'y'=4,'core'=2,'x'=4] {'z','y','core'}, dimensions={0} | all-to-all | bytes 1310720 | tf_op jit(solution)/shard_map/all_to_all | solution.py:696
  46.4 3.9 %all-to-all-start.1 = ((bf16[32,64,128]{2,1,0:T(8,128)(2,1)}), bf16[32,64,128]{2,1,0:T(8,128)(2,1)S(1)}, u32[]{:S(2)}, u32[]{:S(2)}) async-start(bf16[32,64,128]{2,1,0:T(8,128)(2,1)} %state_prefix.1), calls=%async_computation.1 | async-start | bytes 1048576 | tf_op jit(solution)/shard_map/all_to_all | solution.py:697
  50.5 2.8 collective-permute-start
  56.6 2.8 collective-permute-done.1
  60.4 7.5 %all-to-all-done.1 = bf16[32,64,128]{2,1,0:T(8,128)(2,1)S(1)} async-done(((bf16[32,64,128]{2,1,0:T(8,128)(2,1)}), bf16[32,64,128]{2,1,0:T(8,128)(2,1)S(1)}, u32[]{:S(2)}, u32[]{:S(2)}) %all-to-all-start.1) | async-done | bytes 524320 | tf_op jit(solution)/shard_map/all_to_all | solution.py:697
  68.7 4.6 %carried_norm.1 = (bf16[4,2,64,1024]{3,2,1,0:T(8,128)(2,1)}, bf16[864,6144]{1,0:T(8,128)(2,1)}) custom-call(bf16[2,256,1024]{2,1,0:T(8,128)(2,1)} %q_ref.3, f32[2,256,1024]{2,1,0:T(8,128)} %get-tuple-element.64.inner_ref, f32[2,256,8]{2,1,0:T(8,128)} %get-tuple-element.65.cum_ref, bf16[16,128,128]{2,1,0:T(8,128)(2,1)} %bitcast.32, ...), custom_call_target="tpu_custom_call", output_to_operand_aliasing={{1}: (5, {})} | custom-call | tf_op jit(solution)/shard_map/carried_norm/pallas_call | solution.py:138
  75.0 9.0 %all-gather.2.cloned.1.call-done.weight.weight_ref = bf16[6144,1024]{1,0:T(8,128)(2,1)} async-done(((bf16[192,1024]{1,0:T(8,128)(2,1)}), bf16[6144,1024]{1,0:T(8,128)(2,1)}) %all-gather.2.cloned.1.call-update) | async-done | bytes 12582928 | tf_op jit(solution)/shard_map/all_gather | solution.py:686
  83.9 4.4 %selected_projection.2 = (bf16[48,3072]{1,0:T(8,128)(2,1)S(1)}, bf16[48,3072]{1,0:T(8,128)(2,1)S(1)}, bf16[48,3072]{1,0:T(8,128)(2,1)S(1)}, bf16[48,3072]{1,0:T(8,128)(2,1)S(1)}) custom-call(bf16[192,1024]{1,0:T(8,128)(2,1)S(1)} %pick.1.picked, bf16[192,128]{1,0:T(8,128)(2,1)S(1)} %get-tuple-element.68.own, ...), custom_call_target="tpu_custom_call" | custom-call | tf_op jit(solution)/shard_map/selected_projection/pallas_call | solution.py:165
  88.3 3.1 %collective-permute-start.4 = (bf16[48,3072]{1,0:T(8,128)(2,1)S(1)}, bf16[48,3072]{1,0:T(8,128)(2,1)S(1)}, u32[]{:S(2)}, u32[]{:S(2)}) collective-permute-start(bf16[48,3072]{1,0:T(8,128)(2,1)S(1)} %get-tuple-element.70), channel_id=1, source_target_pairs={{0,2},{1,3},{2,0},{3,1},{4,6},{5,7},{6,4},{7,5},{8,10},{9,11},{10,... | collective-permute-start | bytes 884744 | tf_op jit(solution)/shard_map/ppermute | solution.py:660
  94.6 4.4 %selected_projection.3 = (bf16[48,3072]{1,0:T(8,128)(2,1)S(1)}, bf16[48,3072]{1,0:T(8,128)(2,1)S(1)}, bf16[48,3072]{1,0:T(8,128)(2,1)S(1)}, bf16[48,3072]{1,0:T(8,128)(2,1)S(1)}) custom-call(bf16[192,1024]{1,0:T(8,128)(2,1)S(1)} %pick.1.picked, bf16[192,128]{1,0:T(8,128)(2,1)S(1)} %get-tuple-element.68.own, ...), custom_call_target="tpu_custom_call" | custom-call | tf_op jit(solution)/shard_map/selected_projection/pallas_call | solution.py:165
  102.5 12.3 %whole_projection.1 = (bf16[512,6144]{1,0:T(8,128)(2,1)}, f32[8,128]{1,0:T(8,128)}) custom-call(bf16[512,1024]{1,0:T(8,128)(2,1)} %bitcast.19, bf16[6144,1024]{1,0:T(8,128)(2,1)} %all-gather.2.cloned.1.call-done.weight.weight_ref), custom_call_target="tpu_custom_call" | custom-call | flops 6442450944 | bytes 25165824 | tf_op jit(solution)/shard_map/whole_projection/pallas_call | solution.py:165
  114.8 3.3 %collective-permute-done.8.refs_6_ = bf16[48,3072]{1,0:T(8,128)(2,1)S(1)} collective-permute-done((bf16[48,3072]{1,0:T(8,128)(2,1)S(1)}, bf16[48,3072]{1,0:T(8,128)(2,1)S(1)}, u32[]{:S(2)}, u32[]{:S(2)}) %collective-permute-start.8) | collective-permute-done | bytes 294944 | tf_op jit(solution)/shard_map/ppermute | solution.py:652
  119.4 3.1 %collective-permute-start.10 = (bf16[48,3072]{1,0:T(8,128)(2,1)S(1)}, bf16[48,3072]{1,0:T(8,128)(2,1)S(1)}, u32[]{:S(2)}, u32[]{:S(2)}) collective-permute-start(bf16[48,3072]{1,0:T(8,128)(2,1)S(1)} %get-tuple-element.78.a0), channel_id=1, source_target_pairs={{0,16},{8,24},{16,0},{24,8},{1,17},{9,25},{17,1},{25,9},{2,18},{10... | collective-permute-start | bytes 884744 | tf_op jit(solution)/shard_map/ppermute | solution.py:660
  127.4 3.5 %collective-permute-done.10.a3 = bf16[48,3072]{1,0:T(8,128)(2,1)S(1)} collective-permute-done((bf16[48,3072]{1,0:T(8,128)(2,1)S(1)}, bf16[48,3072]{1,0:T(8,128)(2,1)S(1)}, u32[]{:S(2)}, u32[]{:S(2)}) %collective-permute-start.10) | collective-permute-done | bytes 294944 | tf_op jit(solution)/shard_map/ppermute | solution.py:660
  136.1 3.1 %collective-permute-done.13.b1 = bf16[48,3072]{1,0:T(8,128)(2,1)S(1)} collective-permute-done((bf16[48,3072]{1,0:T(8,128)(2,1)S(1)}, bf16[48,3072]{1,0:T(8,128)(2,1)S(1)}, u32[]{:S(2)}, u32[]{:S(2)}) %collective-permute-start.13) | collective-permute-done | bytes 294944 | tf_op jit(solution)/shard_map/ppermute | solution.py:652
  146.1 3.0 collective-permute-start.19
  149.1 22.6 %collective-permute-done.16.a1.a_below = bf16[4,48,3072]{2,1,0:T(8,128)(2,1)S(1)} collective-permute-done((bf16[4,48,3072]{2,1,0:T(8,128)(2,1)S(1)}, bf16[4,48,3072]{2,1,0:T(8,128)(2,1)S(1)}, u32[]{:S(2)}, u32[]{:S(2)}) %collective-permute-start.16) | collective-permute-done | bytes 1179680 | tf_op jit(solution)/shard_map/ppermute | solution.py:652
  175.7 3.2 %collective-permute-start.22 = (bf16[2,48,3072]{2,1,0:T(8,128)(2,1)S(1)}, bf16[2,48,3072]{2,1,0:T(8,128)(2,1)S(1)}, u32[]{:S(2)}, u32[]{:S(2)}) collective-permute-start(bf16[2,48,3072]{2,1,0:T(8,128)(2,1)S(1)} %get-tuple-element.88), channel_id=1, source_target_pairs={{0,96},{32,0},{64,32},{96,64},{1,97},{33,1},{65,33},{97,65},{2,98}... | collective-permute-start | bytes 1769480 | tf_op jit(solution)/shard_map/ppermute | solution.py:656
  181.0 16.3 %near_rows.1 = (f32[768,1152]{1,0:T(8,128)S(1)}, bf16[576,6144]{1,0:T(8,128)(2,1)S(1)}, bf16[576,6144]{1,0:T(8,128)(2,1)S(1)}) custom-call(bf16[4,48,3072]{2,1,0:T(8,128)(2,1)S(1)} %copy-done.8, bf16[4,48,3072]{2,1,0:T(8,128)(2,1)S(1)} %copy-done.9, bf16[4,48,3072]{2,1,0:T(8,128)(2,1)S(1)} %collective-permute-done.16.a1.a_below, ...), custom_call_target="tpu_custom_call" | custom-call | flops 8153726976 | bytes 1048576 | tf_op jit(solution)/shard_map/near_rows/pallas_call | solution.py:165
  197.4 11.9 %far_rows.1 = (bf16[768,576]{1,0:T(8,128)(2,1)S(1)}, bf16[2,48,3072]{2,1,0:T(8,128)(2,1)}, bf16[2,48,3072]{2,1,0:T(8,128)(2,1)S(1)}, bf16[2,48,3072]{2,1,0:T(8,128)(2,1)S(1)}, bf16[2,48,3072]{2,1,0:T(8,128)(2,1)S(1)}) custom-call(f32[768,1152]{1,0:T(8,128)S(1)} %get-tuple-element.85.acc, bf16[2,48,3072]{2,1,0:T(8,128)(2,1)S(1)} %collective-permute-done.20.a3, ...), custom_call_target="tpu_custom_call" | custom-call | tf_op jit(solution)/shard_map/far_rows/pallas_call | solution.py:165
  209.7 3.1 %collective-permute-start.26 = (bf16[2,48,3072]{2,1,0:T(8,128)(2,1)S(1)}, bf16[2,48,3072]{2,1,0:T(8,128)(2,1)S(1)}, u32[]{:S(2)}, u32[]{:S(2)}) collective-permute-start(bf16[2,48,3072]{2,1,0:T(8,128)(2,1)S(1)} %get-tuple-element.99), channel_id=1, source_target_pairs={{0,96},{32,0},{64,32},{96,64},{1,97},{33,1},{65,33},{97,65},{2,98}... | collective-permute-start | bytes 1769480 | tf_op jit(solution)/shard_map/ppermute | solution.py:656
  212.8 3.2 %collective-permute-start.27 = (bf16[2,48,3072]{2,1,0:T(8,128)(2,1)S(1)}, bf16[2,48,3072]{2,1,0:T(8,128)(2,1)S(1)}, u32[]{:S(2)}, u32[]{:S(2)}) collective-permute-start(bf16[2,48,3072]{2,1,0:T(8,128)(2,1)S(1)} %get-tuple-element.100), channel_id=1, source_target_pairs={{0,24},{8,0},{16,8},{24,16},{1,25},{9,1},{17,9},{25,17},{2,26},{10... | collective-permute-start | bytes 1769480 | tf_op jit(solution)/shard_map/ppermute | solution.py:656
  216.1 8.6 %rest_rows.1 = (bf16[4,48,3072]{2,1,0:T(8,128)(2,1)S(1)}, bf16[4,48,3072]{2,1,0:T(8,128)(2,1)S(1)}, bf16[4,48,3072]{2,1,0:T(8,128)(2,1)S(1)}, bf16[4,48,3072]{2,...) custom-call(bf16[768,576]{1,0:T(8,128)(2,1)S(1)} %get-tuple-element.92.hidden, ...), custom_call_target="tpu_custom_call" | custom-call | flops 4076863488 | bytes 1048576 | tf_op jit(solution)/shard_map/rest_rows/pallas_call | solution.py:165
  227.0 3.2 %collective-permute-start.30 = (bf16[4,48,3072]{2,1,0:T(8,128)(2,1)S(1)}, bf16[4,48,3072]{2,1,0:T(8,128)(2,1)S(1)}, u32[]{:S(2)}, u32[]{:S(2)}) collective-permute-start(bf16[4,48,3072]{2,1,0:T(8,128)(2,1)S(1)} %get-tuple-element.101.late), channel_id=1, source_target_pairs={{0,96},{32,0},{64,32},{96,64},{1,97},{33,1},{65,33},{97,65},{2,98}... | collective-permute-start | bytes 3538952 | tf_op jit(solution)/shard_map/ppermute | solution.py:656
  230.2 3.0 collective-permute-start.31
  233.1 17.9 %collective-permute-done.28.u0 = bf16[4,48,3072]{2,1,0:T(8,128)(2,1)S(1)} collective-permute-done((bf16[4,48,3072]{2,1,0:T(8,128)(2,1)S(1)}, bf16[4,48,3072]{2,1,0:T(8,128)(2,1)S(1)}, u32[]{:S(2)}, u32[]{:S(2)}) %collective-permute-start.28) | collective-permute-done | bytes 1179680 | tf_op jit(solution)/shard_map/ppermute | solution.py:652
  251.9 5.0 %collective-permute-done.31.d1 = bf16[4,48,3072]{2,1,0:T(8,128)(2,1)S(1)} collective-permute-done((bf16[4,48,3072]{2,1,0:T(8,128)(2,1)S(1)}, bf16[4,48,3072]{2,1,0:T(8,128)(2,1)S(1)}, u32[]{:S(2)}, u32[]{:S(2)}) %collective-permute-start.31) | collective-permute-done | bytes 1179680 | tf_op jit(solution)/shard_map/ppermute | solution.py:656
  263.9 3.2 %collective-permute-start.36 = (bf16[48,3072]{1,0:T(8,128)(2,1)S(1)}, bf16[48,3072]{1,0:T(8,128)(2,1)S(1)}, u32[]{:S(2)}, u32[]{:S(2)}) collective-permute-start(bf16[48,3072]{1,0:T(8,128)(2,1)S(1)} %get-tuple-element.115), channel_id=1, source_target_pairs={{0,24},{8,0},{16,8},{24,16},{1,25},{9,1},{17,9},{25,17},{2,26},{10... | collective-permute-start | bytes 884744 | tf_op jit(solution)/shard_map/ppermute | solution.py:656
  282.7 4.5 %collective-permute-done.39.b2 = bf16[16,6144]{1,0:T(8,128)(2,1)} collective-permute-done((bf16[16,6144]{1,0:T(8,128)(2,1)}, bf16[16,6144]{1,0:T(8,128)(2,1)}, u32[]{:S(2)}, u32[]{:S(2)}) %collective-permute-start.39) | collective-permute-done | bytes 196640 | tf_op jit(solution)/shard_map/ppermute | solution.py:652
  287.2 2.8 combine.1
  (108 shorter events, 65.8 us)
Async XLA Ops:
  6.5 77.4 %all-gather.2.cloned.1.call-start = ((), (), s32[]{:S(2)}) async-start(), calls=%async_computation.3 | async-start | bytes 12976128 | tf_op jit(solution)/shard_map/all_gather | solution.py:686
  16.6 51.3 %collective-permute-start.3 = (bf16[864,6144]{1,0:T(8,128)(2,1)}, bf16[864,6144]{1,0:T(8,128)(2,1)}, u32[]{:S(2)}, u32[]{:S(2)}) collective-permute-start(bf16[864,6144]{1,0:T(8,128)(2,1)} %pad_maximum_fusion.mine), channel_id=1, source_target_pairs={{0,4},{4,0},{1,5},{5,1},{2,6},{6,2},{3,7},{7,3},{8,12},{12,8},{9,1... | collective-permute-start | bytes 31850504 | tf_op jit(solution)/shard_map/ppermute | solution.py:688
  46.4 21.5 %all-to-all-start.1 = ((bf16[32,64,128]{2,1,0:T(8,128)(2,1)}), bf16[32,64,128]{2,1,0:T(8,128)(2,1)S(1)}, u32[]{:S(2)}, u32[]{:S(2)}) async-start(bf16[32,64,128]{2,1,0:T(8,128)(2,1)} %state_prefix.1), calls=%async_computation.1 | async-start | bytes 1048576 | tf_op jit(solution)/shard_map/all_to_all | solution.py:697
  50.3 229.1 %reduce-scatter.2.cloned.1.call-start = ((), (), s32[]{:S(2)}) async-start(), calls=%async_computation.4 | async-start | bytes 7864320 | tf_op jit(solution)/shard_map/reduce_scatter | solution.py:753
  88.3 11.6 %collective-permute-start.4 = (bf16[48,3072]{1,0:T(8,128)(2,1)S(1)}, bf16[48,3072]{1,0:T(8,128)(2,1)S(1)}, u32[]{:S(2)}, u32[]{:S(2)}) collective-permute-start(bf16[48,3072]{1,0:T(8,128)(2,1)S(1)} %get-tuple-element.70), channel_id=1, source_target_pairs={{0,2},{1,3},{2,0},{3,1},{4,6},{5,7},{6,4},{7,5},{8,10},{9,11},{10,... | collective-permute-start | bytes 884744 | tf_op jit(solution)/shard_map/ppermute | solution.py:660
  91.4 23.4 %collective-permute-start.5 = (bf16[48,3072]{1,0:T(8,128)(2,1)S(1)}, bf16[48,3072]{1,0:T(8,128)(2,1)S(1)}, u32[]{:S(2)}, u32[]{:S(2)}) collective-permute-start(bf16[48,3072]{1,0:T(8,128)(2,1)S(1)} %get-tuple-element.71), channel_id=1, source_target_pairs={{0,1},{1,2},{2,3},{3,0},{4,5},{5,6},{6,7},{7,4},{8,9},{9,10},{10,1... | collective-permute-start | bytes 884744 | tf_op jit(solution)/shard_map/ppermute | solution.py:652
  92.0 22.8 %collective-permute-start.6 = (bf16[48,3072]{1,0:T(8,128)(2,1)S(1)}, bf16[48,3072]{1,0:T(8,128)(2,1)S(1)}, u32[]{:S(2)}, u32[]{:S(2)}) collective-permute-start(bf16[48,3072]{1,0:T(8,128)(2,1)S(1)} %get-tuple-element.72), channel_id=1, source_target_pairs={{0,3},{1,0},{2,1},{3,2},{4,7},{5,4},{6,5},{7,6},{8,11},{9,8},{10,9... | collective-permute-start | bytes 884744 | tf_op jit(solution)/shard_map/ppermute | solution.py:656
  99.0 15.8 %collective-permute-start.7 = (bf16[48,3072]{1,0:T(8,128)(2,1)S(1)}, bf16[48,3072]{1,0:T(8,128)(2,1)S(1)}, u32[]{:S(2)}, u32[]{:S(2)}) collective-permute-start(bf16[48,3072]{1,0:T(8,128)(2,1)S(1)} %get-tuple-element.74), channel_id=1, source_target_pairs={{0,2},{1,3},{2,0},{3,1},{4,6},{5,7},{6,4},{7,5},{8,10},{9,11},{10,... | collective-permute-start | bytes 884744 | tf_op jit(solution)/shard_map/ppermute | solution.py:660
  99.1 18.9 %collective-permute-start.8 = (bf16[48,3072]{1,0:T(8,128)(2,1)S(1)}, bf16[48,3072]{1,0:T(8,128)(2,1)S(1)}, u32[]{:S(2)}, u32[]{:S(2)}) collective-permute-start(bf16[48,3072]{1,0:T(8,128)(2,1)S(1)} %get-tuple-element.75), channel_id=1, source_target_pairs={{0,1},{1,2},{2,3},{3,0},{4,5},{5,6},{6,7},{7,4},{8,9},{9,10},{10,1... | collective-permute-start | bytes 884744 | tf_op jit(solution)/shard_map/ppermute | solution.py:652
  100.0 18.2 %collective-permute-start.9 = (bf16[48,3072]{1,0:T(8,128)(2,1)S(1)}, bf16[48,3072]{1,0:T(8,128)(2,1)S(1)}, u32[]{:S(2)}, u32[]{:S(2)}) collective-permute-start(bf16[48,3072]{1,0:T(8,128)(2,1)S(1)} %get-tuple-element.76), channel_id=1, source_target_pairs={{0,3},{1,0},{2,1},{3,2},{4,7},{5,4},{6,5},{7,6},{8,11},{9,8},{10,9... | collective-permute-start | bytes 884744 | tf_op jit(solution)/shard_map/ppermute | solution.py:656
  119.4 11.5 %collective-permute-start.10 = (bf16[48,3072]{1,0:T(8,128)(2,1)S(1)}, bf16[48,3072]{1,0:T(8,128)(2,1)S(1)}, u32[]{:S(2)}, u32[]{:S(2)}) collective-permute-start(bf16[48,3072]{1,0:T(8,128)(2,1)S(1)} %get-tuple-element.78.a0), channel_id=1, source_target_pairs={{0,16},{8,24},{16,0},{24,8},{1,17},{9,25},{17,1},{25,9},{2,18},{10... | collective-permute-start | bytes 884744 | tf_op jit(solution)/shard_map/ppermute | solution.py:660
  122.5 13.6 %collective-permute-start.12 = (bf16[48,3072]{1,0:T(8,128)(2,1)S(1)}, bf16[48,3072]{1,0:T(8,128)(2,1)S(1)}, u32[]{:S(2)}, u32[]{:S(2)}) collective-permute-start(bf16[48,3072]{1,0:T(8,128)(2,1)S(1)} %get-tuple-element.78.a0), channel_id=1, source_target_pairs={{0,8},{8,16},{16,24},{24,0},{1,9},{9,17},{17,25},{25,1},{2,10},{10... | collective-permute-start | bytes 884744 | tf_op jit(solution)/shard_map/ppermute | solution.py:652
  123.1 11.5 %collective-permute-start.11 = (bf16[48,3072]{1,0:T(8,128)(2,1)S(1)}, bf16[48,3072]{1,0:T(8,128)(2,1)S(1)}, u32[]{:S(2)}, u32[]{:S(2)}) collective-permute-start(bf16[48,3072]{1,0:T(8,128)(2,1)S(1)} %get-tuple-element.79.b0), channel_id=1, source_target_pairs={{0,64},{32,96},{64,0},{96,32},{1,65},{33,97},{65,1},{97,33},{2,66}... | collective-permute-start | bytes 884744 | tf_op jit(solution)/shard_map/ppermute | solution.py:660
  124.4 14.8 %collective-permute-start.13 = (bf16[48,3072]{1,0:T(8,128)(2,1)S(1)}, bf16[48,3072]{1,0:T(8,128)(2,1)S(1)}, u32[]{:S(2)}, u32[]{:S(2)}) collective-permute-start(bf16[48,3072]{1,0:T(8,128)(2,1)S(1)} %get-tuple-element.79.b0), channel_id=1, source_target_pairs={{0,32},{32,64},{64,96},{96,0},{1,33},{33,65},{65,97},{97,1},{2,34}... | collective-permute-start | bytes 884744 | tf_op jit(solution)/shard_map/ppermute | solution.py:652
  124.7 14.5 %collective-permute-start.14 = (bf16[48,3072]{1,0:T(8,128)(2,1)S(1)}, bf16[48,3072]{1,0:T(8,128)(2,1)S(1)}, u32[]{:S(2)}, u32[]{:S(2)}) collective-permute-start(bf16[48,3072]{1,0:T(8,128)(2,1)S(1)} %get-tuple-element.78.a0), channel_id=1, source_target_pairs={{0,24},{8,0},{16,8},{24,16},{1,25},{9,1},{17,9},{25,17},{2,26},{10... | collective-permute-start | bytes 884744 | tf_op jit(solution)/shard_map/ppermute | solution.py:656
  142.6 29.1 %collective-permute-start.16 = (bf16[4,48,3072]{2,1,0:T(8,128)(2,1)S(1)}, bf16[4,48,3072]{2,1,0:T(8,128)(2,1)S(1)}, u32[]{:S(2)}, u32[]{:S(2)}) collective-permute-start(bf16[4,48,3072]{2,1,0:T(8,128)(2,1)S(1)} %copy-done.7), channel_id=1, source_target_pairs={{0,32},{32,64},{64,96},{96,0},{1,33},{33,65},{65,97},{97,1},{2,34}... | collective-permute-start | bytes 3538952 | tf_op jit(solution)/shard_map/ppermute | solution.py:652
  142.6 29.3 %collective-permute-start.17 = (bf16[4,48,3072]{2,1,0:T(8,128)(2,1)}, bf16[4,48,3072]{2,1,0:T(8,128)(2,1)S(1)}, u32[]{:S(2)}, u32[]{:S(2)}) collective-permute-start(bf16[4,48,3072]{2,1,0:T(8,128)(2,1)} %get-tuple-element.83.b0), channel_id=1, source_target_pairs={{0,8},{8,16},{16,24},{24,0},{1,9},{9,17},{17,25},{25,1},{2,10},{10... | collective-permute-start | bytes 3538952 | tf_op jit(solution)/shard_map/ppermute | solution.py:652
  143.7 28.2 %collective-permute-start.18 = (bf16[4,48,3072]{2,1,0:T(8,128)(2,1)S(1)}, bf16[4,48,3072]{2,1,0:T(8,128)(2,1)S(1)}, u32[]{:S(2)}, u32[]{:S(2)}) collective-permute-start(bf16[4,48,3072]{2,1,0:T(8,128)(2,1)S(1)} %copy-done.7), channel_id=1, source_target_pairs={{0,96},{32,0},{64,32},{96,64},{1,97},{33,1},{65,33},{97,65},{2,98}... | collective-permute-start | bytes 3538952 | tf_op jit(solution)/shard_map/ppermute | solution.py:656
  146.1 27.8 %collective-permute-start.19 = (bf16[4,48,3072]{2,1,0:T(8,128)(2,1)}, bf16[4,48,3072]{2,1,0:T(8,128)(2,1)S(1)}, u32[]{:S(2)}, u32[]{:S(2)}) collective-permute-start(bf16[4,48,3072]{2,1,0:T(8,128)(2,1)} %get-tuple-element.83.b0), channel_id=1, source_target_pairs={{0,24},{8,0},{16,8},{24,16},{1,25},{9,1},{17,9},{25,17},{2,26},{10... | collective-permute-start | bytes 3538952 | tf_op jit(solution)/shard_map/ppermute | solution.py:656
  174.1 23.2 %collective-permute-start.20 = (bf16[2,48,3072]{2,1,0:T(8,128)(2,1)S(1)}, bf16[2,48,3072]{2,1,0:T(8,128)(2,1)S(1)}, u32[]{:S(2)}, u32[]{:S(2)}) collective-permute-start(bf16[2,48,3072]{2,1,0:T(8,128)(2,1)S(1)} %get-tuple-element.86), channel_id=1, source_target_pairs={{0,32},{32,64},{64,96},{96,0},{1,33},{33,65},{65,97},{97,1},{2,34}... | collective-permute-start | bytes 1769480 | tf_op jit(solution)/shard_map/ppermute | solution.py:652
  174.2 23.1 %collective-permute-start.21 = (bf16[2,48,3072]{2,1,0:T(8,128)(2,1)S(1)}, bf16[2,48,3072]{2,1,0:T(8,128)(2,1)S(1)}, u32[]{:S(2)}, u32[]{:S(2)}) collective-permute-start(bf16[2,48,3072]{2,1,0:T(8,128)(2,1)S(1)} %get-tuple-element.87), channel_id=1, source_target_pairs={{0,8},{8,16},{16,24},{24,0},{1,9},{9,17},{17,25},{25,1},{2,10},{10... | collective-permute-start | bytes 1769480 | tf_op jit(solution)/shard_map/ppermute | solution.py:652
  175.7 21.6 %collective-permute-start.22 = (bf16[2,48,3072]{2,1,0:T(8,128)(2,1)S(1)}, bf16[2,48,3072]{2,1,0:T(8,128)(2,1)S(1)}, u32[]{:S(2)}, u32[]{:S(2)}) collective-permute-start(bf16[2,48,3072]{2,1,0:T(8,128)(2,1)S(1)} %get-tuple-element.88), channel_id=1, source_target_pairs={{0,96},{32,0},{64,32},{96,64},{1,97},{33,1},{65,33},{97,65},{2,98}... | collective-permute-start | bytes 1769480 | tf_op jit(solution)/shard_map/ppermute | solution.py:656
  178.9 18.5 %collective-permute-start.23 = (bf16[2,48,3072]{2,1,0:T(8,128)(2,1)S(1)}, bf16[2,48,3072]{2,1,0:T(8,128)(2,1)S(1)}, u32[]{:S(2)}, u32[]{:S(2)}) collective-permute-start(bf16[2,48,3072]{2,1,0:T(8,128)(2,1)S(1)} %get-tuple-element.89), channel_id=1, source_target_pairs={{0,24},{8,0},{16,8},{24,16},{1,25},{9,1},{17,9},{25,17},{2,26},{10... | collective-permute-start | bytes 1769480 | tf_op jit(solution)/shard_map/ppermute | solution.py:656
  209.3 15.3 %collective-permute-start.24 = (bf16[2,48,3072]{2,1,0:T(8,128)(2,1)}, bf16[2,48,3072]{2,1,0:T(8,128)(2,1)S(1)}, u32[]{:S(2)}, u32[]{:S(2)}) collective-permute-start(bf16[2,48,3072]{2,1,0:T(8,128)(2,1)} %get-tuple-element.97), channel_id=1, source_target_pairs={{0,32},{32,64},{64,96},{96,0},{1,33},{33,65},{65,97},{97,1},{2,34}... | collective-permute-start | bytes 1769480 | tf_op jit(solution)/shard_map/ppermute | solution.py:652
  209.6 15.0 %collective-permute-start.25 = (bf16[2,48,3072]{2,1,0:T(8,128)(2,1)S(1)}, bf16[2,48,3072]{2,1,0:T(8,128)(2,1)S(1)}, u32[]{:S(2)}, u32[]{:S(2)}) collective-permute-start(bf16[2,48,3072]{2,1,0:T(8,128)(2,1)S(1)} %get-tuple-element.98), channel_id=1, source_target_pairs={{0,8},{8,16},{16,24},{24,0},{1,9},{9,17},{17,25},{25,1},{2,10},{10... | collective-permute-start | bytes 1769480 | tf_op jit(solution)/shard_map/ppermute | solution.py:652
  209.7 15.0 %collective-permute-start.26 = (bf16[2,48,3072]{2,1,0:T(8,128)(2,1)S(1)}, bf16[2,48,3072]{2,1,0:T(8,128)(2,1)S(1)}, u32[]{:S(2)}, u32[]{:S(2)}) collective-permute-start(bf16[2,48,3072]{2,1,0:T(8,128)(2,1)S(1)} %get-tuple-element.99), channel_id=1, source_target_pairs={{0,96},{32,0},{64,32},{96,64},{1,97},{33,1},{65,33},{97,65},{2,98}... | collective-permute-start | bytes 1769480 | tf_op jit(solution)/shard_map/ppermute | solution.py:656
  212.8 12.7 %collective-permute-start.27 = (bf16[2,48,3072]{2,1,0:T(8,128)(2,1)S(1)}, bf16[2,48,3072]{2,1,0:T(8,128)(2,1)S(1)}, u32[]{:S(2)}, u32[]{:S(2)}) collective-permute-start(bf16[2,48,3072]{2,1,0:T(8,128)(2,1)S(1)} %get-tuple-element.100), channel_id=1, source_target_pairs={{0,24},{8,0},{16,8},{24,16},{1,25},{9,1},{17,9},{25,17},{2,26},{10... | collective-permute-start | bytes 1769480 | tf_op jit(solution)/shard_map/ppermute | solution.py:656
  226.1 24.9 %collective-permute-start.28 = (bf16[4,48,3072]{2,1,0:T(8,128)(2,1)S(1)}, bf16[4,48,3072]{2,1,0:T(8,128)(2,1)S(1)}, u32[]{:S(2)}, u32[]{:S(2)}) collective-permute-start(bf16[4,48,3072]{2,1,0:T(8,128)(2,1)S(1)} %get-tuple-element.106), channel_id=1, source_target_pairs={{0,32},{32,64},{64,96},{96,0},{1,33},{33,65},{65,97},{97,1},{2,34}... | collective-permute-start | bytes 3538952 | tf_op jit(solution)/shard_map/ppermute | solution.py:652
  226.2 25.7 %collective-permute-start.29 = (bf16[4,48,3072]{2,1,0:T(8,128)(2,1)S(1)}, bf16[4,48,3072]{2,1,0:T(8,128)(2,1)S(1)}, u32[]{:S(2)}, u32[]{:S(2)}) collective-permute-start(bf16[4,48,3072]{2,1,0:T(8,128)(2,1)S(1)} %get-tuple-element.107), channel_id=1, source_target_pairs={{0,8},{8,16},{16,24},{24,0},{1,9},{9,17},{17,25},{25,1},{2,10},{10... | collective-permute-start | bytes 3538952 | tf_op jit(solution)/shard_map/ppermute | solution.py:652
  227.0 24.9 %collective-permute-start.30 = (bf16[4,48,3072]{2,1,0:T(8,128)(2,1)S(1)}, bf16[4,48,3072]{2,1,0:T(8,128)(2,1)S(1)}, u32[]{:S(2)}, u32[]{:S(2)}) collective-permute-start(bf16[4,48,3072]{2,1,0:T(8,128)(2,1)S(1)} %get-tuple-element.101.late), channel_id=1, source_target_pairs={{0,96},{32,0},{64,32},{96,64},{1,97},{33,1},{65,33},{97,65},{2,98}... | collective-permute-start | bytes 3538952 | tf_op jit(solution)/shard_map/ppermute | solution.py:656
  230.2 26.8 %collective-permute-start.31 = (bf16[4,48,3072]{2,1,0:T(8,128)(2,1)S(1)}, bf16[4,48,3072]{2,1,0:T(8,128)(2,1)S(1)}, u32[]{:S(2)}, u32[]{:S(2)}) collective-permute-start(bf16[4,48,3072]{2,1,0:T(8,128)(2,1)S(1)} %get-tuple-element.108), channel_id=1, source_target_pairs={{0,24},{8,0},{16,8},{24,16},{1,25},{9,1},{17,9},{25,17},{2,26},{10... | collective-permute-start | bytes 3538952 | tf_op jit(solution)/shard_map/ppermute | solution.py:656
  277.9 9.3 %collective-permute-start.39 = (bf16[16,6144]{1,0:T(8,128)(2,1)}, bf16[16,6144]{1,0:T(8,128)(2,1)}, u32[]{:S(2)}, u32[]{:S(2)}) collective-permute-start(bf16[16,6144]{1,0:T(8,128)(2,1)} %get-tuple-element.119), channel_id=1, source_target_pairs={{0,1},{1,2},{2,3},{3,0},{4,5},{5,6},{6,7},{7,4},{8,9},{9,10},{10,1... | collective-permute-start | bytes 589832 | tf_op jit(solution)/shard_map/ppermute | solution.py:652
  (24 other events, 268.9 us)
Sparse Core Ops, SparseCore 0:
  9.6 74.2 all-gather.1
  141.5 62.6 reduce-scatter.1

commit v11 on v10

--- a/solution.py
+++ b/solution.py
@@ -299,7 +299,7 @@
 
 
 def norm_kernel(*refs):
-    gain, _, o0, o1 = refs[8:]
+    gain, _, _, o0, o1, _ = refs[8:]
     half = o0.shape[1]
     x = [sum(r[...].astype(F32) for r in refs[4 * k : 4 * k + 4]) for k in range(2)]
     squares = sum(jnp.sum(v * v, -1, keepdims=True) for v in x)
@@ -315,7 +315,7 @@
     b_down[...] = b_above[2:4]
 
 
-def stack_kernel(a0, b0, a3, b3, a1, b1, a2, b2, held, o0, o1, same):
+def stack_kernel(a0, b0, a3, b3, a1, b1, a2, b2, o0, o1):
     for i, (a, b) in enumerate(((a0, b0), (a1, b1), (a2, b2), (a3, b3))):
         o0[i] = a[...]
         o1[i] = b[...]
@@ -721,21 +721,25 @@
     whole, done = whole_projection(normed, weight_out)
 
     size = terms[0].shape[0]
-    a0, b0 = call(
+    a0, b0, whole = call(
         norm_kernel,
         "selected_norm",
-        [((size, half), BF)] * 2,
+        [((size, half), BF)] * 2 + [(whole.shape, BF)],
         *terms,
         gain,
         done,
-        in_specs=[VM] * 10,
-        out_specs=[VM] * 2,
-    )
-
-    a4, b4, whole = call(
+        whole,
+        in_specs=[VM] * 10 + [ANY],
+        out_specs=[VM] * 2 + [ANY],
+        input_output_aliases={10: 2},
+        vmem=50,
+    )
+    mixed = lax.psum_scatter(whole, "x", scatter_dimension=0, tiled=True)
+
+    a4, b4 = call(
         stack_kernel,
         "stack",
-        [((4, size, half), BF)] * 2 + [(whole.shape, BF)],
+        [((4, size, half), BF)] * 2,
         a0,
         b0,
         across(a0, "y"),
@@ -744,13 +748,10 @@
         up_one(b0, "z"),
         down_one(a0, "y"),
         down_one(b0, "z"),
-        whole,
-        in_specs=[VM] * 8 + [ANY],
-        out_specs=[VM] * 2 + [ANY],
-        input_output_aliases={8: 2},
-        vmem=50,
-    )
-    mixed = lax.psum_scatter(whole, "x", scatter_dimension=0, tiled=True)
+        in_specs=[VM] * 8,
+        out_specs=[VM] * 2,
+        vmem=8,
+    )
     a_below, b_below = up_one(a4, "z"), up_one(b4, "y")
     a_above, b_above = down_one(a4, "z"), down_one(b4, "y")
     a_up, b_up, a_down, b_down = call(

time: 298 us -> 295 us (0.990)
    unnamed x25 -> x17, local copies, waits for them, and re-layouts: 6.51 us -> 4.23 us
where the time goes in v11:
time: 295 us; the launch traced here: 294 us
  waiting for transfers between devices  94.8 us (32%)
  Pallas kernels  79.6 us (27%)
  starting transfers between devices  70.2 us (24%)
  blocking collectives  21.7 us (7%)
  between operations  13.7 us (5%)
  other arithmetic  9.37 us (3%)
  local copies, waits for them, and re-layouts  4.47 us (2%)
    pallas_call x16, Pallas kernels, call(): pl.pallas_call(kernel, out_shape=[jax.ShapeDtypeStruct(s, d) for s, d in...  66.9 us
    ppermute x15, waiting for transfers between devices, up_one(): return lax.ppermute(x, axis, ring(4, 1))  57 us
    ppermute x15, starting transfers between devices, down_one(): return lax.ppermute(x, axis, ring(4, -1))  40.3 us
    all_to_all x1, blocking collectives, shards(): arrived = lax.all_to_all(states, SEQ, 0, 0, tiled=True)  21.7 us
    ppermute x7, starting transfers between devices, across(): return lax.ppermute(x, axis, ring(4, 2))  11.3 us
    ppermute x15, waiting for transfers between devices, down_one(): return lax.ppermute(x, axis, ring(4, -1))  10.2 us
    ppermute x15, starting transfers between devices, up_one(): return lax.ppermute(x, axis, ring(4, 1))  10.1 us
    concatenate x1, other arithmetic, shards(): weights = jnp.concatenate([gate_weight[0], up_weight[0], down_weight[0]])  9.37 us
  transfers between devices with their start and end apart: 44, of which 23 were waited for; matrix products, arithmetic and copies ran while one was open for 3% of the time, Pallas kernels for 24%

profile of v11, /device:TPU:0, one launch (start us, length us, event | category | flops | bytes accessed | tf_op | source)
XLA Modules:
  0.0 293.9 jit_solution(16630413704549910391)
XLA Ops:
  7.3 9.4 %pad_maximum_fusion.mine = bf16[864,6144]{1,0:T(8,128)(2,1)} fusion(bf16[288,6144]{1,0:T(8,128)(2,1)} %bitcast.29, bf16[288,6144]{1,0:T(8,128)(2,1)} %bitcast.30, bf16[288,6144]{1,0:T(8,128)(2,1)} %bitcast.31), kind=kLoop, calls=%fused_computation | loop fusion | flops 31850496 | bytes 21233664 | tf_op jit(solution)/shard_map/concatenate | solution.py:687
  16.6 7.1 %local_attention.1 = (f32[2,256,1024]{2,1,0:T(8,128)}, bf16[32,80,128]{2,1,0:T(8,128)(2,1)}, f32[2,256,8]{2,1,0:T(8,128)}) custom-call(bf16[2,256,1024]{2,1,0:T(8,128)(2,1)} %q_ref.3, bf16[2,256,1024]{2,1,0:T(8,128)(2,1)} %k_ref.1, bf16[2,256,1024]{2,1,0:T(8,128)(2,1)} %v_ref.1, f32[2,8,256]{2,1,0:T(8,128)} %bitcast.34), custom_call_target="tpu_custom_call" | custom-call | tf_op jit(solution)/shard_map/local_attention/pallas_call | solution.py:84
  23.8 21.7 %all_to_all.10.in_ref = bf16[32,80,128]{2,1,0:T(8,128)(2,1)S(1)} all-to-all(bf16[32,80,128]{2,1,0:T(8,128)(2,1)} %get-tuple-element.66), channel_id=1, replica_groups=mesh['z'=4,'y'=4,'core'=2,'x'=4] {'z','y','core'}, dimensions={0} | all-to-all | bytes 1310720 | tf_op jit(solution)/shard_map/all_to_all | solution.py:696
  46.4 3.9 %all-to-all-start.1 = ((bf16[32,64,128]{2,1,0:T(8,128)(2,1)}), bf16[32,64,128]{2,1,0:T(8,128)(2,1)S(1)}, u32[]{:S(2)}, u32[]{:S(2)}) async-start(bf16[32,64,128]{2,1,0:T(8,128)(2,1)} %state_prefix.1), calls=%async_computation.1 | async-start | bytes 1048576 | tf_op jit(solution)/shard_map/all_to_all | solution.py:697
  56.6 2.8 collective-permute-done.1
  60.5 7.5 %all-to-all-done.1 = bf16[32,64,128]{2,1,0:T(8,128)(2,1)S(1)} async-done(((bf16[32,64,128]{2,1,0:T(8,128)(2,1)}), bf16[32,64,128]{2,1,0:T(8,128)(2,1)S(1)}, u32[]{:S(2)}, u32[]{:S(2)}) %all-to-all-start.1) | async-done | bytes 524320 | tf_op jit(solution)/shard_map/all_to_all | solution.py:697
  68.7 4.6 %carried_norm.1 = (bf16[4,2,64,1024]{3,2,1,0:T(8,128)(2,1)}, bf16[864,6144]{1,0:T(8,128)(2,1)}) custom-call(bf16[2,256,1024]{2,1,0:T(8,128)(2,1)} %q_ref.3, f32[2,256,1024]{2,1,0:T(8,128)} %get-tuple-element.64.inner_ref, f32[2,256,8]{2,1,0:T(8,128)} %get-tuple-element.65.cum_ref, bf16[16,128,128]{2,1,0:T(8,128)(2,1)} %bitcast.32, ...), custom_call_target="tpu_custom_call", output_to_operand_aliasing={{1}: (5, {})} | custom-call | tf_op jit(solution)/shard_map/carried_norm/pallas_call | solution.py:138
  75.0 9.0 %all-gather.2.cloned.1.call-done.weight.weight_ref = bf16[6144,1024]{1,0:T(8,128)(2,1)} async-done(((bf16[192,1024]{1,0:T(8,128)(2,1)}), bf16[6144,1024]{1,0:T(8,128)(2,1)}) %all-gather.2.cloned.1.call-update) | async-done | bytes 12582928 | tf_op jit(solution)/shard_map/all_gather | solution.py:686
  84.0 4.4 %selected_projection.2 = (bf16[48,3072]{1,0:T(8,128)(2,1)S(1)}, bf16[48,3072]{1,0:T(8,128)(2,1)S(1)}, bf16[48,3072]{1,0:T(8,128)(2,1)S(1)}, bf16[48,3072]{1,0:T(8,128)(2,1)S(1)}) custom-call(bf16[192,1024]{1,0:T(8,128)(2,1)S(1)} %pick.1.picked, bf16[192,128]{1,0:T(8,128)(2,1)S(1)} %get-tuple-element.68.own, ...), custom_call_target="tpu_custom_call" | custom-call | tf_op jit(solution)/shard_map/selected_projection/pallas_call | solution.py:165
  88.4 3.0 %collective-permute-start.4 = (bf16[48,3072]{1,0:T(8,128)(2,1)S(1)}, bf16[48,3072]{1,0:T(8,128)(2,1)S(1)}, u32[]{:S(2)}, u32[]{:S(2)}) collective-permute-start(bf16[48,3072]{1,0:T(8,128)(2,1)S(1)} %get-tuple-element.70), channel_id=1, source_target_pairs={{0,2},{1,3},{2,0},{3,1},{4,6},{5,7},{6,4},{7,5},{8,10},{9,11},{10,... | collective-permute-start | bytes 884744 | tf_op jit(solution)/shard_map/ppermute | solution.py:660
  94.7 4.4 %selected_projection.3 = (bf16[48,3072]{1,0:T(8,128)(2,1)S(1)}, bf16[48,3072]{1,0:T(8,128)(2,1)S(1)}, bf16[48,3072]{1,0:T(8,128)(2,1)S(1)}, bf16[48,3072]{1,0:T(8,128)(2,1)S(1)}) custom-call(bf16[192,1024]{1,0:T(8,128)(2,1)S(1)} %pick.1.picked, bf16[192,128]{1,0:T(8,128)(2,1)S(1)} %get-tuple-element.68.own, ...), custom_call_target="tpu_custom_call" | custom-call | tf_op jit(solution)/shard_map/selected_projection/pallas_call | solution.py:165
  102.5 12.3 %whole_projection.1 = (bf16[512,6144]{1,0:T(8,128)(2,1)}, f32[8,128]{1,0:T(8,128)}) custom-call(bf16[512,1024]{1,0:T(8,128)(2,1)} %bitcast.19, bf16[6144,1024]{1,0:T(8,128)(2,1)} %all-gather.2.cloned.1.call-done.weight.weight_ref), custom_call_target="tpu_custom_call" | custom-call | flops 6442450944 | bytes 25165824 | tf_op jit(solution)/shard_map/whole_projection/pallas_call | solution.py:165
  114.9 3.2 %collective-permute-done.8.refs_6_ = bf16[48,3072]{1,0:T(8,128)(2,1)S(1)} collective-permute-done((bf16[48,3072]{1,0:T(8,128)(2,1)S(1)}, bf16[48,3072]{1,0:T(8,128)(2,1)S(1)}, u32[]{:S(2)}, u32[]{:S(2)}) %collective-permute-start.8) | collective-permute-done | bytes 294944 | tf_op jit(solution)/shard_map/ppermute | solution.py:652
  119.5 3.1 %collective-permute-start.10 = (bf16[48,3072]{1,0:T(8,128)(2,1)S(1)}, bf16[48,3072]{1,0:T(8,128)(2,1)S(1)}, u32[]{:S(2)}, u32[]{:S(2)}) collective-permute-start(bf16[48,3072]{1,0:T(8,128)(2,1)S(1)} %get-tuple-element.80.a0), channel_id=1, source_target_pairs={{0,16},{8,24},{16,0},{24,8},{1,17},{9,25},{17,1},{25,9},{2,18},{10... | collective-permute-start | bytes 884744 | tf_op jit(solution)/shard_map/ppermute | solution.py:660
  127.4 3.5 %collective-permute-done.10.a3 = bf16[48,3072]{1,0:T(8,128)(2,1)S(1)} collective-permute-done((bf16[48,3072]{1,0:T(8,128)(2,1)S(1)}, bf16[48,3072]{1,0:T(8,128)(2,1)S(1)}, u32[]{:S(2)}, u32[]{:S(2)}) %collective-permute-start.10) | collective-permute-done | bytes 294944 | tf_op jit(solution)/shard_map/ppermute | solution.py:660
  136.2 3.0 %collective-permute-done.13.b1 = bf16[48,3072]{1,0:T(8,128)(2,1)S(1)} collective-permute-done((bf16[48,3072]{1,0:T(8,128)(2,1)S(1)}, bf16[48,3072]{1,0:T(8,128)(2,1)S(1)}, u32[]{:S(2)}, u32[]{:S(2)}) %collective-permute-start.13) | collective-permute-done | bytes 294944 | tf_op jit(solution)/shard_map/ppermute | solution.py:652
  143.0 3.0 %collective-permute-start.19 = (bf16[4,48,3072]{2,1,0:T(8,128)(2,1)S(1)}, bf16[4,48,3072]{2,1,0:T(8,128)(2,1)S(1)}, u32[]{:S(2)}, u32[]{:S(2)}) collective-permute-start(bf16[4,48,3072]{2,1,0:T(8,128)(2,1)S(1)} %get-tuple-element.83.b0), channel_id=1, source_target_pairs={{0,24},{8,0},{16,8},{24,16},{1,25},{9,1},{17,9},{25,17},{2,26},{10... | collective-permute-start | bytes 3538952 | tf_op jit(solution)/shard_map/ppermute | solution.py:656
  145.9 22.7 %collective-permute-done.16.a1.a_below = bf16[4,48,3072]{2,1,0:T(8,128)(2,1)S(1)} collective-permute-done((bf16[4,48,3072]{2,1,0:T(8,128)(2,1)S(1)}, bf16[4,48,3072]{2,1,0:T(8,128)(2,1)S(1)}, u32[]{:S(2)}, u32[]{:S(2)}) %collective-permute-start.16) | collective-permute-done | bytes 1179680 | tf_op jit(solution)/shard_map/ppermute | solution.py:652
  172.5 3.2 %collective-permute-start.22 = (bf16[2,48,3072]{2,1,0:T(8,128)(2,1)S(1)}, bf16[2,48,3072]{2,1,0:T(8,128)(2,1)S(1)}, u32[]{:S(2)}, u32[]{:S(2)}) collective-permute-start(bf16[2,48,3072]{2,1,0:T(8,128)(2,1)S(1)} %get-tuple-element.88), channel_id=1, source_target_pairs={{0,96},{32,0},{64,32},{96,64},{1,97},{33,1},{65,33},{97,65},{2,98}... | collective-permute-start | bytes 1769480 | tf_op jit(solution)/shard_map/ppermute | solution.py:656
  177.8 16.3 %near_rows.1 = (f32[768,1152]{1,0:T(8,128)S(1)}, bf16[576,6144]{1,0:T(8,128)(2,1)S(1)}, bf16[576,6144]{1,0:T(8,128)(2,1)S(1)}) custom-call(bf16[4,48,3072]{2,1,0:T(8,128)(2,1)S(1)} %get-tuple-element.82.a0, bf16[4,48,3072]{2,1,0:T(8,128)(2,1)S(1)} %get-tuple-element.83.b0, bf16[4,48,3072]{2,1,0:T(8,128)(2,1)S(1)} %collective-permute-done.16.a1.a_below, ...), custom_call_target="tpu_custom_call" | custom-call | flops 8153726976 | bytes 1048576 | tf_op jit(solution)/shard_map/near_rows/pallas_call | solution.py:165
  194.1 11.9 %far_rows.1 = (bf16[768,576]{1,0:T(8,128)(2,1)S(1)}, bf16[2,48,3072]{2,1,0:T(8,128)(2,1)}, bf16[2,48,3072]{2,1,0:T(8,128)(2,1)S(1)}, bf16[2,48,3072]{2,1,0:T(8,128)(2,1)S(1)}, bf16[2,48,3072]{2,1,0:T(8,128)(2,1)S(1)}) custom-call(f32[768,1152]{1,0:T(8,128)S(1)} %get-tuple-element.85.acc, bf16[2,48,3072]{2,1,0:T(8,128)(2,1)S(1)} %collective-permute-done.20.a3, ...), custom_call_target="tpu_custom_call" | custom-call | tf_op jit(solution)/shard_map/far_rows/pallas_call | solution.py:165
  206.4 3.1 %collective-permute-start.26 = (bf16[2,48,3072]{2,1,0:T(8,128)(2,1)S(1)}, bf16[2,48,3072]{2,1,0:T(8,128)(2,1)S(1)}, u32[]{:S(2)}, u32[]{:S(2)}) collective-permute-start(bf16[2,48,3072]{2,1,0:T(8,128)(2,1)S(1)} %get-tuple-element.99), channel_id=1, source_target_pairs={{0,96},{32,0},{64,32},{96,64},{1,97},{33,1},{65,33},{97,65},{2,98}... | collective-permute-start | bytes 1769480 | tf_op jit(solution)/shard_map/ppermute | solution.py:656
  209.6 3.2 %collective-permute-start.27 = (bf16[2,48,3072]{2,1,0:T(8,128)(2,1)S(1)}, bf16[2,48,3072]{2,1,0:T(8,128)(2,1)S(1)}, u32[]{:S(2)}, u32[]{:S(2)}) collective-permute-start(bf16[2,48,3072]{2,1,0:T(8,128)(2,1)S(1)} %get-tuple-element.100), channel_id=1, source_target_pairs={{0,24},{8,0},{16,8},{24,16},{1,25},{9,1},{17,9},{25,17},{2,26},{10... | collective-permute-start | bytes 1769480 | tf_op jit(solution)/shard_map/ppermute | solution.py:656
  212.8 8.6 %rest_rows.1 = (bf16[4,48,3072]{2,1,0:T(8,128)(2,1)S(1)}, bf16[4,48,3072]{2,1,0:T(8,128)(2,1)S(1)}, bf16[4,48,3072]{2,1,0:T(8,128)(2,1)S(1)}, bf16[4,48,3072]{2,...) custom-call(bf16[768,576]{1,0:T(8,128)(2,1)S(1)} %get-tuple-element.92.hidden, ...), custom_call_target="tpu_custom_call" | custom-call | flops 4076863488 | bytes 1048576 | tf_op jit(solution)/shard_map/rest_rows/pallas_call | solution.py:165
  223.7 3.2 %collective-permute-start.30 = (bf16[4,48,3072]{2,1,0:T(8,128)(2,1)S(1)}, bf16[4,48,3072]{2,1,0:T(8,128)(2,1)S(1)}, u32[]{:S(2)}, u32[]{:S(2)}) collective-permute-start(bf16[4,48,3072]{2,1,0:T(8,128)(2,1)S(1)} %get-tuple-element.101.late), channel_id=1, source_target_pairs={{0,96},{32,0},{64,32},{96,64},{1,97},{33,1},{65,33},{97,65},{2,98}... | collective-permute-start | bytes 3538952 | tf_op jit(solution)/shard_map/ppermute | solution.py:656
  226.9 3.0 %collective-permute-start.31 = (bf16[4,48,3072]{2,1,0:T(8,128)(2,1)S(1)}, bf16[4,48,3072]{2,1,0:T(8,128)(2,1)S(1)}, u32[]{:S(2)}, u32[]{:S(2)}) collective-permute-start(bf16[4,48,3072]{2,1,0:T(8,128)(2,1)S(1)} %get-tuple-element.108), channel_id=1, source_target_pairs={{0,24},{8,0},{16,8},{24,16},{1,25},{9,1},{17,9},{25,17},{2,26},{10... | collective-permute-start | bytes 3538952 | tf_op jit(solution)/shard_map/ppermute | solution.py:656
  229.9 17.9 %collective-permute-done.28.u0 = bf16[4,48,3072]{2,1,0:T(8,128)(2,1)S(1)} collective-permute-done((bf16[4,48,3072]{2,1,0:T(8,128)(2,1)S(1)}, bf16[4,48,3072]{2,1,0:T(8,128)(2,1)S(1)}, u32[]{:S(2)}, u32[]{:S(2)}) %collective-permute-start.28) | collective-permute-done | bytes 1179680 | tf_op jit(solution)/shard_map/ppermute | solution.py:652
  248.7 5.0 %collective-permute-done.31.d1 = bf16[4,48,3072]{2,1,0:T(8,128)(2,1)S(1)} collective-permute-done((bf16[4,48,3072]{2,1,0:T(8,128)(2,1)S(1)}, bf16[4,48,3072]{2,1,0:T(8,128)(2,1)S(1)}, u32[]{:S(2)}, u32[]{:S(2)}) %collective-permute-start.31) | collective-permute-done | bytes 1179680 | tf_op jit(solution)/shard_map/ppermute | solution.py:656
  260.6 3.2 %collective-permute-start.36 = (bf16[48,3072]{1,0:T(8,128)(2,1)S(1)}, bf16[48,3072]{1,0:T(8,128)(2,1)S(1)}, u32[]{:S(2)}, u32[]{:S(2)}) collective-permute-start(bf16[48,3072]{1,0:T(8,128)(2,1)S(1)} %get-tuple-element.115), channel_id=1, source_target_pairs={{0,24},{8,0},{16,8},{24,16},{1,25},{9,1},{17,9},{25,17},{2,26},{10... | collective-permute-start | bytes 884744 | tf_op jit(solution)/shard_map/ppermute | solution.py:656
  271.9 2.9 collective-permute-start.38
  279.7 4.5 %collective-permute-done.39.b2 = bf16[16,6144]{1,0:T(8,128)(2,1)} collective-permute-done((bf16[16,6144]{1,0:T(8,128)(2,1)}, bf16[16,6144]{1,0:T(8,128)(2,1)}, u32[]{:S(2)}, u32[]{:S(2)}) %collective-permute-start.39) | collective-permute-done | bytes 196640 | tf_op jit(solution)/shard_map/ppermute | solution.py:652
  284.2 2.8 combine.1
  (100 shorter events, 62.4 us)
Async XLA Ops:
  6.5 77.4 %all-gather.2.cloned.1.call-start = ((), (), s32[]{:S(2)}) async-start(), calls=%async_computation.3 | async-start | bytes 12976128 | tf_op jit(solution)/shard_map/all_gather | solution.py:686
  16.6 51.3 %collective-permute-start.3 = (bf16[864,6144]{1,0:T(8,128)(2,1)}, bf16[864,6144]{1,0:T(8,128)(2,1)}, u32[]{:S(2)}, u32[]{:S(2)}) collective-permute-start(bf16[864,6144]{1,0:T(8,128)(2,1)} %pad_maximum_fusion.mine), channel_id=1, source_target_pairs={{0,4},{4,0},{1,5},{5,1},{2,6},{6,2},{3,7},{7,3},{8,12},{12,8},{9,1... | collective-permute-start | bytes 31850504 | tf_op jit(solution)/shard_map/ppermute | solution.py:688
  46.4 21.5 %all-to-all-start.1 = ((bf16[32,64,128]{2,1,0:T(8,128)(2,1)}), bf16[32,64,128]{2,1,0:T(8,128)(2,1)S(1)}, u32[]{:S(2)}, u32[]{:S(2)}) async-start(bf16[32,64,128]{2,1,0:T(8,128)(2,1)} %state_prefix.1), calls=%async_computation.1 | async-start | bytes 1048576 | tf_op jit(solution)/shard_map/all_to_all | solution.py:697
  50.3 226.0 %reduce-scatter.2.cloned.1.call-start = ((), (), s32[]{:S(2)}) async-start(), calls=%async_computation.4 | async-start | bytes 7864320 | tf_op jit(solution)/shard_map/reduce_scatter | solution.py:737
  88.4 11.6 %collective-permute-start.4 = (bf16[48,3072]{1,0:T(8,128)(2,1)S(1)}, bf16[48,3072]{1,0:T(8,128)(2,1)S(1)}, u32[]{:S(2)}, u32[]{:S(2)}) collective-permute-start(bf16[48,3072]{1,0:T(8,128)(2,1)S(1)} %get-tuple-element.70), channel_id=1, source_target_pairs={{0,2},{1,3},{2,0},{3,1},{4,6},{5,7},{6,4},{7,5},{8,10},{9,11},{10,... | collective-permute-start | bytes 884744 | tf_op jit(solution)/shard_map/ppermute | solution.py:660
  91.4 23.4 %collective-permute-start.5 = (bf16[48,3072]{1,0:T(8,128)(2,1)S(1)}, bf16[48,3072]{1,0:T(8,128)(2,1)S(1)}, u32[]{:S(2)}, u32[]{:S(2)}) collective-permute-start(bf16[48,3072]{1,0:T(8,128)(2,1)S(1)} %get-tuple-element.71), channel_id=1, source_target_pairs={{0,1},{1,2},{2,3},{3,0},{4,5},{5,6},{6,7},{7,4},{8,9},{9,10},{10,1... | collective-permute-start | bytes 884744 | tf_op jit(solution)/shard_map/ppermute | solution.py:652
  92.0 22.8 %collective-permute-start.6 = (bf16[48,3072]{1,0:T(8,128)(2,1)S(1)}, bf16[48,3072]{1,0:T(8,128)(2,1)S(1)}, u32[]{:S(2)}, u32[]{:S(2)}) collective-permute-start(bf16[48,3072]{1,0:T(8,128)(2,1)S(1)} %get-tuple-element.72), channel_id=1, source_target_pairs={{0,3},{1,0},{2,1},{3,2},{4,7},{5,4},{6,5},{7,6},{8,11},{9,8},{10,9... | collective-permute-start | bytes 884744 | tf_op jit(solution)/shard_map/ppermute | solution.py:656
  99.1 15.8 %collective-permute-start.7 = (bf16[48,3072]{1,0:T(8,128)(2,1)S(1)}, bf16[48,3072]{1,0:T(8,128)(2,1)S(1)}, u32[]{:S(2)}, u32[]{:S(2)}) collective-permute-start(bf16[48,3072]{1,0:T(8,128)(2,1)S(1)} %get-tuple-element.74), channel_id=1, source_target_pairs={{0,2},{1,3},{2,0},{3,1},{4,6},{5,7},{6,4},{7,5},{8,10},{9,11},{10,... | collective-permute-start | bytes 884744 | tf_op jit(solution)/shard_map/ppermute | solution.py:660
  99.2 18.9 %collective-permute-start.8 = (bf16[48,3072]{1,0:T(8,128)(2,1)S(1)}, bf16[48,3072]{1,0:T(8,128)(2,1)S(1)}, u32[]{:S(2)}, u32[]{:S(2)}) collective-permute-start(bf16[48,3072]{1,0:T(8,128)(2,1)S(1)} %get-tuple-element.75), channel_id=1, source_target_pairs={{0,1},{1,2},{2,3},{3,0},{4,5},{5,6},{6,7},{7,4},{8,9},{9,10},{10,1... | collective-permute-start | bytes 884744 | tf_op jit(solution)/shard_map/ppermute | solution.py:652
  100.0 18.2 %collective-permute-start.9 = (bf16[48,3072]{1,0:T(8,128)(2,1)S(1)}, bf16[48,3072]{1,0:T(8,128)(2,1)S(1)}, u32[]{:S(2)}, u32[]{:S(2)}) collective-permute-start(bf16[48,3072]{1,0:T(8,128)(2,1)S(1)} %get-tuple-element.76), channel_id=1, source_target_pairs={{0,3},{1,0},{2,1},{3,2},{4,7},{5,4},{6,5},{7,6},{8,11},{9,8},{10,9... | collective-permute-start | bytes 884744 | tf_op jit(solution)/shard_map/ppermute | solution.py:656
  119.5 11.5 %collective-permute-start.10 = (bf16[48,3072]{1,0:T(8,128)(2,1)S(1)}, bf16[48,3072]{1,0:T(8,128)(2,1)S(1)}, u32[]{:S(2)}, u32[]{:S(2)}) collective-permute-start(bf16[48,3072]{1,0:T(8,128)(2,1)S(1)} %get-tuple-element.80.a0), channel_id=1, source_target_pairs={{0,16},{8,24},{16,0},{24,8},{1,17},{9,25},{17,1},{25,9},{2,18},{10... | collective-permute-start | bytes 884744 | tf_op jit(solution)/shard_map/ppermute | solution.py:660
  122.5 13.6 %collective-permute-start.12 = (bf16[48,3072]{1,0:T(8,128)(2,1)S(1)}, bf16[48,3072]{1,0:T(8,128)(2,1)S(1)}, u32[]{:S(2)}, u32[]{:S(2)}) collective-permute-start(bf16[48,3072]{1,0:T(8,128)(2,1)S(1)} %get-tuple-element.80.a0), channel_id=1, source_target_pairs={{0,8},{8,16},{16,24},{24,0},{1,9},{9,17},{17,25},{25,1},{2,10},{10... | collective-permute-start | bytes 884744 | tf_op jit(solution)/shard_map/ppermute | solution.py:652
  123.1 11.5 %collective-permute-start.11 = (bf16[48,3072]{1,0:T(8,128)(2,1)S(1)}, bf16[48,3072]{1,0:T(8,128)(2,1)S(1)}, u32[]{:S(2)}, u32[]{:S(2)}) collective-permute-start(bf16[48,3072]{1,0:T(8,128)(2,1)S(1)} %get-tuple-element.81.b0), channel_id=1, source_target_pairs={{0,64},{32,96},{64,0},{96,32},{1,65},{33,97},{65,1},{97,33},{2,66}... | collective-permute-start | bytes 884744 | tf_op jit(solution)/shard_map/ppermute | solution.py:660
  124.5 14.8 %collective-permute-start.13 = (bf16[48,3072]{1,0:T(8,128)(2,1)S(1)}, bf16[48,3072]{1,0:T(8,128)(2,1)S(1)}, u32[]{:S(2)}, u32[]{:S(2)}) collective-permute-start(bf16[48,3072]{1,0:T(8,128)(2,1)S(1)} %get-tuple-element.81.b0), channel_id=1, source_target_pairs={{0,32},{32,64},{64,96},{96,0},{1,33},{33,65},{65,97},{97,1},{2,34}... | collective-permute-start | bytes 884744 | tf_op jit(solution)/shard_map/ppermute | solution.py:652
  124.7 14.5 %collective-permute-start.14 = (bf16[48,3072]{1,0:T(8,128)(2,1)S(1)}, bf16[48,3072]{1,0:T(8,128)(2,1)S(1)}, u32[]{:S(2)}, u32[]{:S(2)}) collective-permute-start(bf16[48,3072]{1,0:T(8,128)(2,1)S(1)} %get-tuple-element.80.a0), channel_id=1, source_target_pairs={{0,24},{8,0},{16,8},{24,16},{1,25},{9,1},{17,9},{25,17},{2,26},{10... | collective-permute-start | bytes 884744 | tf_op jit(solution)/shard_map/ppermute | solution.py:656
  139.4 29.3 %collective-permute-start.16 = (bf16[4,48,3072]{2,1,0:T(8,128)(2,1)S(1)}, bf16[4,48,3072]{2,1,0:T(8,128)(2,1)S(1)}, u32[]{:S(2)}, u32[]{:S(2)}) collective-permute-start(bf16[4,48,3072]{2,1,0:T(8,128)(2,1)S(1)} %get-tuple-element.82.a0), channel_id=1, source_target_pairs={{0,32},{32,64},{64,96},{96,0},{1,33},{33,65},{65,97},{97,1},{2,34}... | collective-permute-start | bytes 3538952 | tf_op jit(solution)/shard_map/ppermute | solution.py:652
  139.5 29.2 %collective-permute-start.17 = (bf16[4,48,3072]{2,1,0:T(8,128)(2,1)S(1)}, bf16[4,48,3072]{2,1,0:T(8,128)(2,1)S(1)}, u32[]{:S(2)}, u32[]{:S(2)}) collective-permute-start(bf16[4,48,3072]{2,1,0:T(8,128)(2,1)S(1)} %get-tuple-element.83.b0), channel_id=1, source_target_pairs={{0,8},{8,16},{16,24},{24,0},{1,9},{9,17},{17,25},{25,1},{2,10},{10... | collective-permute-start | bytes 3538952 | tf_op jit(solution)/shard_map/ppermute | solution.py:652
  140.6 28.2 %collective-permute-start.18 = (bf16[4,48,3072]{2,1,0:T(8,128)(2,1)S(1)}, bf16[4,48,3072]{2,1,0:T(8,128)(2,1)S(1)}, u32[]{:S(2)}, u32[]{:S(2)}) collective-permute-start(bf16[4,48,3072]{2,1,0:T(8,128)(2,1)S(1)} %get-tuple-element.82.a0), channel_id=1, source_target_pairs={{0,96},{32,0},{64,32},{96,64},{1,97},{33,1},{65,33},{97,65},{2,98}... | collective-permute-start | bytes 3538952 | tf_op jit(solution)/shard_map/ppermute | solution.py:656
  143.0 27.6 %collective-permute-start.19 = (bf16[4,48,3072]{2,1,0:T(8,128)(2,1)S(1)}, bf16[4,48,3072]{2,1,0:T(8,128)(2,1)S(1)}, u32[]{:S(2)}, u32[]{:S(2)}) collective-permute-start(bf16[4,48,3072]{2,1,0:T(8,128)(2,1)S(1)} %get-tuple-element.83.b0), channel_id=1, source_target_pairs={{0,24},{8,0},{16,8},{24,16},{1,25},{9,1},{17,9},{25,17},{2,26},{10... | collective-permute-start | bytes 3538952 | tf_op jit(solution)/shard_map/ppermute | solution.py:656
  170.8 23.3 %collective-permute-start.20 = (bf16[2,48,3072]{2,1,0:T(8,128)(2,1)S(1)}, bf16[2,48,3072]{2,1,0:T(8,128)(2,1)S(1)}, u32[]{:S(2)}, u32[]{:S(2)}) collective-permute-start(bf16[2,48,3072]{2,1,0:T(8,128)(2,1)S(1)} %get-tuple-element.86), channel_id=1, source_target_pairs={{0,32},{32,64},{64,96},{96,0},{1,33},{33,65},{65,97},{97,1},{2,34}... | collective-permute-start | bytes 1769480 | tf_op jit(solution)/shard_map/ppermute | solution.py:652
  170.8 23.3 %collective-permute-start.21 = (bf16[2,48,3072]{2,1,0:T(8,128)(2,1)S(1)}, bf16[2,48,3072]{2,1,0:T(8,128)(2,1)S(1)}, u32[]{:S(2)}, u32[]{:S(2)}) collective-permute-start(bf16[2,48,3072]{2,1,0:T(8,128)(2,1)S(1)} %get-tuple-element.87), channel_id=1, source_target_pairs={{0,8},{8,16},{16,24},{24,0},{1,9},{9,17},{17,25},{25,1},{2,10},{10... | collective-permute-start | bytes 1769480 | tf_op jit(solution)/shard_map/ppermute | solution.py:652
  172.5 21.6 %collective-permute-start.22 = (bf16[2,48,3072]{2,1,0:T(8,128)(2,1)S(1)}, bf16[2,48,3072]{2,1,0:T(8,128)(2,1)S(1)}, u32[]{:S(2)}, u32[]{:S(2)}) collective-permute-start(bf16[2,48,3072]{2,1,0:T(8,128)(2,1)S(1)} %get-tuple-element.88), channel_id=1, source_target_pairs={{0,96},{32,0},{64,32},{96,64},{1,97},{33,1},{65,33},{97,65},{2,98}... | collective-permute-start | bytes 1769480 | tf_op jit(solution)/shard_map/ppermute | solution.py:656
  175.6 18.5 %collective-permute-start.23 = (bf16[2,48,3072]{2,1,0:T(8,128)(2,1)S(1)}, bf16[2,48,3072]{2,1,0:T(8,128)(2,1)S(1)}, u32[]{:S(2)}, u32[]{:S(2)}) collective-permute-start(bf16[2,48,3072]{2,1,0:T(8,128)(2,1)S(1)} %get-tuple-element.89), channel_id=1, source_target_pairs={{0,24},{8,0},{16,8},{24,16},{1,25},{9,1},{17,9},{25,17},{2,26},{10... | collective-permute-start | bytes 1769480 | tf_op jit(solution)/shard_map/ppermute | solution.py:656
  206.1 15.3 %collective-permute-start.24 = (bf16[2,48,3072]{2,1,0:T(8,128)(2,1)}, bf16[2,48,3072]{2,1,0:T(8,128)(2,1)S(1)}, u32[]{:S(2)}, u32[]{:S(2)}) collective-permute-start(bf16[2,48,3072]{2,1,0:T(8,128)(2,1)} %get-tuple-element.97), channel_id=1, source_target_pairs={{0,32},{32,64},{64,96},{96,0},{1,33},{33,65},{65,97},{97,1},{2,34}... | collective-permute-start | bytes 1769480 | tf_op jit(solution)/shard_map/ppermute | solution.py:652
  206.4 15.0 %collective-permute-start.25 = (bf16[2,48,3072]{2,1,0:T(8,128)(2,1)S(1)}, bf16[2,48,3072]{2,1,0:T(8,128)(2,1)S(1)}, u32[]{:S(2)}, u32[]{:S(2)}) collective-permute-start(bf16[2,48,3072]{2,1,0:T(8,128)(2,1)S(1)} %get-tuple-element.98), channel_id=1, source_target_pairs={{0,8},{8,16},{16,24},{24,0},{1,9},{9,17},{17,25},{25,1},{2,10},{10... | collective-permute-start | bytes 1769480 | tf_op jit(solution)/shard_map/ppermute | solution.py:652
  206.4 15.0 %collective-permute-start.26 = (bf16[2,48,3072]{2,1,0:T(8,128)(2,1)S(1)}, bf16[2,48,3072]{2,1,0:T(8,128)(2,1)S(1)}, u32[]{:S(2)}, u32[]{:S(2)}) collective-permute-start(bf16[2,48,3072]{2,1,0:T(8,128)(2,1)S(1)} %get-tuple-element.99), channel_id=1, source_target_pairs={{0,96},{32,0},{64,32},{96,64},{1,97},{33,1},{65,33},{97,65},{2,98}... | collective-permute-start | bytes 1769480 | tf_op jit(solution)/shard_map/ppermute | solution.py:656
  209.6 12.7 %collective-permute-start.27 = (bf16[2,48,3072]{2,1,0:T(8,128)(2,1)S(1)}, bf16[2,48,3072]{2,1,0:T(8,128)(2,1)S(1)}, u32[]{:S(2)}, u32[]{:S(2)}) collective-permute-start(bf16[2,48,3072]{2,1,0:T(8,128)(2,1)S(1)} %get-tuple-element.100), channel_id=1, source_target_pairs={{0,24},{8,0},{16,8},{24,16},{1,25},{9,1},{17,9},{25,17},{2,26},{10... | collective-permute-start | bytes 1769480 | tf_op jit(solution)/shard_map/ppermute | solution.py:656
  222.9 25.0 %collective-permute-start.28 = (bf16[4,48,3072]{2,1,0:T(8,128)(2,1)S(1)}, bf16[4,48,3072]{2,1,0:T(8,128)(2,1)S(1)}, u32[]{:S(2)}, u32[]{:S(2)}) collective-permute-start(bf16[4,48,3072]{2,1,0:T(8,128)(2,1)S(1)} %get-tuple-element.106), channel_id=1, source_target_pairs={{0,32},{32,64},{64,96},{96,0},{1,33},{33,65},{65,97},{97,1},{2,34}... | collective-permute-start | bytes 3538952 | tf_op jit(solution)/shard_map/ppermute | solution.py:652
  223.0 25.7 %collective-permute-start.29 = (bf16[4,48,3072]{2,1,0:T(8,128)(2,1)S(1)}, bf16[4,48,3072]{2,1,0:T(8,128)(2,1)S(1)}, u32[]{:S(2)}, u32[]{:S(2)}) collective-permute-start(bf16[4,48,3072]{2,1,0:T(8,128)(2,1)S(1)} %get-tuple-element.107), channel_id=1, source_target_pairs={{0,8},{8,16},{16,24},{24,0},{1,9},{9,17},{17,25},{25,1},{2,10},{10... | collective-permute-start | bytes 3538952 | tf_op jit(solution)/shard_map/ppermute | solution.py:652
  223.7 25.0 %collective-permute-start.30 = (bf16[4,48,3072]{2,1,0:T(8,128)(2,1)S(1)}, bf16[4,48,3072]{2,1,0:T(8,128)(2,1)S(1)}, u32[]{:S(2)}, u32[]{:S(2)}) collective-permute-start(bf16[4,48,3072]{2,1,0:T(8,128)(2,1)S(1)} %get-tuple-element.101.late), channel_id=1, source_target_pairs={{0,96},{32,0},{64,32},{96,64},{1,97},{33,1},{65,33},{97,65},{2,98}... | collective-permute-start | bytes 3538952 | tf_op jit(solution)/shard_map/ppermute | solution.py:656
  226.9 26.8 %collective-permute-start.31 = (bf16[4,48,3072]{2,1,0:T(8,128)(2,1)S(1)}, bf16[4,48,3072]{2,1,0:T(8,128)(2,1)S(1)}, u32[]{:S(2)}, u32[]{:S(2)}) collective-permute-start(bf16[4,48,3072]{2,1,0:T(8,128)(2,1)S(1)} %get-tuple-element.108), channel_id=1, source_target_pairs={{0,24},{8,0},{16,8},{24,16},{1,25},{9,1},{17,9},{25,17},{2,26},{10... | collective-permute-start | bytes 3538952 | tf_op jit(solution)/shard_map/ppermute | solution.py:656
  274.9 9.3 %collective-permute-start.39 = (bf16[16,6144]{1,0:T(8,128)(2,1)}, bf16[16,6144]{1,0:T(8,128)(2,1)}, u32[]{:S(2)}, u32[]{:S(2)}) collective-permute-start(bf16[16,6144]{1,0:T(8,128)(2,1)} %get-tuple-element.119), channel_id=1, source_target_pairs={{0,1},{1,2},{2,3},{3,0},{4,5},{5,6},{6,7},{7,4},{8,9},{9,10},{10,1... | collective-permute-start | bytes 589832 | tf_op jit(solution)/shard_map/ppermute | solution.py:652
  (20 other events, 187.6 us)
Sparse Core Ops, SparseCore 0:
  9.6 74.3 all-gather.1
  119.6 62.9 reduce-scatter.1
